TPU v7x, 32 devices: a whole 2x2x4 slice. The times are simulated.
32 devices in a mesh: dp: 8 (over z, x), hid: 4 (over y, core).
Axes of the slice: x: 2, y: 2, z: 4, core: 2. Of those that a mesh axis runs over, the one named last changes fastest.
Arguments:
- bag_offsets: int32 [8192], P('dp'), may hold values from 0 to 4095, as said below
- embed_ids: int32 [32768], P('dp'), may hold values from 0 to 3071
- block_owners: int32 [48], replicated, may hold values from 0 to 7, as said below
- cotangent: bfloat16 [8192, 768], P('dp', 'hid'), may hold values from -6 to 6
- table_w: float32 [6144, 512], P('dp', 'hid'), may hold values from -3 to 3
- table_m: float32 [6144, 512], P('dp', 'hid'), may hold values from -20 to 20
- table_v: float32 [6144, 512], P('dp', 'hid'), may hold values from 11 to 44
- table_ema: float32 [6144, 512], P('dp', 'hid'), may hold values from -3 to 3
- first_w: float32 [512, 1536], P('dp', 'hid'), may hold values from -0.25 to 0.25
- first_m: float32 [512, 1536], P('dp', 'hid'), may hold values from -160 to 160
- first_v: float32 [512, 1536], P('dp', 'hid'), may hold values from 737.28 to 2949.12
- first_ema: float32 [512, 1536], P('dp', 'hid'), may hold values from -0.25 to 0.25
- second_w: float32 [256, 1536], P('hid', 'dp'), may hold values from -0.375 to 0.375
- second_m: float32 [256, 1536], P('hid', 'dp'), may hold values from -160 to 160
- second_v: float32 [256, 1536], P('hid', 'dp'), may hold values from 737.28 to 2949.12
- second_ema: float32 [256, 1536], P('hid', 'dp'), may hold values from -0.375 to 0.375
- vector_w: float32 [3, 1536], P(None, 'hid')
- vector_m: float32 [3, 1536], P(None, 'hid'), may hold values from -160 to 160
- vector_v: float32 [3, 1536], P(None, 'hid'), may hold values from 737.28 to 2949.12
- vector_ema: float32 [3, 1536], P(None, 'hid')
- gate_w: float32 [512, 14], replicated, may hold values from -0.1875 to 0.1875
- gate_m: float32 [512, 14], replicated, may hold values from -2048 to 2048
- gate_v: float32 [512, 14], replicated, may hold values from 131072 to 524288
- gate_ema: float32 [512, 14], replicated, may hold values from -0.1875 to 0.1875
Outputs:
- mixed: bfloat16 [8192, 768], P('dp')
- table_w_new: float32 [6144, 512], P('dp', 'hid')
- table_m_new: float32 [6144, 512], P('dp', 'hid')
- table_v_new: float32 [6144, 512], P('dp', 'hid')
- table_ema_new: float32 [6144, 512], P('dp', 'hid')
- first_w_new: float32 [512, 1536], P('dp', 'hid')
- first_m_new: float32 [512, 1536], P('dp', 'hid')
- first_v_new: float32 [512, 1536], P('dp', 'hid')
- first_ema_new: float32 [512, 1536], P('dp', 'hid')
- second_w_new: float32 [256, 1536], P('hid', 'dp')
- second_m_new: float32 [256, 1536], P('hid', 'dp')
- second_v_new: float32 [256, 1536], P('hid', 'dp')
- second_ema_new: float32 [256, 1536], P('hid', 'dp')
- vector_w_new: float32 [3, 1536], P(None, 'hid')
- vector_m_new: float32 [3, 1536], P(None, 'hid')
- vector_v_new: float32 [3, 1536], P(None, 'hid')
- vector_ema_new: float32 [3, 1536], P(None, 'hid')
- gate_w_new: float32 [512, 14], replicated
- gate_m_new: float32 [512, 14], replicated
- gate_v_new: float32 [512, 14], replicated
- gate_ema_new: float32 [512, 14], replicated
Inputs may be any that keep to these rules, and one draw needn't show every extreme that they name: `bag_offsets`: each device's 1024 offsets rise strictly from 0; its last bag holds the single id at position 4095. `block_owners`: no owner holds more than 12 of the 48 blocks, and some owner holds exactly 12.
All inputs are finite; a program needn't handle non-finite values.
Results may differ from a plain program's by a relative error of at most 0.01.
Values may be sent and summed in bfloat16 or wider, within the bound.
No kernel may reach another device: no remote copies, remote signals or barrier semaphores. Data moves between devices by JAX's collectives and lax.ppermute only.
A program may use at most 128 MiB of HBM per device.

v0:
```python
import jax
import jax.numpy as jnp
from jax import lax
from jax.sharding import PartitionSpec as P

O = 256
EXPERTS = 6
STREAMS = 3
ROWS_BLOCK = 64
STEP = 5
CAP = 12


highest = lax.Precision.HIGHEST
norm_eps = 1e-05
adam_eps = 1e-08
decay_rate = 0.01
ema_decay = 0.9


def smooth(value):
    return jax.nn.gelu(value, approximate=False)


def slot_rows(block_owners, embed_ids, dp_count):
    owner_hot = (block_owners[:, None] == jnp.arange(dp_count, dtype=jnp.int32)[None, :]).astype(
        jnp.int32
    )
    rank_of = jnp.sum((jnp.cumsum(owner_hot, 0) - owner_hot) * owner_hot, 1)
    starts = (block_owners * CAP + rank_of) * ROWS_BLOCK
    block_of = embed_ids // ROWS_BLOCK
    block_hot = block_of[:, None] == jnp.arange(block_owners.shape[0], dtype=jnp.int32)[None, :]
    return jnp.sum(jnp.where(block_hot, starts[None, :], 0), 1) + embed_ids % ROWS_BLOCK


def coefficients(logits):
    count = logits.shape[0]
    task_zero = jax.nn.softmax(logits[:, 0:4], axis=1)
    task_one = jax.nn.softmax(logits[:, 4:8], axis=1)
    shared = jax.nn.softmax(logits[:, 8:14], axis=1)
    blank = jnp.zeros((count, 2), jnp.float32)
    column_zero = jnp.concatenate([task_zero[:, 0:2], blank, task_zero[:, 2:4]], 1)
    column_one = jnp.concatenate([blank, task_one[:, 0:2], task_one[:, 2:4]], 1)
    return jnp.stack([column_zero, column_one, shared], 2)


def softmax_back(logits, d_coef):
    pieces = []
    for first_col, last_col, members, stream in (
        (0, 4, (0, 1, 4, 5), 0),
        (4, 8, (2, 3, 4, 5), 1),
        (8, 14, (0, 1, 2, 3, 4, 5), 2),
    ):
        chances = jax.nn.softmax(logits[:, first_col:last_col], axis=1)
        upward = jnp.stack([d_coef[:, member, stream] for member in members], 1)
        pieces.append(chances * (upward - jnp.sum(chances * upward, 1, keepdims=True)))
    return jnp.concatenate(pieces, 1)


def adam_step(weight, moment, second, average, grad, rate):
    new_moment = 0.5 * moment + 0.5 * grad
    new_second = 0.5 * second + 0.5 * grad * grad
    correct = 1.0 - 0.5**STEP
    new_weight = weight - rate * (
        new_moment / correct / (jnp.sqrt(new_second / correct) + adam_eps) + decay_rate * weight
    )
    new_average = ema_decay * average + (1.0 - ema_decay) * new_weight
    return (new_weight, new_moment, new_second, new_average)


def per_device(
    bag_offsets,
    embed_ids,
    block_owners,
    cotangent,
    table_w,
    table_m,
    table_v,
    table_ema,
    first_w,
    first_m,
    first_v,
    first_ema,
    second_w,
    second_m,
    second_v,
    second_ema,
    vector_w,
    vector_m,
    vector_v,
    vector_ema,
    gate_w,
    gate_m,
    gate_v,
    gate_ema,
):
    dp_count = lax.axis_size("dp")
    rows_dev = bag_offsets.shape[0]
    ids_dev = embed_ids.shape[0]
    gathered = lax.all_gather(table_w.astype(jnp.bfloat16), "dp", axis=0, tiled=True)
    first_full, second_full = (
        lax.all_gather(first_w.astype(jnp.bfloat16), "dp", axis=0, tiled=True),
        lax.all_gather(second_w.astype(jnp.bfloat16), "dp", axis=1, tiled=True),
    )
    hid_local = first_full.shape[1] // EXPERTS
    out_local = vector_w.shape[1] // EXPERTS
    row_index = slot_rows(block_owners, embed_ids, dp_count)
    marks = jnp.zeros((ids_dev,), jnp.int32).at[bag_offsets].add(1)
    event_of = jnp.cumsum(marks) - 1
    pooled = jax.ops.segment_sum(
        gathered[row_index].astype(jnp.float32), event_of, rows_dev, indices_are_sorted=True
    )
    pooled_low = pooled.astype(jnp.bfloat16)
    gate_low = gate_w.astype(jnp.bfloat16)
    inputs = lax.all_gather(pooled_low, "hid", axis=1, tiled=True)
    pre = jnp.dot(inputs, first_full, preferred_element_type=jnp.float32) + vector_w[0][None, :]
    hidden = smooth(pre).astype(jnp.bfloat16).reshape(rows_dev, hid_local, EXPERTS)
    second_shaped = second_full.reshape(hid_local, O, EXPERTS)
    partial_value = jnp.einsum(
        "rhe,hoe->roe", hidden, second_shaped, preferred_element_type=jnp.float32
    )
    local_inner = lax.psum_scatter(
        partial_value.reshape(rows_dev, O * EXPERTS), "hid", scatter_dimension=1, tiled=True
    )
    local_inner = local_inner.reshape(rows_dev, out_local, EXPERTS)
    sum_first, sum_second = lax.psum(
        (jnp.sum(local_inner, 1), jnp.sum(local_inner * local_inner, 1)), "hid"
    )
    center = sum_first / O
    spread = sum_second / O - center * center
    inverse = lax.rsqrt(spread + norm_eps)
    normed = (local_inner - center[:, None, :]) * inverse[:, None, :]
    gain = vector_w[1].reshape(out_local, EXPERTS)
    shift = vector_w[2].reshape(out_local, EXPERTS)
    outputs = normed * gain[None] + shift[None]
    logits = jnp.dot(inputs, gate_low, preferred_element_type=jnp.float32)
    coef = coefficients(logits)
    whole = lax.all_gather(
        outputs.reshape(rows_dev, out_local * EXPERTS), "hid", axis=1, tiled=True
    )
    whole = whole.reshape(rows_dev, O, EXPERTS)
    mixed = jnp.einsum("roe,ret->rot", whole, coef, precision=highest).reshape(
        rows_dev, O * STREAMS
    )
    upstream = cotangent.astype(jnp.float32).reshape(rows_dev, out_local, STREAMS)
    d_out = jnp.einsum("rot,ret->roe", upstream, coef, precision=highest)
    d_coef = jnp.einsum("rot,roe->ret", upstream, outputs, precision=highest)
    d_norm = d_out * gain[None]
    d_coef, back_first, back_second = lax.psum(
        (d_coef, jnp.sum(d_norm, 1), jnp.sum(d_norm * normed, 1)), "hid"
    )
    d_inner = (
        d_norm - back_first[:, None, :] / O - normed * back_second[:, None, :] / O
    ) * inverse[:, None, :]
    d_gain = jnp.sum(d_out * normed, 0)
    d_shift = jnp.sum(d_out, 0)
    d_logits = softmax_back(logits, d_coef).astype(jnp.bfloat16)
    d_full = lax.all_gather(
        d_inner.astype(jnp.bfloat16).reshape(rows_dev, out_local * EXPERTS),
        "hid",
        axis=1,
        tiled=True,
    )
    d_full = d_full.reshape(rows_dev, O, EXPERTS)
    d_second = jnp.einsum(
        "rhe,roe->hoe", hidden, d_full, preferred_element_type=jnp.float32
    ).reshape(hid_local, O * EXPERTS)
    d_hidden = jnp.einsum(
        "roe,hoe->rhe", d_full, second_shaped, preferred_element_type=jnp.float32
    ).reshape(rows_dev, hid_local * EXPERTS)
    unused, gelu_back = jax.vjp(smooth, pre)
    d_pre = gelu_back(d_hidden)[0].astype(jnp.bfloat16)
    d_first = jnp.einsum("rd,rc->dc", inputs, d_pre, preferred_element_type=jnp.float32)
    d_bias = jnp.sum(d_pre.astype(jnp.float32), 0)
    d_gate = jnp.einsum("rd,rc->dc", inputs, d_logits, preferred_element_type=jnp.float32)
    d_inputs = jnp.einsum("rc,dc->rd", d_pre, first_full, preferred_element_type=jnp.float32)
    d_pooled = lax.psum_scatter(
        d_inputs.astype(jnp.bfloat16), "hid", scatter_dimension=1, tiled=True
    ).astype(jnp.float32)
    feat_local = d_pooled.shape[1]
    gate_rows = lax.dynamic_slice_in_dim(
        gate_low, lax.axis_index("hid") * feat_local, feat_local, 0
    )
    d_pooled = d_pooled + jnp.einsum(
        "rc,dc->rd", d_logits, gate_rows, preferred_element_type=jnp.float32
    )
    d_vector = jnp.stack([d_bias, d_gain.reshape(-1), d_shift.reshape(-1)])
    d_vector, d_gate = lax.psum((d_vector, d_gate), "dp")
    d_table = jax.ops.segment_sum(d_pooled[event_of], row_index, dp_count * CAP * ROWS_BLOCK)
    d_table = lax.psum_scatter(d_table, "dp", scatter_dimension=0, tiled=True)
    d_first, d_second = (
        lax.psum_scatter(d_first, "dp", scatter_dimension=0, tiled=True),
        lax.psum_scatter(d_second, "dp", scatter_dimension=1, tiled=True),
    )
    table_new = adam_step(table_w, table_m, table_v, table_ema, d_table, 0.3)
    first_new = adam_step(first_w, first_m, first_v, first_ema, d_first, 0.04)
    second_new = adam_step(second_w, second_m, second_v, second_ema, d_second, 0.06)
    vector_new = adam_step(vector_w, vector_m, vector_v, vector_ema, d_vector, 0.2)
    gate_new = adam_step(gate_w, gate_m, gate_v, gate_ema, d_gate, 0.03)
    return (
        mixed.astype(jnp.bfloat16),
        table_new[0],
        table_new[1],
        table_new[2],
        table_new[3],
        first_new[0],
        first_new[1],
        first_new[2],
        first_new[3],
        second_new[0],
        second_new[1],
        second_new[2],
        second_new[3],
        vector_new[0],
        vector_new[1],
        vector_new[2],
        vector_new[3],
        gate_new[0],
        gate_new[1],
        gate_new[2],
        gate_new[3],
    )


def solution(mesh):
    return jax.shard_map(
        per_device,
        mesh=mesh,
        in_specs=(
            P("dp"),
            P("dp"),
            P(),
            P("dp", "hid"),
            P("dp", "hid"),
            P("dp", "hid"),
            P("dp", "hid"),
            P("dp", "hid"),
            P("dp", "hid"),
            P("dp", "hid"),
            P("dp", "hid"),
            P("dp", "hid"),
            P("hid", "dp"),
            P("hid", "dp"),
            P("hid", "dp"),
            P("hid", "dp"),
            P(None, "hid"),
            P(None, "hid"),
            P(None, "hid"),
            P(None, "hid"),
            P(),
            P(),
            P(),
            P(),
        ),
        out_specs=(
            P("dp", None),
            P("dp", "hid"),
            P("dp", "hid"),
            P("dp", "hid"),
            P("dp", "hid"),
            P("dp", "hid"),
            P("dp", "hid"),
            P("dp", "hid"),
            P("dp", "hid"),
            P("hid", "dp"),
            P("hid", "dp"),
            P("hid", "dp"),
            P("hid", "dp"),
            P(None, "hid"),
            P(None, "hid"),
            P(None, "hid"),
            P(None, "hid"),
            P(),
            P(),
            P(),
            P(),
        ),
        check_vma=False,
    )
```

profile of v0, /device:TPU:0, one launch (start us, length us, event | category | flops | bytes accessed | tf_op | source)
XLA Modules:
  0.0 802.4 jit_solution(9580325658722919008)
XLA Ops:
  7.2 1.7 convert_element_type.47
  9.7 7.6 scatter_custom_fusion
  23.1 34.6 %all-gather.6.cloned.1.call-done = bf16[6144,128]{1,0:T(8,128)(2,1)} async-done(((bf16[768,128]{1,0:T(8,128)(2,1)}), bf16[6144,128]{1,0:T(8,128)(2,1)}) %all-gather.6.cloned.1.call-update) | async-done | bytes 1572880 | tf_op jit(solution)/shard_map/all_gather | solution.py:100
  57.7 50.7 %scatter_custom_fusion.1 = f32[1024,128]{1,0:T(8,128)S(1)} fusion(s32[4096]{0:T(1024)S(1)} %bitcast.104, f32[]{:T(128)} %constant.57.clone.1, bf16[6144,128]{1,0:T(8,128)(2,1)} %all-gather.6.cloned.1.call-done, s32[4096]{0:T(1024)S(1)} %get-tuple-element.208), kind=kCustom, calls=%fused_computation.25 | custom fusion | flops 1048576 | bytes 2113540 | tf_op jit(solution)/shard_map/scatter-add | solution.py:110
  109.3 30.7 %all-gather = bf16[8,192,64]{1,2,0:T(8,128)(2,1)S(1)} all-gather(bf16[1,192,64]{1,2,0:T(8,128)(2,1)S(1)} %convert_bitcast_fusion), channel_id=1, replica_groups=mesh['dp'=8,'hid'=4] {'dp'}, dimensions={0}, use_global_device_ids=true | all-gather | bytes 221184 | tf_op jit(solution)/shard_map/all_gather | solution.py:103
  141.2 31.2 %all_gather.20 = bf16[512,384]{1,0:T(8,128)(2,1)S(1)} all-gather(bf16[64,384]{1,0:T(8,128)(2,1)S(1)} %convert_element_type.51), channel_id=1, replica_groups=mesh['dp'=8,'hid'=4] {'dp'}, dimensions={0}, use_global_device_ids=true | all-gather | bytes 442368 | tf_op jit(solution)/shard_map/all_gather | solution.py:102
  172.4 6.9 multiply_convert_fusion.1
  180.9 7.0 copy.238
  187.9 8.3 %reshape.159 = f32[1024,1536]{0,1:T(8,128)} reshape(f32[1024,256,6]{0,2,1:T(8,128)} %copy.238) | data formatting | bytes 12582912 | tf_op jit(solution)/shard_map/reshape | solution.py:123
  197.4 1.6 copy.247
  200.1 53.1 %reduce-scatter.10.cloned.1.call-done = f32[1024,384]{0,1:T(8,128)} async-done(((f32[1024,1536]{0,1:T(8,128)}), f32[1024,384]{0,1:T(8,128)}) %reduce-scatter.10.cloned.1.call-update) | async-done | bytes 1572880 | tf_op jit(solution)/shard_map/reduce_scatter | solution.py:122
  253.1 1.5 reshape.160
  254.9 3.3 copy.251
  258.2 10.7 %all-reduce.3 = (f32[1024,6]{0,1:T(8,128)S(1)}, f32[1024,6]{0,1:T(8,128)S(1)}) all-reduce(f32[1024,6]{0,1:T(8,128)S(1)} %get-tuple-element.166, f32[1024,6]{0,1:T(8,128)S(1)} %get-tuple-element.165), channel_id=1, replica_groups=mesh['dp'=8,'hid'=4] {'hid'}, use_global_device_ids=true, to_apply=%region_11.12 | all-reduce | flops 12288 | bytes 98304 | tf_op jit(solution)/shard_map/psum | solution.py:126
  269.8 7.4 fusion.1
  277.4 52.7 %all-reduce.6.cloned.1.call-done = f32[1024,6,3]{1,2,0:T(4,128)} async-done(((f32[1024,6,3]{1,2,0:T(4,128)}), f32[1024,6,3]{1,2,0:T(4,128)}) %all-reduce.6.cloned.1.call-update) | async-done | bytes 73744 | tf_op jit(solution)/shard_map/psum | solution.py:149
  330.1 77.0 %slice_reduce_fusion.13 = (f32[1024]{0:T(1024)S(1)}, f32[1024]{0:T(1024)S(1)}, f32[1024]{0:T(1024)S(1)}, f32[1024]{0:T(1024)S(1)}, f32[1024]{0:T(1024)S(1)}, /*i...) fusion(f32[1024,6,3]{1,2,0:T(4,128)} %all-reduce.6.cloned.1.cal, ...), kind=kLoop, calls=%fused_computation.71 | loop fusion | bytes 114688 | tf_op jit(solution)/shard_map/slice | solution.py:55
  409.5 14.7 %fusion = (f32[64,6]{0,1:T(8,128)}, f32[1024,6]{1,0:T(8,128)}, f32[1024,6]{1,0:T(8,128)}, f32[64,6]{0,1:T(8,128)}, f32[1024,6,64]{2,1,0:T(8,128)}) fusion(f32[1024,64,6]{1,2,0:T(8,128)} %copy.251, f32[1024,6]{1,0:T(8,128)S(1)} %copy.241, f32[1024,6]{1,0:T(8,128)S(1)} %copy.239, f32[64,6]{0,1:T(8,128)} %copy-done.63, f32[1024,6,3]{1,2,0:T(4,128)S(1)} %copy.244, ...), kind=kOutput, calls=%fused_computation.8 | convolution fusion | flops 17681664 | bytes 3715584 | tf_op jit(solution)/shard_map/rot,ret->roe/dot_general | solution.py:146
  425.4 17.5 %all-reduce.2 = (f32[1024,6]{1,0:T(8,128)}, f32[1024,6]{0,1:T(8,128)S(1)}) all-reduce(f32[1024,6]{1,0:T(8,128)} %get-tuple-element.148, f32[1024,6]{0,1:T(8,128)S(1)} %copy.249), channel_id=1, replica_groups=mesh['dp'=8,'hid'=4] {'hid'}, use_global_device_ids=true, to_apply=%region_21.22 | all-reduce | flops 12288 | bytes 98304 | tf_op jit(solution)/shard_map/psum | solution.py:149
  444.0 7.3 multiply_convert_fusion
  451.3 2.5 copy.252
  455.1 29.2 %all-gather.12.cloned.1.call-done = bf16[1024,1536]{0,1:T(8,128)(2,1)} async-done(((bf16[1024,384]{0,1:T(8,128)(2,1)}), bf16[1024,1536]{0,1:T(8,128)(2,1)}) %all-gather.12.cloned.1.call-update) | async-done | bytes 3145744 | tf_op jit(solution)/shard_map/all_gather | solution.py:158
  484.3 6.4 reshape.164
  490.7 5.4 copy.253
  497.2 2.3 copy.255
  499.5 2.6 reshape.165
  502.1 3.8 convert_reduce_fusion
  506.8 1.7 convolution_convert_fusion.1
  508.6 2.3 copy.265
  510.9 2.0 convolution_bitcast_fusion.2
  515.1 1.6 fusion.60
  517.0 1.4 mul.326
  518.7 1.4 sub.122
  520.1 3.8 multiply_add_fusion
  524.8 11.1 %reduce-scatter.16.cloned.1.call-done = bf16[128,1024]{1,0:T(8,128)(2,1)} async-done(((bf16[512,1024]{1,0:T(8,128)(2,1)}), bf16[128,1024]{1,0:T(8,128)(2,1)}) %reduce-scatter.16.cloned.1.call-update) | async-done | bytes 262160
  538.0 36.4 %scatter_custom_fusion.2 = f32[6144,128]{1,0:T(8,128)} fusion(s32[4096]{0:T(1024)} %get-tuple-element.209, f32[1024,128]{1,0:T(8,128)S(1)} %convolution_add_fusion.1, s32[4096]{0:T(1024)S(1)} %broadcast_clamp_fusion, f32[]{:T(128)} %constant.57.clone.1), kind=kCustom, calls=%fused_computation.18 | custom fusion | flops 524288 | bytes 3146240 | tf_op jit(solution)/shard_map/scatter-add | solution.py:189
  575.8 37.7 %all-reduce.1 = (f32[3,384]{1,0:T(4,128)S(1)}, f32[512,14]{0,1:T(8,128)S(1)}) all-reduce(f32[3,384]{1,0:T(4,128)S(1)} %pad_maximum_fusion.6, f32[512,14]{0,1:T(8,128)S(1)} %fusion.33), channel_id=1, replica_groups=mesh['dp'=8,'hid'=4] {'dp'}, use_global_device_ids=true, to_apply=%region_34.35 | all-reduce | flops 8320 | bytes 66560 | tf_op jit(solution)/shard_map/psum | solution.py:188
  616.6 50.3 %reduce-scatter.14.cloned.1.call-done = f32[64,384]{1,0:T(8,128)} async-done(((f32[512,384]{1,0:T(8,128)}), f32[64,384]{1,0:T(8,128)}) %reduce-scatter.14.cloned.1.call-update) | async-done | bytes 98320 | tf_op jit(solution)/shard_map/reduce_scatter | solution.py:192
  666.9 1.7 multiply_add_fusion.4
  668.6 46.0 %all-gather.10.cloned.1.call-done = f32[1024,1536]{0,1:T(8,128)} async-done(((f32[1024,384]{0,1:T(8,128)}), f32[1024,1536]{0,1:T(8,128)}) %all-gather.10.cloned.1.call-update) | async-done | bytes 6291472 | tf_op jit(solution)/shard_map/all_gather | solution.py:138
  714.5 7.8 reshape.161
  722.4 9.5 %copy.243 = f32[1024,256,6]{1,2,0:T(8,128)} copy(f32[1024,256,6]{0,2,1:T(8,128)} %reshape.161) | data formatting | bytes 12582912 | tf_op jit(solution)/shard_map/reshape | solution.py:141
  731.8 11.4 %convolution_convert_fusion = bf16[1024,256,3]{1,2,0:T(4,128)(2,1)} fusion(f32[1024,256,6]{1,2,0:T(8,128)} %copy.243, f32[1024,6,3]{1,2,0:T(4,128)S(1)} %copy-done.3), kind=kOutput, calls=%fused_computation.27 | convolution fusion | flops 57409536 | bytes 7938048 | tf_op jit(solution)/shard_map/roe,ret->rot/dot_general | solution.py:142
  743.2 4.6 copy.245
  747.8 2.5 convert_element_type.56
  750.4 2.7 copy.264
  753.1 39.8 %reduce-scatter.12.cloned.1.call-done = f32[768,128]{1,0:T(8,128)} async-done(((f32[6144,128]{1,0:T(8,128)}), f32[768,128]{1,0:T(8,128)}) %reduce-scatter.12.cloned.1.call-update) | async-done | bytes 393232 | tf_op jit(solution)/shard_map/reduce_scatter | solution.py:190
  792.9 2.4 multiply_add_fusion.2
  (245 shorter events, 31.2 us)
Async XLA Ops:
  7.2 50.5 %all-gather.6.cloned.1.call-start = ((), (), s32[]{:S(2)}) async-start(), calls=%async_computation.5 | async-start | bytes 1769472 | tf_op jit(solution)/shard_map/all_gather | solution.py:100
  9.0 163.4 %all-gather.8.cloned.1.call-start = ((), (), s32[]{:S(2)}) async-start(), calls=%async_computation.6 | async-start | bytes 1310720 | tf_op jit(solution)/shard_map/all_gather | solution.py:115
  21.8 87.4 %copy-start.36 = (s32[32,128]{1,0:T(8,128)}, s32[32,128]{1,0:T(8,128)S(1)}, u32[]{:S(2)}) copy-start(s32[32,128]{1,0:T(8,128)S(1)} %get-tuple-element.217) | copy-start | bytes 49156
  57.7 51.5 %copy-start.14 = (f32[64,384]{1,0:T(8,128)S(1)}, f32[64,384]{1,0:T(8,128)}, u32[]{:S(2)}) copy-start(f32[64,384]{1,0:T(8,128)} %param.32) | copy-start | bytes 294916
  57.7 51.5 %copy-start.20 = (f32[64,192]{1,0:T(8,128)S(1)}, f32[64,192]{1,0:T(8,128)}, u32[]{:S(2)}) copy-start(f32[64,192]{1,0:T(8,128)} %param.36) | copy-start | bytes 147460
  109.2 143.9 %reduce-scatter.10.cloned.1.call-start = ((), (), s32[]{:S(2)}) async-start(), calls=%async_computation.7 | async-start | bytes 7864320 | tf_op jit(solution)/shard_map/reduce_scatter | solution.py:122
  141.2 55.1 %copy-start.59 = (f32[384]{0:T(512)}, f32[384]{0:T(512)S(1)}, u32[]{:S(2)}) copy-start(f32[384]{0:T(512)S(1)} %get-tuple-element.171) | copy-start | bytes 4612
  141.2 55.3 %copy-start.61 = (f32[384]{0:T(512)}, f32[384]{0:T(512)S(1)}, u32[]{:S(2)}) copy-start(f32[384]{0:T(512)S(1)} %get-tuple-element.173) | copy-start | bytes 4612
  172.4 6.9 copy-start.8
  196.2 2.8 copy-start.26
  196.2 3.4 copy-start
  196.2 133.8 %all-reduce.6.cloned.1.call-start = ((), (), s32[]{:S(2)}) async-start(), calls=%async_computation.10 | async-start | bytes 4194304 | tf_op jit(solution)/shard_map/psum | solution.py:149
  196.5 73.3 %copy-start.63 = (f32[64,6]{0,1:T(8,128)}, f32[64,6]{0,1:T(8,128)S(1)}, u32[]{:S(2)}) copy-start(f32[64,6]{0,1:T(8,128)S(1)} %copy.248) | copy-start | bytes 4612
  269.0 8.3 %copy-start.18 = (f32[1024,6]{0,1:T(8,128)}, f32[1024,6]{0,1:T(8,128)S(1)}, u32[]{:S(2)}) copy-start(f32[1024,6]{0,1:T(8,128)S(1)} %get-tuple-element.215) | copy-start | bytes 73732
  277.3 207.0 %all-gather.12.cloned.1.call-start = ((), (), s32[]{:S(2)}) async-start(), calls=%async_computation.9 | async-start | bytes 3932160 | tf_op jit(solution)/shard_map/all_gather | solution.py:158
  277.4 130.7 %copy-start.73 = (f32[6]{0:T(128)S(1)}, f32[6]{0:T(128)}, u32[]{:S(2)}) copy-start(f32[6]{0:T(128)} %pad.19.clone) | copy-start | bytes 76
  409.5 14.7 %copy-start.2 = (f32[1024,6,3]{1,2,0:T(4,128)}, f32[1024,6,3]{1,2,0:T(4,128)S(1)}, u32[]{:S(2)}) copy-start(f32[1024,6,3]{1,2,0:T(4,128)S(1)} %copy.244) | copy-start | bytes 221188
  424.2 19.8 %copy-start.64 = (f32[64,6]{0,1:T(8,128)S(1)}, f32[64,6]{0,1:T(8,128)}, u32[]{:S(2)}) copy-start(f32[64,6]{0,1:T(8,128)} %copy-done.63) | copy-start | bytes 4612
  455.1 80.8 %reduce-scatter.16.cloned.1.call-start = ((), (), s32[]{:S(2)}) async-start(), calls=%async_computation.13 | async-start | bytes 1310720
  502.1 4.7 copy-start.9
  510.9 104.0 %reduce-scatter.18.cloned.1.call-start = ((), (), s32[]{:S(2)}) async-start(), calls=%async_computation.14 | async-start | bytes 884736
  513.3 1.5 copy-start.1
  513.3 1.7 copy-start.5
  514.4 2.4 copy-start.19
  514.4 152.5 %reduce-scatter.14.cloned.1.call-start = ((), (), s32[]{:S(2)}) async-start(), calls=%async_computation.12 | async-start | bytes 884736 | tf_op jit(solution)/shard_map/reduce_scatter | solution.py:192
  516.7 197.8 %all-gather.10.cloned.1.call-start = ((), (), s32[]{:S(2)}) async-start(), calls=%async_computation.8 | async-start | bytes 7864320 | tf_op jit(solution)/shard_map/all_gather | solution.py:138
  524.0 268.9 %reduce-scatter.12.cloned.1.call-start = ((), (), s32[]{:S(2)}) async-start(), calls=%async_computation.11 | async-start | bytes 3538944 | tf_op jit(solution)/shard_map/reduce_scatter | solution.py:190
  574.4 39.1 %copy-start.58 = (f32[3,384]{1,0:T(4,128)S(1)}, f32[3,384]{1,0:T(4,128)}, u32[]{:S(2)}) copy-start(f32[3,384]{1,0:T(4,128)} %param.40) | copy-start | bytes 13828
  574.4 39.1 %copy-start.68 = (f32[3,384]{1,0:T(4,128)S(1)}, f32[3,384]{1,0:T(4,128)}, u32[]{:S(2)}) copy-start(f32[3,384]{1,0:T(4,128)} %param.43) | copy-start | bytes 13828
  574.4 39.1 %copy-start.69 = (f32[3,384]{1,0:T(4,128)S(1)}, f32[3,384]{1,0:T(4,128)}, u32[]{:S(2)}) copy-start(f32[3,384]{1,0:T(4,128)} %param.41) | copy-start | bytes 13828
  574.4 39.1 %copy-start.70 = (f32[3,384]{1,0:T(4,128)S(1)}, f32[3,384]{1,0:T(4,128)}, u32[]{:S(2)}) copy-start(f32[3,384]{1,0:T(4,128)} %param.42) | copy-start | bytes 13828
  574.4 39.8 %copy-start.27 = (f32[512,14]{0,1:T(8,128)S(1)}, f32[512,14]{0,1:T(8,128)}, u32[]{:S(2)}) copy-start(f32[512,14]{0,1:T(8,128)} %param.44) | copy-start | bytes 86020
  574.5 39.7 %copy-start.54 = (f32[512,14]{0,1:T(8,128)S(1)}, f32[512,14]{0,1:T(8,128)}, u32[]{:S(2)}) copy-start(f32[512,14]{0,1:T(8,128)} %param.47) | copy-start | bytes 86020
  574.5 39.7 %copy-start.55 = (f32[512,14]{0,1:T(8,128)S(1)}, f32[512,14]{0,1:T(8,128)}, u32[]{:S(2)}) copy-start(f32[512,14]{0,1:T(8,128)} %param.45) | copy-start | bytes 86020
  574.5 39.7 %copy-start.56 = (f32[512,14]{0,1:T(8,128)S(1)}, f32[512,14]{0,1:T(8,128)}, u32[]{:S(2)}) copy-start(f32[512,14]{0,1:T(8,128)} %param.46) | copy-start | bytes 86020
  574.5 41.3 %copy-start.21 = (f32[64,192]{1,0:T(8,128)S(1)}, f32[64,192]{1,0:T(8,128)}, u32[]{:S(2)}) copy-start(f32[64,192]{1,0:T(8,128)} %param.36) | copy-start | bytes 147460
  574.5 41.3 %copy-start.32 = (f32[64,192]{1,0:T(8,128)S(1)}, f32[64,192]{1,0:T(8,128)}, u32[]{:S(2)}) copy-start(f32[64,192]{1,0:T(8,128)} %param.39) | copy-start | bytes 147460
  574.5 41.3 %copy-start.33 = (f32[64,192]{1,0:T(8,128)S(1)}, f32[64,192]{1,0:T(8,128)}, u32[]{:S(2)}) copy-start(f32[64,192]{1,0:T(8,128)} %param.37) | copy-start | bytes 147460
  574.5 41.3 %copy-start.34 = (f32[64,192]{1,0:T(8,128)S(1)}, f32[64,192]{1,0:T(8,128)}, u32[]{:S(2)}) copy-start(f32[64,192]{1,0:T(8,128)} %param.38) | copy-start | bytes 147460
  574.6 92.3 %copy-start.15 = (f32[64,384]{1,0:T(8,128)S(1)}, f32[64,384]{1,0:T(8,128)}, u32[]{:S(2)}) copy-start(f32[64,384]{1,0:T(8,128)} %param.32) | copy-start | bytes 294916
  574.6 92.3 %copy-start.28 = (f32[64,384]{1,0:T(8,128)S(1)}, f32[64,384]{1,0:T(8,128)}, u32[]{:S(2)}) copy-start(f32[64,384]{1,0:T(8,128)} %param.35) | copy-start | bytes 294916
  574.6 92.3 %copy-start.29 = (f32[64,384]{1,0:T(8,128)S(1)}, f32[64,384]{1,0:T(8,128)}, u32[]{:S(2)}) copy-start(f32[64,384]{1,0:T(8,128)} %param.33) | copy-start | bytes 294916
  574.6 92.3 %copy-start.30 = (f32[64,384]{1,0:T(8,128)S(1)}, f32[64,384]{1,0:T(8,128)}, u32[]{:S(2)}) copy-start(f32[64,384]{1,0:T(8,128)} %param.34) | copy-start | bytes 294916
  722.4 9.5 %copy-start.3 = (f32[1024,6,3]{1,2,0:T(4,128)S(1)}, f32[1024,6,3]{1,2,0:T(4,128)}, u32[]{:S(2)}) copy-start(f32[1024,6,3]{1,2,0:T(4,128)} %copy-done.2) | copy-start | bytes 221188
  750.3 42.6 %copy-start.7 = (f32[768,128]{1,0:T(8,128)S(1)}, f32[768,128]{1,0:T(8,128)}, u32[]{:S(2)}) copy-start(f32[768,128]{1,0:T(8,128)} %param.28) | copy-start | bytes 1179652
  750.3 42.6 %copy-start.11 = (f32[768,128]{1,0:T(8,128)S(1)}, f32[768,128]{1,0:T(8,128)}, u32[]{:S(2)}) copy-start(f32[768,128]{1,0:T(8,128)} %param.31) | copy-start | bytes 1179652
  750.4 42.6 %copy-start.12 = (f32[768,128]{1,0:T(8,128)S(1)}, f32[768,128]{1,0:T(8,128)}, u32[]{:S(2)}) copy-start(f32[768,128]{1,0:T(8,128)} %param.29) | copy-start | bytes 1179652
  750.4 42.6 %copy-start.13 = (f32[768,128]{1,0:T(8,128)S(1)}, f32[768,128]{1,0:T(8,128)}, u32[]{:S(2)}) copy-start(f32[768,128]{1,0:T(8,128)} %param.30) | copy-start | bytes 1179652
  (36 other events, 32.3 us)
Sparse Core Ops, SparseCore 0:
  10.8 46.9 all-gather.5
  109.3 16.1 all-gather.7
  196.3 56.7 reduce-scatter.9
  277.4 52.6 all-reduce.5
  455.2 29.0 all-gather.11
  511.0 24.8 reduce-scatter.15
  539.5 62.4 reduce-scatter.17
  605.3 61.4 reduce-scatter.13
  669.1 45.4 all-gather.9
  718.4 74.4 reduce-scatter.11
where the time goes:
time: 805 us; the launch traced here: 802 us
  waiting for transfers between devices  317 us (39%)
  local copies, waits for them, and re-layouts  166 us (21%)
  blocking collectives  128 us (16%)
  other arithmetic  126 us (16%)
  matrix products  49.7 us (6%)
  between operations  15.6 us (2%)
    slice x1, local copies, waits for them, and re-layouts, softmax_back(): upward = jnp.stack([d_coef[:, member, stream] for member in members], 1)  77 us
    reduce_scatter x1, waiting for transfers between devices, per_device(): lax.psum_scatter(partial_value.reshape(rows_dev, O * EXPERTS), 'hid', sca...  53.1 us
    psum x1, waiting for transfers between devices, per_device(): lax.psum((d_coef, jnp.sum(d_norm, 1), jnp.sum(d_norm * normed, 1)), 'hid')  52.7 us
    scatter-add x1, other arithmetic, per_device(): jax.ops.segment_sum(gathered[row_index].astype(jnp.float32), event_of, ro...  50.7 us
    reduce_scatter x1, waiting for transfers between devices, per_device(): lax.psum_scatter(d_first, 'dp', scatter_dimension=0, tiled=True)  50.3 us
    all_gather x1, waiting for transfers between devices, per_device(): lax.all_gather(outputs.reshape(rows_dev, out_local * EXPERTS), 'hid', axi...  46 us
    reduce_scatter x1, waiting for transfers between devices, per_device(): d_table = lax.psum_scatter(d_table, 'dp', scatter_dimension=0, tiled=True)  39.8 us
    psum x1, blocking collectives, per_device(): d_vector, d_gate = lax.psum((d_vector, d_gate), 'dp')  37.7 us
  transfers between devices with their start and end apart: 10, of which 8 were waited for; matrix products, arithmetic and copies ran while one was open for 14% of the time, Pallas kernels for 0%

commit v1 on v0

v1 whole, which is shorter than its diff:
```python
import functools

import jax
import jax.numpy as jnp
from jax import lax
from jax.experimental import pallas as pl
from jax.experimental.pallas import tpu as pltpu
from jax.sharding import PartitionSpec as P

D = 512
H = 256
O = 256
EXPERTS = 6
STREAMS = 3
ROWS_BLOCK = 64
STEP = 5
CAP = 12
HALF = 128
IDS_STEP = 256
EVENTS_STEP = 256

norm_eps = 1e-05
adam_eps = 1e-08
decay_rate = 0.01
ema_decay = 0.9

bf16 = jnp.bfloat16
f32 = jnp.float32
MIB = 1 << 20

STREAM_EXPERTS = ((0, 1, 4, 5), (2, 3, 4, 5), (0, 1, 2, 3, 4, 5))
STREAM_COLS = (0, 4, 8)

VMEM = pl.BlockSpec(memory_space=pltpu.VMEM)
SMEM = pl.BlockSpec(memory_space=pltpu.SMEM)


def shape(dims, dtype):
    return jax.ShapeDtypeStruct(tuple(dims), dtype)


def nn(a, b):
    return lax.dot_general(a, b, (((1,), (0,)), ((), ())), preferred_element_type=f32)


def nt(a, b):
    return lax.dot_general(a, b, (((1,), (1,)), ((), ())), preferred_element_type=f32)


def tn(a, b):
    return lax.dot_general(a, b, (((0,), (0,)), ((), ())), preferred_element_type=f32)


def call(kernel, out_shape, args, in_specs=None, scratch=(), vmem=24, flops=0, moved=0):
    single = not isinstance(out_shape, (list, tuple))
    outs = [out_shape] if single else list(out_shape)
    result = pl.pallas_call(
        kernel,
        out_shape=outs,
        in_specs=in_specs or [VMEM] * len(args),
        out_specs=[VMEM] * len(outs),
        scratch_shapes=list(scratch),
        compiler_params=pltpu.CompilerParams(vmem_limit_bytes=vmem * MIB),
        cost_estimate=pl.CostEstimate(flops=flops, bytes_accessed=moved, transcendentals=0),
    )(*args)
    return result[0] if single else result


def swap(value, axis, mask):
    count = lax.axis_size(axis)
    return lax.ppermute(value, axis, [(i, i ^ mask) for i in range(count)])


def inner_size(dp_count):
    return 1 << ((dp_count.bit_length() - 1) // 2)


def gather_dp(value):
    count = lax.axis_size("dp")
    inner = inner_size(count)
    far = {0: value}
    for step in reversed(range(1, count // inner)):
        far[step] = swap(value, "dp", step * inner)
    pieces = [None] * count
    for step in [0] + list(reversed(range(1, count // inner))):
        pieces[step * inner] = far[step]
        for near in range(1, inner):
            pieces[step * inner + near] = swap(far[step], "dp", near)
    return pieces


def low_kernel(table_ref, first_ref, second_ref, cot_ref, *outs, hid):
    table_out, weight_out = outs[0], outs[1]
    table_out[...] = table_ref[...].astype(bf16)
    rows = first_ref.shape[0]
    weight_out[0:rows, :] = first_ref[...].astype(bf16)
    second = second_ref[...]
    fold = weight_out.shape[0] - rows
    weight_out[rows:, :] = jnp.concatenate(
        [second[i * fold : (i + 1) * fold, :] for i in range(second.shape[0] // fold)], axis=1
    ).astype(bf16)
    me = lax.axis_index("hid")
    width = outs[2].shape[1]
    for m in range(hid):
        start = pl.multiple_of((me ^ m) * width, width)
        outs[2 + m][...] = cot_ref[:, pl.ds(start, width)]


def counts_kernel(offs_ref, ids_ref, off_ref, nxt_ref, c_ref, idb, acc):
    id_rows, lanes = ids_ref.shape
    events, vocab = c_ref.shape
    per = IDS_STEP // lanes
    idt = ids_ref[...].T
    for q in range(id_rows):
        idb[q // per, (q % per) * lanes : (q % per + 1) * lanes, :] = jnp.broadcast_to(
            idt[:, q : q + 1], (lanes, HALF)
        )
    offt = off_ref[...].T
    nxtt = nxt_ref[...].T
    cols = EVENTS_STEP // lanes
    width = 512
    for ec in range(events // EVENTS_STEP):
        first = jnp.concatenate([offt[:, ec * cols + i : ec * cols + i + 1] for i in range(cols)], 0)
        last = jnp.concatenate([nxtt[:, ec * cols + i : ec * cols + i + 1] for i in range(cols)], 0)
        acc[...] = jnp.zeros_like(acc)
        low = offs_ref[ec * EVENTS_STEP]
        if (ec + 1) * EVENTS_STEP < events:
            high = offs_ref[(ec + 1) * EVENTS_STEP]
        else:
            high = jnp.int32(id_rows * lanes)

        def body(step, carry):
            place = step * IDS_STEP + lax.broadcasted_iota(jnp.int32, (EVENTS_STEP, IDS_STEP), 1)
            member = jnp.where((place >= first) & (place < last), 1.0, 0.0).astype(bf16)
            ids = idb[step]
            for v in range(vocab // width):
                hot = jnp.concatenate(
                    [
                        jnp.where(
                            ids
                            == lax.broadcasted_iota(jnp.int32, (IDS_STEP, HALF), 1)
                            + (v * width + i * HALF),
                            1.0,
                            0.0,
                        ).astype(bf16)
                        for i in range(width // HALF)
                    ],
                    axis=1,
                )
                acc[:, v * width : (v + 1) * width] += nn(member, hot)
            return carry

        lax.fori_loop(low // IDS_STEP, (high + IDS_STEP - 1) // IDS_STEP, body, 0)
        c_ref[ec * EVENTS_STEP : (ec + 1) * EVENTS_STEP, :] = acc[...].astype(bf16)


def each_block(owners_ref, count_ref, owners, body):
    for o in range(owners):
        count_ref[o] = 0

    def step(block, carry):
        owner = owners_ref[block]
        rank = count_ref[owner]
        count_ref[owner] = rank + 1
        body(block, owner, rank)
        return carry

    lax.fori_loop(0, owners_ref.shape[0], step, 0)


def pool_kernel(owners_ref, c_ref, *refs, dp, hid):
    pieces, outs = refs[:dp], refs[dp : dp + hid]
    whole, table, pooled, count_ref = refs[dp + hid :]
    me_dp, me_hid = lax.axis_index("dp"), lax.axis_index("hid")
    for r in range(dp):
        whole[me_dp ^ r] = pieces[r][...]

    def place(block, owner, rank):
        table[pl.ds(pl.multiple_of(block * ROWS_BLOCK, ROWS_BLOCK), ROWS_BLOCK), :] = whole[
            owner, pl.ds(pl.multiple_of(rank * ROWS_BLOCK, ROWS_BLOCK), ROWS_BLOCK), :
        ]

    each_block(owners_ref, count_ref, dp, place)
    rows = pooled.shape[1]
    for q in range(hid):
        pooled[q] = nn(c_ref[q * rows : (q + 1) * rows, :], table[...])
    for m in range(hid):
        outs[m][...] = pooled[me_hid ^ m].T.astype(bf16)


def hot_cv(rows, cols, mult, start):
    group = cols // mult
    col = lax.broadcasted_iota(jnp.int32, (8, cols), 1)
    target = ((col % group) * mult + col // group - start)[0:1]
    row = lax.broadcasted_iota(jnp.int32, (rows, cols), 0)
    return jnp.where(row == target, 1.0, 0.0).astype(bf16)


def hot_vc(rows, cols, mult, start):
    group = rows // mult
    row = lax.broadcasted_iota(jnp.int32, (rows, HALF), 0)
    target = ((row % group) * mult + row // group - start)[:, 0:1]
    col = lax.broadcasted_iota(jnp.int32, (rows, cols), 1)
    return jnp.where(col == target, 1.0, 0.0).astype(bf16)


def weights_kernel(*refs, dp, hid):
    pieces, vec_ref = refs[:hid], refs[hid]
    w1p, w1t, w2p, w2t, col_ref, q_ref, q3_ref, q3t_ref = refs[hid + 1 : hid + 9]
    w1s, w2s = refs[hid + 9 :]
    me_dp, me_hid = lax.axis_index("dp"), lax.axis_index("hid")
    rows = D // dp
    fold = H // dp
    width = (O * EXPERTS) // dp
    high = H // hid
    for r in range(hid):
        j = me_hid ^ r
        for s in range(dp):
            k = me_dp ^ s
            w1s[j, pl.ds(pl.multiple_of(k * rows, rows), rows), :] = pieces[r][s, 0:rows, :]
            part = pieces[r][s, rows : rows + fold, :].astype(f32)
            for q in range(high // fold):
                start = pl.multiple_of(j * high + q * fold, fold)
                w2s[k, pl.ds(start, fold), :] = part[:, q * width : (q + 1) * width].astype(bf16)
    span = HALF * EXPERTS
    q_ref[...] = hot_cv(span, span, EXPERTS, 0)
    q3_ref[...] = hot_cv(O * STREAMS, O * STREAMS, STREAMS, 0)
    q3t_ref[...] = hot_vc(O * STREAMS, O * STREAMS, STREAMS, 0)
    j_step = w1s.shape[2]
    k_step = w2s.shape[2]
    for half in range(2):
        lanes = slice(half * HALF, (half + 1) * HALF)
        total_p, total_t = None, None
        for i in range(span // j_step):
            w1 = w1s[half * (span // j_step) + i]
            p = nn(w1, q_ref[i * j_step : (i + 1) * j_step, :])
            t = nt(hot_vc(span, j_step, EXPERTS, i * j_step), w1)
            total_p = p if total_p is None else total_p + p
            total_t = t if total_t is None else total_t + t
        for e in range(EXPERTS):
            w1p[e, :, lanes] = total_p[:, e * HALF : (e + 1) * HALF].astype(bf16)
            w1t[e, lanes, :] = total_t[e * HALF : (e + 1) * HALF, :].astype(bf16)
        total_p, total_t = None, None
        for i in range(span // k_step):
            w2 = w2s[half * (span // k_step) + i]
            p = nn(w2, q_ref[i * k_step : (i + 1) * k_step, :])
            t = nt(hot_vc(span, k_step, EXPERTS, i * k_step), w2)
            total_p = p if total_p is None else total_p + p
            total_t = t if total_t is None else total_t + t
        for e in range(EXPERTS):
            w2p[e, :, lanes] = total_p[:, e * HALF : (e + 1) * HALF].astype(bf16)
            w2t[e, lanes, :] = total_t[e * HALF : (e + 1) * HALF, :].astype(bf16)
        vec = vec_ref[:, half * span : (half + 1) * span]
        v0 = vec.astype(bf16)
        rest = vec - v0.astype(f32)
        v1 = rest.astype(bf16)
        v2 = (rest - v1.astype(f32)).astype(bf16)
        turn = hot_vc(span, span, EXPERTS, 0)
        cols = nt(turn, v0) + nt(turn, v1) + nt(turn, v2)
        for e in range(EXPERTS):
            for i in range(3):
                col_ref[i, e, lanes, :] = jnp.broadcast_to(
                    cols[e * HALF : (e + 1) * HALF, i : i + 1], (HALF, HALF)
                )


def softmax_rows(logits):
    top = jnp.max(logits, axis=0, keepdims=True)
    grown = jnp.exp(logits - top)
    return grown / jnp.sum(grown, axis=0, keepdims=True)


def wide(column, width):
    return jnp.concatenate([column] * (width // HALF), axis=1) if width > HALF else column


def main_kernel(*refs, hid):
    xts, cots = refs[:hid], refs[hid : 2 * hid]
    w1p, w1t, w2p, w2t, col_ref, q_ref, q3_ref, q3t_ref, gate_ref = refs[2 * hid : 2 * hid + 9]
    outs = refs[2 * hid + 9 :]
    mixed_ref, small_ref, xt, hid_ref, dinner_ref, dpre_ref = outs[:6]
    dx_outs = outs[6 : 6 + hid]
    up, upq, mix, work, slope, norm, dout, dx, vec = outs[6 + hid :]
    me = lax.axis_index("hid")
    feats, rows = xts[0].shape
    for m in range(hid):
        j = me ^ m
        xt[pl.ds(pl.multiple_of(j * feats, feats), feats), :] = xts[m][...]
        cols = cots[m].shape[0]
        upq[pl.ds(pl.multiple_of(j * cols, cols), cols), :] = cots[m][...]
    up[...] = nn(q3t_ref[...], upq[...])
    gate = gate_ref[...].astype(bf16)
    logits = nn(gate, xt[...])
    chances = [
        softmax_rows(logits[STREAM_COLS[t] : STREAM_COLS[t] + len(STREAM_EXPERTS[t])])
        for t in range(STREAMS)
    ]
    mix[...] = jnp.zeros_like(mix)
    chunk = 64
    parts = [slice(i * chunk, (i + 1) * chunk) for i in range(O // chunk)]
    ones = jnp.ones((8, rows), bf16)
    d_chances = [[None] * len(STREAM_EXPERTS[t]) for t in range(STREAMS)]
    for e in range(EXPERTS):
        streams = [t for t in range(STREAMS) if e in STREAM_EXPERTS[t]]
        coef = {
            t: chances[t][STREAM_EXPERTS[t].index(e) : STREAM_EXPERTS[t].index(e) + 1]
            for t in streams
        }
        work[...] = nn(w1t[e], xt[...])
        for p in parts:
            pre = work[p, :] + wide(col_ref[0, e, p, :], rows)
            phi = 0.5 + 0.5 * lax.erf(pre * 0.7071067811865476)
            hid_ref[e, p, :] = (pre * phi).astype(bf16)
            slope[p, :] = phi + pre * (jnp.exp(-0.5 * pre * pre) * 0.3989422804014327)
        work[...] = nn(w2t[e], hid_ref[e])
        total = jnp.zeros((1, rows), f32)
        for p in parts:
            total = total + jnp.sum(work[p, :], axis=0, keepdims=True)
        mean = total * (1.0 / O)
        total = jnp.zeros((1, rows), f32)
        for p in parts:
            off = work[p, :] - mean
            total = total + jnp.sum(off * off, axis=0, keepdims=True)
        inverse = lax.rsqrt(total * (1.0 / O) + norm_eps)
        sums = {t: jnp.zeros((1, rows), f32) for t in streams}
        first, second = jnp.zeros((1, rows), f32), jnp.zeros((1, rows), f32)
        for i, p in enumerate(parts):
            normed = (work[p, :] - mean) * inverse
            gain = wide(col_ref[1, e, p, :], rows)
            value = normed * gain + wide(col_ref[2, e, p, :], rows)
            grad = None
            for t in streams:
                rows_t = slice(t * O + i * chunk, t * O + (i + 1) * chunk)
                mix[rows_t, :] += value * coef[t]
                upward = up[rows_t, :]
                sums[t] = sums[t] + jnp.sum(upward * value, axis=0, keepdims=True)
                term = upward * coef[t]
                grad = term if grad is None else grad + term
            d_norm = grad * gain
            first = first + jnp.sum(d_norm, axis=0, keepdims=True)
            second = second + jnp.sum(d_norm * normed, axis=0, keepdims=True)
            norm[p, :] = normed
            work[p, :] = d_norm
            dout[0, p, :] = (grad * normed).astype(bf16)
            dout[1, p, :] = grad.astype(bf16)
        for t in streams:
            d_chances[t][STREAM_EXPERTS[t].index(e)] = sums[t]
        first, second = first * (1.0 / O), second * (1.0 / O)
        for p in parts:
            dinner_ref[e, p, :] = ((work[p, :] - first - norm[p, :] * second) * inverse).astype(bf16)
        work[...] = nn(w2p[e], dinner_ref[e])
        for p in parts:
            dpre_ref[e, p, :] = (work[p, :] * slope[p, :]).astype(bf16)
        vec[0, e] = nt(ones, dpre_ref[e])
        vec[1, e] = nt(ones, dout[0])
        vec[2, e] = nt(ones, dout[1])
        back = nn(w1p[e], dpre_ref[e])
        if e == 0:
            dx[...] = back
        else:
            dx[...] += back
    d_logits = []
    for t in range(STREAMS):
        upward = jnp.concatenate(d_chances[t], axis=0)
        g = chances[t]
        d_logits.append(g * (upward - jnp.sum(g * upward, axis=0, keepdims=True)))
    pad = jnp.zeros((gate_ref.shape[0] - 14, rows), f32)
    d_logits = jnp.concatenate(d_logits + [pad], axis=0).astype(bf16)
    dx[...] += tn(gate, d_logits)
    for m in range(hid):
        start = pl.multiple_of((me ^ m) * feats, feats)
        dx_outs[m][...] = dx[pl.ds(start, feats), :].astype(bf16)
    gates = gate_ref.shape[0]
    small_ref[0:gates, :] = nt(d_logits, xt[...]).astype(bf16)
    small_ref[gates:, :] = jnp.zeros((small_ref.shape[0] - gates, small_ref.shape[1]), bf16)
    width = (H * EXPERTS) // hid
    for half in range(2):
        lanes = slice(half * HALF, (half + 1) * HALF)
        stack = jnp.concatenate(
            [
                jnp.concatenate([vec[i, e, 0:1, lanes] for e in range(EXPERTS)], axis=1)
                for i in range(3)
            ]
            + [jnp.zeros((5, HALF * EXPERTS), f32)],
            axis=0,
        ).astype(bf16)
        turned = nt(stack, q_ref[...])
        per = (HALF * EXPERTS) // width
        for i in range(per):
            j = half * per + i
            small_ref[gates + 16 * j : gates + 16 * j + 8, 0:width] = turned[
                :, i * width : (i + 1) * width
            ].astype(bf16)
    mixed_ref[...] = tn(mix[...].astype(bf16), q3t_ref[...]).astype(bf16)


def grads_kernel(xt, hid_ref, dinner_ref, dpre_ref, q_ref, *refs, dp, hid):
    outs = refs[:hid]
    turned, w1g, w2g = refs[hid:]
    me_dp, me_hid = lax.axis_index("dp"), lax.axis_index("hid")
    span = HALF * EXPERTS
    rows = D // dp
    fold = H // dp
    width = (O * EXPERTS) // dp
    high = H // hid
    cols = (H * EXPERTS) // hid
    inner = inner_size(dp)
    whole = [nt(hid_ref[e], dinner_ref[e]).astype(bf16) for e in range(EXPERTS)]
    for half in range(2):
        part = slice(half * HALF, (half + 1) * HALF)
        block = jnp.concatenate([dpre_ref[e, part, :] for e in range(EXPERTS)], axis=0)
        turned[half * span : (half + 1) * span, :] = nn(q_ref[...], block).astype(bf16)
        block = jnp.concatenate([w[:, part] for w in whole], axis=1)
        w2g[:, half * span : (half + 1) * span] = nt(block, q_ref[...])
    for m in range(hid):
        j = me_hid ^ m
        left = turned[pl.ds(pl.multiple_of(j * cols, cols), cols), :]
        w1g[...] = nt(xt[...], left).astype(bf16)
        for near in range(inner):
            for far in range(dp // inner):
                k = me_dp ^ (far * inner + near)
                start = pl.multiple_of(k * rows, rows)
                outs[m][near, far, 0:rows, :] = w1g[pl.ds(start, rows), :]
        start = pl.multiple_of(j * high, high)
        for k in range(dp):
            part = w2g[pl.ds(start, high), k * width : (k + 1) * width]
            folded = jnp.concatenate(
                [part[i * fold : (i + 1) * fold, :] for i in range(high // fold)], axis=1
            ).astype(bf16)
            r = me_dp ^ k
            outs[m][r % inner, r // inner, rows : rows + fold, :] = folded


def table_kernel(owners_ref, c_ref, *refs, dp, hid):
    pieces, outs = refs[:hid], refs[hid : hid + dp]
    back, grads, slots, count_ref = refs[hid + dp :]
    me_dp, me_hid = lax.axis_index("dp"), lax.axis_index("hid")
    rows = pieces[0].shape[1]
    for m in range(hid):
        start = pl.multiple_of((me_hid ^ m) * rows, rows)
        back[:, pl.ds(start, rows)] = pieces[m][...]
    grads[...] = nn(back[...], c_ref[...]).T.astype(bf16)
    slots[...] = jnp.zeros_like(slots)

    def place(block, owner, rank):
        slots[
            owner ^ me_dp, pl.ds(pl.multiple_of(rank * ROWS_BLOCK, ROWS_BLOCK), ROWS_BLOCK), :
        ] = grads[pl.ds(pl.multiple_of(block * ROWS_BLOCK, ROWS_BLOCK), ROWS_BLOCK), :]

    each_block(owners_ref, count_ref, dp, place)
    for r in range(dp):
        outs[r][...] = slots[r]


def adam(weight, moment, second, average, grad, rate):
    new_moment = 0.5 * moment + 0.5 * grad
    new_second = 0.5 * second + 0.5 * grad * grad
    correct = 1.0 - 0.5**STEP
    new_weight = weight - rate * (
        new_moment / correct / (jnp.sqrt(new_second / correct) + adam_eps) + decay_rate * weight
    )
    new_average = ema_decay * average + (1.0 - ema_decay) * new_weight
    return (new_weight, new_moment, new_second, new_average)


def total(refs, *at):
    value = refs[0][at].astype(f32) if at else refs[0][...].astype(f32)
    for ref in refs[1:]:
        value = value + (ref[at] if at else ref[...]).astype(f32)
    return value


def table_adam_kernel(*refs, terms):
    state, parts, outs = refs[:4], refs[4 : 4 + terms], refs[4 + terms :]
    rows = state[0].shape[0]
    chunk = 64
    for i in range(rows // chunk):
        p = slice(i * chunk, (i + 1) * chunk)
        new = adam(*[s[p, :] for s in state], total(parts, p), 0.3)
        for out, value in zip(outs, new):
            out[p, :] = value


def weight_adam_kernel(*refs, terms, dp, hid):
    first, second, vector, gate = refs[0:4], refs[4:8], refs[8:12], refs[12:16]
    parts, smalls = refs[16 : 16 + terms], refs[16 + terms : 16 + 2 * terms]
    outs = refs[16 + 2 * terms :]
    first_out, second_out, vector_out, gate_out = outs[0:4], outs[4:8], outs[8:12], outs[12:16]
    rows, fold = D // dp, H // dp
    width = (O * EXPERTS) // dp
    new = adam(*[s[...] for s in first], total(parts, slice(0, rows)), 0.04)
    for out, value in zip(first_out, new):
        out[...] = value
    grad = total(parts, slice(rows, rows + fold))
    for i in range((H // hid) // fold):
        p = slice(i * fold, (i + 1) * fold)
        new = adam(*[s[p, :] for s in second], grad[:, i * width : (i + 1) * width], 0.06)
        for out, value in zip(second_out, new):
            out[p, :] = value
    pairs = list(smalls)
    gates = gate[0].shape[0]
    me = lax.axis_index("hid")

    def tree(at):
        values = [s[at].astype(f32) for s in pairs]
        while len(values) > 1:
            values = [values[i] + values[i + 1] for i in range(0, len(values), 2)]
        return values[0]

    new = adam(*[s[...] for s in gate], tree(slice(0, gates)), 0.03)
    for out, value in zip(gate_out, new):
        out[...] = value
    cols = (H * EXPERTS) // hid
    start = pl.multiple_of(16 + me * 16, 16)
    grad = tree(pl.ds(start, 16))[0:3, 0:cols]
    new = adam(*[s[...] for s in vector], grad, 0.2)
    for out, value in zip(vector_out, new):
        out[...] = value


def per_device(
    bag_offsets,
    embed_ids,
    block_owners,
    cotangent,
    table_w,
    table_m,
    table_v,
    table_ema,
    first_w,
    first_m,
    first_v,
    first_ema,
    second_w,
    second_m,
    second_v,
    second_ema,
    vector_w,
    vector_m,
    vector_v,
    vector_ema,
    gate_w,
    gate_m,
    gate_v,
    gate_ema,
):
    dp, hid = lax.axis_size("dp"), lax.axis_size("hid")
    inner = inner_size(dp)
    outer = dp // inner
    events, ids = bag_offsets.shape[0], embed_ids.shape[0]
    rows = events // hid
    slots, feats = table_w.shape
    vocab = block_owners.shape[0] * ROWS_BLOCK
    piece_rows = D // dp + H // dp
    piece_cols = first_w.shape[1]

    table_low, weight_low, *cot_pieces = call(
        functools.partial(low_kernel, hid=hid),
        [
            shape(table_w.shape, bf16),
            shape((piece_rows, piece_cols), bf16),
            *[shape((cotangent.shape[1], rows), bf16) for m in range(hid)],
        ],
        (table_w, first_w, second_w, cotangent.T),
    )
    weight_pieces = gather_dp(weight_low)
    table_pieces = gather_dp(table_low)
    cots = [cot_pieces[0]] + [swap(cot_pieces[m], "hid", m) for m in range(1, hid)]

    weight_here = jnp.stack(weight_pieces)
    weight_hid = {0: weight_here}
    for m in range(2, hid, 2):
        weight_hid[m] = swap(weight_here, "hid", m)
    for m in range(0, hid, 2):
        weight_hid[m + 1] = swap(weight_hid[m], "hid", 1)
    vector_full = lax.all_gather(vector_w, "hid", axis=1, tiled=True)
    vector_full = jnp.pad(vector_full, ((0, 5), (0, 0)))
    span = HALF * EXPERTS
    w1p, w1t, w2p, w2t, columns, turn, turn3, turn3t = call(
        functools.partial(weights_kernel, dp=dp, hid=hid),
        [
            shape((EXPERTS, D, H), bf16),
            shape((EXPERTS, H, D), bf16),
            shape((EXPERTS, H, O), bf16),
            shape((EXPERTS, O, H), bf16),
            shape((3, EXPERTS, H, HALF), f32),
            shape((span, span), bf16),
            shape((O * STREAMS, O * STREAMS), bf16),
            shape((O * STREAMS, O * STREAMS), bf16),
        ],
        (*[weight_hid[m] for m in range(hid)], vector_full),
        scratch=[
            pltpu.VMEM((hid, D, piece_cols), bf16),
            pltpu.VMEM((dp, H, (O * EXPERTS) // dp), bf16),
        ],
        vmem=40,
    )

    lanes = 128
    nexts = jnp.concatenate([bag_offsets[1:], jnp.full((1,), ids, jnp.int32)])
    counts = call(
        counts_kernel,
        shape((events, vocab), bf16),
        (
            bag_offsets,
            embed_ids.reshape(ids // lanes, lanes),
            bag_offsets.reshape(events // lanes, lanes),
            nexts.reshape(events // lanes, lanes),
        ),
        in_specs=[SMEM, VMEM, VMEM, VMEM],
        scratch=[
            pltpu.VMEM((ids // IDS_STEP, IDS_STEP, HALF), jnp.int32),
            pltpu.VMEM((EVENTS_STEP, vocab), f32),
        ],
        vmem=56,
    )
    pooled = call(
        functools.partial(pool_kernel, dp=dp, hid=hid),
        [shape((feats, rows), bf16) for m in range(hid)],
        (block_owners, counts, *table_pieces),
        in_specs=[SMEM] + [VMEM] * (1 + dp),
        scratch=[
            pltpu.VMEM((dp, slots, feats), bf16),
            pltpu.VMEM((vocab, feats), bf16),
            pltpu.VMEM((hid, rows, feats), f32),
            pltpu.SMEM((dp,), jnp.int32),
        ],
        vmem=56,
    )
    xts = [pooled[0]] + [swap(pooled[m], "hid", m) for m in range(1, hid)]

    gates = 16
    gate_pad = jnp.pad(gate_w.T, ((0, gates - gate_w.shape[1]), (0, 0)))
    small_rows = gates + 16 * hid
    mixed_part, small, xt, hidden, d_inner, d_pre, *d_pieces = call(
        functools.partial(main_kernel, hid=hid),
        [
            shape((rows, O * STREAMS), bf16),
            shape((small_rows, D), bf16),
            shape((D, rows), bf16),
            shape((EXPERTS, H, rows), bf16),
            shape((EXPERTS, O, rows), bf16),
            shape((EXPERTS, H, rows), bf16),
            *[shape((feats, rows), bf16) for m in range(hid)],
        ],
        (*xts, *cots, w1p, w1t, w2p, w2t, columns, turn, turn3, turn3t, gate_pad),
        scratch=[
            pltpu.VMEM((O * STREAMS, rows), f32),
            pltpu.VMEM((O * STREAMS, rows), bf16),
            pltpu.VMEM((O * STREAMS, rows), f32),
            pltpu.VMEM((H, rows), f32),
            pltpu.VMEM((H, rows), f32),
            pltpu.VMEM((H, rows), f32),
            pltpu.VMEM((2, H, rows), bf16),
            pltpu.VMEM((D, rows), f32),
            pltpu.VMEM((3, EXPERTS, 8, H), f32),
        ],
        vmem=40,
    )
    mixed = lax.all_gather(mixed_part, "hid", axis=0, tiled=True)
    d_pooled = [d_pieces[0]] + [swap(d_pieces[m], "hid", m) for m in range(1, hid)]

    grads = call(
        functools.partial(grads_kernel, dp=dp, hid=hid),
        [shape((inner, outer, piece_rows, piece_cols), bf16) for m in range(hid)],
        (xt, hidden, d_inner, d_pre, turn),
        scratch=[
            pltpu.VMEM((H * EXPERTS, rows), bf16),
            pltpu.VMEM((D, piece_cols), bf16),
            pltpu.VMEM((H, O * EXPERTS), f32),
        ],
        vmem=40,
    )

    def add(a, b):
        return (a.astype(f32) + b.astype(f32)).astype(bf16)

    half = [add(grads[m], swap(grads[m + 1], "hid", 1)) for m in range(0, hid, 2)]
    small = add(small, swap(small, "hid", 1))
    mine = half[0]
    smalls = [small]
    for m in range(1, hid // 2):
        mine = add(mine, swap(half[m], "hid", 2 * m))
    step = 2
    while step < hid:
        small = add(small, swap(small, "hid", step))
        step *= 2
    near = mine[0]
    for m in range(1, inner):
        near = add(near, swap(mine[m], "dp", m))
    step = 1
    while step < inner:
        small = add(small, swap(small, "dp", step))
        step *= 2
    weight_terms = [near[0]] + [swap(near[m], "dp", m * inner) for m in range(1, outer)]
    small_terms = [small] + [swap(small, "dp", m * inner) for m in range(1, outer)]

    d_table = call(
        functools.partial(table_kernel, dp=dp, hid=hid),
        [shape((slots, feats), bf16) for r in range(dp)],
        (block_owners, counts, *d_pooled),
        in_specs=[SMEM] + [VMEM] * (1 + hid),
        scratch=[
            pltpu.VMEM((feats, events), bf16),
            pltpu.VMEM((vocab, feats), bf16),
            pltpu.VMEM((dp, slots, feats), bf16),
            pltpu.SMEM((dp,), jnp.int32),
        ],
        vmem=56,
    )
    table_terms = []
    for far in reversed(range(outer)):
        value = d_table[far * inner]
        for m in range(1, inner):
            value = add(value, swap(d_table[far * inner + m], "dp", m))
        table_terms.append(swap(value, "dp", far * inner) if far else value)

    table_new = call(
        functools.partial(table_adam_kernel, terms=outer),
        [shape(table_w.shape, f32)] * 4,
        (table_w, table_m, table_v, table_ema, *table_terms),
        vmem=24,
    )
    weights_new = call(
        functools.partial(weight_adam_kernel, terms=outer, dp=dp, hid=hid),
        [shape(first_w.shape, f32)] * 4
        + [shape(second_w.shape, f32)] * 4
        + [shape(vector_w.shape, f32)] * 4
        + [shape((gates, D), f32)] * 4,
        (
            first_w,
            first_m,
            first_v,
            first_ema,
            second_w,
            second_m,
            second_v,
            second_ema,
            vector_w,
            vector_m,
            vector_v,
            vector_ema,
            gate_pad,
            *[jnp.pad(g.T, ((0, gates - g.shape[1]), (0, 0))) for g in (gate_m, gate_v, gate_ema)],
            *weight_terms,
            *small_terms,
        ),
        vmem=24,
    )
    return (
        mixed,
        *table_new,
        *weights_new[0:12],
        *[g[0 : gate_w.shape[1]].T for g in weights_new[12:16]],
    )


def solution(mesh):
    split, spread, whole = P("dp", "hid"), P("hid", "dp"), P()
    return jax.shard_map(
        per_device,
        mesh=mesh,
        in_specs=(P("dp"), P("dp"), whole, split)
        + (split,) * 8
        + (spread,) * 4
        + (P(None, "hid"),) * 4
        + (whole,) * 4,
        out_specs=(P("dp", None),)
        + (split,) * 8
        + (spread,) * 4
        + (P(None, "hid"),) * 4
        + (whole,) * 4,
        check_vma=False,
    )
```

time: 805 us -> 226 us (0.28)
  waiting for transfers between devices: 317 us -> 99.7 us
  local copies, waits for them, and re-layouts: 166 us -> 10.2 us
  other arithmetic: 126 us -> 3.2 us
  blocking collectives: 128 us -> 5.4 us
  Pallas kernels: 0 us -> 54.5 us
  matrix products: 49.7 us -> 0 us
  starting transfers between devices: 0.41 us -> 38 us
    reduce_scatter x3 -> x0, waiting for transfers between devices: 143 us -> none  [the longest x1 53.1 us: per_device(): lax.psum_scatter(partial_value.reshape(rows_dev, O * EXPERTS), 'hid', sca...]
    all_gather x4 -> x1, waiting for transfers between devices: 110 us -> 0.01 us  [per_device(): mixed = lax.all_gather(mixed_part, 'hid', axis=0, tiled=True)]
    ppermute x0 -> x46, waiting for transfers between devices: none -> 99.7 us  [swap(): return lax.ppermute(value, axis, [(i, i ^ mask) for i in range(count)])]
    scatter-add x3 -> x0, other arithmetic: 94.7 us -> none  [the longest x1 50.7 us: per_device(): jax.ops.segment_sum(gathered[row_index].astype(jnp.float32), event_of, ro...]
    slice x4 -> x1, local copies, waits for them, and re-layouts: 77.1 us -> 0.07 us  [per_device(): nexts = jnp.concatenate([bag_offsets[1:], jnp.full((1,), ids, jnp.int32)])]
    psum x3 -> x0, blocking collectives: 66 us -> none  [the longest x1 37.7 us: per_device(): d_vector, d_gate = lax.psum((d_vector, d_gate), 'dp')]
    all_gather x2 -> x1, blocking collectives: 62 us -> 5.4 us  [per_device(): vector_full = lax.all_gather(vector_w, 'hid', axis=1, tiled=True)]
    pallas_call x0 -> x9, Pallas kernels: none -> 54.5 us  [call(): pl.pallas_call(kernel, out_shape=outs, in_specs=in_specs or [VMEM] * len(...]
  transfers between devices with their start and end apart: 10 -> 47, of which waited for: 8 -> 20; matrix products, arithmetic and copies ran while one was open for 14% -> 2% of each run, Pallas kernels for 0% -> 19%
where the time goes in v1:
time: 226 us
  waiting for transfers between devices  99.7 us (44%)
  Pallas kernels  54.5 us (24%)
  starting transfers between devices  38 us (17%)
  between operations  14.7 us (7%)
  local copies, waits for them, and re-layouts  10.2 us (5%)
  blocking collectives  5.4 us (2%)
  other arithmetic  3.2 us (1%)
    ppermute x46, waiting for transfers between devices, swap(): return lax.ppermute(value, axis, [(i, i ^ mask) for i in range(count)])  99.7 us
    pallas_call x9, Pallas kernels, call(): pl.pallas_call(kernel, out_shape=outs, in_specs=in_specs or [VMEM] * len(...  54.5 us
    ppermute x46, starting transfers between devices, swap(): return lax.ppermute(value, axis, [(i, i ^ mask) for i in range(count)])  38 us
    unnamed x92, local copies, waits for them, and re-layouts  8.77 us
    all_gather x1, blocking collectives, per_device(): vector_full = lax.all_gather(vector_w, 'hid', axis=1, tiled=True)  5.4 us
  transfers between devices with their start and end apart: 47, of which 20 were waited for; matrix products, arithmetic and copies ran while one was open for 2% of the time, Pallas kernels for 19%

profile of v1, /device:TPU:0, one launch (start us, length us, event | category | flops | bytes accessed | tf_op | source)
XLA Modules:
  0.0 225.7 jit_solution(720487923259639874)
XLA Ops:
  7.2 1.0 copy-done.1
  8.2 0.9 copy-done.6
  9.1 1.0 copy-done.8
  11.1 3.0 %collective-permute-start.13 = (bf16[96,384]{1,0:T(8,128)(2,1)S(1)}, bf16[96,384]{1,0:T(8,128)(2,1)S(1)}, u32[]{:S(2)}, u32[]{:S(2)}) collective-permute-start(bf16[96,384]{1,0:T(8,128)(2,1)S(1)} %get-tuple-element.90), channel_id=1, source_target_pairs={{0,4},{4,0},{8,12},{12,8},{16,20},{20,16},{24,28},{28,24},{1,5},{5... | collective-permute-start | bytes 221192 | tf_op jit(solution)/shard_map/ppermute | solution.py:71
  14.1 1.6 collective-permute-start.14
  15.6 2.6 %collective-permute-start.16 = (bf16[96,384]{1,0:T(8,128)(2,1)S(1)}, bf16[96,384]{1,0:T(8,128)(2,1)S(1)}, u32[]{:S(2)}, u32[]{:S(2)}) collective-permute-start(bf16[96,384]{1,0:T(8,128)(2,1)S(1)} %get-tuple-element.90), channel_id=1, source_target_pairs={{0,16},{4,20},{8,24},{12,28},{16,0},{20,4},{24,8},{28,12},{1,17},{... | collective-permute-start | bytes 221192 | tf_op jit(solution)/shard_map/ppermute | solution.py:71
  18.9 4.2 %collective-permute-done.16 = bf16[96,384]{1,0:T(8,128)(2,1)S(1)} collective-permute-done((bf16[96,384]{1,0:T(8,128)(2,1)S(1)}, bf16[96,384]{1,0:T(8,128)(2,1)S(1)}, u32[]{:S(2)}, u32[]{:S(2)}) %collective-permute-start.16) | collective-permute-done | bytes 73760 | tf_op jit(solution)/shard_map/ppermute | solution.py:71
  25.2 2.3 %collective-permute-done.17 = bf16[96,384]{1,0:T(8,128)(2,1)S(1)} collective-permute-done((bf16[96,384]{1,0:T(8,128)(2,1)S(1)}, bf16[96,384]{1,0:T(8,128)(2,1)S(1)}, u32[]{:S(2)}, u32[]{:S(2)}) %collective-permute-start.17) | collective-permute-done | bytes 73760 | tf_op jit(solution)/shard_map/ppermute | solution.py:71
  27.5 1.3 collective-permute-done.19
  28.9 1.6 collective-permute-start.21
  31.3 9.5 %collective-permute-done.21.refs_2_ = bf16[8,96,384]{2,1,0:T(8,128)(2,1)S(1)} collective-permute-done((bf16[8,96,384]{2,1,0:T(8,128)(2,1)S(1)}, bf16[8,96,384]{2,1,0:T(8,128)(2,1)S(1)}, u32[]{:S(2)}, u32[]{:S(2)}) %collective-permute-start.21) | collective-permute-done | bytes 589856 | tf_op jit(solution)/shard_map/ppermute | solution.py:71
  40.8 3.0 %collective-permute-start.3 = (bf16[768,128]{1,0:T(8,128)(2,1)S(1)}, bf16[768,128]{1,0:T(8,128)(2,1)S(1)}, u32[]{:S(2)}, u32[]{:S(2)}) collective-permute-start(bf16[768,128]{1,0:T(8,128)(2,1)S(1)} %get-tuple-element.81.refs_0_), channel_id=1, source_target_pairs={{0,16},{4,20},{8,24},{12,28},{16,0},{20,4},{24,8},{28,12},{1,17},{... | collective-permute-start | bytes 589832 | tf_op jit(solution)/shard_map/ppermute | solution.py:71
  44.8 13.2 %collective-permute-done.3.refs_4_ = bf16[768,128]{1,0:T(8,128)(2,1)S(1)} collective-permute-done((bf16[768,128]{1,0:T(8,128)(2,1)S(1)}, bf16[768,128]{1,0:T(8,128)(2,1)S(1)}, u32[]{:S(2)}, u32[]{:S(2)}) %collective-permute-start.3) | collective-permute-done | bytes 196640 | tf_op jit(solution)/shard_map/ppermute | solution.py:71
  58.5 1.5 collective-permute-start.4
  60.6 5.2 %collective-permute-done.2.refs_3_ = bf16[768,128]{1,0:T(8,128)(2,1)S(1)} collective-permute-done((bf16[768,128]{1,0:T(8,128)(2,1)S(1)}, bf16[768,128]{1,0:T(8,128)(2,1)S(1)}, u32[]{:S(2)}, u32[]{:S(2)}) %collective-permute-start.2) | collective-permute-done | bytes 196640 | tf_op jit(solution)/shard_map/ppermute | solution.py:71
  65.8 4.2 %collective-permute-done.4.refs_5_ = bf16[768,128]{1,0:T(8,128)(2,1)S(1)} collective-permute-done((bf16[768,128]{1,0:T(8,128)(2,1)S(1)}, bf16[768,128]{1,0:T(8,128)(2,1)S(1)}, u32[]{:S(2)}, u32[]{:S(2)}) %collective-permute-start.4) | collective-permute-done | bytes 196640 | tf_op jit(solution)/shard_map/ppermute | solution.py:71
  70.0 1.5 collective-permute-start.11
  71.5 1.5 collective-permute-done.6.refs_7_
  73.6 19.5 %shard_map.391.c_ref = bf16[1024,3072]{1,0:T(8,128)(2,1)} custom-call(s32[1024]{0:T(1024)} %offs_ref.1, s32[32,128]{1,0:T(8,128)} %bitcast.54, s32[8,128]{1,0:T(8,128)} %bitcast.49, s32[8,128]{1,0:T(8,128)} %add_bitcast_fusion.nxt_ref), custom_call_target="tpu_custom_call" | custom-call | tf_op jit(solution)/shard_map/pallas_call | solution.py:57
  93.2 6.5 %shard_map.393 = (bf16[128,256]{1,0:T(8,128)(2,1)}, bf16[128,256]{1,0:T(8,128)(2,1)}, bf16[128,256]{1,0:T(8,128)(2,1)}, bf16[128,256]{1,0:T(8,128)(2,1)}) custom-call(s32[48]{0:T(128)} %owners_ref.3, bf16[1024,3072]{1,0:T(8,128)(2,1)} %shard_map.391.c_ref, bf16[768,128]{1,0:T(8,128)(2,1)} %copy-done.11, bf16[768,128]{1,0:T(8,128)(2,1)} %copy-done.30, ...), custom_call_target="tpu_custom_call" | custom-call | tf_op jit(solution)/shard_map/pallas_call | solution.py:57
  99.7 1.7 collective-permute-start.7
  101.9 0.9 collective-permute-start.9
  102.9 5.4 %all_gather.6 = f32[3,1536]{1,0:T(4,128)S(1)} all-gather(f32[3,384]{1,0:T(4,128)S(1)} %copy-done.20), channel_id=1, replica_groups=mesh['dp'=8,'hid'=4] {'hid'}, dimensions={1}, use_global_device_ids=true | all-gather | bytes 23040 | tf_op jit(solution)/shard_map/all_gather | solution.py:576
  108.3 7.8 %shard_map.394 = (bf16[6,512,256]{2,1,0:T(8,128)(2,1)S(1)}, bf16[6,256,512]{2,1,0:T(8,128)(2,1)S(1)}, bf16[6,256,256]{2,1,0:T(8,128)(2,1)S(1)}, bf16[6,256,256]{...) custom-call(bf16[8,96,384]{2,1,0:T(8,128)(2,1)S(1)} %bitcast_dynamic, ...), custom_call_target="tpu_custom_call" | custom-call | tf_op jit(solution)/shard_map/pallas_call | solution.py:57
  116.1 1.5 copy-done
  117.6 9.7 %shard_map.395 = (bf16[256,768]{1,0:T(8,128)(2,1)}, bf16[80,512]{1,0:T(8,128)(2,1)S(1)}, bf16[512,256]{1,0:T(8,128)(2,1)S(1)}, bf16[6,256,256]{2,1,0:T(8,128)(2,...) custom-call(bf16[128,256]{1,0:T(8,128)(2,1)S(1)} %copy-done.15, ...), custom_call_target="tpu_custom_call" | custom-call | tf_op jit(solution)/shard_map/pallas_call | solution.py:57
  127.3 2.6 %shard_map.398 = (bf16[2,4,96,384]{3,2,1,0:T(8,128)(2,1)S(1)}, bf16[2,4,96,384]{3,2,1,0:T(8,128)(2,1)S(1)}, bf16[2,4,96,384]{3,2,1,0:T(8,128)(2,1)S(1)}, bf16[2,4,96,384]{3,2,1,0:T(8,128)(2,1)S(1)}) custom-call(bf16[512,256]{1,0:T(8,128)(2,1)S(1)} %get-tuple-element.116.xt, bf16[6,256,256]{2,1,0:T(8,128)(2,1)S(1)} %get-tuple-element.117.hid_ref, ...), custom_call_target="tpu_custom_call" | custom-call | tf_op jit(solution)/shard_map/pallas_call | solution.py:57
  131.1 1.1 collective-permute-done.40
  133.2 1.3 collective-permute-start.35
  134.5 3.0 %collective-permute-done.41 = bf16[80,512]{1,0:T(8,128)(2,1)S(1)} collective-permute-done((bf16[80,512]{1,0:T(8,128)(2,1)S(1)}, bf16[80,512]{1,0:T(8,128)(2,1)S(1)}, u32[]{:S(2)}, u32[]{:S(2)}) %collective-permute-start.41) | collective-permute-done | bytes 81952 | tf_op jit(solution)/shard_map/ppermute | solution.py:71
  139.0 15.5 %collective-permute-done.24.refs_2_ = bf16[128,256]{1,0:T(8,128)(2,1)S(1)} collective-permute-done((bf16[128,256]{1,0:T(8,128)(2,1)S(1)}, bf16[128,256]{1,0:T(8,128)(2,1)S(1)}, u32[]{:S(2)}, u32[]{:S(2)}) %collective-permute-start.24) | collective-permute-done | bytes 65568 | tf_op jit(solution)/shard_map/ppermute | solution.py:71
  154.6 1.0 collective-permute-done.25.refs_3_
  156.2 5.8 %shard_map.396 = (bf16[768,128]{1,0:T(8,128)(2,1)}, bf16[768,128]{1,0:T(8,128)(2,1)}, bf16[768,128]{1,0:T(8,128)(2,1)}, bf16[768,128]{1,0:T(8,128)(2,1)}, bf16[7...) custom-call(s32[48]{0:T(128)} %owners_ref.3, ...), custom_call_target="tpu_custom_call" | custom-call | tf_op jit(solution)/shard_map/pallas_call | solution.py:57
  162.0 2.0 collective-permute-start.30
  164.1 0.9 add_convert_fusion.7.refs_20_
  165.0 8.8 %collective-permute-done.30 = bf16[768,128]{1,0:T(8,128)(2,1)S(1)} collective-permute-done((bf16[768,128]{1,0:T(8,128)(2,1)}, bf16[768,128]{1,0:T(8,128)(2,1)S(1)}, u32[]{:S(2)}, u32[]{:S(2)}) %collective-permute-start.30) | collective-permute-done | bytes 196640 | tf_op jit(solution)/shard_map/ppermute | solution.py:71
  173.8 1.0 add_convert_fusion.4
  174.9 2.0 collective-permute-start.31
  178.0 1.3 collective-permute-start.36
  179.3 2.9 %collective-permute-done.26 = bf16[768,128]{1,0:T(8,128)(2,1)S(1)} collective-permute-done((bf16[768,128]{1,0:T(8,128)(2,1)}, bf16[768,128]{1,0:T(8,128)(2,1)S(1)}, u32[]{:S(2)}, u32[]{:S(2)}) %collective-permute-start.26) | collective-permute-done | bytes 196640 | tf_op jit(solution)/shard_map/ppermute | solution.py:71
  182.3 6.2 %collective-permute-done.36 = bf16[4,96,384]{2,1,0:T(8,128)(2,1)S(1)} collective-permute-done((bf16[4,96,384]{2,1,0:T(8,128)(2,1)S(1)}, bf16[4,96,384]{2,1,0:T(8,128)(2,1)S(1)}, u32[]{:S(2)}, u32[]{:S(2)}) %collective-permute-start.36) | collective-permute-done | bytes 294944 | tf_op jit(solution)/shard_map/ppermute | solution.py:71
  189.3 3.4 %collective-permute-start.45 = (bf16[80,512]{1,0:T(8,128)(2,1)S(1)}, bf16[80,512]{1,0:T(8,128)(2,1)S(1)}, u32[]{:S(2)}, u32[]{:S(2)}) collective-permute-start(bf16[80,512]{1,0:T(8,128)(2,1)S(1)} %add_convert_fusion.7.refs_20_), channel_id=1, source_target_pairs={{0,24},{4,28},{8,16},{12,20},{16,8},{20,12},{24,0},{28,4},{1,25},{... | collective-permute-start | bytes 245768 | tf_op jit(solution)/shard_map/ppermute | solution.py:71
  193.2 7.9 %collective-permute-done.29.refs_5_ = bf16[768,128]{1,0:T(8,128)(2,1)S(1)} collective-permute-done((bf16[768,128]{1,0:T(8,128)(2,1)S(1)}, bf16[768,128]{1,0:T(8,128)(2,1)S(1)}, u32[]{:S(2)}, u32[]{:S(2)}) %collective-permute-start.29) | collective-permute-done | bytes 196640 | tf_op jit(solution)/shard_map/ppermute | solution.py:71
  202.2 1.5 shard_map.397
  203.7 6.8 %collective-permute-done.44.refs_22_ = bf16[80,512]{1,0:T(8,128)(2,1)S(1)} collective-permute-done((bf16[80,512]{1,0:T(8,128)(2,1)S(1)}, bf16[80,512]{1,0:T(8,128)(2,1)S(1)}, u32[]{:S(2)}, u32[]{:S(2)}) %collective-permute-start.44) | collective-permute-done | bytes 81952 | tf_op jit(solution)/shard_map/ppermute | solution.py:71
  210.5 3.3 %collective-permute-done.38.refs_18_ = bf16[96,384]{1,0:T(8,128)(2,1)S(1)} collective-permute-done((bf16[96,384]{1,0:T(8,128)(2,1)S(1)}, bf16[96,384]{1,0:T(8,128)(2,1)S(1)}, u32[]{:S(2)}, u32[]{:S(2)}) %collective-permute-start.38) | collective-permute-done | bytes 73760 | tf_op jit(solution)/shard_map/ppermute | solution.py:71
  213.9 1.0 shard_map.399
  216.2 2.7 %copy.53 = bf16[1024,768]{1,0:T(8,128)(2,1)} copy(bf16[1024,768]{1,0:T(8,128)(2,1)} %all-gather.2.cloned.1.call-done) | data formatting | bytes 3145728
  (171 shorter events, 17.0 us)
Async XLA Ops:
  7.2 209.0 %all-gather.2.cloned.1.call-start = ((), (), s32[]{:S(2)}) async-start(), calls=%async_computation | async-start | bytes 1966080 | tf_op jit(solution)/shard_map/all_gather | solution.py:660
  11.1 82.1 %copy-start.11 = (bf16[768,128]{1,0:T(8,128)(2,1)}, bf16[768,128]{1,0:T(8,128)(2,1)S(1)}, u32[]{:S(2)}) copy-start(bf16[768,128]{1,0:T(8,128)(2,1)S(1)} %get-tuple-element.81.refs_0_) | copy-start | bytes 589828
  11.1 7.8 %collective-permute-start.13 = (bf16[96,384]{1,0:T(8,128)(2,1)S(1)}, bf16[96,384]{1,0:T(8,128)(2,1)S(1)}, u32[]{:S(2)}, u32[]{:S(2)}) collective-permute-start(bf16[96,384]{1,0:T(8,128)(2,1)S(1)} %get-tuple-element.90), channel_id=1, source_target_pairs={{0,4},{4,0},{8,12},{12,8},{16,20},{20,16},{24,28},{28,24},{1,5},{5... | collective-permute-start | bytes 221192 | tf_op jit(solution)/shard_map/ppermute | solution.py:71
  14.1 4.4 %collective-permute-start.14 = (bf16[96,384]{1,0:T(8,128)(2,1)S(1)}, bf16[96,384]{1,0:T(8,128)(2,1)S(1)}, u32[]{:S(2)}, u32[]{:S(2)}) collective-permute-start(bf16[96,384]{1,0:T(8,128)(2,1)S(1)} %get-tuple-element.90), channel_id=1, source_target_pairs={{0,8},{4,12},{8,0},{12,4},{16,24},{20,28},{24,16},{28,20},{1,9},{5... | collective-permute-start | bytes 221192 | tf_op jit(solution)/shard_map/ppermute | solution.py:71
  15.6 7.5 %collective-permute-start.16 = (bf16[96,384]{1,0:T(8,128)(2,1)S(1)}, bf16[96,384]{1,0:T(8,128)(2,1)S(1)}, u32[]{:S(2)}, u32[]{:S(2)}) collective-permute-start(bf16[96,384]{1,0:T(8,128)(2,1)S(1)} %get-tuple-element.90), channel_id=1, source_target_pairs={{0,16},{4,20},{8,24},{12,28},{16,0},{20,4},{24,8},{28,12},{1,17},{... | collective-permute-start | bytes 221192 | tf_op jit(solution)/shard_map/ppermute | solution.py:71
  18.2 6.3 %collective-permute-start.18 = (bf16[96,384]{1,0:T(8,128)(2,1)S(1)}, bf16[96,384]{1,0:T(8,128)(2,1)S(1)}, u32[]{:S(2)}, u32[]{:S(2)}) collective-permute-start(bf16[96,384]{1,0:T(8,128)(2,1)S(1)} %get-tuple-element.90), channel_id=1, source_target_pairs={{0,24},{4,28},{8,16},{12,20},{16,8},{20,12},{24,0},{28,4},{1,25},{... | collective-permute-start | bytes 221192 | tf_op jit(solution)/shard_map/ppermute | solution.py:71
  18.5 6.7 %collective-permute-start.15 = (bf16[96,384]{1,0:T(8,128)(2,1)S(1)}, bf16[96,384]{1,0:T(8,128)(2,1)S(1)}, u32[]{:S(2)}, u32[]{:S(2)}) collective-permute-start(bf16[96,384]{1,0:T(8,128)(2,1)S(1)} %collective-permute-done.14), channel_id=1, source_target_pairs={{0,4},{4,0},{8,12},{12,8},{16,20},{20,16},{24,28},{28,24},{1,5},{5... | collective-permute-start | bytes 221192 | tf_op jit(solution)/shard_map/ppermute | solution.py:71
  23.2 4.4 %collective-permute-start.17 = (bf16[96,384]{1,0:T(8,128)(2,1)S(1)}, bf16[96,384]{1,0:T(8,128)(2,1)S(1)}, u32[]{:S(2)}, u32[]{:S(2)}) collective-permute-start(bf16[96,384]{1,0:T(8,128)(2,1)S(1)} %collective-permute-done.16), channel_id=1, source_target_pairs={{0,4},{4,0},{8,12},{12,8},{16,20},{20,16},{24,28},{28,24},{1,5},{5... | collective-permute-start | bytes 221192 | tf_op jit(solution)/shard_map/ppermute | solution.py:71
  24.5 4.4 %collective-permute-start.19 = (bf16[96,384]{1,0:T(8,128)(2,1)S(1)}, bf16[96,384]{1,0:T(8,128)(2,1)S(1)}, u32[]{:S(2)}, u32[]{:S(2)}) collective-permute-start(bf16[96,384]{1,0:T(8,128)(2,1)S(1)} %collective-permute-done.18), channel_id=1, source_target_pairs={{0,4},{4,0},{8,12},{12,8},{16,20},{20,16},{24,28},{28,24},{1,5},{5... | collective-permute-start | bytes 221192 | tf_op jit(solution)/shard_map/ppermute | solution.py:71
  28.9 11.9 %collective-permute-start.21 = (bf16[8,96,384]{2,1,0:T(8,128)(2,1)S(1)}, bf16[8,96,384]{2,1,0:T(8,128)(2,1)S(1)}, u32[]{:S(2)}, u32[]{:S(2)}) collective-permute-start(bf16[8,96,384]{2,1,0:T(8,128)(2,1)S(1)} %bitcast_dynamic-update-slice_fusion.refs_0_), channel_id=1, source_target_pairs={{0,2},{1,3},{2,0},{3,1},{4,6},{5,7},{6,4},{7,5},{8,10},{9,11},{10,... | collective-permute-start | bytes 1769480 | tf_op jit(solution)/shard_map/ppermute | solution.py:71
  30.4 13.8 %collective-permute-start.1 = (bf16[768,128]{1,0:T(8,128)(2,1)S(1)}, bf16[768,128]{1,0:T(8,128)(2,1)S(1)}, u32[]{:S(2)}, u32[]{:S(2)}) collective-permute-start(bf16[768,128]{1,0:T(8,128)(2,1)S(1)} %get-tuple-element.81.refs_0_), channel_id=1, source_target_pairs={{0,8},{4,12},{8,0},{12,4},{16,24},{20,28},{24,16},{28,20},{1,9},{5... | collective-permute-start | bytes 589832 | tf_op jit(solution)/shard_map/ppermute | solution.py:71
  31.3 70.2 %collective-permute-start.20 = (bf16[8,96,384]{2,1,0:T(8,128)(2,1)S(1)}, bf16[8,96,384]{2,1,0:T(8,128)(2,1)S(1)}, u32[]{:S(2)}, u32[]{:S(2)}) collective-permute-start(bf16[8,96,384]{2,1,0:T(8,128)(2,1)S(1)} %bitcast_dynamic-update-slice_fusion.refs_0_), channel_id=1, source_target_pairs={{0,1},{1,0},{2,3},{3,2},{4,5},{5,4},{6,7},{7,6},{8,9},{9,8},{10,11... | collective-permute-start | bytes 1769480 | tf_op jit(solution)/shard_map/ppermute | solution.py:71
  40.8 61.2 %collective-permute-start.22 = (bf16[8,96,384]{2,1,0:T(8,128)(2,1)S(1)}, bf16[8,96,384]{2,1,0:T(8,128)(2,1)S(1)}, u32[]{:S(2)}, u32[]{:S(2)}) collective-permute-start(bf16[8,96,384]{2,1,0:T(8,128)(2,1)S(1)} %collective-permute-done.21.refs_2_), channel_id=1, source_target_pairs={{0,1},{1,0},{2,3},{3,2},{4,5},{5,4},{6,7},{7,6},{8,9},{9,8},{10,11... | collective-permute-start | bytes 1769480 | tf_op jit(solution)/shard_map/ppermute | solution.py:71
  40.8 17.2 %collective-permute-start.3 = (bf16[768,128]{1,0:T(8,128)(2,1)S(1)}, bf16[768,128]{1,0:T(8,128)(2,1)S(1)}, u32[]{:S(2)}, u32[]{:S(2)}) collective-permute-start(bf16[768,128]{1,0:T(8,128)(2,1)S(1)} %get-tuple-element.81.refs_0_), channel_id=1, source_target_pairs={{0,16},{4,20},{8,24},{12,28},{16,0},{20,4},{24,8},{28,12},{1,17},{... | collective-permute-start | bytes 589832 | tf_op jit(solution)/shard_map/ppermute | solution.py:71
  43.8 14.7 %collective-permute-start.5 = (bf16[768,128]{1,0:T(8,128)(2,1)S(1)}, bf16[768,128]{1,0:T(8,128)(2,1)S(1)}, u32[]{:S(2)}, u32[]{:S(2)}) collective-permute-start(bf16[768,128]{1,0:T(8,128)(2,1)S(1)} %get-tuple-element.81.refs_0_), channel_id=1, source_target_pairs={{0,24},{4,28},{8,16},{12,20},{16,8},{20,12},{24,0},{28,4},{1,25},{... | collective-permute-start | bytes 589832 | tf_op jit(solution)/shard_map/ppermute | solution.py:71
  44.2 15.7 %collective-permute-start = (bf16[768,128]{1,0:T(8,128)(2,1)S(1)}, bf16[768,128]{1,0:T(8,128)(2,1)S(1)}, u32[]{:S(2)}, u32[]{:S(2)}) collective-permute-start(bf16[768,128]{1,0:T(8,128)(2,1)S(1)} %get-tuple-element.81.refs_0_), channel_id=1, source_target_pairs={{0,4},{4,0},{8,12},{12,8},{16,20},{20,16},{24,28},{28,24},{1,5},{5... | collective-permute-start | bytes 589832 | tf_op jit(solution)/shard_map/ppermute | solution.py:71
  57.9 7.8 %collective-permute-start.2 = (bf16[768,128]{1,0:T(8,128)(2,1)S(1)}, bf16[768,128]{1,0:T(8,128)(2,1)S(1)}, u32[]{:S(2)}, u32[]{:S(2)}) collective-permute-start(bf16[768,128]{1,0:T(8,128)(2,1)S(1)} %collective-permute-done.1.refs_2_), channel_id=1, source_target_pairs={{0,4},{4,0},{8,12},{12,8},{16,20},{20,16},{24,28},{28,24},{1,5},{5... | collective-permute-start | bytes 589832 | tf_op jit(solution)/shard_map/ppermute | solution.py:71
  58.5 11.5 %collective-permute-start.4 = (bf16[768,128]{1,0:T(8,128)(2,1)S(1)}, bf16[768,128]{1,0:T(8,128)(2,1)S(1)}, u32[]{:S(2)}, u32[]{:S(2)}) collective-permute-start(bf16[768,128]{1,0:T(8,128)(2,1)S(1)} %collective-permute-done.3.refs_4_), channel_id=1, source_target_pairs={{0,4},{4,0},{8,12},{12,8},{16,20},{20,16},{24,28},{28,24},{1,5},{5... | collective-permute-start | bytes 589832 | tf_op jit(solution)/shard_map/ppermute | solution.py:71
  60.0 13.0 %collective-permute-start.6 = (bf16[768,128]{1,0:T(8,128)(2,1)S(1)}, bf16[768,128]{1,0:T(8,128)(2,1)S(1)}, u32[]{:S(2)}, u32[]{:S(2)}) collective-permute-start(bf16[768,128]{1,0:T(8,128)(2,1)S(1)} %collective-permute-done.5.refs_6_), channel_id=1, source_target_pairs={{0,4},{4,0},{8,12},{12,8},{16,20},{20,16},{24,28},{28,24},{1,5},{5... | collective-permute-start | bytes 589832 | tf_op jit(solution)/shard_map/ppermute | solution.py:71
  65.7 34.0 %collective-permute-start.10 = (bf16[192,256]{1,0:T(8,128)(2,1)S(1)}, bf16[192,256]{1,0:T(8,128)(2,1)S(1)}, u32[]{:S(2)}, u32[]{:S(2)}) collective-permute-start(bf16[192,256]{1,0:T(8,128)(2,1)S(1)} %get-tuple-element.87), channel_id=1, source_target_pairs={{0,1},{1,0},{2,3},{3,2},{4,5},{5,4},{6,7},{7,6},{8,9},{9,8},{10,11... | collective-permute-start | bytes 294920 | tf_op jit(solution)/shard_map/ppermute | solution.py:71
  70.0 47.6 %collective-permute-start.11 = (bf16[192,256]{1,0:T(8,128)(2,1)S(1)}, bf16[192,256]{1,0:T(8,128)(2,1)S(1)}, u32[]{:S(2)}, u32[]{:S(2)}) collective-permute-start(bf16[192,256]{1,0:T(8,128)(2,1)S(1)} %get-tuple-element.88), channel_id=1, source_target_pairs={{0,2},{1,3},{2,0},{3,1},{4,6},{5,7},{6,4},{7,5},{8,10},{9,11},{10,... | collective-permute-start | bytes 294920 | tf_op jit(solution)/shard_map/ppermute | solution.py:71
  73.0 44.6 %collective-permute-start.12 = (bf16[192,256]{1,0:T(8,128)(2,1)S(1)}, bf16[192,256]{1,0:T(8,128)(2,1)S(1)}, u32[]{:S(2)}, u32[]{:S(2)}) collective-permute-start(bf16[192,256]{1,0:T(8,128)(2,1)S(1)} %get-tuple-element.89), channel_id=1, source_target_pairs={{0,3},{1,2},{2,1},{3,0},{4,7},{5,6},{6,5},{7,4},{8,11},{9,10},{10,... | collective-permute-start | bytes 294920 | tf_op jit(solution)/shard_map/ppermute | solution.py:71
  99.7 17.9 %collective-permute-start.7 = (bf16[128,256]{1,0:T(8,128)(2,1)}, bf16[128,256]{1,0:T(8,128)(2,1)S(1)}, u32[]{:S(2)}, u32[]{:S(2)}) collective-permute-start(bf16[128,256]{1,0:T(8,128)(2,1)} %get-tuple-element.83), channel_id=1, source_target_pairs={{0,1},{1,0},{2,3},{3,2},{4,5},{5,4},{6,7},{7,6},{8,9},{9,8},{10,11... | collective-permute-start | bytes 196616 | tf_op jit(solution)/shard_map/ppermute | solution.py:71
  101.4 16.2 %collective-permute-start.8 = (bf16[128,256]{1,0:T(8,128)(2,1)}, bf16[128,256]{1,0:T(8,128)(2,1)S(1)}, u32[]{:S(2)}, u32[]{:S(2)}) collective-permute-start(bf16[128,256]{1,0:T(8,128)(2,1)} %get-tuple-element.84), channel_id=1, source_target_pairs={{0,2},{1,3},{2,0},{3,1},{4,6},{5,7},{6,4},{7,5},{8,10},{9,11},{10,... | collective-permute-start | bytes 196616 | tf_op jit(solution)/shard_map/ppermute | solution.py:71
  101.9 15.7 %collective-permute-start.9 = (bf16[128,256]{1,0:T(8,128)(2,1)}, bf16[128,256]{1,0:T(8,128)(2,1)S(1)}, u32[]{:S(2)}, u32[]{:S(2)}) collective-permute-start(bf16[128,256]{1,0:T(8,128)(2,1)} %get-tuple-element.85), channel_id=1, source_target_pairs={{0,3},{1,2},{2,1},{3,0},{4,7},{5,6},{6,5},{7,4},{8,11},{9,10},{10,... | collective-permute-start | bytes 196616 | tf_op jit(solution)/shard_map/ppermute | solution.py:71
  130.0 3.1 %collective-permute-start.34 = (bf16[2,4,96,384]{3,2,1,0:T(8,128)(2,1)S(1)}, bf16[2,4,96,384]{3,2,1,0:T(8,128)(2,1)S(1)}, u32[]{:S(2)}, u32[]{:S(2)}) collective-permute-start(bf16[2,4,96,384]{3,2,1,0:T(8,128)(2,1)S(1)} %get-tuple-element.123), channel_id=1, source_target_pairs={{0,1},{1,0},{2,3},{3,2},{4,5},{5,4},{6,7},{7,6},{8,9},{9,8},{10,11... | collective-permute-start | bytes 1769480 | tf_op jit(solution)/shard_map/ppermute | solution.py:71
  130.4 1.8 collective-permute-start.40
  130.6 44.2 %collective-permute-start.33 = (bf16[2,4,96,384]{3,2,1,0:T(8,128)(2,1)S(1)}, bf16[2,4,96,384]{3,2,1,0:T(8,128)(2,1)S(1)}, u32[]{:S(2)}, u32[]{:S(2)}) collective-permute-start(bf16[2,4,96,384]{3,2,1,0:T(8,128)(2,1)S(1)} %get-tuple-element.121), channel_id=1, source_target_pairs={{0,1},{1,0},{2,3},{3,2},{4,5},{5,4},{6,7},{7,6},{8,9},{9,8},{10,11... | collective-permute-start | bytes 1769480 | tf_op jit(solution)/shard_map/ppermute | solution.py:71
  130.9 8.0 %collective-permute-start.23 = (bf16[128,256]{1,0:T(8,128)(2,1)S(1)}, bf16[128,256]{1,0:T(8,128)(2,1)S(1)}, u32[]{:S(2)}, u32[]{:S(2)}) collective-permute-start(bf16[128,256]{1,0:T(8,128)(2,1)S(1)} %get-tuple-element.101), channel_id=1, source_target_pairs={{0,1},{1,0},{2,3},{3,2},{4,5},{5,4},{6,7},{7,6},{8,9},{9,8},{10,11... | collective-permute-start | bytes 196616 | tf_op jit(solution)/shard_map/ppermute | solution.py:71
  132.2 5.3 %collective-permute-start.41 = (bf16[80,512]{1,0:T(8,128)(2,1)S(1)}, bf16[80,512]{1,0:T(8,128)(2,1)S(1)}, u32[]{:S(2)}, u32[]{:S(2)}) collective-permute-start(bf16[80,512]{1,0:T(8,128)(2,1)S(1)} %add_convert_fusion.9), channel_id=1, source_target_pairs={{0,2},{1,3},{2,0},{3,1},{4,6},{5,7},{6,4},{7,5},{8,10},{9,11},{10,... | collective-permute-start | bytes 245768 | tf_op jit(solution)/shard_map/ppermute | solution.py:71
  133.2 41.7 %collective-permute-start.35 = (bf16[2,4,96,384]{3,2,1,0:T(8,128)(2,1)S(1)}, bf16[2,4,96,384]{3,2,1,0:T(8,128)(2,1)S(1)}, u32[]{:S(2)}, u32[]{:S(2)}) collective-permute-start(bf16[2,4,96,384]{3,2,1,0:T(8,128)(2,1)S(1)} %add_convert_fusion.1), channel_id=1, source_target_pairs={{0,2},{1,3},{2,0},{3,1},{4,6},{5,7},{6,4},{7,5},{8,10},{9,11},{10,... | collective-permute-start | bytes 1769480 | tf_op jit(solution)/shard_map/ppermute | solution.py:71
  137.6 26.4 %collective-permute-start.42 = (bf16[80,512]{1,0:T(8,128)(2,1)S(1)}, bf16[80,512]{1,0:T(8,128)(2,1)}, u32[]{:S(2)}, u32[]{:S(2)}) collective-permute-start(bf16[80,512]{1,0:T(8,128)(2,1)S(1)} %add_convert_fusion.8), channel_id=1, source_target_pairs={{0,4},{4,0},{8,12},{12,8},{16,20},{20,16},{24,28},{28,24},{1,5},{5... | collective-permute-start | bytes 245768 | tf_op jit(solution)/shard_map/ppermute | solution.py:71
  138.2 16.4 %collective-permute-start.24 = (bf16[128,256]{1,0:T(8,128)(2,1)S(1)}, bf16[128,256]{1,0:T(8,128)(2,1)S(1)}, u32[]{:S(2)}, u32[]{:S(2)}) collective-permute-start(bf16[128,256]{1,0:T(8,128)(2,1)S(1)} %get-tuple-element.102), channel_id=1, source_target_pairs={{0,2},{1,3},{2,0},{3,1},{4,6},{5,7},{6,4},{7,5},{8,10},{9,11},{10,... | collective-permute-start | bytes 196616 | tf_op jit(solution)/shard_map/ppermute | solution.py:71
  138.9 16.6 %collective-permute-start.25 = (bf16[128,256]{1,0:T(8,128)(2,1)S(1)}, bf16[128,256]{1,0:T(8,128)(2,1)S(1)}, u32[]{:S(2)}, u32[]{:S(2)}) collective-permute-start(bf16[128,256]{1,0:T(8,128)(2,1)S(1)} %get-tuple-element.103), channel_id=1, source_target_pairs={{0,3},{1,2},{2,1},{3,0},{4,7},{5,6},{6,5},{7,4},{8,11},{9,10},{10,... | collective-permute-start | bytes 196616 | tf_op jit(solution)/shard_map/ppermute | solution.py:71
  162.0 26.7 %collective-permute-start.32 = (bf16[768,128]{1,0:T(8,128)(2,1)}, bf16[768,128]{1,0:T(8,128)(2,1)S(1)}, u32[]{:S(2)}, u32[]{:S(2)}) collective-permute-start(bf16[768,128]{1,0:T(8,128)(2,1)} %get-tuple-element.111), channel_id=1, source_target_pairs={{0,4},{4,0},{8,12},{12,8},{16,20},{20,16},{24,28},{28,24},{1,5},{5... | collective-permute-start | bytes 589832 | tf_op jit(solution)/shard_map/ppermute | solution.py:71
  162.0 11.8 %collective-permute-start.30 = (bf16[768,128]{1,0:T(8,128)(2,1)}, bf16[768,128]{1,0:T(8,128)(2,1)S(1)}, u32[]{:S(2)}, u32[]{:S(2)}) collective-permute-start(bf16[768,128]{1,0:T(8,128)(2,1)} %get-tuple-element.109), channel_id=1, source_target_pairs={{0,4},{4,0},{8,12},{12,8},{16,20},{20,16},{24,28},{28,24},{1,5},{5... | collective-permute-start | bytes 589832 | tf_op jit(solution)/shard_map/ppermute | solution.py:71
  164.0 14.0 %collective-permute-start.28 = (bf16[768,128]{1,0:T(8,128)(2,1)}, bf16[768,128]{1,0:T(8,128)(2,1)S(1)}, u32[]{:S(2)}, u32[]{:S(2)}) collective-permute-start(bf16[768,128]{1,0:T(8,128)(2,1)} %get-tuple-element.107), channel_id=1, source_target_pairs={{0,4},{4,0},{8,12},{12,8},{16,20},{20,16},{24,28},{28,24},{1,5},{5... | collective-permute-start | bytes 589832 | tf_op jit(solution)/shard_map/ppermute | solution.py:71
  173.8 8.4 %collective-permute-start.26 = (bf16[768,128]{1,0:T(8,128)(2,1)}, bf16[768,128]{1,0:T(8,128)(2,1)S(1)}, u32[]{:S(2)}, u32[]{:S(2)}) collective-permute-start(bf16[768,128]{1,0:T(8,128)(2,1)} %get-tuple-element.105), channel_id=1, source_target_pairs={{0,4},{4,0},{8,12},{12,8},{16,20},{20,16},{24,28},{28,24},{1,5},{5... | collective-permute-start | bytes 589832 | tf_op jit(solution)/shard_map/ppermute | solution.py:71
  174.8 14.5 %collective-permute-start.43 = (bf16[80,512]{1,0:T(8,128)(2,1)S(1)}, bf16[80,512]{1,0:T(8,128)(2,1)S(1)}, u32[]{:S(2)}, u32[]{:S(2)}) collective-permute-start(bf16[80,512]{1,0:T(8,128)(2,1)S(1)} %add_convert_fusion.7.refs_20_), channel_id=1, source_target_pairs={{0,8},{4,12},{8,0},{12,4},{16,24},{20,28},{24,16},{28,20},{1,9},{5... | collective-permute-start | bytes 245768 | tf_op jit(solution)/shard_map/ppermute | solution.py:71
  174.9 17.8 %collective-permute-start.31 = (bf16[768,128]{1,0:T(8,128)(2,1)S(1)}, bf16[768,128]{1,0:T(8,128)(2,1)S(1)}, u32[]{:S(2)}, u32[]{:S(2)}) collective-permute-start(bf16[768,128]{1,0:T(8,128)(2,1)S(1)} %add_convert_fusion.4), channel_id=1, source_target_pairs={{0,8},{4,12},{8,0},{12,4},{16,24},{20,28},{24,16},{28,20},{1,9},{5... | collective-permute-start | bytes 589832 | tf_op jit(solution)/shard_map/ppermute | solution.py:71
  178.0 10.5 %collective-permute-start.36 = (bf16[4,96,384]{2,1,0:T(8,128)(2,1)S(1)}, bf16[4,96,384]{2,1,0:T(8,128)(2,1)S(1)}, u32[]{:S(2)}, u32[]{:S(2)}) collective-permute-start(bf16[4,96,384]{2,1,0:T(8,128)(2,1)S(1)} %slice_bitcast_fusion), channel_id=1, source_target_pairs={{0,4},{4,0},{8,12},{12,8},{16,20},{20,16},{24,28},{28,24},{1,5},{5... | collective-permute-start | bytes 884744 | tf_op jit(solution)/shard_map/ppermute | solution.py:71
  182.2 18.9 %collective-permute-start.29 = (bf16[768,128]{1,0:T(8,128)(2,1)S(1)}, bf16[768,128]{1,0:T(8,128)(2,1)S(1)}, u32[]{:S(2)}, u32[]{:S(2)}) collective-permute-start(bf16[768,128]{1,0:T(8,128)(2,1)S(1)} %add_convert_fusion.5), channel_id=1, source_target_pairs={{0,16},{4,20},{8,24},{12,28},{16,0},{20,4},{24,8},{28,12},{1,17},{... | collective-permute-start | bytes 589832 | tf_op jit(solution)/shard_map/ppermute | solution.py:71
  188.6 12.6 %collective-permute-start.27 = (bf16[768,128]{1,0:T(8,128)(2,1)S(1)}, bf16[768,128]{1,0:T(8,128)(2,1)S(1)}, u32[]{:S(2)}, u32[]{:S(2)}) collective-permute-start(bf16[768,128]{1,0:T(8,128)(2,1)S(1)} %add_convert_fusion.6), channel_id=1, source_target_pairs={{0,24},{4,28},{8,16},{12,20},{16,8},{20,12},{24,0},{28,4},{1,25},{... | collective-permute-start | bytes 589832 | tf_op jit(solution)/shard_map/ppermute | solution.py:71
  188.7 21.8 %collective-permute-start.44 = (bf16[80,512]{1,0:T(8,128)(2,1)S(1)}, bf16[80,512]{1,0:T(8,128)(2,1)S(1)}, u32[]{:S(2)}, u32[]{:S(2)}) collective-permute-start(bf16[80,512]{1,0:T(8,128)(2,1)S(1)} %add_convert_fusion.7.refs_20_), channel_id=1, source_target_pairs={{0,16},{4,20},{8,24},{12,28},{16,0},{20,4},{24,8},{28,12},{1,17},{... | collective-permute-start | bytes 245768 | tf_op jit(solution)/shard_map/ppermute | solution.py:71
  189.3 21.2 %collective-permute-start.45 = (bf16[80,512]{1,0:T(8,128)(2,1)S(1)}, bf16[80,512]{1,0:T(8,128)(2,1)S(1)}, u32[]{:S(2)}, u32[]{:S(2)}) collective-permute-start(bf16[80,512]{1,0:T(8,128)(2,1)S(1)} %add_convert_fusion.7.refs_20_), channel_id=1, source_target_pairs={{0,24},{4,28},{8,16},{12,20},{16,8},{20,12},{24,0},{28,4},{1,25},{... | collective-permute-start | bytes 245768 | tf_op jit(solution)/shard_map/ppermute | solution.py:71
  192.7 17.9 %collective-permute-start.37 = (bf16[96,384]{1,0:T(8,128)(2,1)S(1)}, bf16[96,384]{1,0:T(8,128)(2,1)S(1)}, u32[]{:S(2)}, u32[]{:S(2)}) collective-permute-start(bf16[96,384]{1,0:T(8,128)(2,1)S(1)} %get-tuple-element.143), channel_id=1, source_target_pairs={{0,8},{4,12},{8,0},{12,4},{16,24},{20,28},{24,16},{28,20},{1,9},{5... | collective-permute-start | bytes 221192 | tf_op jit(solution)/shard_map/ppermute | solution.py:71
  201.1 12.7 %collective-permute-start.38 = (bf16[96,384]{1,0:T(8,128)(2,1)S(1)}, bf16[96,384]{1,0:T(8,128)(2,1)S(1)}, u32[]{:S(2)}, u32[]{:S(2)}) collective-permute-start(bf16[96,384]{1,0:T(8,128)(2,1)S(1)} %get-tuple-element.142), channel_id=1, source_target_pairs={{0,16},{4,20},{8,24},{12,28},{16,0},{20,4},{24,8},{28,12},{1,17},{... | collective-permute-start | bytes 221192 | tf_op jit(solution)/shard_map/ppermute | solution.py:71
  201.1 12.7 %collective-permute-start.39 = (bf16[96,384]{1,0:T(8,128)(2,1)S(1)}, bf16[96,384]{1,0:T(8,128)(2,1)S(1)}, u32[]{:S(2)}, u32[]{:S(2)}) collective-permute-start(bf16[96,384]{1,0:T(8,128)(2,1)S(1)} %get-tuple-element.141), channel_id=1, source_target_pairs={{0,24},{4,28},{8,16},{12,20},{16,8},{20,12},{24,0},{28,4},{1,25},{... | collective-permute-start | bytes 221192 | tf_op jit(solution)/shard_map/ppermute | solution.py:71
  (41 other events, 597.0 us)
Sparse Core Ops, SparseCore 0:
  139.2 23.1 all-gather.1

commit v2 on v1

--- a/solution.py
+++ b/solution.py
@@ -33,6 +33,8 @@
 
 VMEM = pl.BlockSpec(memory_space=pltpu.VMEM)
 SMEM = pl.BlockSpec(memory_space=pltpu.SMEM)
+HBM = pl.BlockSpec(memory_space=pltpu.HBM)
+ANY = pl.BlockSpec(memory_space=pl.ANY)
 
 
 def shape(dims, dtype):
@@ -51,7 +53,7 @@
     return lax.dot_general(a, b, (((0,), (0,)), ((), ())), preferred_element_type=f32)
 
 
-def call(kernel, out_shape, args, in_specs=None, scratch=(), vmem=24, flops=0, moved=0):
+def call(kernel, out_shape, args, in_specs=None, scratch=(), vmem=24, us=2.0):
     single = not isinstance(out_shape, (list, tuple))
     outs = [out_shape] if single else list(out_shape)
     result = pl.pallas_call(
@@ -61,7 +63,9 @@
         out_specs=[VMEM] * len(outs),
         scratch_shapes=list(scratch),
         compiler_params=pltpu.CompilerParams(vmem_limit_bytes=vmem * MIB),
-        cost_estimate=pl.CostEstimate(flops=flops, bytes_accessed=moved, transcendentals=0),
+        cost_estimate=pl.CostEstimate(
+            flops=int(us * 1.0e9), bytes_accessed=int(us * 3.0e6), transcendentals=0
+        ),
     )(*args)
     return result[0] if single else result
 
@@ -89,69 +93,100 @@
     return pieces
 
 
-def low_kernel(table_ref, first_ref, second_ref, cot_ref, *outs, hid):
-    table_out, weight_out = outs[0], outs[1]
-    table_out[...] = table_ref[...].astype(bf16)
-    rows = first_ref.shape[0]
-    weight_out[0:rows, :] = first_ref[...].astype(bf16)
-    second = second_ref[...]
-    fold = weight_out.shape[0] - rows
-    weight_out[rows:, :] = jnp.concatenate(
+def low_kernel(table_hbm, first_hbm, second_hbm, vector_hbm, cot_hbm, *refs, hid):
+    piece, weight_out, cots = refs[0], refs[1], refs[2 : 2 + hid]
+    table, first, second, vector, cot, sems = refs[2 + hid :]
+    copies = [
+        pltpu.make_async_copy(source, target, sems.at[i])
+        for i, (source, target) in enumerate(
+            (
+                (table_hbm, table),
+                (first_hbm, first),
+                (second_hbm, second),
+                (vector_hbm, vector),
+                (cot_hbm, cot),
+            )
+        )
+    ]
+    for copy in copies:
+        copy.start()
+    copies[0].wait()
+    slots, feats = table.shape
+    piece[0:slots, :] = table[...].astype(bf16)
+    copies[1].wait()
+    copies[2].wait()
+    rows = first.shape[0]
+    each = weight_out.shape[0] // 3
+    fold = each - rows
+    folded = jnp.concatenate(
         [second[i * fold : (i + 1) * fold, :] for i in range(second.shape[0] // fold)], axis=1
-    ).astype(bf16)
+    )
+    for g in range(3):
+        lanes = slice(g * feats, (g + 1) * feats)
+        for out, start in ((piece, slots), (weight_out, 0)):
+            out[start + g * each : start + g * each + rows, :] = first[:, lanes].astype(bf16)
+            out[start + g * each + rows : start + (g + 1) * each, :] = folded[:, lanes].astype(bf16)
+    copies[3].wait()
+    copies[4].wait()
     me = lax.axis_index("hid")
-    width = outs[2].shape[1]
+    cols, width = cot.shape[0], cots[0].shape[1]
+    rest = vector[...]
+    terms = []
+    for i in range(3):
+        terms.append(rest.astype(bf16).astype(f32))
+        rest = rest - terms[i]
+    span = vector.shape[1]
+    stack = jnp.concatenate(terms + [jnp.zeros((7, span), f32)], axis=0)
+    over = jnp.concatenate([stack[:, width:], jnp.zeros((16, 2 * width - span), f32)], axis=1)
     for m in range(hid):
         start = pl.multiple_of((me ^ m) * width, width)
-        outs[2 + m][...] = cot_ref[:, pl.ds(start, width)]
-
-
-def counts_kernel(offs_ref, ids_ref, off_ref, nxt_ref, c_ref, idb, acc):
+        cots[m][0:cols, :] = cot[:, pl.ds(start, width)]
+        cots[m][cols : cols + 16, :] = stack[:, 0:width].astype(bf16)
+        cots[m][cols + 16 :, :] = over.astype(bf16)
+
+
+def counts_kernel(offs_ref, ids_ref, off_ref, nxt_ref, c_ref, idb, acc, *, chunk):
     id_rows, lanes = ids_ref.shape
-    events, vocab = c_ref.shape
+    vocab = c_ref.shape[1]
+    events = off_ref.shape[0] * lanes
     per = IDS_STEP // lanes
     idt = ids_ref[...].T
     for q in range(id_rows):
         idb[q // per, (q % per) * lanes : (q % per + 1) * lanes, :] = jnp.broadcast_to(
             idt[:, q : q + 1], (lanes, HALF)
-        )
+        ).astype(jnp.int16)
     offt = off_ref[...].T
     nxtt = nxt_ref[...].T
     cols = EVENTS_STEP // lanes
     width = 512
-    for ec in range(events // EVENTS_STEP):
-        first = jnp.concatenate([offt[:, ec * cols + i : ec * cols + i + 1] for i in range(cols)], 0)
-        last = jnp.concatenate([nxtt[:, ec * cols + i : ec * cols + i + 1] for i in range(cols)], 0)
-        acc[...] = jnp.zeros_like(acc)
-        low = offs_ref[ec * EVENTS_STEP]
-        if (ec + 1) * EVENTS_STEP < events:
-            high = offs_ref[(ec + 1) * EVENTS_STEP]
-        else:
-            high = jnp.int32(id_rows * lanes)
-
-        def body(step, carry):
-            place = step * IDS_STEP + lax.broadcasted_iota(jnp.int32, (EVENTS_STEP, IDS_STEP), 1)
-            member = jnp.where((place >= first) & (place < last), 1.0, 0.0).astype(bf16)
-            ids = idb[step]
-            for v in range(vocab // width):
-                hot = jnp.concatenate(
-                    [
-                        jnp.where(
-                            ids
-                            == lax.broadcasted_iota(jnp.int32, (IDS_STEP, HALF), 1)
-                            + (v * width + i * HALF),
-                            1.0,
-                            0.0,
-                        ).astype(bf16)
-                        for i in range(width // HALF)
-                    ],
-                    axis=1,
-                )
-                acc[:, v * width : (v + 1) * width] += nn(member, hot)
-            return carry
-
-        lax.fori_loop(low // IDS_STEP, (high + IDS_STEP - 1) // IDS_STEP, body, 0)
-        c_ref[ec * EVENTS_STEP : (ec + 1) * EVENTS_STEP, :] = acc[...].astype(bf16)
+    lane = lax.broadcasted_iota(jnp.int32, (IDS_STEP, HALF), 1).astype(jnp.int16)
+    one, zero = jnp.ones((IDS_STEP, HALF), bf16), jnp.zeros((IDS_STEP, HALF), bf16)
+    first = jnp.concatenate([offt[:, chunk * cols + i : chunk * cols + i + 1] for i in range(cols)], 0)
+    last = jnp.concatenate([nxtt[:, chunk * cols + i : chunk * cols + i + 1] for i in range(cols)], 0)
+    acc[...] = jnp.zeros_like(acc)
+    low = offs_ref[chunk * EVENTS_STEP]
+    if (chunk + 1) * EVENTS_STEP < events:
+        high = offs_ref[(chunk + 1) * EVENTS_STEP]
+    else:
+        high = jnp.int32(id_rows * lanes)
+
+    def body(step, carry):
+        place = step * IDS_STEP + lax.broadcasted_iota(jnp.int32, (EVENTS_STEP, IDS_STEP), 1)
+        member = jnp.where((place >= first) & (place < last), 1.0, 0.0).astype(bf16)
+        ids = idb[step]
+        for v in range(vocab // width):
+            hot = jnp.concatenate(
+                [
+                    jnp.where(ids == lane + jnp.int16(v * width + i * HALF), one, zero)
+                    for i in range(width // HALF)
+                ],
+                axis=1,
+            )
+            acc[:, v * width : (v + 1) * width] += nn(member, hot)
+        return carry
+
+    lax.fori_loop(low // IDS_STEP, (high + IDS_STEP - 1) // IDS_STEP, body, 0)
+    c_ref[...] = acc[...].astype(bf16)
 
 
 def each_block(owners_ref, count_ref, owners, body):
@@ -168,12 +203,14 @@
     lax.fori_loop(0, owners_ref.shape[0], step, 0)
 
 
-def pool_kernel(owners_ref, c_ref, *refs, dp, hid):
-    pieces, outs = refs[:dp], refs[dp : dp + hid]
-    whole, table, pooled, count_ref = refs[dp + hid :]
+def pool_kernel(owners_ref, *refs, chunks, dp, hid):
+    counts, pieces = refs[:chunks], refs[chunks : chunks + dp]
+    outs = refs[chunks + dp : chunks + dp + hid]
+    whole, table, pooled, count_ref = refs[chunks + dp + hid :]
     me_dp, me_hid = lax.axis_index("dp"), lax.axis_index("hid")
+    slots = whole.shape[1]
     for r in range(dp):
-        whole[me_dp ^ r] = pieces[r][...]
+        whole[me_dp ^ r] = pieces[r][0:slots, :]
 
     def place(block, owner, rank):
         table[pl.ds(pl.multiple_of(block * ROWS_BLOCK, ROWS_BLOCK), ROWS_BLOCK), :] = whole[
@@ -182,8 +219,10 @@
 
     each_block(owners_ref, count_ref, dp, place)
     rows = pooled.shape[1]
+    per = EVENTS_STEP // rows
     for q in range(hid):
-        pooled[q] = nn(c_ref[q * rows : (q + 1) * rows, :], table[...])
+        part = slice((q % per) * rows, (q % per + 1) * rows)
+        pooled[q] = nn(counts[q // per][part, :], table[...])
     for m in range(hid):
         outs[m][...] = pooled[me_hid ^ m].T.astype(bf16)
 
@@ -205,41 +244,61 @@
 
 
 def weights_kernel(*refs, dp, hid):
-    pieces, vec_ref = refs[:hid], refs[hid]
-    w1p, w1t, w2p, w2t, col_ref, q_ref, q3_ref, q3t_ref = refs[hid + 1 : hid + 9]
-    w1s, w2s = refs[hid + 9 :]
+    pieces, cots = refs[:hid], refs[hid : 2 * hid]
+    w1p, w1t, w2p, w2t, col_ref, q_ref, q3t_ref = refs[2 * hid : 2 * hid + 7]
+    w1s, w2s, vecs = refs[2 * hid + 7 :]
     me_dp, me_hid = lax.axis_index("dp"), lax.axis_index("hid")
     rows = D // dp
     fold = H // dp
+    each = rows + fold
     width = (O * EXPERTS) // dp
     high = H // hid
+    feats = pieces[0].shape[2]
+    j_step = w1s.shape[2]
+    k_step = w2s.shape[2]
     for r in range(hid):
         j = me_hid ^ r
         for s in range(dp):
             k = me_dp ^ s
-            w1s[j, pl.ds(pl.multiple_of(k * rows, rows), rows), :] = pieces[r][s, 0:rows, :]
-            part = pieces[r][s, rows : rows + fold, :].astype(f32)
+            for g in range(3):
+                w1s[j, pl.ds(pl.multiple_of(k * rows, rows), rows), g * feats : (g + 1) * feats] = (
+                    pieces[r][s, g * each : g * each + rows, :]
+                )
+            part = jnp.concatenate(
+                [pieces[r][s, g * each + rows : (g + 1) * each, :].astype(f32) for g in range(3)],
+                axis=1,
+            )
             for q in range(high // fold):
                 start = pl.multiple_of(j * high + q * fold, fold)
                 w2s[k, pl.ds(start, fold), :] = part[:, q * width : (q + 1) * width].astype(bf16)
+        cols, near = cots[r].shape[0] - 32, cots[r].shape[1]
+        vecs[j] = jnp.concatenate(
+            [cots[r][cols : cols + 16, :], cots[r][cols + 16 : cols + 32, 0 : j_step - near]], axis=1
+        )
     span = HALF * EXPERTS
     q_ref[...] = hot_cv(span, span, EXPERTS, 0)
-    q3_ref[...] = hot_cv(O * STREAMS, O * STREAMS, STREAMS, 0)
     q3t_ref[...] = hot_vc(O * STREAMS, O * STREAMS, STREAMS, 0)
-    j_step = w1s.shape[2]
-    k_step = w2s.shape[2]
     for half in range(2):
         lanes = slice(half * HALF, (half + 1) * HALF)
-        total_p, total_t = None, None
+        total_p, total_t, total_c = None, None, None
         for i in range(span // j_step):
             w1 = w1s[half * (span // j_step) + i]
+            hot = hot_vc(span, j_step, EXPERTS, i * j_step)
             p = nn(w1, q_ref[i * j_step : (i + 1) * j_step, :])
-            t = nt(hot_vc(span, j_step, EXPERTS, i * j_step), w1)
+            t = nt(hot, w1)
+            c = nt(hot, vecs[half * (span // j_step) + i])
             total_p = p if total_p is None else total_p + p
             total_t = t if total_t is None else total_t + t
+            total_c = c if total_c is None else total_c + c
         for e in range(EXPERTS):
             w1p[e, :, lanes] = total_p[:, e * HALF : (e + 1) * HALF].astype(bf16)
             w1t[e, lanes, :] = total_t[e * HALF : (e + 1) * HALF, :].astype(bf16)
+        cols = total_c[:, 0:3] + total_c[:, 3:6] + total_c[:, 6:9]
+        for e in range(EXPERTS):
+            for i in range(3):
+                col_ref[i, e, lanes, :] = jnp.broadcast_to(
+                    cols[e * HALF : (e + 1) * HALF, i : i + 1], (HALF, HALF)
+                )
         total_p, total_t = None, None
         for i in range(span // k_step):
             w2 = w2s[half * (span // k_step) + i]
@@ -250,18 +309,6 @@
         for e in range(EXPERTS):
             w2p[e, :, lanes] = total_p[:, e * HALF : (e + 1) * HALF].astype(bf16)
             w2t[e, lanes, :] = total_t[e * HALF : (e + 1) * HALF, :].astype(bf16)
-        vec = vec_ref[:, half * span : (half + 1) * span]
-        v0 = vec.astype(bf16)
-        rest = vec - v0.astype(f32)
-        v1 = rest.astype(bf16)
-        v2 = (rest - v1.astype(f32)).astype(bf16)
-        turn = hot_vc(span, span, EXPERTS, 0)
-        cols = nt(turn, v0) + nt(turn, v1) + nt(turn, v2)
-        for e in range(EXPERTS):
-            for i in range(3):
-                col_ref[i, e, lanes, :] = jnp.broadcast_to(
-                    cols[e * HALF : (e + 1) * HALF, i : i + 1], (HALF, HALF)
-                )
 
 
 def softmax_rows(logits):
@@ -276,8 +323,8 @@
 
 def main_kernel(*refs, hid):
     xts, cots = refs[:hid], refs[hid : 2 * hid]
-    w1p, w1t, w2p, w2t, col_ref, q_ref, q3_ref, q3t_ref, gate_ref = refs[2 * hid : 2 * hid + 9]
-    outs = refs[2 * hid + 9 :]
+    w1p, w1t, w2p, w2t, col_ref, q_ref, q3t_ref, gate_ref = refs[2 * hid : 2 * hid + 8]
+    outs = refs[2 * hid + 8 :]
     mixed_ref, small_ref, xt, hid_ref, dinner_ref, dpre_ref = outs[:6]
     dx_outs = outs[6 : 6 + hid]
     up, upq, mix, work, slope, norm, dout, dx, vec = outs[6 + hid :]
@@ -286,8 +333,8 @@
     for m in range(hid):
         j = me ^ m
         xt[pl.ds(pl.multiple_of(j * feats, feats), feats), :] = xts[m][...]
-        cols = cots[m].shape[0]
-        upq[pl.ds(pl.multiple_of(j * cols, cols), cols), :] = cots[m][...]
+        cols = cots[m].shape[0] - 32
+        upq[pl.ds(pl.multiple_of(j * cols, cols), cols), :] = cots[m][0:cols, :]
     up[...] = nn(q3t_ref[...], upq[...])
     gate = gate_ref[...].astype(bf16)
     logits = nn(gate, xt[...])
@@ -431,15 +478,20 @@
             outs[m][r % inner, r // inner, rows : rows + fold, :] = folded
 
 
-def table_kernel(owners_ref, c_ref, *refs, dp, hid):
-    pieces, outs = refs[:hid], refs[hid : hid + dp]
-    back, grads, slots, count_ref = refs[hid + dp :]
+def table_kernel(owners_ref, *refs, chunks, dp, hid):
+    counts, pieces = refs[:chunks], refs[chunks : chunks + hid]
+    outs = refs[chunks + hid : chunks + hid + dp]
+    back, grads, slots, count_ref = refs[chunks + hid + dp :]
     me_dp, me_hid = lax.axis_index("dp"), lax.axis_index("hid")
     rows = pieces[0].shape[1]
     for m in range(hid):
         start = pl.multiple_of((me_hid ^ m) * rows, rows)
         back[:, pl.ds(start, rows)] = pieces[m][...]
-    grads[...] = nn(back[...], c_ref[...]).T.astype(bf16)
+    part = None
+    for i in range(chunks):
+        p = nn(back[:, i * EVENTS_STEP : (i + 1) * EVENTS_STEP], counts[i][...])
+        part = p if part is None else part + p
+    grads[...] = part.T.astype(bf16)
     slots[...] = jnp.zeros_like(slots)
 
     def place(block, owner, rank):
@@ -450,6 +502,43 @@
     each_block(owners_ref, count_ref, dp, place)
     for r in range(dp):
         outs[r][...] = slots[r]
+
+
+def plus(a, b):
+    return (a.astype(f32) + b.astype(f32)).astype(bf16)
+
+
+def core_merge_kernel(*refs, pairs):
+    ins, outs = refs[: 2 * pairs], refs[2 * pairs + 1 :]
+    for i in range(pairs):
+        outs[i][...] = plus(ins[2 * i][...], ins[2 * i + 1][...])
+
+
+def chip_merge_kernel(*refs, terms, inner):
+    parts, small, other, mixed = refs[:terms], refs[terms], refs[terms + 1], refs[terms + 2]
+    outs = refs[terms + 3 :]
+    for near in range(inner):
+        value = parts[0][near].astype(f32)
+        for part in parts[1:]:
+            value = value + part[near].astype(f32)
+        outs[near][...] = value.astype(bf16)
+    outs[inner][...] = plus(small[...], other[...])
+    outs[inner + 1][...] = mixed[...]
+
+
+def near_merge_kernel(*refs, terms, outer):
+    parts, small, other, outs = refs[:terms], refs[terms], refs[terms + 1], refs[terms + 2 :]
+    for far in range(outer):
+        outs[far][...] = total(parts, far).astype(bf16)
+    outs[outer][...] = plus(small[...], other[...])
+
+
+def mixed_kernel(*refs, hid):
+    out = refs[hid]
+    rows = refs[0].shape[0]
+    me = lax.axis_index("hid")
+    for m in range(hid):
+        out[pl.ds(pl.multiple_of((me ^ m) * rows, rows), rows), :] = refs[m][...]
 
 
 def adam(weight, moment, second, average, grad, rate):
@@ -554,29 +643,39 @@
     piece_rows = D // dp + H // dp
     piece_cols = first_w.shape[1]
 
-    table_low, weight_low, *cot_pieces = call(
+    cot_rows = cotangent.shape[1] + 32
+    weight_rows = 3 * piece_rows
+    piece, weight_low, *cot_pieces = call(
         functools.partial(low_kernel, hid=hid),
         [
-            shape(table_w.shape, bf16),
-            shape((piece_rows, piece_cols), bf16),
-            *[shape((cotangent.shape[1], rows), bf16) for m in range(hid)],
+            shape((slots + weight_rows, feats), bf16),
+            shape((weight_rows, feats), bf16),
+            *[shape((cot_rows, rows), bf16) for m in range(hid)],
         ],
-        (table_w, first_w, second_w, cotangent.T),
-    )
-    weight_pieces = gather_dp(weight_low)
-    table_pieces = gather_dp(table_low)
+        (table_w, first_w, second_w, vector_w, cotangent.T),
+        in_specs=[HBM] * 5,
+        scratch=[
+            pltpu.VMEM(table_w.shape, f32),
+            pltpu.VMEM(first_w.shape, f32),
+            pltpu.VMEM(second_w.shape, f32),
+            pltpu.VMEM(vector_w.shape, f32),
+            pltpu.VMEM(cotangent.shape[::-1], bf16),
+            pltpu.SemaphoreType.DMA((5,)),
+        ],
+        vmem=8,
+    )
+    pieces = gather_dp(piece)
     cots = [cot_pieces[0]] + [swap(cot_pieces[m], "hid", m) for m in range(1, hid)]
 
-    weight_here = jnp.stack(weight_pieces)
-    weight_hid = {0: weight_here}
+    weight_parts = {0: [weight_low] + [p[slots:] for p in pieces[1:]]}
     for m in range(2, hid, 2):
-        weight_hid[m] = swap(weight_here, "hid", m)
+        weight_parts[m] = [swap(w, "hid", m) for w in weight_parts[0]]
+    weight_hid = {}
     for m in range(0, hid, 2):
+        weight_hid[m] = jnp.stack(weight_parts[m])
         weight_hid[m + 1] = swap(weight_hid[m], "hid", 1)
-    vector_full = lax.all_gather(vector_w, "hid", axis=1, tiled=True)
-    vector_full = jnp.pad(vector_full, ((0, 5), (0, 0)))
     span = HALF * EXPERTS
-    w1p, w1t, w2p, w2t, columns, turn, turn3, turn3t = call(
+    w1p, w1t, w2p, w2t, columns, turn, turn3t = call(
         functools.partial(weights_kernel, dp=dp, hid=hid),
         [
             shape((EXPERTS, D, H), bf16),
@@ -586,46 +685,53 @@
             shape((3, EXPERTS, H, HALF), f32),
             shape((span, span), bf16),
             shape((O * STREAMS, O * STREAMS), bf16),
-            shape((O * STREAMS, O * STREAMS), bf16),
         ],
-        (*[weight_hid[m] for m in range(hid)], vector_full),
+        (*[weight_hid[m] for m in range(hid)], *cots),
         scratch=[
             pltpu.VMEM((hid, D, piece_cols), bf16),
             pltpu.VMEM((dp, H, (O * EXPERTS) // dp), bf16),
+            pltpu.VMEM((hid, 16, piece_cols), bf16),
         ],
-        vmem=40,
+        vmem=32,
+        us=8.0,
     )
 
     lanes = 128
     nexts = jnp.concatenate([bag_offsets[1:], jnp.full((1,), ids, jnp.int32)])
-    counts = call(
-        counts_kernel,
-        shape((events, vocab), bf16),
-        (
-            bag_offsets,
-            embed_ids.reshape(ids // lanes, lanes),
-            bag_offsets.reshape(events // lanes, lanes),
-            nexts.reshape(events // lanes, lanes),
-        ),
-        in_specs=[SMEM, VMEM, VMEM, VMEM],
-        scratch=[
-            pltpu.VMEM((ids // IDS_STEP, IDS_STEP, HALF), jnp.int32),
-            pltpu.VMEM((EVENTS_STEP, vocab), f32),
-        ],
-        vmem=56,
-    )
+    chunks = events // EVENTS_STEP
+    counts = [
+        call(
+            functools.partial(counts_kernel, chunk=i),
+            shape((EVENTS_STEP, vocab), bf16),
+            (
+                bag_offsets,
+                embed_ids.reshape(ids // lanes, lanes),
+                bag_offsets.reshape(events // lanes, lanes),
+                nexts.reshape(events // lanes, lanes),
+            ),
+            in_specs=[SMEM, VMEM, VMEM, VMEM],
+            scratch=[
+                pltpu.VMEM((ids // IDS_STEP, IDS_STEP, HALF), jnp.int16),
+                pltpu.VMEM((EVENTS_STEP, vocab), f32),
+            ],
+            vmem=12 if vocab <= 4096 else 40,
+            us=5.0,
+        )
+        for i in range(chunks)
+    ]
     pooled = call(
-        functools.partial(pool_kernel, dp=dp, hid=hid),
+        functools.partial(pool_kernel, chunks=chunks, dp=dp, hid=hid),
         [shape((feats, rows), bf16) for m in range(hid)],
-        (block_owners, counts, *table_pieces),
-        in_specs=[SMEM] + [VMEM] * (1 + dp),
+        (block_owners, *counts, *pieces),
+        in_specs=[SMEM] + [VMEM] * (chunks + dp),
         scratch=[
             pltpu.VMEM((dp, slots, feats), bf16),
             pltpu.VMEM((vocab, feats), bf16),
             pltpu.VMEM((hid, rows, feats), f32),
             pltpu.SMEM((dp,), jnp.int32),
         ],
-        vmem=56,
+        vmem=20 if vocab <= 4096 else 58,
+        us=4.0,
     )
     xts = [pooled[0]] + [swap(pooled[m], "hid", m) for m in range(1, hid)]
 
@@ -643,7 +749,7 @@
             shape((EXPERTS, H, rows), bf16),
             *[shape((feats, rows), bf16) for m in range(hid)],
         ],
-        (*xts, *cots, w1p, w1t, w2p, w2t, columns, turn, turn3, turn3t, gate_pad),
+        (*xts, *cots, w1p, w1t, w2p, w2t, columns, turn, turn3t, gate_pad),
         scratch=[
             pltpu.VMEM((O * STREAMS, rows), f32),
             pltpu.VMEM((O * STREAMS, rows), bf16),
@@ -655,9 +761,9 @@
             pltpu.VMEM((D, rows), f32),
             pltpu.VMEM((3, EXPERTS, 8, H), f32),
         ],
-        vmem=40,
-    )
-    mixed = lax.all_gather(mixed_part, "hid", axis=0, tiled=True)
+        vmem=24,
+        us=10.0,
+    )
     d_pooled = [d_pieces[0]] + [swap(d_pieces[m], "hid", m) for m in range(1, hid)]
 
     grads = call(
@@ -669,57 +775,86 @@
             pltpu.VMEM((D, piece_cols), bf16),
             pltpu.VMEM((H, O * EXPERTS), f32),
         ],
-        vmem=40,
-    )
-
-    def add(a, b):
-        return (a.astype(f32) + b.astype(f32)).astype(bf16)
-
-    half = [add(grads[m], swap(grads[m + 1], "hid", 1)) for m in range(0, hid, 2)]
-    small = add(small, swap(small, "hid", 1))
-    mine = half[0]
-    smalls = [small]
-    for m in range(1, hid // 2):
-        mine = add(mine, swap(half[m], "hid", 2 * m))
+        vmem=16,
+        us=3.0,
+    )
+
+    whole_shape = shape(grads[0].shape, bf16)
+    small_shape = shape(small.shape, bf16)
+    operands = []
+    for m in range(0, hid, 2):
+        operands += [grads[m], swap(grads[m + 1], "hid", 1)]
+    *half, small = call(
+        functools.partial(core_merge_kernel, pairs=hid // 2 + 1),
+        [whole_shape] * (hid // 2) + [small_shape],
+        (*operands, small, swap(small, "hid", 1), d_pooled[hid - 1]),
+        in_specs=[VMEM] * (hid + 2) + [ANY],
+        us=1.5,
+    )
     step = 2
-    while step < hid:
-        small = add(small, swap(small, "hid", step))
+    while step < hid // 2:
+        small = plus(small, swap(small, "hid", step))
         step *= 2
-    near = mine[0]
-    for m in range(1, inner):
-        near = add(near, swap(mine[m], "dp", m))
+    *near, small, mixed_part = call(
+        functools.partial(chip_merge_kernel, terms=hid // 2, inner=inner),
+        [shape(grads[0].shape[1:], bf16)] * inner + [small_shape, shape(mixed_part.shape, bf16)],
+        (half[0], *[swap(half[m], "hid", 2 * m) for m in range(1, hid // 2)])
+        + (small, swap(small, "hid", step), mixed_part),
+        us=1.5,
+    )
     step = 1
-    while step < inner:
-        small = add(small, swap(small, "dp", step))
+    while step < inner // 2:
+        small = plus(small, swap(small, "dp", step))
         step *= 2
-    weight_terms = [near[0]] + [swap(near[m], "dp", m * inner) for m in range(1, outer)]
+    *far_parts, small = call(
+        functools.partial(near_merge_kernel, terms=inner, outer=outer),
+        [shape((piece_rows, piece_cols), bf16)] * outer + [small_shape],
+        (near[0], *[swap(near[m], "dp", m) for m in range(1, inner)])
+        + (small, swap(small, "dp", step)),
+        us=1.5,
+    )
+    weight_terms = [far_parts[0]] + [swap(far_parts[m], "dp", m * inner) for m in range(1, outer)]
     small_terms = [small] + [swap(small, "dp", m * inner) for m in range(1, outer)]
 
+    mixed_parts = {0: mixed_part}
+    for m in range(2, hid, 2):
+        mixed_parts[m] = swap(mixed_part, "hid", m)
+    for m in range(0, hid, 2):
+        mixed_parts[m + 1] = swap(mixed_parts[m], "hid", 1)
+    mixed = call(
+        functools.partial(mixed_kernel, hid=hid),
+        shape((events, O * STREAMS), bf16),
+        tuple(mixed_parts[m] for m in range(hid)),
+        vmem=8,
+        us=2.0,
+    )
+
     d_table = call(
-        functools.partial(table_kernel, dp=dp, hid=hid),
+        functools.partial(table_kernel, chunks=chunks, dp=dp, hid=hid),
         [shape((slots, feats), bf16) for r in range(dp)],
-        (block_owners, counts, *d_pooled),
-        in_specs=[SMEM] + [VMEM] * (1 + hid),
+        (block_owners, *counts, *d_pooled),
+        in_specs=[SMEM] + [VMEM] * (chunks + hid),
         scratch=[
             pltpu.VMEM((feats, events), bf16),
             pltpu.VMEM((vocab, feats), bf16),
             pltpu.VMEM((dp, slots, feats), bf16),
             pltpu.SMEM((dp,), jnp.int32),
         ],
-        vmem=56,
+        vmem=20 if vocab <= 4096 else 58,
+        us=6.0,
     )
     table_terms = []
     for far in reversed(range(outer)):
         value = d_table[far * inner]
         for m in range(1, inner):
-            value = add(value, swap(d_table[far * inner + m], "dp", m))
+            value = plus(value, swap(d_table[far * inner + m], "dp", m))
         table_terms.append(swap(value, "dp", far * inner) if far else value)
 
     table_new = call(
         functools.partial(table_adam_kernel, terms=outer),
         [shape(table_w.shape, f32)] * 4,
         (table_w, table_m, table_v, table_ema, *table_terms),
-        vmem=24,
+        vmem=8,
     )
     weights_new = call(
         functools.partial(weight_adam_kernel, terms=outer, dp=dp, hid=hid),
@@ -745,7 +880,7 @@
             *weight_terms,
             *small_terms,
         ),
-        vmem=24,
+        vmem=8,
     )
     return (
         mixed,

time: 226 us -> 167 us (0.74)
  waiting for transfers between devices: 99.7 us -> 56.8 us
  starting transfers between devices: 38 us -> 55.5 us
  between operations: 14.7 us -> 1.32 us
  Pallas kernels: 54.5 us -> 46.9 us
  blocking collectives: 5.4 us -> 0 us
  local copies, waits for them, and re-layouts: 10.2 us -> 6.13 us
  other arithmetic: 3.2 us -> 0.29 us
    ppermute x46 -> x49, waiting for transfers between devices: 99.7 us -> 56.8 us  [swap(): return lax.ppermute(value, axis, [(i, i ^ mask) for i in range(count)])]
    ppermute x46 -> x49, starting transfers between devices: 38 us -> 55.5 us  [swap(): return lax.ppermute(value, axis, [(i, i ^ mask) for i in range(count)])]
    pallas_call x9 -> x16, Pallas kernels: 54.5 us -> 46.9 us  [call(): pl.pallas_call(kernel, out_shape=outs, in_specs=in_specs or [VMEM] * len(...]
    all_gather x1 -> x0, blocking collectives: 5.4 us -> none  [per_device(): vector_full = lax.all_gather(vector_w, 'hid', axis=1, tiled=True)]
    unnamed x92 -> x70, local copies, waits for them, and re-layouts: 8.77 us -> 4.7 us
    convert_element_type x10 -> x4, other arithmetic: 2.53 us -> 0.22 us  [plus(): return (a.astype(f32) + b.astype(f32)).astype(bf16)]
  transfers between devices with their start and end apart: 47 -> 49, of which waited for: 20 -> 18; matrix products, arithmetic and copies ran while one was open for 2% -> 1% of each run, Pallas kernels for 19% -> 21%
where the time goes in v2:
time: 167 us
  waiting for transfers between devices  56.8 us (34%)
  starting transfers between devices  55.5 us (33%)
  Pallas kernels  46.9 us (28%)
  local copies, waits for them, and re-layouts  6.13 us (4%)
    ppermute x49, waiting for transfers between devices, swap(): return lax.ppermute(value, axis, [(i, i ^ mask) for i in range(count)])  56.8 us
    ppermute x49, starting transfers between devices, swap(): return lax.ppermute(value, axis, [(i, i ^ mask) for i in range(count)])  55.5 us
    pallas_call x16, Pallas kernels, call(): pl.pallas_call(kernel, out_shape=outs, in_specs=in_specs or [VMEM] * len(...  46.9 us
    unnamed x70, local copies, waits for them, and re-layouts  4.7 us
  transfers between devices with their start and end apart: 49, of which 18 were waited for; matrix products, arithmetic and copies ran while one was open for 1% of the time, Pallas kernels for 21%

profile of v2, /device:TPU:0, one launch (start us, length us, event | category | flops | bytes accessed | tf_op | source)
XLA Modules:
  0.0 167.0 jit_solution(9319308082152764974)
XLA Ops:
  5.9 3.0 %collective-permute-start = (bf16[1056,128]{1,0:T(8,128)(2,1)S(1)}, bf16[1056,128]{1,0:T(8,128)(2,1)S(1)}, u32[]{:S(2)}, u32[]{:S(2)}) collective-permute-start(bf16[1056,128]{1,0:T(8,128)(2,1)S(1)} %get-tuple-element.92.refs_4_), channel_id=1, source_target_pairs={{0,4},{4,0},{8,12},{12,8},{16,20},{20,16},{24,28},{28,24},{1,5},{5... | collective-permute-start | bytes 811016 | tf_op jit(solution)/shard_map/ppermute | solution.py:75
  8.9 1.6 collective-permute-start.1
  10.5 2.6 %collective-permute-start.3 = (bf16[1056,128]{1,0:T(8,128)(2,1)S(1)}, bf16[1056,128]{1,0:T(8,128)(2,1)S(1)}, u32[]{:S(2)}, u32[]{:S(2)}) collective-permute-start(bf16[1056,128]{1,0:T(8,128)(2,1)S(1)} %get-tuple-element.92.refs_4_), channel_id=1, source_target_pairs={{0,16},{4,20},{8,24},{12,28},{16,0},{20,4},{24,8},{28,12},{1,17},{... | collective-permute-start | bytes 811016 | tf_op jit(solution)/shard_map/ppermute | solution.py:75
  13.3 1.5 collective-permute-start.14
  15.0 4.4 %shard_map.391.refs_0_ = bf16[256,3072]{1,0:T(8,128)(2,1)S(1)} custom-call(s32[1024]{0:T(1024)S(1)} %copy-done, s32[32,128]{1,0:T(8,128)S(1)} %bitcast.54, s32[8,128]{1,0:T(8,128)S(1)} %bitcast.49, s32[8,128]{1,0:T(8,128)S(1)} %add_bitcast_fusion.nxt_ref), custom_call_target="tpu_custom_call" | custom-call | flops 5000000000 | bytes 15000000 | tf_op jit(solution)/shard_map/pallas_call | solution.py:59
  19.4 5.7 %shard_map.392.refs_1_ = bf16[256,3072]{1,0:T(8,128)(2,1)S(1)} custom-call(s32[1024]{0:T(1024)S(1)} %copy-done, s32[32,128]{1,0:T(8,128)S(1)} %bitcast.55, s32[8,128]{1,0:T(8,128)S(1)} %bitcast.50, s32[8,128]{1,0:T(8,128)S(1)} %add_bitcast_fusion.nxt_ref), custom_call_target="tpu_custom_call" | custom-call | flops 5000000000 | bytes 15000000 | tf_op jit(solution)/shard_map/pallas_call | solution.py:59
  25.1 5.1 %shard_map.393.refs_2_ = bf16[256,3072]{1,0:T(8,128)(2,1)S(1)} custom-call(s32[1024]{0:T(1024)S(1)} %copy-done, s32[32,128]{1,0:T(8,128)S(1)} %bitcast.56, s32[8,128]{1,0:T(8,128)S(1)} %bitcast.51, s32[8,128]{1,0:T(8,128)S(1)} %add_bitcast_fusion.nxt_ref), custom_call_target="tpu_custom_call" | custom-call | flops 5000000000 | bytes 15000000 | tf_op jit(solution)/shard_map/pallas_call | solution.py:59
  30.9 1.6 collective-permute-start.15
  32.6 1.6 collective-permute-start.16
  34.2 3.6 %collective-permute-done.15 = bf16[288,128]{1,0:T(8,128)(2,1)S(1)} collective-permute-done((bf16[288,128]{1,0:T(8,128)(2,1)S(1)}, bf16[288,128]{1,0:T(8,128)(2,1)S(1)}, u32[]{:S(2)}, u32[]{:S(2)}) %collective-permute-start.15) | collective-permute-done | bytes 73760 | tf_op jit(solution)/shard_map/ppermute | solution.py:75
  38.4 3.1 %collective-permute-done.16 = bf16[288,128]{1,0:T(8,128)(2,1)S(1)} collective-permute-done((bf16[288,128]{1,0:T(8,128)(2,1)S(1)}, bf16[288,128]{1,0:T(8,128)(2,1)S(1)}, u32[]{:S(2)}, u32[]{:S(2)}) %collective-permute-start.16) | collective-permute-done | bytes 73760 | tf_op jit(solution)/shard_map/ppermute | solution.py:75
  42.0 3.6 %collective-permute-done.2.refs_7_ = bf16[1056,128]{1,0:T(8,128)(2,1)S(1)} collective-permute-done((bf16[1056,128]{1,0:T(8,128)(2,1)S(1)}, bf16[1056,128]{1,0:T(8,128)(2,1)S(1)}, u32[]{:S(2)}, u32[]{:S(2)}) %collective-permute-start.2) | collective-permute-done | bytes 270368 | tf_op jit(solution)/shard_map/ppermute | solution.py:75
  46.1 6.2 %collective-permute-done.4.refs_9_ = bf16[1056,128]{1,0:T(8,128)(2,1)S(1)} collective-permute-done((bf16[1056,128]{1,0:T(8,128)(2,1)S(1)}, bf16[1056,128]{1,0:T(8,128)(2,1)S(1)}, u32[]{:S(2)}, u32[]{:S(2)}) %collective-permute-start.4) | collective-permute-done | bytes 270368 | tf_op jit(solution)/shard_map/ppermute | solution.py:75
  52.9 5.9 %collective-permute-done.6.refs_11_ = bf16[1056,128]{1,0:T(8,128)(2,1)S(1)} collective-permute-done((bf16[1056,128]{1,0:T(8,128)(2,1)S(1)}, bf16[1056,128]{1,0:T(8,128)(2,1)S(1)}, u32[]{:S(2)}, u32[]{:S(2)}) %collective-permute-start.6) | collective-permute-done | bytes 270368 | tf_op jit(solution)/shard_map/ppermute | solution.py:75
  59.3 4.2 %collective-permute-done.17 = bf16[288,128]{1,0:T(8,128)(2,1)S(1)} collective-permute-done((bf16[288,128]{1,0:T(8,128)(2,1)S(1)}, bf16[288,128]{1,0:T(8,128)(2,1)S(1)}, u32[]{:S(2)}, u32[]{:S(2)}) %collective-permute-start.17) | collective-permute-done | bytes 73760 | tf_op jit(solution)/shard_map/ppermute | solution.py:75
  64.3 1.4 collective-permute-start.19
  65.7 3.0 %collective-permute-done.19 = bf16[288,128]{1,0:T(8,128)(2,1)S(1)} collective-permute-done((bf16[288,128]{1,0:T(8,128)(2,1)S(1)}, bf16[288,128]{1,0:T(8,128)(2,1)S(1)}, u32[]{:S(2)}, u32[]{:S(2)}) %collective-permute-start.19) | collective-permute-done | bytes 73760 | tf_op jit(solution)/shard_map/ppermute | solution.py:75
  68.7 1.3 collective-permute-start.21
  70.2 2.9 %collective-permute-done.21 = bf16[288,128]{1,0:T(8,128)(2,1)S(1)} collective-permute-done((bf16[288,128]{1,0:T(8,128)(2,1)S(1)}, bf16[288,128]{1,0:T(8,128)(2,1)S(1)}, u32[]{:S(2)}, u32[]{:S(2)}) %collective-permute-start.21) | collective-permute-done | bytes 73760 | tf_op jit(solution)/shard_map/ppermute | solution.py:75
  73.2 4.4 %shard_map.394.refs_3_ = bf16[256,3072]{1,0:T(8,128)(2,1)S(1)} custom-call(s32[1024]{0:T(1024)S(1)} %copy-done, s32[32,128]{1,0:T(8,128)S(1)} %bitcast.57, s32[8,128]{1,0:T(8,128)S(1)} %bitcast.52, s32[8,128]{1,0:T(8,128)S(1)} %add_bitcast_fusion.nxt_ref), custom_call_target="tpu_custom_call" | custom-call | flops 5000000000 | bytes 15000000 | tf_op jit(solution)/shard_map/pallas_call | solution.py:59
  77.6 3.4 %shard_map.396 = (bf16[128,256]{1,0:T(8,128)(2,1)S(1)}, bf16[128,256]{1,0:T(8,128)(2,1)S(1)}, bf16[128,256]{1,0:T(8,128)(2,1)S(1)}, bf16[128,256]{1,0:T(8,128)(2,1)S(1)}) custom-call(s32[48]{0:T(128)S(1)} %copy-done.23, bf16[256,3072]{1,0:T(8,128)(2,1)S(1)} %shard_map.391.refs_0_, bf16[256,3072]{1,0:T(8,128)(2,1)S(1)} %shard_map.392.refs_1_, ...), custom_call_target="tpu_custom_call" | custom-call | flops 4000000000 | bytes 12000000 | tf_op jit(solution)/shard_map/pallas_call | solution.py:59
  81.6 1.4 collective-permute-start.8
  83.0 6.4 %shard_map.397 = (bf16[6,512,256]{2,1,0:T(8,128)(2,1)S(1)}, bf16[6,256,512]{2,1,0:T(8,128)(2,1)S(1)}, bf16[6,256,256]{2,1,0:T(8,128)(2,1)S(1)}, bf16[6,256,256]{...) custom-call(bf16[8,288,128]{2,1,0:T(8,128)(2,1)S(1)} %bitcast_dynami, ...), custom_call_target="tpu_custom_call" | custom-call | flops 8000000000 | bytes 24000000 | tf_op jit(solution)/shard_map/pallas_call | solution.py:59
  89.5 7.4 %shard_map.398 = (bf16[256,768]{1,0:T(8,128)(2,1)S(1)}, bf16[80,512]{1,0:T(8,128)(2,1)S(1)}, bf16[512,256]{1,0:T(8,128)(2,1)S(1)}, bf16[6,256,256]{2,1,0:T(8,128...) custom-call(bf16[128,256]{1,0:T(8,128)(2,1)S(1)} %get-tuple-element., ...), custom_call_target="tpu_custom_call" | custom-call | flops 10000000000 | bytes 30000000 | tf_op jit(solution)/shard_map/pallas_call | solution.py:59
  96.9 2.6 %shard_map.399 = (bf16[2,4,96,384]{3,2,1,0:T(8,128)(2,1)S(1)}, bf16[2,4,96,384]{3,2,1,0:T(8,128)(2,1)S(1)}, bf16[2,4,96,384]{3,2,1,0:T(8,128)(2,1)S(1)}, bf16[2,4,96,384]{3,2,1,0:T(8,128)(2,1)S(1)}) custom-call(bf16[512,256]{1,0:T(8,128)(2,1)S(1)} %get-tuple-element.109.xt, bf16[6,256,256]{2,1,0:T(8,128)(2,1)S(1)} %get-tuple-element.110.hid_ref, ...), custom_call_target="tpu_custom_call" | custom-call | flops 3000000000 | bytes 9000000 | tf_op jit(solution)/shard_map/pallas_call | solution.py:59
  100.8 1.1 collective-permute-start.26
  102.3 2.6 %collective-permute-done.26.refs_6_.refs_7_ = bf16[128,256]{1,0:T(8,128)(2,1)S(1)} collective-permute-done((bf16[128,256]{1,0:T(8,128)(2,1)S(1)}, bf16[128,256]{1,0:T(8,128)(2,1)S(1)}, u32[]{:S(2)}, u32[]{:S(2)}) %collective-permute-start.26) | collective-permute-done | bytes 65568 | tf_op jit(solution)/shard_map/ppermute | solution.py:75
  104.9 1.4 collective-permute-start.33
  107.3 1.9 %collective-permute-done.33.refs_6_ = bf16[128,256]{1,0:T(8,128)(2,1)S(1)} collective-permute-done((bf16[128,256]{1,0:T(8,128)(2,1)S(1)}, bf16[128,256]{1,0:T(8,128)(2,1)S(1)}, u32[]{:S(2)}, u32[]{:S(2)}) %collective-permute-start.33) | collective-permute-done | bytes 65568 | tf_op jit(solution)/shard_map/ppermute | solution.py:75
  109.3 2.4 %shard_map.403 = (bf16[768,128]{1,0:T(8,128)(2,1)S(1)}, bf16[768,128]{1,0:T(8,128)(2,1)S(1)}, bf16[768,128]{1,0:T(8,128)(2,1)S(1)}, bf16[768,128]{1,0:T(8,128)(2...) custom-call(s32[48]{0:T(128)S(1)} %copy-done.23, ...), custom_call_target="tpu_custom_call" | custom-call | flops 6000000000 | bytes 18000000 | tf_op jit(solution)/shard_map/pallas_call | solution.py:59
  112.3 1.6 collective-permute-start.40
  114.4 1.5 collective-permute-start.34
  115.9 3.7 %collective-permute-done.38 = bf16[768,128]{1,0:T(8,128)(2,1)S(1)} collective-permute-done((bf16[768,128]{1,0:T(8,128)(2,1)S(1)}, bf16[768,128]{1,0:T(8,128)(2,1)S(1)}, u32[]{:S(2)}, u32[]{:S(2)}) %collective-permute-start.38) | collective-permute-done | bytes 196640 | tf_op jit(solution)/shard_map/ppermute | solution.py:75
  119.6 2.0 %collective-permute-start.28 = (bf16[80,512]{1,0:T(8,128)(2,1)S(1)}, bf16[80,512]{1,0:T(8,128)(2,1)S(1)}, u32[]{:S(2)}, u32[]{:S(2)}) collective-permute-start(bf16[80,512]{1,0:T(8,128)(2,1)S(1)} %get-tuple-element.121.refs_2_), channel_id=1, source_target_pairs={{0,2},{1,3},{2,0},{3,1},{4,6},{5,7},{6,4},{7,5},{8,10},{9,11},{10,... | collective-permute-start | bytes 245768 | tf_op jit(solution)/shard_map/ppermute | solution.py:75
  121.7 2.4 %collective-permute-done.28.refs_3_ = bf16[80,512]{1,0:T(8,128)(2,1)S(1)} collective-permute-done((bf16[80,512]{1,0:T(8,128)(2,1)S(1)}, bf16[80,512]{1,0:T(8,128)(2,1)S(1)}, u32[]{:S(2)}, u32[]{:S(2)}) %collective-permute-start.28) | collective-permute-done | bytes 81952 | tf_op jit(solution)/shard_map/ppermute | solution.py:75
  125.4 2.6 %collective-permute-done.36 = bf16[768,128]{1,0:T(8,128)(2,1)S(1)} collective-permute-done((bf16[768,128]{1,0:T(8,128)(2,1)S(1)}, bf16[768,128]{1,0:T(8,128)(2,1)S(1)}, u32[]{:S(2)}, u32[]{:S(2)}) %collective-permute-start.36) | collective-permute-done | bytes 196640 | tf_op jit(solution)/shard_map/ppermute | solution.py:75
  128.1 1.9 %collective-permute-start.37 = (bf16[768,128]{1,0:T(8,128)(2,1)S(1)}, bf16[768,128]{1,0:T(8,128)(2,1)S(1)}, u32[]{:S(2)}, u32[]{:S(2)}) collective-permute-start(bf16[768,128]{1,0:T(8,128)(2,1)S(1)} %add_convert_fusion.2), channel_id=1, source_target_pairs={{0,16},{4,20},{8,24},{12,28},{16,0},{20,4},{24,8},{28,12},{1,17},{... | collective-permute-start | bytes 589832 | tf_op jit(solution)/shard_map/ppermute | solution.py:75
  130.0 2.2 %collective-permute-done.34 = bf16[768,128]{1,0:T(8,128)(2,1)S(1)} collective-permute-done((bf16[768,128]{1,0:T(8,128)(2,1)S(1)}, bf16[768,128]{1,0:T(8,128)(2,1)S(1)}, u32[]{:S(2)}, u32[]{:S(2)}) %collective-permute-start.34) | collective-permute-done | bytes 196640 | tf_op jit(solution)/shard_map/ppermute | solution.py:75
  132.8 5.4 %collective-permute-done.42.refs_3_ = bf16[80,512]{1,0:T(8,128)(2,1)S(1)} collective-permute-done((bf16[80,512]{1,0:T(8,128)(2,1)S(1)}, bf16[80,512]{1,0:T(8,128)(2,1)S(1)}, u32[]{:S(2)}, u32[]{:S(2)}) %collective-permute-start.42) | collective-permute-done | bytes 81952 | tf_op jit(solution)/shard_map/ppermute | solution.py:75
  138.1 3.7 %collective-permute-start.35 = (bf16[768,128]{1,0:T(8,128)(2,1)S(1)}, bf16[768,128]{1,0:T(8,128)(2,1)S(1)}, u32[]{:S(2)}, u32[]{:S(2)}) collective-permute-start(bf16[768,128]{1,0:T(8,128)(2,1)S(1)} %add_convert_fusion.3), channel_id=1, source_target_pairs={{0,24},{4,28},{8,16},{12,20},{16,8},{20,12},{24,0},{28,4},{1,25},{... | collective-permute-start | bytes 589832 | tf_op jit(solution)/shard_map/ppermute | solution.py:75
  141.8 1.3 collective-permute-start.30
  144.2 1.3 collective-permute-start.46
  145.5 1.8 %collective-permute-done.35.refs_4_ = bf16[768,128]{1,0:T(8,128)(2,1)S(1)} collective-permute-done((bf16[768,128]{1,0:T(8,128)(2,1)S(1)}, bf16[768,128]{1,0:T(8,128)(2,1)S(1)}, u32[]{:S(2)}, u32[]{:S(2)}) %collective-permute-start.35) | collective-permute-done | bytes 196640 | tf_op jit(solution)/shard_map/ppermute | solution.py:75
  147.2 8.4 %collective-permute-start.47 = (bf16[80,512]{1,0:T(8,128)(2,1)S(1)}, bf16[80,512]{1,0:T(8,128)(2,1)S(1)}, u32[]{:S(2)}, u32[]{:S(2)}) collective-permute-start(bf16[80,512]{1,0:T(8,128)(2,1)S(1)} %get-tuple-element.146.refs_20_), channel_id=1, source_target_pairs={{0,16},{4,20},{8,24},{12,28},{16,0},{20,4},{24,8},{28,12},{1,17},{... | collective-permute-start | bytes 245768 | tf_op jit(solution)/shard_map/ppermute | solution.py:75
  156.0 3.6 %collective-permute-start.45 = (bf16[96,384]{1,0:T(8,128)(2,1)S(1)}, bf16[96,384]{1,0:T(8,128)(2,1)S(1)}, u32[]{:S(2)}, u32[]{:S(2)}) collective-permute-start(bf16[96,384]{1,0:T(8,128)(2,1)S(1)} %get-tuple-element.145), channel_id=1, source_target_pairs={{0,24},{4,28},{8,16},{12,20},{16,8},{20,12},{24,0},{28,4},{1,25},{... | collective-permute-start | bytes 221192 | tf_op jit(solution)/shard_map/ppermute | solution.py:75
  159.6 1.5 shard_map.404
  161.1 1.5 collective-permute-done.45.refs_19_
  165.7 1.3 shard_map.402
  (157 shorter events, 20.7 us)
Async XLA Ops:
  5.9 24.4 %collective-permute-start = (bf16[1056,128]{1,0:T(8,128)(2,1)S(1)}, bf16[1056,128]{1,0:T(8,128)(2,1)S(1)}, u32[]{:S(2)}, u32[]{:S(2)}) collective-permute-start(bf16[1056,128]{1,0:T(8,128)(2,1)S(1)} %get-tuple-element.92.refs_4_), channel_id=1, source_target_pairs={{0,4},{4,0},{8,12},{12,8},{16,20},{20,16},{24,28},{28,24},{1,5},{5... | collective-permute-start | bytes 811016 | tf_op jit(solution)/shard_map/ppermute | solution.py:75
  8.9 22.0 %collective-permute-start.1 = (bf16[1056,128]{1,0:T(8,128)(2,1)S(1)}, bf16[1056,128]{1,0:T(8,128)(2,1)S(1)}, u32[]{:S(2)}, u32[]{:S(2)}) collective-permute-start(bf16[1056,128]{1,0:T(8,128)(2,1)S(1)} %get-tuple-element.92.refs_4_), channel_id=1, source_target_pairs={{0,8},{4,12},{8,0},{12,4},{16,24},{20,28},{24,16},{28,20},{1,9},{5... | collective-permute-start | bytes 811016 | tf_op jit(solution)/shard_map/ppermute | solution.py:75
  10.5 22.1 %collective-permute-start.3 = (bf16[1056,128]{1,0:T(8,128)(2,1)S(1)}, bf16[1056,128]{1,0:T(8,128)(2,1)S(1)}, u32[]{:S(2)}, u32[]{:S(2)}) collective-permute-start(bf16[1056,128]{1,0:T(8,128)(2,1)S(1)} %get-tuple-element.92.refs_4_), channel_id=1, source_target_pairs={{0,16},{4,20},{8,24},{12,28},{16,0},{20,4},{24,8},{28,12},{1,17},{... | collective-permute-start | bytes 811016 | tf_op jit(solution)/shard_map/ppermute | solution.py:75
  13.1 19.6 %collective-permute-start.5 = (bf16[1056,128]{1,0:T(8,128)(2,1)S(1)}, bf16[1056,128]{1,0:T(8,128)(2,1)S(1)}, u32[]{:S(2)}, u32[]{:S(2)}) collective-permute-start(bf16[1056,128]{1,0:T(8,128)(2,1)S(1)} %get-tuple-element.92.refs_4_), channel_id=1, source_target_pairs={{0,24},{4,28},{8,16},{12,20},{16,8},{20,12},{24,0},{28,4},{1,25},{... | collective-permute-start | bytes 811016 | tf_op jit(solution)/shard_map/ppermute | solution.py:75
  13.3 16.9 %collective-permute-start.14 = (bf16[288,128]{1,0:T(8,128)(2,1)S(1)}, bf16[288,128]{1,0:T(8,128)(2,1)S(1)}, u32[]{:S(2)}, u32[]{:S(2)}) collective-permute-start(bf16[288,128]{1,0:T(8,128)(2,1)S(1)} %get-tuple-element.101), channel_id=1, source_target_pairs={{0,2},{1,3},{2,0},{3,1},{4,6},{5,7},{6,4},{7,5},{8,10},{9,11},{10,... | collective-permute-start | bytes 221192 | tf_op jit(solution)/shard_map/ppermute | solution.py:75
  30.2 50.8 %collective-permute-start.10 = (bf16[224,256]{1,0:T(8,128)(2,1)S(1)}, bf16[224,256]{1,0:T(8,128)(2,1)S(1)}, u32[]{:S(2)}, u32[]{:S(2)}) collective-permute-start(bf16[224,256]{1,0:T(8,128)(2,1)S(1)} %get-tuple-element.98), channel_id=1, source_target_pairs={{0,1},{1,0},{2,3},{3,2},{4,5},{5,4},{6,7},{7,6},{8,9},{9,8},{10,11... | collective-permute-start | bytes 344072 | tf_op jit(solution)/shard_map/ppermute | solution.py:75
  30.3 51.2 %collective-permute-start.11 = (bf16[224,256]{1,0:T(8,128)(2,1)S(1)}, bf16[224,256]{1,0:T(8,128)(2,1)S(1)}, u32[]{:S(2)}, u32[]{:S(2)}) collective-permute-start(bf16[224,256]{1,0:T(8,128)(2,1)S(1)} %get-tuple-element.99), channel_id=1, source_target_pairs={{0,2},{1,3},{2,0},{3,1},{4,6},{5,7},{6,4},{7,5},{8,10},{9,11},{10,... | collective-permute-start | bytes 344072 | tf_op jit(solution)/shard_map/ppermute | solution.py:75
  30.9 7.0 %collective-permute-start.15 = (bf16[288,128]{1,0:T(8,128)(2,1)S(1)}, bf16[288,128]{1,0:T(8,128)(2,1)S(1)}, u32[]{:S(2)}, u32[]{:S(2)}) collective-permute-start(bf16[288,128]{1,0:T(8,128)(2,1)S(1)} %slice.48), channel_id=1, source_target_pairs={{0,2},{1,3},{2,0},{3,1},{4,6},{5,7},{6,4},{7,5},{8,10},{9,11},{10,... | collective-permute-start | bytes 221192 | tf_op jit(solution)/shard_map/ppermute | solution.py:75
  32.5 50.4 %collective-permute-start.12 = (bf16[224,256]{1,0:T(8,128)(2,1)S(1)}, bf16[224,256]{1,0:T(8,128)(2,1)S(1)}, u32[]{:S(2)}, u32[]{:S(2)}) collective-permute-start(bf16[224,256]{1,0:T(8,128)(2,1)S(1)} %get-tuple-element.100), channel_id=1, source_target_pairs={{0,3},{1,2},{2,1},{3,0},{4,7},{5,6},{6,5},{7,4},{8,11},{9,10},{10,... | collective-permute-start | bytes 344072 | tf_op jit(solution)/shard_map/ppermute | solution.py:75
  32.6 8.9 %collective-permute-start.16 = (bf16[288,128]{1,0:T(8,128)(2,1)S(1)}, bf16[288,128]{1,0:T(8,128)(2,1)S(1)}, u32[]{:S(2)}, u32[]{:S(2)}) collective-permute-start(bf16[288,128]{1,0:T(8,128)(2,1)S(1)} %slice.49), channel_id=1, source_target_pairs={{0,2},{1,3},{2,0},{3,1},{4,6},{5,7},{6,4},{7,5},{8,10},{9,11},{10,... | collective-permute-start | bytes 221192 | tf_op jit(solution)/shard_map/ppermute | solution.py:75
  37.9 7.7 %collective-permute-start.2 = (bf16[1056,128]{1,0:T(8,128)(2,1)S(1)}, bf16[1056,128]{1,0:T(8,128)(2,1)S(1)}, u32[]{:S(2)}, u32[]{:S(2)}) collective-permute-start(bf16[1056,128]{1,0:T(8,128)(2,1)S(1)} %collective-permute-done.1.refs_6_), channel_id=1, source_target_pairs={{0,4},{4,0},{8,12},{12,8},{16,20},{20,16},{24,28},{28,24},{1,5},{5... | collective-permute-start | bytes 811016 | tf_op jit(solution)/shard_map/ppermute | solution.py:75
  41.5 22.7 %collective-permute-start.18 = (bf16[288,128]{1,0:T(8,128)(2,1)S(1)}, bf16[288,128]{1,0:T(8,128)(2,1)S(1)}, u32[]{:S(2)}, u32[]{:S(2)}) collective-permute-start(bf16[288,128]{1,0:T(8,128)(2,1)S(1)} %slice.51), channel_id=1, source_target_pairs={{0,2},{1,3},{2,0},{3,1},{4,6},{5,7},{6,4},{7,5},{8,10},{9,11},{10,... | collective-permute-start | bytes 221192 | tf_op jit(solution)/shard_map/ppermute | solution.py:75
  45.6 6.8 %collective-permute-start.4 = (bf16[1056,128]{1,0:T(8,128)(2,1)S(1)}, bf16[1056,128]{1,0:T(8,128)(2,1)S(1)}, u32[]{:S(2)}, u32[]{:S(2)}) collective-permute-start(bf16[1056,128]{1,0:T(8,128)(2,1)S(1)} %collective-permute-done.3.refs_8_), channel_id=1, source_target_pairs={{0,4},{4,0},{8,12},{12,8},{16,20},{20,16},{24,28},{28,24},{1,5},{5... | collective-permute-start | bytes 811016 | tf_op jit(solution)/shard_map/ppermute | solution.py:75
  52.3 6.5 %collective-permute-start.6 = (bf16[1056,128]{1,0:T(8,128)(2,1)S(1)}, bf16[1056,128]{1,0:T(8,128)(2,1)S(1)}, u32[]{:S(2)}, u32[]{:S(2)}) collective-permute-start(bf16[1056,128]{1,0:T(8,128)(2,1)S(1)} %collective-permute-done.5.refs_10_), channel_id=1, source_target_pairs={{0,4},{4,0},{8,12},{12,8},{16,20},{20,16},{24,28},{28,24},{1,5},{5... | collective-permute-start | bytes 811016 | tf_op jit(solution)/shard_map/ppermute | solution.py:75
  58.8 4.8 %collective-permute-start.17 = (bf16[288,128]{1,0:T(8,128)(2,1)S(1)}, bf16[288,128]{1,0:T(8,128)(2,1)S(1)}, u32[]{:S(2)}, u32[]{:S(2)}) collective-permute-start(bf16[288,128]{1,0:T(8,128)(2,1)S(1)} %slice.50), channel_id=1, source_target_pairs={{0,2},{1,3},{2,0},{3,1},{4,6},{5,7},{6,4},{7,5},{8,10},{9,11},{10,... | collective-permute-start | bytes 221192 | tf_op jit(solution)/shard_map/ppermute | solution.py:75
  63.6 6.5 %collective-permute-start.20 = (bf16[288,128]{1,0:T(8,128)(2,1)S(1)}, bf16[288,128]{1,0:T(8,128)(2,1)S(1)}, u32[]{:S(2)}, u32[]{:S(2)}) collective-permute-start(bf16[288,128]{1,0:T(8,128)(2,1)S(1)} %slice.53), channel_id=1, source_target_pairs={{0,2},{1,3},{2,0},{3,1},{4,6},{5,7},{6,4},{7,5},{8,10},{9,11},{10,... | collective-permute-start | bytes 221192 | tf_op jit(solution)/shard_map/ppermute | solution.py:75
  64.3 4.5 %collective-permute-start.19 = (bf16[288,128]{1,0:T(8,128)(2,1)S(1)}, bf16[288,128]{1,0:T(8,128)(2,1)S(1)}, u32[]{:S(2)}, u32[]{:S(2)}) collective-permute-start(bf16[288,128]{1,0:T(8,128)(2,1)S(1)} %slice.52), channel_id=1, source_target_pairs={{0,2},{1,3},{2,0},{3,1},{4,6},{5,7},{6,4},{7,5},{8,10},{9,11},{10,... | collective-permute-start | bytes 221192 | tf_op jit(solution)/shard_map/ppermute | solution.py:75
  68.7 4.4 %collective-permute-start.21 = (bf16[288,128]{1,0:T(8,128)(2,1)S(1)}, bf16[288,128]{1,0:T(8,128)(2,1)S(1)}, u32[]{:S(2)}, u32[]{:S(2)}) collective-permute-start(bf16[288,128]{1,0:T(8,128)(2,1)S(1)} %slice.54), channel_id=1, source_target_pairs={{0,2},{1,3},{2,0},{3,1},{4,6},{5,7},{6,4},{7,5},{8,10},{9,11},{10,... | collective-permute-start | bytes 221192 | tf_op jit(solution)/shard_map/ppermute | solution.py:75
  70.1 12.9 %collective-permute-start.13 = (bf16[8,288,128]{2,1,0:T(8,128)(2,1)S(1)}, bf16[8,288,128]{2,1,0:T(8,128)(2,1)S(1)}, u32[]{:S(2)}, u32[]{:S(2)}) collective-permute-start(bf16[8,288,128]{2,1,0:T(8,128)(2,1)S(1)} %bitcast_dynamic-update-slice_fusion.8.refs_0_), channel_id=1, source_target_pairs={{0,1},{1,0},{2,3},{3,2},{4,5},{5,4},{6,7},{7,6},{8,9},{9,8},{10,11... | collective-permute-start | bytes 1769480 | tf_op jit(solution)/shard_map/ppermute | solution.py:75
  73.1 9.9 %collective-permute-start.22 = (bf16[8,288,128]{2,1,0:T(8,128)(2,1)S(1)}, bf16[8,288,128]{2,1,0:T(8,128)(2,1)S(1)}, u32[]{:S(2)}, u32[]{:S(2)}) collective-permute-start(bf16[8,288,128]{2,1,0:T(8,128)(2,1)S(1)} %bitcast_dynamic-update-slice_fusion.refs_2_), channel_id=1, source_target_pairs={{0,1},{1,0},{2,3},{3,2},{4,5},{5,4},{6,7},{7,6},{8,9},{9,8},{10,11... | collective-permute-start | bytes 1769480 | tf_op jit(solution)/shard_map/ppermute | solution.py:75
  81.0 8.5 %collective-permute-start.7 = (bf16[128,256]{1,0:T(8,128)(2,1)S(1)}, bf16[128,256]{1,0:T(8,128)(2,1)S(1)}, u32[]{:S(2)}, u32[]{:S(2)}) collective-permute-start(bf16[128,256]{1,0:T(8,128)(2,1)S(1)} %get-tuple-element.94), channel_id=1, source_target_pairs={{0,1},{1,0},{2,3},{3,2},{4,5},{5,4},{6,7},{7,6},{8,9},{9,8},{10,11... | collective-permute-start | bytes 196616 | tf_op jit(solution)/shard_map/ppermute | solution.py:75
  81.6 7.9 %collective-permute-start.8 = (bf16[128,256]{1,0:T(8,128)(2,1)S(1)}, bf16[128,256]{1,0:T(8,128)(2,1)S(1)}, u32[]{:S(2)}, u32[]{:S(2)}) collective-permute-start(bf16[128,256]{1,0:T(8,128)(2,1)S(1)} %get-tuple-element.95), channel_id=1, source_target_pairs={{0,2},{1,3},{2,0},{3,1},{4,6},{5,7},{6,4},{7,5},{8,10},{9,11},{10,... | collective-permute-start | bytes 196616 | tf_op jit(solution)/shard_map/ppermute | solution.py:75
  82.9 6.6 %collective-permute-start.9 = (bf16[128,256]{1,0:T(8,128)(2,1)S(1)}, bf16[128,256]{1,0:T(8,128)(2,1)S(1)}, u32[]{:S(2)}, u32[]{:S(2)}) collective-permute-start(bf16[128,256]{1,0:T(8,128)(2,1)S(1)} %get-tuple-element.96), channel_id=1, source_target_pairs={{0,3},{1,2},{2,1},{3,0},{4,7},{5,6},{6,5},{7,4},{8,11},{9,10},{10,... | collective-permute-start | bytes 196616 | tf_op jit(solution)/shard_map/ppermute | solution.py:75
  99.5 6.8 %collective-permute-start.23 = (bf16[2,4,96,384]{3,2,1,0:T(8,128)(2,1)S(1)}, bf16[2,4,96,384]{3,2,1,0:T(8,128)(2,1)S(1)}, u32[]{:S(2)}, u32[]{:S(2)}) collective-permute-start(bf16[2,4,96,384]{3,2,1,0:T(8,128)(2,1)S(1)} %get-tuple-element.114), channel_id=1, source_target_pairs={{0,1},{1,0},{2,3},{3,2},{4,5},{5,4},{6,7},{7,6},{8,9},{9,8},{10,11... | collective-permute-start | bytes 1769480 | tf_op jit(solution)/shard_map/ppermute | solution.py:75
  100.2 6.1 %collective-permute-start.24 = (bf16[2,4,96,384]{3,2,1,0:T(8,128)(2,1)S(1)}, bf16[2,4,96,384]{3,2,1,0:T(8,128)(2,1)S(1)}, u32[]{:S(2)}, u32[]{:S(2)}) collective-permute-start(bf16[2,4,96,384]{3,2,1,0:T(8,128)(2,1)S(1)} %get-tuple-element.116), channel_id=1, source_target_pairs={{0,1},{1,0},{2,3},{3,2},{4,5},{5,4},{6,7},{7,6},{8,9},{9,8},{10,11... | collective-permute-start | bytes 1769480 | tf_op jit(solution)/shard_map/ppermute | solution.py:75
  100.3 6.0 %collective-permute-start.25 = (bf16[80,512]{1,0:T(8,128)(2,1)S(1)}, bf16[80,512]{1,0:T(8,128)(2,1)S(1)}, u32[]{:S(2)}, u32[]{:S(2)}) collective-permute-start(bf16[80,512]{1,0:T(8,128)(2,1)S(1)} %get-tuple-element.117.refs_4_), channel_id=1, source_target_pairs={{0,1},{1,0},{2,3},{3,2},{4,5},{5,4},{6,7},{7,6},{8,9},{9,8},{10,11... | collective-permute-start | bytes 245768 | tf_op jit(solution)/shard_map/ppermute | solution.py:75
  100.8 4.1 %collective-permute-start.26 = (bf16[128,256]{1,0:T(8,128)(2,1)S(1)}, bf16[128,256]{1,0:T(8,128)(2,1)S(1)}, u32[]{:S(2)}, u32[]{:S(2)}) collective-permute-start(bf16[128,256]{1,0:T(8,128)(2,1)S(1)} %get-tuple-element.118), channel_id=1, source_target_pairs={{0,3},{1,2},{2,1},{3,0},{4,7},{5,6},{6,5},{7,4},{8,11},{9,10},{10,... | collective-permute-start | bytes 196616 | tf_op jit(solution)/shard_map/ppermute | solution.py:75
  101.8 5.5 %collective-permute-start.32 = (bf16[128,256]{1,0:T(8,128)(2,1)S(1)}, bf16[128,256]{1,0:T(8,128)(2,1)S(1)}, u32[]{:S(2)}, u32[]{:S(2)}) collective-permute-start(bf16[128,256]{1,0:T(8,128)(2,1)S(1)} %get-tuple-element.125), channel_id=1, source_target_pairs={{0,1},{1,0},{2,3},{3,2},{4,5},{5,4},{6,7},{7,6},{8,9},{9,8},{10,11... | collective-permute-start | bytes 196616 | tf_op jit(solution)/shard_map/ppermute | solution.py:75
  104.9 4.4 %collective-permute-start.33 = (bf16[128,256]{1,0:T(8,128)(2,1)S(1)}, bf16[128,256]{1,0:T(8,128)(2,1)S(1)}, u32[]{:S(2)}, u32[]{:S(2)}) collective-permute-start(bf16[128,256]{1,0:T(8,128)(2,1)S(1)} %get-tuple-element.126), channel_id=1, source_target_pairs={{0,2},{1,3},{2,0},{3,1},{4,6},{5,7},{6,4},{7,5},{8,10},{9,11},{10,... | collective-permute-start | bytes 196616 | tf_op jit(solution)/shard_map/ppermute | solution.py:75
  106.6 18.2 %collective-permute-start.27 = (bf16[2,4,96,384]{3,2,1,0:T(8,128)(2,1)S(1)}, bf16[2,4,96,384]{3,2,1,0:T(8,128)(2,1)S(1)}, u32[]{:S(2)}, u32[]{:S(2)}) collective-permute-start(bf16[2,4,96,384]{3,2,1,0:T(8,128)(2,1)S(1)} %get-tuple-element.120), channel_id=1, source_target_pairs={{0,2},{1,3},{2,0},{3,1},{4,6},{5,7},{6,4},{7,5},{8,10},{9,11},{10,... | collective-permute-start | bytes 1769480 | tf_op jit(solution)/shard_map/ppermute | solution.py:75
  111.7 7.9 %collective-permute-start.38 = (bf16[768,128]{1,0:T(8,128)(2,1)S(1)}, bf16[768,128]{1,0:T(8,128)(2,1)S(1)}, u32[]{:S(2)}, u32[]{:S(2)}) collective-permute-start(bf16[768,128]{1,0:T(8,128)(2,1)S(1)} %get-tuple-element.132), channel_id=1, source_target_pairs={{0,4},{4,0},{8,12},{12,8},{16,20},{20,16},{24,28},{28,24},{1,5},{5... | collective-permute-start | bytes 589832 | tf_op jit(solution)/shard_map/ppermute | solution.py:75
  112.3 30.9 %collective-permute-start.40 = (bf16[768,128]{1,0:T(8,128)(2,1)S(1)}, bf16[768,128]{1,0:T(8,128)(2,1)S(1)}, u32[]{:S(2)}, u32[]{:S(2)}) collective-permute-start(bf16[768,128]{1,0:T(8,128)(2,1)S(1)} %get-tuple-element.134), channel_id=1, source_target_pairs={{0,4},{4,0},{8,12},{12,8},{16,20},{20,16},{24,28},{28,24},{1,5},{5... | collective-permute-start | bytes 589832 | tf_op jit(solution)/shard_map/ppermute | solution.py:75
  113.9 14.1 %collective-permute-start.36 = (bf16[768,128]{1,0:T(8,128)(2,1)S(1)}, bf16[768,128]{1,0:T(8,128)(2,1)S(1)}, u32[]{:S(2)}, u32[]{:S(2)}) collective-permute-start(bf16[768,128]{1,0:T(8,128)(2,1)S(1)} %get-tuple-element.130), channel_id=1, source_target_pairs={{0,4},{4,0},{8,12},{12,8},{16,20},{20,16},{24,28},{28,24},{1,5},{5... | collective-permute-start | bytes 589832 | tf_op jit(solution)/shard_map/ppermute | solution.py:75
  114.4 17.8 %collective-permute-start.34 = (bf16[768,128]{1,0:T(8,128)(2,1)S(1)}, bf16[768,128]{1,0:T(8,128)(2,1)S(1)}, u32[]{:S(2)}, u32[]{:S(2)}) collective-permute-start(bf16[768,128]{1,0:T(8,128)(2,1)S(1)} %get-tuple-element.128), channel_id=1, source_target_pairs={{0,4},{4,0},{8,12},{12,8},{16,20},{20,16},{24,28},{28,24},{1,5},{5... | collective-permute-start | bytes 589832 | tf_op jit(solution)/shard_map/ppermute | solution.py:75
  119.6 4.4 %collective-permute-start.28 = (bf16[80,512]{1,0:T(8,128)(2,1)S(1)}, bf16[80,512]{1,0:T(8,128)(2,1)S(1)}, u32[]{:S(2)}, u32[]{:S(2)}) collective-permute-start(bf16[80,512]{1,0:T(8,128)(2,1)S(1)} %get-tuple-element.121.refs_2_), channel_id=1, source_target_pairs={{0,2},{1,3},{2,0},{3,1},{4,6},{5,7},{6,4},{7,5},{8,10},{9,11},{10,... | collective-permute-start | bytes 245768 | tf_op jit(solution)/shard_map/ppermute | solution.py:75
  124.0 19.3 %collective-permute-start.39 = (bf16[768,128]{1,0:T(8,128)(2,1)S(1)}, bf16[768,128]{1,0:T(8,128)(2,1)S(1)}, u32[]{:S(2)}, u32[]{:S(2)}) collective-permute-start(bf16[768,128]{1,0:T(8,128)(2,1)S(1)} %add_convert_fusion.1), channel_id=1, source_target_pairs={{0,8},{4,12},{8,0},{12,4},{16,24},{20,28},{24,16},{28,20},{1,9},{5... | collective-permute-start | bytes 589832 | tf_op jit(solution)/shard_map/ppermute | solution.py:75
  125.0 16.8 %collective-permute-start.41 = (bf16[4,96,384]{2,1,0:T(8,128)(2,1)S(1)}, bf16[4,96,384]{2,1,0:T(8,128)(2,1)S(1)}, u32[]{:S(2)}, u32[]{:S(2)}) collective-permute-start(bf16[4,96,384]{2,1,0:T(8,128)(2,1)S(1)} %get-tuple-element.140), channel_id=1, source_target_pairs={{0,4},{4,0},{8,12},{12,8},{16,20},{20,16},{24,28},{28,24},{1,5},{5... | collective-permute-start | bytes 884744 | tf_op jit(solution)/shard_map/ppermute | solution.py:75
  128.1 16.1 %collective-permute-start.37 = (bf16[768,128]{1,0:T(8,128)(2,1)S(1)}, bf16[768,128]{1,0:T(8,128)(2,1)S(1)}, u32[]{:S(2)}, u32[]{:S(2)}) collective-permute-start(bf16[768,128]{1,0:T(8,128)(2,1)S(1)} %add_convert_fusion.2), channel_id=1, source_target_pairs={{0,16},{4,20},{8,24},{12,28},{16,0},{20,4},{24,8},{28,12},{1,17},{... | collective-permute-start | bytes 589832 | tf_op jit(solution)/shard_map/ppermute | solution.py:75
  132.2 5.9 %collective-permute-start.42 = (bf16[80,512]{1,0:T(8,128)(2,1)S(1)}, bf16[80,512]{1,0:T(8,128)(2,1)S(1)}, u32[]{:S(2)}, u32[]{:S(2)}) collective-permute-start(bf16[80,512]{1,0:T(8,128)(2,1)S(1)} %get-tuple-element.141.refs_2_), channel_id=1, source_target_pairs={{0,4},{4,0},{8,12},{12,8},{16,20},{20,16},{24,28},{28,24},{1,5},{5... | collective-permute-start | bytes 245768 | tf_op jit(solution)/shard_map/ppermute | solution.py:75
  138.1 9.1 %collective-permute-start.35 = (bf16[768,128]{1,0:T(8,128)(2,1)S(1)}, bf16[768,128]{1,0:T(8,128)(2,1)S(1)}, u32[]{:S(2)}, u32[]{:S(2)}) collective-permute-start(bf16[768,128]{1,0:T(8,128)(2,1)S(1)} %add_convert_fusion.3), channel_id=1, source_target_pairs={{0,24},{4,28},{8,16},{12,20},{16,8},{20,12},{24,0},{28,4},{1,25},{... | collective-permute-start | bytes 589832 | tf_op jit(solution)/shard_map/ppermute | solution.py:75
  141.8 22.0 %collective-permute-start.30 = (bf16[256,768]{1,0:T(8,128)(2,1)S(1)}, bf16[256,768]{1,0:T(8,128)(2,1)S(1)}, u32[]{:S(2)}, u32[]{:S(2)}) collective-permute-start(bf16[256,768]{1,0:T(8,128)(2,1)S(1)} %get-tuple-element.123.refs_0_), channel_id=1, source_target_pairs={{0,2},{1,3},{2,0},{3,1},{4,6},{5,7},{6,4},{7,5},{8,10},{9,11},{10,... | collective-permute-start | bytes 1179656 | tf_op jit(solution)/shard_map/ppermute | solution.py:75
  143.2 12.4 %collective-permute-start.43 = (bf16[96,384]{1,0:T(8,128)(2,1)S(1)}, bf16[96,384]{1,0:T(8,128)(2,1)S(1)}, u32[]{:S(2)}, u32[]{:S(2)}) collective-permute-start(bf16[96,384]{1,0:T(8,128)(2,1)S(1)} %get-tuple-element.143), channel_id=1, source_target_pairs={{0,8},{4,12},{8,0},{12,4},{16,24},{20,28},{24,16},{28,20},{1,9},{5... | collective-permute-start | bytes 221192 | tf_op jit(solution)/shard_map/ppermute | solution.py:75
  143.3 12.6 %collective-permute-start.44 = (bf16[96,384]{1,0:T(8,128)(2,1)S(1)}, bf16[96,384]{1,0:T(8,128)(2,1)S(1)}, u32[]{:S(2)}, u32[]{:S(2)}) collective-permute-start(bf16[96,384]{1,0:T(8,128)(2,1)S(1)} %get-tuple-element.144), channel_id=1, source_target_pairs={{0,16},{4,20},{8,24},{12,28},{16,0},{20,4},{24,8},{28,12},{1,17},{... | collective-permute-start | bytes 221192 | tf_op jit(solution)/shard_map/ppermute | solution.py:75
  144.2 18.5 %collective-permute-start.46 = (bf16[80,512]{1,0:T(8,128)(2,1)S(1)}, bf16[80,512]{1,0:T(8,128)(2,1)S(1)}, u32[]{:S(2)}, u32[]{:S(2)}) collective-permute-start(bf16[80,512]{1,0:T(8,128)(2,1)S(1)} %get-tuple-element.146.refs_20_), channel_id=1, source_target_pairs={{0,8},{4,12},{8,0},{12,4},{16,24},{20,28},{24,16},{28,20},{1,9},{5... | collective-permute-start | bytes 245768 | tf_op jit(solution)/shard_map/ppermute | solution.py:75
  147.2 15.4 %collective-permute-start.47 = (bf16[80,512]{1,0:T(8,128)(2,1)S(1)}, bf16[80,512]{1,0:T(8,128)(2,1)S(1)}, u32[]{:S(2)}, u32[]{:S(2)}) collective-permute-start(bf16[80,512]{1,0:T(8,128)(2,1)S(1)} %get-tuple-element.146.refs_20_), channel_id=1, source_target_pairs={{0,16},{4,20},{8,24},{12,28},{16,0},{20,4},{24,8},{28,12},{1,17},{... | collective-permute-start | bytes 245768 | tf_op jit(solution)/shard_map/ppermute | solution.py:75
  155.6 7.0 %collective-permute-start.48 = (bf16[80,512]{1,0:T(8,128)(2,1)S(1)}, bf16[80,512]{1,0:T(8,128)(2,1)S(1)}, u32[]{:S(2)}, u32[]{:S(2)}) collective-permute-start(bf16[80,512]{1,0:T(8,128)(2,1)S(1)} %get-tuple-element.146.refs_20_), channel_id=1, source_target_pairs={{0,24},{4,28},{8,16},{12,20},{16,8},{20,12},{24,0},{28,4},{1,25},{... | collective-permute-start | bytes 245768 | tf_op jit(solution)/shard_map/ppermute | solution.py:75
  156.0 6.6 %collective-permute-start.45 = (bf16[96,384]{1,0:T(8,128)(2,1)S(1)}, bf16[96,384]{1,0:T(8,128)(2,1)S(1)}, u32[]{:S(2)}, u32[]{:S(2)}) collective-permute-start(bf16[96,384]{1,0:T(8,128)(2,1)S(1)} %get-tuple-element.145), channel_id=1, source_target_pairs={{0,24},{4,28},{8,16},{12,20},{16,8},{20,12},{24,0},{28,4},{1,25},{... | collective-permute-start | bytes 221192 | tf_op jit(solution)/shard_map/ppermute | solution.py:75
  162.7 3.0 %collective-permute-start.29 = (bf16[256,768]{1,0:T(8,128)(2,1)S(1)}, bf16[256,768]{1,0:T(8,128)(2,1)S(1)}, u32[]{:S(2)}, u32[]{:S(2)}) collective-permute-start(bf16[256,768]{1,0:T(8,128)(2,1)S(1)} %get-tuple-element.123.refs_0_), channel_id=1, source_target_pairs={{0,1},{1,0},{2,3},{3,2},{4,5},{5,4},{6,7},{7,6},{8,9},{9,8},{10,11... | collective-permute-start | bytes 1179656 | tf_op jit(solution)/shard_map/ppermute | solution.py:75
  (29 other events, 191.1 us)

commit v3 on v2

--- a/solution.py
+++ b/solution.py
@@ -15,6 +15,7 @@
 ROWS_BLOCK = 64
 STEP = 5
 CAP = 12
+GATES = 14
 HALF = 128
 IDS_STEP = 256
 EVENTS_STEP = 256
@@ -77,20 +78,6 @@
 
 def inner_size(dp_count):
     return 1 << ((dp_count.bit_length() - 1) // 2)
-
-
-def gather_dp(value):
-    count = lax.axis_size("dp")
-    inner = inner_size(count)
-    far = {0: value}
-    for step in reversed(range(1, count // inner)):
-        far[step] = swap(value, "dp", step * inner)
-    pieces = [None] * count
-    for step in [0] + list(reversed(range(1, count // inner))):
-        pieces[step * inner] = far[step]
-        for near in range(1, inner):
-            pieces[step * inner + near] = swap(far[step], "dp", near)
-    return pieces
 
 
 def low_kernel(table_hbm, first_hbm, second_hbm, vector_hbm, cot_hbm, *refs, hid):
@@ -145,7 +132,8 @@
         cots[m][cols + 16 :, :] = over.astype(bf16)
 
 
-def counts_kernel(offs_ref, ids_ref, off_ref, nxt_ref, c_ref, idb, acc, *, chunk):
+def counts_kernel(offs_ref, ids_ref, off_ref, nxt_ref, *refs, chunk):
+    c_ref, idb, acc = refs[-3:]
     id_rows, lanes = ids_ref.shape
     vocab = c_ref.shape[1]
     events = off_ref.shape[0] * lanes
@@ -244,28 +232,31 @@
 
 
 def weights_kernel(*refs, dp, hid):
-    pieces, cots = refs[:hid], refs[hid : 2 * hid]
-    w1p, w1t, w2p, w2t, col_ref, q_ref, q3t_ref = refs[2 * hid : 2 * hid + 7]
-    w1s, w2s, vecs = refs[2 * hid + 7 :]
+    inner = inner_size(dp)
+    given = hid * inner
+    stacks, cots = refs[:given], refs[given : given + hid]
+    w1p, w1t, w2p, w2t, col_ref, q_ref, q3t_ref = refs[given + hid : given + hid + 7]
+    w1s, w2s, vecs = refs[given + hid + 7 :]
     me_dp, me_hid = lax.axis_index("dp"), lax.axis_index("hid")
     rows = D // dp
     fold = H // dp
     each = rows + fold
     width = (O * EXPERTS) // dp
     high = H // hid
-    feats = pieces[0].shape[2]
+    feats = stacks[0].shape[2]
     j_step = w1s.shape[2]
     k_step = w2s.shape[2]
     for r in range(hid):
         j = me_hid ^ r
         for s in range(dp):
             k = me_dp ^ s
+            stack, at = stacks[r * inner + s % inner], s // inner
             for g in range(3):
                 w1s[j, pl.ds(pl.multiple_of(k * rows, rows), rows), g * feats : (g + 1) * feats] = (
-                    pieces[r][s, g * each : g * each + rows, :]
+                    stack[at, g * each : g * each + rows, :]
                 )
             part = jnp.concatenate(
-                [pieces[r][s, g * each + rows : (g + 1) * each, :].astype(f32) for g in range(3)],
+                [stack[at, g * each + rows : (g + 1) * each, :].astype(f32) for g in range(3)],
                 axis=1,
             )
             for q in range(high // fold):
@@ -309,6 +300,15 @@
         for e in range(EXPERTS):
             w2p[e, :, lanes] = total_p[:, e * HALF : (e + 1) * HALF].astype(bf16)
             w2t[e, lanes, :] = total_t[e * HALF : (e + 1) * HALF, :].astype(bf16)
+
+
+def small_plan(hid):
+    width = (H * EXPERTS) // hid
+    whole = D // width
+    packed = width // HALF
+    rest = -(-GATES // packed)
+    used = GATES * whole + rest + 3 * hid
+    return width, whole, packed, rest, -(-used // 16) * 16
 
 
 def softmax_rows(logits):
@@ -411,16 +411,22 @@
         upward = jnp.concatenate(d_chances[t], axis=0)
         g = chances[t]
         d_logits.append(g * (upward - jnp.sum(g * upward, axis=0, keepdims=True)))
-    pad = jnp.zeros((gate_ref.shape[0] - 14, rows), f32)
+    pad = jnp.zeros((gate_ref.shape[0] - GATES, rows), f32)
     d_logits = jnp.concatenate(d_logits + [pad], axis=0).astype(bf16)
     dx[...] += tn(gate, d_logits)
     for m in range(hid):
         start = pl.multiple_of((me ^ m) * feats, feats)
         dx_outs[m][...] = dx[pl.ds(start, feats), :].astype(bf16)
-    gates = gate_ref.shape[0]
-    small_ref[0:gates, :] = nt(d_logits, xt[...]).astype(bf16)
-    small_ref[gates:, :] = jnp.zeros((small_ref.shape[0] - gates, small_ref.shape[1]), bf16)
-    width = (H * EXPERTS) // hid
+    width, whole, packed, rest, small_rows = small_plan(hid)
+    d_gate = nt(d_logits, xt[...])[0:GATES]
+    lines = [d_gate[:, i * width : (i + 1) * width] for i in range(whole)]
+    tail = d_gate[:, whole * width :]
+    if rest * packed > GATES:
+        tail = jnp.concatenate([tail, jnp.zeros((rest * packed - GATES, HALF), f32)], axis=0)
+    tail = jnp.concatenate([tail[i * rest : (i + 1) * rest] for i in range(packed)], axis=1)
+    if packed * HALF < width:
+        tail = jnp.concatenate([tail, jnp.zeros((rest, width - packed * HALF), f32)], axis=1)
+    lines.append(tail)
     for half in range(2):
         lanes = slice(half * HALF, (half + 1) * HALF)
         stack = jnp.concatenate(
@@ -432,26 +438,27 @@
             axis=0,
         ).astype(bf16)
         turned = nt(stack, q_ref[...])
-        per = (HALF * EXPERTS) // width
-        for i in range(per):
-            j = half * per + i
-            small_ref[gates + 16 * j : gates + 16 * j + 8, 0:width] = turned[
-                :, i * width : (i + 1) * width
-            ].astype(bf16)
+        for i in range((HALF * EXPERTS) // width):
+            lines.append(turned[0:3, i * width : (i + 1) * width])
+    spare = small_rows - sum(line.shape[0] for line in lines)
+    if spare:
+        lines.append(jnp.zeros((spare, width), f32))
+    small_ref[...] = jnp.concatenate(lines, axis=0).astype(bf16)
     mixed_ref[...] = tn(mix[...].astype(bf16), q3t_ref[...]).astype(bf16)
 
 
-def grads_kernel(xt, hid_ref, dinner_ref, dpre_ref, q_ref, *refs, dp, hid):
-    outs = refs[:hid]
-    turned, w1g, w2g = refs[hid:]
+def grads_kernel(xt, hid_ref, dinner_ref, dpre_ref, q_ref, small_ref, order_ref, *refs, dp, hid):
+    home, away, turned, w1g, w2g = refs
     me_dp, me_hid = lax.axis_index("dp"), lax.axis_index("hid")
     span = HALF * EXPERTS
     rows = D // dp
     fold = H // dp
+    each = rows + fold
     width = (O * EXPERTS) // dp
     high = H // hid
     cols = (H * EXPERTS) // hid
     inner = inner_size(dp)
+    outer = dp // inner
     whole = [nt(hid_ref[e], dinner_ref[e]).astype(bf16) for e in range(EXPERTS)]
     for half in range(2):
         part = slice(half * HALF, (half + 1) * HALF)
@@ -460,14 +467,16 @@
         block = jnp.concatenate([w[:, part] for w in whole], axis=1)
         w2g[:, half * span : (half + 1) * span] = nt(block, q_ref[...])
     for m in range(hid):
+        out, base = (away if m % 2 else home), (m // 2) * dp * each
         j = me_hid ^ m
         left = turned[pl.ds(pl.multiple_of(j * cols, cols), cols), :]
         w1g[...] = nt(xt[...], left).astype(bf16)
         for near in range(inner):
-            for far in range(dp // inner):
+            for far in range(outer):
                 k = me_dp ^ (far * inner + near)
                 start = pl.multiple_of(k * rows, rows)
-                outs[m][near, far, 0:rows, :] = w1g[pl.ds(start, rows), :]
+                to = base + (near * outer + far) * each
+                out[to : to + rows, :] = w1g[pl.ds(start, rows), :]
         start = pl.multiple_of(j * high, high)
         for k in range(dp):
             part = w2g[pl.ds(start, high), k * width : (k + 1) * width]
@@ -475,7 +484,9 @@
                 [part[i * fold : (i + 1) * fold, :] for i in range(high // fold)], axis=1
             ).astype(bf16)
             r = me_dp ^ k
-            outs[m][r % inner, r // inner, rows : rows + fold, :] = folded
+            to = base + ((r % inner) * outer + r // inner) * each + rows
+            out[pl.ds(pl.multiple_of(to, fold), fold), :] = folded
+    away[(hid // 2) * dp * each :, :] = small_ref[...]
 
 
 def table_kernel(owners_ref, *refs, chunks, dp, hid):
@@ -504,33 +515,45 @@
         outs[r][...] = slots[r]
 
 
+def total(refs, *at):
+    values = [(ref[at] if at else ref[...]).astype(f32) for ref in refs]
+    while len(values) > 1:
+        values = [values[i] + values[i + 1] for i in range(0, len(values), 2)]
+    return values[0]
+
+
 def plus(a, b):
     return (a.astype(f32) + b.astype(f32)).astype(bf16)
 
 
-def core_merge_kernel(*refs, pairs):
-    ins, outs = refs[: 2 * pairs], refs[2 * pairs + 1 :]
-    for i in range(pairs):
-        outs[i][...] = plus(ins[2 * i][...], ins[2 * i + 1][...])
-
-
-def chip_merge_kernel(*refs, terms, inner):
-    parts, small, other, mixed = refs[:terms], refs[terms], refs[terms + 1], refs[terms + 2]
-    outs = refs[terms + 3 :]
+def core_merge_kernel(home, come, small, order_ref, *outs, rows):
+    count = len(outs)
+    for i in range(count):
+        outs[i][0:rows, :] = plus(home[i * rows : (i + 1) * rows, :], come[i * rows : (i + 1) * rows, :])
+        outs[i][rows:, :] = plus(small[...], come[count * rows :, :])
+
+
+def chip_merge_kernel(*refs, terms, rows, inner):
+    parts, mixed = refs[:terms], refs[terms]
+    outs, mixed_out = refs[terms + 1 : terms + 1 + inner], refs[terms + 1 + inner]
+    last = total(parts, slice(inner * rows, None)).astype(bf16)
     for near in range(inner):
-        value = parts[0][near].astype(f32)
-        for part in parts[1:]:
-            value = value + part[near].astype(f32)
-        outs[near][...] = value.astype(bf16)
-    outs[inner][...] = plus(small[...], other[...])
-    outs[inner + 1][...] = mixed[...]
-
-
-def near_merge_kernel(*refs, terms, outer):
-    parts, small, other, outs = refs[:terms], refs[terms], refs[terms + 1], refs[terms + 2 :]
+        outs[near][0:rows, :] = total(parts, slice(near * rows, (near + 1) * rows)).astype(bf16)
+        outs[near][rows:, :] = last
+    mixed_out[...] = mixed[...]
+
+
+def near_merge_kernel(*refs, terms, rows, outer):
+    parts, outs = refs[:terms], refs[terms:]
+    last = total(parts, slice(outer * rows, None)).astype(bf16)
     for far in range(outer):
-        outs[far][...] = total(parts, far).astype(bf16)
-    outs[outer][...] = plus(small[...], other[...])
+        outs[far][0:rows, :] = total(parts, slice(far * rows, (far + 1) * rows)).astype(bf16)
+        outs[far][rows:, :] = last
+
+
+def stack_kernel_ordered(*refs, count, start):
+    for r in range(count):
+        refs[-1][r] = refs[r][start:, :]
 
 
 def mixed_kernel(*refs, hid):
@@ -550,13 +573,6 @@
     )
     new_average = ema_decay * average + (1.0 - ema_decay) * new_weight
     return (new_weight, new_moment, new_second, new_average)
-
-
-def total(refs, *at):
-    value = refs[0][at].astype(f32) if at else refs[0][...].astype(f32)
-    for ref in refs[1:]:
-        value = value + (ref[at] if at else ref[...]).astype(f32)
-    return value
 
 
 def table_adam_kernel(*refs, terms):
@@ -572,8 +588,7 @@
 
 def weight_adam_kernel(*refs, terms, dp, hid):
     first, second, vector, gate = refs[0:4], refs[4:8], refs[8:12], refs[12:16]
-    parts, smalls = refs[16 : 16 + terms], refs[16 + terms : 16 + 2 * terms]
-    outs = refs[16 + 2 * terms :]
+    parts, outs = refs[16 : 16 + terms], refs[16 + terms :]
     first_out, second_out, vector_out, gate_out = outs[0:4], outs[4:8], outs[8:12], outs[12:16]
     rows, fold = D // dp, H // dp
     width = (O * EXPERTS) // dp
@@ -586,22 +601,21 @@
         new = adam(*[s[p, :] for s in second], grad[:, i * width : (i + 1) * width], 0.06)
         for out, value in zip(second_out, new):
             out[p, :] = value
-    pairs = list(smalls)
-    gates = gate[0].shape[0]
-    me = lax.axis_index("hid")
-
-    def tree(at):
-        values = [s[at].astype(f32) for s in pairs]
-        while len(values) > 1:
-            values = [values[i] + values[i + 1] for i in range(0, len(values), 2)]
-        return values[0]
-
-    new = adam(*[s[...] for s in gate], tree(slice(0, gates)), 0.03)
+    small = total(parts, slice(rows + fold, None))
+    cols, whole, packed, rest, _ = small_plan(hid)
+    tail = small[GATES * whole : GATES * whole + rest]
+    tail = jnp.concatenate([tail[:, i * HALF : (i + 1) * HALF] for i in range(packed)], axis=0)
+    grad = jnp.concatenate(
+        [small[i * GATES : (i + 1) * GATES] for i in range(whole)] + [tail[0:GATES]], axis=1
+    )
+    new = adam(*[s[...] for s in gate], grad, 0.03)
     for out, value in zip(gate_out, new):
         out[...] = value
-    cols = (H * EXPERTS) // hid
-    start = pl.multiple_of(16 + me * 16, 16)
-    grad = tree(pl.ds(start, 16))[0:3, 0:cols]
+    me = lax.axis_index("hid")
+    base = GATES * whole + rest
+    grad = jnp.zeros((3, cols), f32)
+    for j in range(hid):
+        grad = jnp.where(me == j, small[base + 3 * j : base + 3 * j + 3], grad)
     new = adam(*[s[...] for s in vector], grad, 0.2)
     for out, value in zip(vector_out, new):
         out[...] = value
@@ -664,16 +678,57 @@
         ],
         vmem=8,
     )
-    pieces = gather_dp(piece)
     cots = [cot_pieces[0]] + [swap(cot_pieces[m], "hid", m) for m in range(1, hid)]
-
-    weight_parts = {0: [weight_low] + [p[slots:] for p in pieces[1:]]}
-    for m in range(2, hid, 2):
-        weight_parts[m] = [swap(w, "hid", m) for w in weight_parts[0]]
-    weight_hid = {}
-    for m in range(0, hid, 2):
-        weight_hid[m] = jnp.stack(weight_parts[m])
-        weight_hid[m + 1] = swap(weight_hid[m], "hid", 1)
+    nexts = jnp.concatenate([bag_offsets[1:], jnp.full((1,), ids, jnp.int32)])
+    lanes = 128
+    chunks = events // EVENTS_STEP
+
+    def count_bags(i, *order):
+        return call(
+            functools.partial(counts_kernel, chunk=i),
+            shape((EVENTS_STEP, vocab), bf16),
+            (
+                bag_offsets,
+                embed_ids.reshape(ids // lanes, lanes),
+                bag_offsets.reshape(events // lanes, lanes),
+                nexts.reshape(events // lanes, lanes),
+                *order,
+            ),
+            in_specs=[SMEM, VMEM, VMEM, VMEM] + [ANY] * len(order),
+            scratch=[
+                pltpu.VMEM((ids // IDS_STEP, IDS_STEP, HALF), jnp.int16),
+                pltpu.VMEM((EVENTS_STEP, vocab), f32),
+            ],
+            vmem=12 if vocab <= 4096 else 40,
+            us=5.0,
+        )
+
+    far_pieces = [piece] + [None] * (outer - 1)
+    for step in reversed(range(1, outer)):
+        far_pieces[step] = swap(piece, "dp", step * inner)
+    counts = [count_bags(i) for i in range(chunks // 2)]
+    groups = [far_pieces] + [[swap(p, "dp", near) for p in far_pieces] for near in range(1, inner)]
+
+    def stack(group, *order):
+        return call(
+            functools.partial(stack_kernel_ordered, count=outer, start=slots),
+            shape((outer, weight_rows, feats), bf16),
+            (*group, *order),
+            in_specs=[VMEM] * outer + [ANY] * len(order),
+            vmem=8,
+            us=0.7,
+        )
+
+    stacks = {(0, 0): stack(groups[0], *counts)}
+    counts += [count_bags(i, stacks[0, 0]) for i in range(chunks // 2, chunks)]
+    for near in range(1, inner):
+        stacks[0, near] = stack(groups[near])
+    for near in range(inner):
+        for m in range(2, hid, 2):
+            stacks[m, near] = swap(stacks[0, near], "hid", m)
+        for m in range(0, hid, 2):
+            stacks[m + 1, near] = swap(stacks[m, near], "hid", 1)
+    pieces = [groups[r % inner][r // inner] for r in range(dp)]
     span = HALF * EXPERTS
     w1p, w1t, w2p, w2t, columns, turn, turn3t = call(
         functools.partial(weights_kernel, dp=dp, hid=hid),
@@ -686,7 +741,7 @@
             shape((span, span), bf16),
             shape((O * STREAMS, O * STREAMS), bf16),
         ],
-        (*[weight_hid[m] for m in range(hid)], *cots),
+        (*[stacks[m, near] for m in range(hid) for near in range(inner)], *cots),
         scratch=[
             pltpu.VMEM((hid, D, piece_cols), bf16),
             pltpu.VMEM((dp, H, (O * EXPERTS) // dp), bf16),
@@ -696,29 +751,6 @@
         us=8.0,
     )
 
-    lanes = 128
-    nexts = jnp.concatenate([bag_offsets[1:], jnp.full((1,), ids, jnp.int32)])
-    chunks = events // EVENTS_STEP
-    counts = [
-        call(
-            functools.partial(counts_kernel, chunk=i),
-            shape((EVENTS_STEP, vocab), bf16),
-            (
-                bag_offsets,
-                embed_ids.reshape(ids // lanes, lanes),
-                bag_offsets.reshape(events // lanes, lanes),
-                nexts.reshape(events // lanes, lanes),
-            ),
-            in_specs=[SMEM, VMEM, VMEM, VMEM],
-            scratch=[
-                pltpu.VMEM((ids // IDS_STEP, IDS_STEP, HALF), jnp.int16),
-                pltpu.VMEM((EVENTS_STEP, vocab), f32),
-            ],
-            vmem=12 if vocab <= 4096 else 40,
-            us=5.0,
-        )
-        for i in range(chunks)
-    ]
     pooled = call(
         functools.partial(pool_kernel, chunks=chunks, dp=dp, hid=hid),
         [shape((feats, rows), bf16) for m in range(hid)],
@@ -737,12 +769,12 @@
 
     gates = 16
     gate_pad = jnp.pad(gate_w.T, ((0, gates - gate_w.shape[1]), (0, 0)))
-    small_rows = gates + 16 * hid
+    small_rows = small_plan(hid)[-1]
     mixed_part, small, xt, hidden, d_inner, d_pre, *d_pieces = call(
         functools.partial(main_kernel, hid=hid),
         [
             shape((rows, O * STREAMS), bf16),
-            shape((small_rows, D), bf16),
+            shape((small_rows, piece_cols), bf16),
             shape((D, rows), bf16),
             shape((EXPERTS, H, rows), bf16),
             shape((EXPERTS, O, rows), bf16),
@@ -766,10 +798,15 @@
     )
     d_pooled = [d_pieces[0]] + [swap(d_pieces[m], "hid", m) for m in range(1, hid)]
 
-    grads = call(
+    some = dp * piece_rows
+    home, away = call(
         functools.partial(grads_kernel, dp=dp, hid=hid),
-        [shape((inner, outer, piece_rows, piece_cols), bf16) for m in range(hid)],
-        (xt, hidden, d_inner, d_pre, turn),
+        [
+            shape((hid // 2 * some, piece_cols), bf16),
+            shape((hid // 2 * some + small_rows, piece_cols), bf16),
+        ],
+        (xt, hidden, d_inner, d_pre, turn, small, d_pooled[1]),
+        in_specs=[VMEM] * 6 + [ANY],
         scratch=[
             pltpu.VMEM((H * EXPERTS, rows), bf16),
             pltpu.VMEM((D, piece_cols), bf16),
@@ -779,42 +816,30 @@
         us=3.0,
     )
 
-    whole_shape = shape(grads[0].shape, bf16)
-    small_shape = shape(small.shape, bf16)
-    operands = []
-    for m in range(0, hid, 2):
-        operands += [grads[m], swap(grads[m + 1], "hid", 1)]
-    *half, small = call(
-        functools.partial(core_merge_kernel, pairs=hid // 2 + 1),
-        [whole_shape] * (hid // 2) + [small_shape],
-        (*operands, small, swap(small, "hid", 1), d_pooled[hid - 1]),
-        in_specs=[VMEM] * (hid + 2) + [ANY],
-        us=1.5,
-    )
-    step = 2
-    while step < hid // 2:
-        small = plus(small, swap(small, "hid", step))
-        step *= 2
-    *near, small, mixed_part = call(
-        functools.partial(chip_merge_kernel, terms=hid // 2, inner=inner),
-        [shape(grads[0].shape[1:], bf16)] * inner + [small_shape, shape(mixed_part.shape, bf16)],
-        (half[0], *[swap(half[m], "hid", 2 * m) for m in range(1, hid // 2)])
-        + (small, swap(small, "hid", step), mixed_part),
-        us=1.5,
-    )
-    step = 1
-    while step < inner // 2:
-        small = plus(small, swap(small, "dp", step))
-        step *= 2
-    *far_parts, small = call(
-        functools.partial(near_merge_kernel, terms=inner, outer=outer),
-        [shape((piece_rows, piece_cols), bf16)] * outer + [small_shape],
-        (near[0], *[swap(near[m], "dp", m) for m in range(1, inner)])
-        + (small, swap(small, "dp", step)),
-        us=1.5,
+    half = call(
+        functools.partial(core_merge_kernel, rows=some),
+        [shape((some + small_rows, piece_cols), bf16)] * (hid // 2),
+        (home, swap(away, "hid", 1), small, d_pooled[hid - 1]),
+        in_specs=[VMEM] * 3 + [ANY],
+        vmem=12,
+        us=1.0,
+    )
+    *near, mixed_part = call(
+        functools.partial(chip_merge_kernel, terms=hid // 2, rows=some // inner, inner=inner),
+        [shape((some // inner + small_rows, piece_cols), bf16)] * inner
+        + [shape(mixed_part.shape, bf16)],
+        (half[0], *[swap(half[m], "hid", 2 * m) for m in range(1, hid // 2)], mixed_part),
+        vmem=12,
+        us=1.0,
+    )
+    far_parts = call(
+        functools.partial(near_merge_kernel, terms=inner, rows=piece_rows, outer=outer),
+        [shape((piece_rows + small_rows, piece_cols), bf16)] * outer,
+        (near[0], *[swap(near[m], "dp", m) for m in range(1, inner)]),
+        vmem=12,
+        us=1.0,
     )
     weight_terms = [far_parts[0]] + [swap(far_parts[m], "dp", m * inner) for m in range(1, outer)]
-    small_terms = [small] + [swap(small, "dp", m * inner) for m in range(1, outer)]
 
     mixed_parts = {0: mixed_part}
     for m in range(2, hid, 2):
@@ -861,7 +886,7 @@
         [shape(first_w.shape, f32)] * 4
         + [shape(second_w.shape, f32)] * 4
         + [shape(vector_w.shape, f32)] * 4
-        + [shape((gates, D), f32)] * 4,
+        + [shape((GATES, D), f32)] * 4,
         (
             first_w,
             first_m,
@@ -875,10 +900,8 @@
             vector_m,
             vector_v,
             vector_ema,
-            gate_pad,
-            *[jnp.pad(g.T, ((0, gates - g.shape[1]), (0, 0))) for g in (gate_m, gate_v, gate_ema)],
+            *[g.T for g in (gate_w, gate_m, gate_v, gate_ema)],
             *weight_terms,
-            *small_terms,
         ),
         vmem=8,
     )
@@ -886,7 +909,7 @@
         mixed,
         *table_new,
         *weights_new[0:12],
-        *[g[0 : gate_w.shape[1]].T for g in weights_new[12:16]],
+        *[g.T for g in weights_new[12:16]],
     )
 
 

time: 167 us -> 136 us (0.81)
  starting transfers between devices: 55.5 us -> 36.9 us
  waiting for transfers between devices: 56.8 us -> 45.3 us
    ppermute x49 -> x38, starting transfers between devices: 55.5 us -> 36.9 us  [swap(): return lax.ppermute(value, axis, [(i, i ^ mask) for i in range(count)])]
    ppermute x49 -> x38, waiting for transfers between devices: 56.8 us -> 45.3 us  [swap(): return lax.ppermute(value, axis, [(i, i ^ mask) for i in range(count)])]
    pallas_call x16 -> x18, Pallas kernels: 46.9 us -> 47.6 us  [call(): pl.pallas_call(kernel, out_shape=outs, in_specs=in_specs or [VMEM] * len(...]
    unnamed x70 -> x56, local copies, waits for them, and re-layouts: 4.7 us -> 4.53 us
  transfers between devices with their start and end apart: 49 -> 38, of which waited for: 18 -> 15; matrix products, arithmetic and copies ran while one was open for 1% -> 0% of each run, Pallas kernels for 21% -> 26%
where the time goes in v3:
time: 136 us
  Pallas kernels  47.6 us (35%)
  waiting for transfers between devices  45.3 us (33%)
  starting transfers between devices  36.9 us (27%)
  local copies, waits for them, and re-layouts  4.61 us (3%)
    pallas_call x18, Pallas kernels, call(): pl.pallas_call(kernel, out_shape=outs, in_specs=in_specs or [VMEM] * len(...  47.6 us
    ppermute x38, waiting for transfers between devices, swap(): return lax.ppermute(value, axis, [(i, i ^ mask) for i in range(count)])  45.3 us
    ppermute x38, starting transfers between devices, swap(): return lax.ppermute(value, axis, [(i, i ^ mask) for i in range(count)])  36.9 us
    unnamed x56, local copies, waits for them, and re-layouts  4.53 us
  transfers between devices with their start and end apart: 38, of which 15 were waited for; matrix products, arithmetic and copies ran while one was open for 0% of the time, Pallas kernels for 26%

profile of v3, /device:TPU:0, one launch (start us, length us, event | category | flops | bytes accessed | tf_op | source)
XLA Modules:
  0.0 135.8 jit_solution(12524647026842870588)
XLA Ops:
  0.7 1.0 copy-done.2
  1.7 1.0 copy-done.3
  2.7 0.9 copy-done.8
  3.5 0.8 copy-done.13
  5.1 1.4 %shard_map.393 = (bf16[1056,128]{1,0:T(8,128)(2,1)S(1)}, bf16[288,128]{1,0:T(8,128)(2,1)}, bf16[224,256]{1,0:T(8,128)(2,1)S(1)}, bf16[224,256]{1,0:T(8,128)(2,1)...) custom-call(f32[768,128]{1,0:T(8,128)S(1)} %copy-done.3, f32[64,384]{1,0:T(8,128)S(1)} %copy-done.8, ...), custom_call_target="tpu_custom_call" | custom-call | flops 2000000000 | bytes 6000000 | tf_op jit(solution)/shard_map/pallas_call | solution.py:60
  6.5 3.0 %collective-permute-start.3 = (bf16[1056,128]{1,0:T(8,128)(2,1)S(1)}, bf16[1056,128]{1,0:T(8,128)(2,1)S(1)}, u32[]{:S(2)}, u32[]{:S(2)}) collective-permute-start(bf16[1056,128]{1,0:T(8,128)(2,1)S(1)} %get-tuple-element.86.refs_0_.refs_4_), channel_id=1, source_target_pairs={{0,4},{4,0},{8,12},{12,8},{16,20},{20,16},{24,28},{28,24},{1,5},{5... | collective-permute-start | bytes 811016 | tf_op jit(solution)/shard_map/ppermute | solution.py:76
  9.5 3.6 %collective-permute-start.2 = (bf16[1056,128]{1,0:T(8,128)(2,1)S(1)}, bf16[1056,128]{1,0:T(8,128)(2,1)S(1)}, u32[]{:S(2)}, u32[]{:S(2)}) collective-permute-start(bf16[1056,128]{1,0:T(8,128)(2,1)S(1)} %get-tuple-element.86.refs_0_.refs_4_), channel_id=1, source_target_pairs={{0,24},{4,28},{8,16},{12,20},{16,8},{20,12},{24,0},{28,4},{1,25},{... | collective-permute-start | bytes 811016 | tf_op jit(solution)/shard_map/ppermute | solution.py:76
  14.0 5.0 %shard_map.392.refs_5_.refs_1_ = bf16[256,3072]{1,0:T(8,128)(2,1)S(1)} custom-call(s32[1024]{0:T(1024)S(1)} %copy-done.1, s32[32,128]{1,0:T(8,128)S(1)} %bitcast.23, s32[8,128]{1,0:T(8,128)S(1)} %bitcast.15, s32[8,128]{1,0:T(8,128)S(1)} %add_bitcast_fusion.nxt_ref), custom_call_target="tpu_custom_call" | custom-call | flops 5000000000 | bytes 15000000 | tf_op jit(solution)/shard_map/pallas_call | solution.py:60
  19.1 4.4 %shard_map.391.refs_4_.refs_0_ = bf16[256,3072]{1,0:T(8,128)(2,1)S(1)} custom-call(s32[1024]{0:T(1024)S(1)} %copy-done.1, s32[32,128]{1,0:T(8,128)S(1)} %bitcast.24, s32[8,128]{1,0:T(8,128)S(1)} %bitcast.16, s32[8,128]{1,0:T(8,128)S(1)} %add_bitcast_fusion.nxt_ref), custom_call_target="tpu_custom_call" | custom-call | flops 5000000000 | bytes 15000000 | tf_op jit(solution)/shard_map/pallas_call | solution.py:60
  23.9 11.9 %collective-permute-done.1.refs_2_.refs_8_ = bf16[1056,128]{1,0:T(8,128)(2,1)S(1)} collective-permute-done((bf16[1056,128]{1,0:T(8,128)(2,1)S(1)}, bf16[1056,128]{1,0:T(8,128)(2,1)S(1)}, u32[]{:S(2)}, u32[]{:S(2)}) %collective-permute-start.1) | collective-permute-done | bytes 270368 | tf_op jit(solution)/shard_map/ppermute | solution.py:76
  36.3 1.5 %collective-permute-start.4 = (bf16[1056,128]{1,0:T(8,128)(2,1)S(1)}, bf16[1056,128]{1,0:T(8,128)(2,1)S(1)}, u32[]{:S(2)}, u32[]{:S(2)}) collective-permute-start(bf16[1056,128]{1,0:T(8,128)(2,1)S(1)} %collective-permute-done.refs_1_.refs_6_), channel_id=1, source_target_pairs={{0,4},{4,0},{8,12},{12,8},{16,20},{20,16},{24,28},{28,24},{1,5},{5... | collective-permute-start | bytes 811016 | tf_op jit(solution)/shard_map/ppermute | solution.py:76
  37.9 4.4 %shard_map.396.refs_3_ = bf16[256,3072]{1,0:T(8,128)(2,1)S(1)} custom-call(s32[1024]{0:T(1024)S(1)} %copy-done.1, s32[32,128]{1,0:T(8,128)S(1)} %bitcast.25, s32[8,128]{1,0:T(8,128)S(1)} %bitcast.17, s32[8,128]{1,0:T(8,128)S(1)} %add_bitcast_fusion.nxt_ref, bf16[4,288,128]{2,1,0:T(8,128)(2,1)S(1)} %shard_map.394.refs_0_), custom_call_target="tpu_custom_call" | custom-call | flops 5000000000 | bytes 15000000 | tf_op jit(solution)/shard_map/pallas_call | solution.py:60
  42.3 1.6 %collective-permute-start.11 = (bf16[224,256]{1,0:T(8,128)(2,1)S(1)}, bf16[224,256]{1,0:T(8,128)(2,1)S(1)}, u32[]{:S(2)}, u32[]{:S(2)}) collective-permute-start(bf16[224,256]{1,0:T(8,128)(2,1)S(1)} %get-tuple-element.93), channel_id=1, source_target_pairs={{0,2},{1,3},{2,0},{3,1},{4,6},{5,7},{6,4},{7,5},{8,10},{9,11},{10,... | collective-permute-start | bytes 344072 | tf_op jit(solution)/shard_map/ppermute | solution.py:76
  43.8 1.4 %collective-permute-done.5.refs_9_.refs_2_ = bf16[1056,128]{1,0:T(8,128)(2,1)S(1)} collective-permute-done((bf16[1056,128]{1,0:T(8,128)(2,1)S(1)}, bf16[1056,128]{1,0:T(8,128)(2,1)S(1)}, u32[]{:S(2)}, u32[]{:S(2)}) %collective-permute-start.5) | collective-permute-done | bytes 270368 | tf_op jit(solution)/shard_map/ppermute | solution.py:76
  45.2 1.5 %collective-permute-start.15 = (bf16[4,288,128]{2,1,0:T(8,128)(2,1)S(1)}, bf16[4,288,128]{2,1,0:T(8,128)(2,1)S(1)}, u32[]{:S(2)}, u32[]{:S(2)}) collective-permute-start(bf16[4,288,128]{2,1,0:T(8,128)(2,1)S(1)} %shard_map.394.refs_0_), channel_id=1, source_target_pairs={{0,2},{1,3},{2,0},{3,1},{4,6},{5,7},{6,4},{7,5},{8,10},{9,11},{10,... | collective-permute-start | bytes 884744 | tf_op jit(solution)/shard_map/ppermute | solution.py:76
  46.7 2.4 %collective-permute-done.4.refs_7_.refs_1_ = bf16[1056,128]{1,0:T(8,128)(2,1)S(1)} collective-permute-done((bf16[1056,128]{1,0:T(8,128)(2,1)S(1)}, bf16[1056,128]{1,0:T(8,128)(2,1)S(1)}, u32[]{:S(2)}, u32[]{:S(2)}) %collective-permute-start.4) | collective-permute-done | bytes 270368 | tf_op jit(solution)/shard_map/ppermute | solution.py:76
  49.1 1.6 %collective-permute-start.16 = (bf16[4,288,128]{2,1,0:T(8,128)(2,1)S(1)}, bf16[4,288,128]{2,1,0:T(8,128)(2,1)S(1)}, u32[]{:S(2)}, u32[]{:S(2)}) collective-permute-start(bf16[4,288,128]{2,1,0:T(8,128)(2,1)S(1)} %shard_map.398.refs_1_), channel_id=1, source_target_pairs={{0,2},{1,3},{2,0},{3,1},{4,6},{5,7},{6,4},{7,5},{8,10},{9,11},{10,... | collective-permute-start | bytes 884744 | tf_op jit(solution)/shard_map/ppermute | solution.py:76
  50.7 5.7 %shard_map.395.refs_2_ = bf16[256,3072]{1,0:T(8,128)(2,1)S(1)} custom-call(s32[1024]{0:T(1024)S(1)} %copy-done.1, s32[32,128]{1,0:T(8,128)S(1)} %bitcast.26, s32[8,128]{1,0:T(8,128)S(1)} %bitcast.18, s32[8,128]{1,0:T(8,128)S(1)} %add_bitcast_fusion.nxt_ref, bf16[4,288,128]{2,1,0:T(8,128)(2,1)S(1)} %shard_map.394.refs_0_), custom_call_target="tpu_custom_call" | custom-call | flops 5000000000 | bytes 15000000 | tf_op jit(solution)/shard_map/pallas_call | solution.py:60
  57.1 5.1 %collective-permute-done.16.refs_5_ = bf16[4,288,128]{2,1,0:T(8,128)(2,1)S(1)} collective-permute-done((bf16[4,288,128]{2,1,0:T(8,128)(2,1)S(1)}, bf16[4,288,128]{2,1,0:T(8,128)(2,1)S(1)}, u32[]{:S(2)}, u32[]{:S(2)}) %collective-permute-start.16) | collective-permute-done | bytes 294944 | tf_op jit(solution)/shard_map/ppermute | solution.py:76
  62.2 3.3 %shard_map.397 = (bf16[128,256]{1,0:T(8,128)(2,1)S(1)}, bf16[128,256]{1,0:T(8,128)(2,1)S(1)}, bf16[128,256]{1,0:T(8,128)(2,1)S(1)}, bf16[128,256]{1,0:T(8,128)(2,1)S(1)}) custom-call(s32[48]{0:T(128)S(1)} %copy-done.27, bf16[256,3072]{1,0:T(8,128)(2,1)S(1)} %shard_map.391.refs_4_.refs_0_, bf16[256,3072]{1,0:T(8,128)(2,1)S(1)} %shard_map.392.refs_5_.refs_1_, ...), custom_call_target="tpu_custom_call" | custom-call | flops 4000000000 | bytes 12000000 | tf_op jit(solution)/shard_map/pallas_call | solution.py:60
  66.2 1.5 %collective-permute-start.8 = (bf16[128,256]{1,0:T(8,128)(2,1)S(1)}, bf16[128,256]{1,0:T(8,128)(2,1)S(1)}, u32[]{:S(2)}, u32[]{:S(2)}) collective-permute-start(bf16[128,256]{1,0:T(8,128)(2,1)S(1)} %get-tuple-element.89), channel_id=1, source_target_pairs={{0,2},{1,3},{2,0},{3,1},{4,6},{5,7},{6,4},{7,5},{8,10},{9,11},{10,... | collective-permute-start | bytes 196616 | tf_op jit(solution)/shard_map/ppermute | solution.py:76
  67.7 6.4 %shard_map.399 = (bf16[6,512,256]{2,1,0:T(8,128)(2,1)S(1)}, bf16[6,256,512]{2,1,0:T(8,128)(2,1)S(1)}, bf16[6,256,256]{2,1,0:T(8,128)(2,1)S(1)}, bf16[6,256,256]{...) custom-call(bf16[4,288,128]{2,1,0:T(8,128)(2,1)S(1)} %shard_map.394., ...), custom_call_target="tpu_custom_call" | custom-call | flops 8000000000 | bytes 24000000 | tf_op jit(solution)/shard_map/pallas_call | solution.py:60
  74.2 7.4 %shard_map.400 = (bf16[256,768]{1,0:T(8,128)(2,1)S(1)}, bf16[32,384]{1,0:T(8,128)(2,1)S(1)}, bf16[512,256]{1,0:T(8,128)(2,1)S(1)}, bf16[6,256,256]{2,1,0:T(8,128...) custom-call(bf16[128,256]{1,0:T(8,128)(2,1)S(1)} %get-tuple-element., ...), custom_call_target="tpu_custom_call" | custom-call | flops 10000000000 | bytes 30000000 | tf_op jit(solution)/shard_map/pallas_call | solution.py:60
  82.3 0.9 collective-permute-done.19.order_ref.refs_5_
  83.2 2.6 %shard_map.401 = (bf16[1536,384]{1,0:T(8,128)(2,1)S(1)}, bf16[1568,384]{1,0:T(8,128)(2,1)S(1)}) custom-call(bf16[512,256]{1,0:T(8,128)(2,1)S(1)} %get-tuple-element.102.xt, bf16[6,256,256]{2,1,0:T(8,128)(2,1)S(1)} %get-tuple-element.103.hid_ref, bf16[6,256,256]{2,1,0:T(8,128)(2,1)S(1)} %get-tuple-element.104.dinner_ref, ...), custom_call_target="tpu_custom_call" | custom-call | flops 3000000000 | bytes 9000000 | tf_op jit(solution)/shard_map/pallas_call | solution.py:60
  86.2 1.3 collective-permute-start.21
  88.0 2.3 %collective-permute-done.21.order_ref.refs_7_ = bf16[128,256]{1,0:T(8,128)(2,1)S(1)} collective-permute-done((bf16[128,256]{1,0:T(8,128)(2,1)S(1)}, bf16[128,256]{1,0:T(8,128)(2,1)S(1)}, u32[]{:S(2)}, u32[]{:S(2)}) %collective-permute-start.21) | collective-permute-done | bytes 65568 | tf_op jit(solution)/shard_map/ppermute | solution.py:76
  90.3 1.7 %collective-permute-done.26.refs_6_ = bf16[128,256]{1,0:T(8,128)(2,1)S(1)} collective-permute-done((bf16[128,256]{1,0:T(8,128)(2,1)S(1)}, bf16[128,256]{1,0:T(8,128)(2,1)S(1)}, u32[]{:S(2)}, u32[]{:S(2)}) %collective-permute-start.26) | collective-permute-done | bytes 65568 | tf_op jit(solution)/shard_map/ppermute | solution.py:76
  92.0 2.4 %shard_map.405 = (bf16[768,128]{1,0:T(8,128)(2,1)S(1)}, bf16[768,128]{1,0:T(8,128)(2,1)S(1)}, bf16[768,128]{1,0:T(8,128)(2,1)S(1)}, bf16[768,128]{1,0:T(8,128)(2...) custom-call(s32[48]{0:T(128)S(1)} %copy-done.27, ...), custom_call_target="tpu_custom_call" | custom-call | flops 6000000000 | bytes 18000000 | tf_op jit(solution)/shard_map/pallas_call | solution.py:60
  94.5 1.3 collective-permute-start.27
  96.0 1.6 %collective-permute-start.22 = (bf16[800,384]{1,0:T(8,128)(2,1)S(1)}, bf16[800,384]{1,0:T(8,128)(2,1)S(1)}, u32[]{:S(2)}, u32[]{:S(2)}) collective-permute-start(bf16[800,384]{1,0:T(8,128)(2,1)S(1)} %get-tuple-element.112), channel_id=1, source_target_pairs={{0,2},{1,3},{2,0},{3,1},{4,6},{5,7},{6,4},{7,5},{8,10},{9,11},{10,... | collective-permute-start | bytes 1843208 | tf_op jit(solution)/shard_map/ppermute | solution.py:76
  97.6 0.8 collective-permute-start.29
  98.5 1.2 collective-permute-start.31
  99.7 0.8 collective-permute-start.33
  100.5 1.8 %collective-permute-done.27 = bf16[768,128]{1,0:T(8,128)(2,1)S(1)} collective-permute-done((bf16[768,128]{1,0:T(8,128)(2,1)S(1)}, bf16[768,128]{1,0:T(8,128)(2,1)S(1)}, u32[]{:S(2)}, u32[]{:S(2)}) %collective-permute-start.27) | collective-permute-done | bytes 196640 | tf_op jit(solution)/shard_map/ppermute | solution.py:76
  102.4 3.2 %collective-permute-start.28 = (bf16[768,128]{1,0:T(8,128)(2,1)S(1)}, bf16[768,128]{1,0:T(8,128)(2,1)S(1)}, u32[]{:S(2)}, u32[]{:S(2)}) collective-permute-start(bf16[768,128]{1,0:T(8,128)(2,1)S(1)} %add_convert_fusion.3), channel_id=1, source_target_pairs={{0,24},{4,28},{8,16},{12,20},{16,8},{20,12},{24,0},{28,4},{1,25},{... | collective-permute-start | bytes 589832 | tf_op jit(solution)/shard_map/ppermute | solution.py:76
  105.6 1.0 collective-permute-done.29
  106.8 4.5 %collective-permute-done.22.refs_1_ = bf16[800,384]{1,0:T(8,128)(2,1)S(1)} collective-permute-done((bf16[800,384]{1,0:T(8,128)(2,1)S(1)}, bf16[800,384]{1,0:T(8,128)(2,1)S(1)}, u32[]{:S(2)}, u32[]{:S(2)}) %collective-permute-start.22) | collective-permute-done | bytes 614432 | tf_op jit(solution)/shard_map/ppermute | solution.py:76
  111.5 0.9 collective-permute-start.34
  112.4 1.6 %collective-permute-start.24 = (bf16[256,768]{1,0:T(8,128)(2,1)S(1)}, bf16[256,768]{1,0:T(8,128)(2,1)S(1)}, u32[]{:S(2)}, u32[]{:S(2)}) collective-permute-start(bf16[256,768]{1,0:T(8,128)(2,1)S(1)} %get-tuple-element.114.refs_0_), channel_id=1, source_target_pairs={{0,2},{1,3},{2,0},{3,1},{4,6},{5,7},{6,4},{7,5},{8,10},{9,11},{10,... | collective-permute-start | bytes 1179656 | tf_op jit(solution)/shard_map/ppermute | solution.py:76
  115.3 5.2 %collective-permute-done.34.refs_1_ = bf16[416,384]{1,0:T(8,128)(2,1)S(1)} collective-permute-done((bf16[416,384]{1,0:T(8,128)(2,1)S(1)}, bf16[416,384]{1,0:T(8,128)(2,1)S(1)}, u32[]{:S(2)}, u32[]{:S(2)}) %collective-permute-start.34) | collective-permute-done | bytes 319520 | tf_op jit(solution)/shard_map/ppermute | solution.py:76
  120.5 1.1 collective-permute-done.24.refs_2_
  122.1 3.4 %collective-permute-start.36 = (bf16[128,384]{1,0:T(8,128)(2,1)S(1)}, bf16[128,384]{1,0:T(8,128)(2,1)S(1)}, u32[]{:S(2)}, u32[]{:S(2)}) collective-permute-start(bf16[128,384]{1,0:T(8,128)(2,1)S(1)} %get-tuple-element.133), channel_id=1, source_target_pairs={{0,16},{4,20},{8,24},{12,28},{16,0},{20,4},{24,8},{28,12},{1,17},{... | collective-permute-start | bytes 294920 | tf_op jit(solution)/shard_map/ppermute | solution.py:76
  126.4 1.5 %shard_map.406 = (f32[768,128]{1,0:T(8,128)}, f32[768,128]{1,0:T(8,128)}, f32[768,128]{1,0:T(8,128)}, f32[768,128]{1,0:T(8,128)}) custom-call(f32[768,128]{1,0:T(8,128)S(1)} %copy-done.4, f32[768,128]{1,0:T(8,128)S(1)} %copy-done.5, f32[768,128]{1,0:T(8,128)S(1)} %copy-done.6, f32[768,128]{1,0:T(8,128)S(1)} %copy-done.7, ...), custom_call_target="tpu_custom_call" | custom-call | flops 2000000000 | bytes 6000000 | tf_op jit(solution)/shard_map/pallas_call | solution.py:60
  127.9 0.9 collective-permute-done.35.refs_17_
  128.8 4.5 %collective-permute-done.36.refs_18_ = bf16[128,384]{1,0:T(8,128)(2,1)S(1)} collective-permute-done((bf16[128,384]{1,0:T(8,128)(2,1)S(1)}, bf16[128,384]{1,0:T(8,128)(2,1)S(1)}, u32[]{:S(2)}, u32[]{:S(2)}) %collective-permute-start.36) | collective-permute-done | bytes 98336 | tf_op jit(solution)/shard_map/ppermute | solution.py:76
  133.5 1.0 shard_map.408
  134.5 1.3 shard_map.404
  (109 shorter events, 9.0 us)
Async XLA Ops:
  5.1 8.8 %copy-start.1 = (s32[1024]{0:T(1024)S(1)}, s32[1024]{0:T(1024)}, u32[]{:S(2)}) copy-start(s32[1024]{0:T(1024)} %offs_ref.7) | copy-start | bytes 12292
  5.1 8.9 %copy-start = (f32[512,14]{0,1:T(8,128)S(1)}, f32[512,14]{0,1:T(8,128)}, u32[]{:S(2)}) copy-start(f32[512,14]{0,1:T(8,128)} %param.44) | copy-start | bytes 86020
  5.1 8.9 %copy-start.21 = (s32[4096]{0:T(1024)S(1)}, s32[4096]{0:T(1024)}, u32[]{:S(2)}) copy-start(s32[4096]{0:T(1024)} %param.25) | copy-start | bytes 49156
  6.5 35.8 %collective-permute-start.3 = (bf16[1056,128]{1,0:T(8,128)(2,1)S(1)}, bf16[1056,128]{1,0:T(8,128)(2,1)S(1)}, u32[]{:S(2)}, u32[]{:S(2)}) collective-permute-start(bf16[1056,128]{1,0:T(8,128)(2,1)S(1)} %get-tuple-element.86.refs_0_.refs_4_), channel_id=1, source_target_pairs={{0,4},{4,0},{8,12},{12,8},{16,20},{20,16},{24,28},{28,24},{1,5},{5... | collective-permute-start | bytes 811016 | tf_op jit(solution)/shard_map/ppermute | solution.py:76
  9.5 14.0 %collective-permute-start.2 = (bf16[1056,128]{1,0:T(8,128)(2,1)S(1)}, bf16[1056,128]{1,0:T(8,128)(2,1)S(1)}, u32[]{:S(2)}, u32[]{:S(2)}) collective-permute-start(bf16[1056,128]{1,0:T(8,128)(2,1)S(1)} %get-tuple-element.86.refs_0_.refs_4_), channel_id=1, source_target_pairs={{0,24},{4,28},{8,16},{12,20},{16,8},{20,12},{24,0},{28,4},{1,25},{... | collective-permute-start | bytes 811016 | tf_op jit(solution)/shard_map/ppermute | solution.py:76
  13.1 22.7 %collective-permute-start.1 = (bf16[1056,128]{1,0:T(8,128)(2,1)S(1)}, bf16[1056,128]{1,0:T(8,128)(2,1)S(1)}, u32[]{:S(2)}, u32[]{:S(2)}) collective-permute-start(bf16[1056,128]{1,0:T(8,128)(2,1)S(1)} %get-tuple-element.86.refs_0_.refs_4_), channel_id=1, source_target_pairs={{0,16},{4,20},{8,24},{12,28},{16,0},{20,4},{24,8},{28,12},{1,17},{... | collective-permute-start | bytes 811016 | tf_op jit(solution)/shard_map/ppermute | solution.py:76
  13.1 23.3 %collective-permute-start = (bf16[1056,128]{1,0:T(8,128)(2,1)S(1)}, bf16[1056,128]{1,0:T(8,128)(2,1)S(1)}, u32[]{:S(2)}, u32[]{:S(2)}) collective-permute-start(bf16[1056,128]{1,0:T(8,128)(2,1)S(1)} %get-tuple-element.86.refs_0_.refs_4_), channel_id=1, source_target_pairs={{0,8},{4,12},{8,0},{12,4},{16,24},{20,28},{24,16},{28,20},{1,9},{5... | collective-permute-start | bytes 811016 | tf_op jit(solution)/shard_map/ppermute | solution.py:76
  13.9 42.6 %collective-permute-start.10 = (bf16[224,256]{1,0:T(8,128)(2,1)S(1)}, bf16[224,256]{1,0:T(8,128)(2,1)S(1)}, u32[]{:S(2)}, u32[]{:S(2)}) collective-permute-start(bf16[224,256]{1,0:T(8,128)(2,1)S(1)} %get-tuple-element.92), channel_id=1, source_target_pairs={{0,1},{1,0},{2,3},{3,2},{4,5},{5,4},{6,7},{7,6},{8,9},{9,8},{10,11... | collective-permute-start | bytes 344072 | tf_op jit(solution)/shard_map/ppermute | solution.py:76
  23.5 20.3 %collective-permute-start.6 = (bf16[1056,128]{1,0:T(8,128)(2,1)S(1)}, bf16[1056,128]{1,0:T(8,128)(2,1)S(1)}, u32[]{:S(2)}, u32[]{:S(2)}) collective-permute-start(bf16[1056,128]{1,0:T(8,128)(2,1)S(1)} %collective-permute-done.2.refs_3_.refs_10_), channel_id=1, source_target_pairs={{0,4},{4,0},{8,12},{12,8},{16,20},{20,16},{24,28},{28,24},{1,5},{5... | collective-permute-start | bytes 811016 | tf_op jit(solution)/shard_map/ppermute | solution.py:76
  35.8 9.4 %collective-permute-start.5 = (bf16[1056,128]{1,0:T(8,128)(2,1)S(1)}, bf16[1056,128]{1,0:T(8,128)(2,1)S(1)}, u32[]{:S(2)}, u32[]{:S(2)}) collective-permute-start(bf16[1056,128]{1,0:T(8,128)(2,1)S(1)} %collective-permute-done.1.refs_2_.refs_8_), channel_id=1, source_target_pairs={{0,4},{4,0},{8,12},{12,8},{16,20},{20,16},{24,28},{28,24},{1,5},{5... | collective-permute-start | bytes 811016 | tf_op jit(solution)/shard_map/ppermute | solution.py:76
  36.3 12.8 %collective-permute-start.4 = (bf16[1056,128]{1,0:T(8,128)(2,1)S(1)}, bf16[1056,128]{1,0:T(8,128)(2,1)S(1)}, u32[]{:S(2)}, u32[]{:S(2)}) collective-permute-start(bf16[1056,128]{1,0:T(8,128)(2,1)S(1)} %collective-permute-done.refs_1_.refs_6_), channel_id=1, source_target_pairs={{0,4},{4,0},{8,12},{12,8},{16,20},{20,16},{24,28},{28,24},{1,5},{5... | collective-permute-start | bytes 811016 | tf_op jit(solution)/shard_map/ppermute | solution.py:76
  42.3 14.3 %collective-permute-start.11 = (bf16[224,256]{1,0:T(8,128)(2,1)S(1)}, bf16[224,256]{1,0:T(8,128)(2,1)S(1)}, u32[]{:S(2)}, u32[]{:S(2)}) collective-permute-start(bf16[224,256]{1,0:T(8,128)(2,1)S(1)} %get-tuple-element.93), channel_id=1, source_target_pairs={{0,2},{1,3},{2,0},{3,1},{4,6},{5,7},{6,4},{7,5},{8,10},{9,11},{10,... | collective-permute-start | bytes 344072 | tf_op jit(solution)/shard_map/ppermute | solution.py:76
  43.8 21.8 %collective-permute-start.12 = (bf16[224,256]{1,0:T(8,128)(2,1)S(1)}, bf16[224,256]{1,0:T(8,128)(2,1)S(1)}, u32[]{:S(2)}, u32[]{:S(2)}) collective-permute-start(bf16[224,256]{1,0:T(8,128)(2,1)S(1)} %get-tuple-element.94), channel_id=1, source_target_pairs={{0,3},{1,2},{2,1},{3,0},{4,7},{5,6},{6,5},{7,4},{8,11},{9,10},{10,... | collective-permute-start | bytes 344072 | tf_op jit(solution)/shard_map/ppermute | solution.py:76
  45.2 11.8 %collective-permute-start.15 = (bf16[4,288,128]{2,1,0:T(8,128)(2,1)S(1)}, bf16[4,288,128]{2,1,0:T(8,128)(2,1)S(1)}, u32[]{:S(2)}, u32[]{:S(2)}) collective-permute-start(bf16[4,288,128]{2,1,0:T(8,128)(2,1)S(1)} %shard_map.394.refs_0_), channel_id=1, source_target_pairs={{0,2},{1,3},{2,0},{3,1},{4,6},{5,7},{6,4},{7,5},{8,10},{9,11},{10,... | collective-permute-start | bytes 884744 | tf_op jit(solution)/shard_map/ppermute | solution.py:76
  49.1 13.1 %copy-start.27 = (s32[48]{0:T(128)S(1)}, s32[48]{0:T(128)}, u32[]{:S(2)}) copy-start(s32[48]{0:T(128)} %owners_ref.3) | copy-start | bytes 580
  49.1 13.1 %collective-permute-start.16 = (bf16[4,288,128]{2,1,0:T(8,128)(2,1)S(1)}, bf16[4,288,128]{2,1,0:T(8,128)(2,1)S(1)}, u32[]{:S(2)}, u32[]{:S(2)}) collective-permute-start(bf16[4,288,128]{2,1,0:T(8,128)(2,1)S(1)} %shard_map.398.refs_1_), channel_id=1, source_target_pairs={{0,2},{1,3},{2,0},{3,1},{4,6},{5,7},{6,4},{7,5},{8,10},{9,11},{10,... | collective-permute-start | bytes 884744 | tf_op jit(solution)/shard_map/ppermute | solution.py:76
  56.5 9.7 %collective-permute-start.13 = (bf16[4,288,128]{2,1,0:T(8,128)(2,1)S(1)}, bf16[4,288,128]{2,1,0:T(8,128)(2,1)S(1)}, u32[]{:S(2)}, u32[]{:S(2)}) collective-permute-start(bf16[4,288,128]{2,1,0:T(8,128)(2,1)S(1)} %shard_map.394.refs_0_), channel_id=1, source_target_pairs={{0,1},{1,0},{2,3},{3,2},{4,5},{5,4},{6,7},{7,6},{8,9},{9,8},{10,11... | collective-permute-start | bytes 884744 | tf_op jit(solution)/shard_map/ppermute | solution.py:76
  56.5 11.1 %collective-permute-start.14 = (bf16[4,288,128]{2,1,0:T(8,128)(2,1)S(1)}, bf16[4,288,128]{2,1,0:T(8,128)(2,1)S(1)}, u32[]{:S(2)}, u32[]{:S(2)}) collective-permute-start(bf16[4,288,128]{2,1,0:T(8,128)(2,1)S(1)} %shard_map.398.refs_1_), channel_id=1, source_target_pairs={{0,1},{1,0},{2,3},{3,2},{4,5},{5,4},{6,7},{7,6},{8,9},{9,8},{10,11... | collective-permute-start | bytes 884744 | tf_op jit(solution)/shard_map/ppermute | solution.py:76
  57.0 10.6 %collective-permute-start.17 = (bf16[4,288,128]{2,1,0:T(8,128)(2,1)S(1)}, bf16[4,288,128]{2,1,0:T(8,128)(2,1)S(1)}, u32[]{:S(2)}, u32[]{:S(2)}) collective-permute-start(bf16[4,288,128]{2,1,0:T(8,128)(2,1)S(1)} %collective-permute-done.15.refs_4_), channel_id=1, source_target_pairs={{0,1},{1,0},{2,3},{3,2},{4,5},{5,4},{6,7},{7,6},{8,9},{9,8},{10,11... | collective-permute-start | bytes 884744 | tf_op jit(solution)/shard_map/ppermute | solution.py:76
  62.2 5.4 %collective-permute-start.18 = (bf16[4,288,128]{2,1,0:T(8,128)(2,1)S(1)}, bf16[4,288,128]{2,1,0:T(8,128)(2,1)S(1)}, u32[]{:S(2)}, u32[]{:S(2)}) collective-permute-start(bf16[4,288,128]{2,1,0:T(8,128)(2,1)S(1)} %collective-permute-done.16.refs_5_), channel_id=1, source_target_pairs={{0,1},{1,0},{2,3},{3,2},{4,5},{5,4},{6,7},{7,6},{8,9},{9,8},{10,11... | collective-permute-start | bytes 884744 | tf_op jit(solution)/shard_map/ppermute | solution.py:76
  65.6 8.5 %collective-permute-start.7 = (bf16[128,256]{1,0:T(8,128)(2,1)S(1)}, bf16[128,256]{1,0:T(8,128)(2,1)S(1)}, u32[]{:S(2)}, u32[]{:S(2)}) collective-permute-start(bf16[128,256]{1,0:T(8,128)(2,1)S(1)} %get-tuple-element.88), channel_id=1, source_target_pairs={{0,1},{1,0},{2,3},{3,2},{4,5},{5,4},{6,7},{7,6},{8,9},{9,8},{10,11... | collective-permute-start | bytes 196616 | tf_op jit(solution)/shard_map/ppermute | solution.py:76
  66.2 8.0 %collective-permute-start.8 = (bf16[128,256]{1,0:T(8,128)(2,1)S(1)}, bf16[128,256]{1,0:T(8,128)(2,1)S(1)}, u32[]{:S(2)}, u32[]{:S(2)}) collective-permute-start(bf16[128,256]{1,0:T(8,128)(2,1)S(1)} %get-tuple-element.89), channel_id=1, source_target_pairs={{0,2},{1,3},{2,0},{3,1},{4,6},{5,7},{6,4},{7,5},{8,10},{9,11},{10,... | collective-permute-start | bytes 196616 | tf_op jit(solution)/shard_map/ppermute | solution.py:76
  67.7 6.5 %collective-permute-start.9 = (bf16[128,256]{1,0:T(8,128)(2,1)S(1)}, bf16[128,256]{1,0:T(8,128)(2,1)S(1)}, u32[]{:S(2)}, u32[]{:S(2)}) collective-permute-start(bf16[128,256]{1,0:T(8,128)(2,1)S(1)} %get-tuple-element.90), channel_id=1, source_target_pairs={{0,3},{1,2},{2,1},{3,0},{4,7},{5,6},{6,5},{7,4},{8,11},{9,10},{10,... | collective-permute-start | bytes 196616 | tf_op jit(solution)/shard_map/ppermute | solution.py:76
  81.6 1.6 %collective-permute-start.19 = (bf16[128,256]{1,0:T(8,128)(2,1)S(1)}, bf16[128,256]{1,0:T(8,128)(2,1)S(1)}, u32[]{:S(2)}, u32[]{:S(2)}) collective-permute-start(bf16[128,256]{1,0:T(8,128)(2,1)S(1)} %get-tuple-element.107), channel_id=1, source_target_pairs={{0,1},{1,0},{2,3},{3,2},{4,5},{5,4},{6,7},{7,6},{8,9},{9,8},{10,11... | collective-permute-start | bytes 196616 | tf_op jit(solution)/shard_map/ppermute | solution.py:76
  85.8 9.9 %collective-permute-start.20 = (bf16[1568,384]{1,0:T(8,128)(2,1)S(1)}, bf16[1568,384]{1,0:T(8,128)(2,1)S(1)}, u32[]{:S(2)}, u32[]{:S(2)}) collective-permute-start(bf16[1568,384]{1,0:T(8,128)(2,1)S(1)} %get-tuple-element.109), channel_id=1, source_target_pairs={{0,1},{1,0},{2,3},{3,2},{4,5},{5,4},{6,7},{7,6},{8,9},{9,8},{10,11... | collective-permute-start | bytes 3612680 | tf_op jit(solution)/shard_map/ppermute | solution.py:76
  86.2 4.1 %collective-permute-start.21 = (bf16[128,256]{1,0:T(8,128)(2,1)S(1)}, bf16[128,256]{1,0:T(8,128)(2,1)S(1)}, u32[]{:S(2)}, u32[]{:S(2)}) collective-permute-start(bf16[128,256]{1,0:T(8,128)(2,1)S(1)} %get-tuple-element.110), channel_id=1, source_target_pairs={{0,3},{1,2},{2,1},{3,0},{4,7},{5,6},{6,5},{7,4},{8,11},{9,10},{10,... | collective-permute-start | bytes 196616 | tf_op jit(solution)/shard_map/ppermute | solution.py:76
  87.5 4.5 %collective-permute-start.26 = (bf16[128,256]{1,0:T(8,128)(2,1)S(1)}, bf16[128,256]{1,0:T(8,128)(2,1)S(1)}, u32[]{:S(2)}, u32[]{:S(2)}) collective-permute-start(bf16[128,256]{1,0:T(8,128)(2,1)S(1)} %get-tuple-element.116), channel_id=1, source_target_pairs={{0,2},{1,3},{2,0},{3,1},{4,6},{5,7},{6,4},{7,5},{8,10},{9,11},{10,... | collective-permute-start | bytes 196616 | tf_op jit(solution)/shard_map/ppermute | solution.py:76
  94.5 7.9 %collective-permute-start.27 = (bf16[768,128]{1,0:T(8,128)(2,1)S(1)}, bf16[768,128]{1,0:T(8,128)(2,1)S(1)}, u32[]{:S(2)}, u32[]{:S(2)}) collective-permute-start(bf16[768,128]{1,0:T(8,128)(2,1)S(1)} %get-tuple-element.118), channel_id=1, source_target_pairs={{0,4},{4,0},{8,12},{12,8},{16,20},{20,16},{24,28},{28,24},{1,5},{5... | collective-permute-start | bytes 589832 | tf_op jit(solution)/shard_map/ppermute | solution.py:76
  96.0 15.3 %collective-permute-start.22 = (bf16[800,384]{1,0:T(8,128)(2,1)S(1)}, bf16[800,384]{1,0:T(8,128)(2,1)S(1)}, u32[]{:S(2)}, u32[]{:S(2)}) collective-permute-start(bf16[800,384]{1,0:T(8,128)(2,1)S(1)} %get-tuple-element.112), channel_id=1, source_target_pairs={{0,2},{1,3},{2,0},{3,1},{4,6},{5,7},{6,4},{7,5},{8,10},{9,11},{10,... | collective-permute-start | bytes 1843208 | tf_op jit(solution)/shard_map/ppermute | solution.py:76
  97.6 8.9 %collective-permute-start.29 = (bf16[768,128]{1,0:T(8,128)(2,1)S(1)}, bf16[768,128]{1,0:T(8,128)(2,1)S(1)}, u32[]{:S(2)}, u32[]{:S(2)}) collective-permute-start(bf16[768,128]{1,0:T(8,128)(2,1)S(1)} %get-tuple-element.120), channel_id=1, source_target_pairs={{0,4},{4,0},{8,12},{12,8},{16,20},{20,16},{24,28},{28,24},{1,5},{5... | collective-permute-start | bytes 589832 | tf_op jit(solution)/shard_map/ppermute | solution.py:76
  98.5 13.9 %collective-permute-start.31 = (bf16[768,128]{1,0:T(8,128)(2,1)S(1)}, bf16[768,128]{1,0:T(8,128)(2,1)S(1)}, u32[]{:S(2)}, u32[]{:S(2)}) collective-permute-start(bf16[768,128]{1,0:T(8,128)(2,1)S(1)} %get-tuple-element.122), channel_id=1, source_target_pairs={{0,4},{4,0},{8,12},{12,8},{16,20},{20,16},{24,28},{28,24},{1,5},{5... | collective-permute-start | bytes 589832 | tf_op jit(solution)/shard_map/ppermute | solution.py:76
  99.7 15.0 %collective-permute-start.33 = (bf16[768,128]{1,0:T(8,128)(2,1)S(1)}, bf16[768,128]{1,0:T(8,128)(2,1)S(1)}, u32[]{:S(2)}, u32[]{:S(2)}) collective-permute-start(bf16[768,128]{1,0:T(8,128)(2,1)S(1)} %get-tuple-element.124), channel_id=1, source_target_pairs={{0,4},{4,0},{8,12},{12,8},{16,20},{20,16},{24,28},{28,24},{1,5},{5... | collective-permute-start | bytes 589832 | tf_op jit(solution)/shard_map/ppermute | solution.py:76
  102.4 19.3 %collective-permute-start.28 = (bf16[768,128]{1,0:T(8,128)(2,1)S(1)}, bf16[768,128]{1,0:T(8,128)(2,1)S(1)}, u32[]{:S(2)}, u32[]{:S(2)}) collective-permute-start(bf16[768,128]{1,0:T(8,128)(2,1)S(1)} %add_convert_fusion.3), channel_id=1, source_target_pairs={{0,24},{4,28},{8,16},{12,20},{16,8},{20,12},{24,0},{28,4},{1,25},{... | collective-permute-start | bytes 589832 | tf_op jit(solution)/shard_map/ppermute | solution.py:76
  106.6 15.5 %collective-permute-start.30 = (bf16[768,128]{1,0:T(8,128)(2,1)S(1)}, bf16[768,128]{1,0:T(8,128)(2,1)S(1)}, u32[]{:S(2)}, u32[]{:S(2)}) collective-permute-start(bf16[768,128]{1,0:T(8,128)(2,1)S(1)} %add_convert_fusion.2), channel_id=1, source_target_pairs={{0,16},{4,20},{8,24},{12,28},{16,0},{20,4},{24,8},{28,12},{1,17},{... | collective-permute-start | bytes 589832 | tf_op jit(solution)/shard_map/ppermute | solution.py:76
  111.5 9.0 %collective-permute-start.34 = (bf16[416,384]{1,0:T(8,128)(2,1)S(1)}, bf16[416,384]{1,0:T(8,128)(2,1)S(1)}, u32[]{:S(2)}, u32[]{:S(2)}) collective-permute-start(bf16[416,384]{1,0:T(8,128)(2,1)S(1)} %get-tuple-element.130), channel_id=1, source_target_pairs={{0,4},{4,0},{8,12},{12,8},{16,20},{20,16},{24,28},{28,24},{1,5},{5... | collective-permute-start | bytes 958472 | tf_op jit(solution)/shard_map/ppermute | solution.py:76
  112.4 9.2 %collective-permute-start.24 = (bf16[256,768]{1,0:T(8,128)(2,1)S(1)}, bf16[256,768]{1,0:T(8,128)(2,1)S(1)}, u32[]{:S(2)}, u32[]{:S(2)}) collective-permute-start(bf16[256,768]{1,0:T(8,128)(2,1)S(1)} %get-tuple-element.114.refs_0_), channel_id=1, source_target_pairs={{0,2},{1,3},{2,0},{3,1},{4,6},{5,7},{6,4},{7,5},{8,10},{9,11},{10,... | collective-permute-start | bytes 1179656 | tf_op jit(solution)/shard_map/ppermute | solution.py:76
  114.6 10.9 %collective-permute-start.32 = (bf16[768,128]{1,0:T(8,128)(2,1)S(1)}, bf16[768,128]{1,0:T(8,128)(2,1)S(1)}, u32[]{:S(2)}, u32[]{:S(2)}) collective-permute-start(bf16[768,128]{1,0:T(8,128)(2,1)S(1)} %add_convert_fusion.1), channel_id=1, source_target_pairs={{0,8},{4,12},{8,0},{12,4},{16,24},{20,28},{24,16},{28,20},{1,9},{5... | collective-permute-start | bytes 589832 | tf_op jit(solution)/shard_map/ppermute | solution.py:76
  120.5 14.0 %collective-permute-start.23 = (bf16[256,768]{1,0:T(8,128)(2,1)S(1)}, bf16[256,768]{1,0:T(8,128)(2,1)S(1)}, u32[]{:S(2)}, u32[]{:S(2)}) collective-permute-start(bf16[256,768]{1,0:T(8,128)(2,1)S(1)} %get-tuple-element.114.refs_0_), channel_id=1, source_target_pairs={{0,1},{1,0},{2,3},{3,2},{4,5},{5,4},{6,7},{7,6},{8,9},{9,8},{10,11... | collective-permute-start | bytes 1179656 | tf_op jit(solution)/shard_map/ppermute | solution.py:76
  121.6 12.9 %collective-permute-start.25 = (bf16[256,768]{1,0:T(8,128)(2,1)S(1)}, bf16[256,768]{1,0:T(8,128)(2,1)S(1)}, u32[]{:S(2)}, u32[]{:S(2)}) collective-permute-start(bf16[256,768]{1,0:T(8,128)(2,1)S(1)} %collective-permute-done.24.refs_2_), channel_id=1, source_target_pairs={{0,1},{1,0},{2,3},{3,2},{4,5},{5,4},{6,7},{7,6},{8,9},{9,8},{10,11... | collective-permute-start | bytes 1179656 | tf_op jit(solution)/shard_map/ppermute | solution.py:76
  121.7 7.1 %collective-permute-start.35 = (bf16[128,384]{1,0:T(8,128)(2,1)S(1)}, bf16[128,384]{1,0:T(8,128)(2,1)S(1)}, u32[]{:S(2)}, u32[]{:S(2)}) collective-permute-start(bf16[128,384]{1,0:T(8,128)(2,1)S(1)} %get-tuple-element.132), channel_id=1, source_target_pairs={{0,8},{4,12},{8,0},{12,4},{16,24},{20,28},{24,16},{28,20},{1,9},{5... | collective-permute-start | bytes 294920 | tf_op jit(solution)/shard_map/ppermute | solution.py:76
  122.1 11.2 %collective-permute-start.36 = (bf16[128,384]{1,0:T(8,128)(2,1)S(1)}, bf16[128,384]{1,0:T(8,128)(2,1)S(1)}, u32[]{:S(2)}, u32[]{:S(2)}) collective-permute-start(bf16[128,384]{1,0:T(8,128)(2,1)S(1)} %get-tuple-element.133), channel_id=1, source_target_pairs={{0,16},{4,20},{8,24},{12,28},{16,0},{20,4},{24,8},{28,12},{1,17},{... | collective-permute-start | bytes 294920 | tf_op jit(solution)/shard_map/ppermute | solution.py:76
  125.5 7.8 %copy-start.9 = (f32[64,384]{1,0:T(8,128)S(1)}, f32[64,384]{1,0:T(8,128)}, u32[]{:S(2)}) copy-start(f32[64,384]{1,0:T(8,128)} %refs_0_.3) | copy-start | bytes 294916
  125.5 7.8 %copy-start.10 = (f32[64,384]{1,0:T(8,128)S(1)}, f32[64,384]{1,0:T(8,128)}, u32[]{:S(2)}) copy-start(f32[64,384]{1,0:T(8,128)} %refs_1_.3) | copy-start | bytes 294916
  125.5 7.8 %copy-start.11 = (f32[64,384]{1,0:T(8,128)S(1)}, f32[64,384]{1,0:T(8,128)}, u32[]{:S(2)}) copy-start(f32[64,384]{1,0:T(8,128)} %refs_2_.3) | copy-start | bytes 294916
  125.5 7.8 %copy-start.12 = (f32[64,384]{1,0:T(8,128)S(1)}, f32[64,384]{1,0:T(8,128)}, u32[]{:S(2)}) copy-start(f32[64,384]{1,0:T(8,128)} %refs_3_.3) | copy-start | bytes 294916
  125.5 7.8 %copy-start.14 = (f32[64,192]{1,0:T(8,128)S(1)}, f32[64,192]{1,0:T(8,128)}, u32[]{:S(2)}) copy-start(f32[64,192]{1,0:T(8,128)} %refs_4_.1) | copy-start | bytes 147460
  125.5 7.8 %copy-start.15 = (f32[64,192]{1,0:T(8,128)S(1)}, f32[64,192]{1,0:T(8,128)}, u32[]{:S(2)}) copy-start(f32[64,192]{1,0:T(8,128)} %refs_5_.1) | copy-start | bytes 147460
  125.7 7.7 %collective-permute-start.37 = (bf16[128,384]{1,0:T(8,128)(2,1)S(1)}, bf16[128,384]{1,0:T(8,128)(2,1)S(1)}, u32[]{:S(2)}, u32[]{:S(2)}) collective-permute-start(bf16[128,384]{1,0:T(8,128)(2,1)S(1)} %get-tuple-element.134), channel_id=1, source_target_pairs={{0,24},{4,28},{8,16},{12,20},{16,8},{20,12},{24,0},{28,4},{1,25},{... | collective-permute-start | bytes 294920 | tf_op jit(solution)/shard_map/ppermute | solution.py:76
  (18 other events, 94.0 us)

commit v4 on v3

--- a/solution.py
+++ b/solution.py
@@ -81,7 +81,7 @@
 
 
 def low_kernel(table_hbm, first_hbm, second_hbm, vector_hbm, cot_hbm, *refs, hid):
-    piece, weight_out, cots = refs[0], refs[1], refs[2 : 2 + hid]
+    piece, keep, cots = refs[0], refs[1], refs[2 : 2 + hid]
     table, first, second, vector, cot, sems = refs[2 + hid :]
     copies = [
         pltpu.make_async_copy(source, target, sems.at[i])
@@ -99,20 +99,22 @@
         copy.start()
     copies[0].wait()
     slots, feats = table.shape
-    piece[0:slots, :] = table[...].astype(bf16)
+    for out in (piece, keep):
+        out[0:slots, :] = table[...].astype(bf16)
     copies[1].wait()
     copies[2].wait()
     rows = first.shape[0]
-    each = weight_out.shape[0] // 3
+    each = (piece.shape[0] - slots) // 3
     fold = each - rows
     folded = jnp.concatenate(
         [second[i * fold : (i + 1) * fold, :] for i in range(second.shape[0] // fold)], axis=1
     )
     for g in range(3):
         lanes = slice(g * feats, (g + 1) * feats)
-        for out, start in ((piece, slots), (weight_out, 0)):
-            out[start + g * each : start + g * each + rows, :] = first[:, lanes].astype(bf16)
-            out[start + g * each + rows : start + (g + 1) * each, :] = folded[:, lanes].astype(bf16)
+        start = slots + g * each
+        for out in (piece, keep):
+            out[start : start + rows, :] = first[:, lanes].astype(bf16)
+            out[start + rows : start + each, :] = folded[:, lanes].astype(bf16)
     copies[3].wait()
     copies[4].wait()
     me = lax.axis_index("hid")
@@ -231,39 +233,14 @@
     return jnp.where(col == target, 1.0, 0.0).astype(bf16)
 
 
-def weights_kernel(*refs, dp, hid):
-    inner = inner_size(dp)
-    given = hid * inner
-    stacks, cots = refs[:given], refs[given : given + hid]
-    w1p, w1t, w2p, w2t, col_ref, q_ref, q3t_ref = refs[given + hid : given + hid + 7]
-    w1s, w2s, vecs = refs[given + hid + 7 :]
-    me_dp, me_hid = lax.axis_index("dp"), lax.axis_index("hid")
-    rows = D // dp
-    fold = H // dp
-    each = rows + fold
-    width = (O * EXPERTS) // dp
-    high = H // hid
-    feats = stacks[0].shape[2]
-    j_step = w1s.shape[2]
-    k_step = w2s.shape[2]
+def turns_kernel(*refs, hid):
+    cots = refs[:hid]
+    col_ref, q_ref, q3t_ref, vecs = refs[hid:]
+    me_hid = lax.axis_index("hid")
+    j_step = vecs.shape[2]
     for r in range(hid):
-        j = me_hid ^ r
-        for s in range(dp):
-            k = me_dp ^ s
-            stack, at = stacks[r * inner + s % inner], s // inner
-            for g in range(3):
-                w1s[j, pl.ds(pl.multiple_of(k * rows, rows), rows), g * feats : (g + 1) * feats] = (
-                    stack[at, g * each : g * each + rows, :]
-                )
-            part = jnp.concatenate(
-                [stack[at, g * each + rows : (g + 1) * each, :].astype(f32) for g in range(3)],
-                axis=1,
-            )
-            for q in range(high // fold):
-                start = pl.multiple_of(j * high + q * fold, fold)
-                w2s[k, pl.ds(start, fold), :] = part[:, q * width : (q + 1) * width].astype(bf16)
         cols, near = cots[r].shape[0] - 32, cots[r].shape[1]
-        vecs[j] = jnp.concatenate(
+        vecs[me_hid ^ r] = jnp.concatenate(
             [cots[r][cols : cols + 16, :], cots[r][cols + 16 : cols + 32, 0 : j_step - near]], axis=1
         )
     span = HALF * EXPERTS
@@ -271,35 +248,59 @@
     q3t_ref[...] = hot_vc(O * STREAMS, O * STREAMS, STREAMS, 0)
     for half in range(2):
         lanes = slice(half * HALF, (half + 1) * HALF)
-        total_p, total_t, total_c = None, None, None
+        value = None
         for i in range(span // j_step):
-            w1 = w1s[half * (span // j_step) + i]
-            hot = hot_vc(span, j_step, EXPERTS, i * j_step)
-            p = nn(w1, q_ref[i * j_step : (i + 1) * j_step, :])
-            t = nt(hot, w1)
-            c = nt(hot, vecs[half * (span // j_step) + i])
-            total_p = p if total_p is None else total_p + p
-            total_t = t if total_t is None else total_t + t
-            total_c = c if total_c is None else total_c + c
-        for e in range(EXPERTS):
-            w1p[e, :, lanes] = total_p[:, e * HALF : (e + 1) * HALF].astype(bf16)
-            w1t[e, lanes, :] = total_t[e * HALF : (e + 1) * HALF, :].astype(bf16)
-        cols = total_c[:, 0:3] + total_c[:, 3:6] + total_c[:, 6:9]
+            c = nt(hot_vc(span, j_step, EXPERTS, i * j_step), vecs[half * (span // j_step) + i])
+            value = c if value is None else value + c
+        cols = value[:, 0:3] + value[:, 3:6] + value[:, 6:9]
         for e in range(EXPERTS):
             for i in range(3):
                 col_ref[i, e, lanes, :] = jnp.broadcast_to(
                     cols[e * HALF : (e + 1) * HALF, i : i + 1], (HALF, HALF)
                 )
-        total_p, total_t = None, None
-        for i in range(span // k_step):
-            w2 = w2s[half * (span // k_step) + i]
-            p = nn(w2, q_ref[i * k_step : (i + 1) * k_step, :])
-            t = nt(hot_vc(span, k_step, EXPERTS, i * k_step), w2)
-            total_p = p if total_p is None else total_p + p
-            total_t = t if total_t is None else total_t + t
-        for e in range(EXPERTS):
-            w2p[e, :, lanes] = total_p[:, e * HALF : (e + 1) * HALF].astype(bf16)
-            w2t[e, lanes, :] = total_t[e * HALF : (e + 1) * HALF, :].astype(bf16)
+
+
+def weights_kernel(*refs, dp, hid):
+    inner = inner_size(dp)
+    given = hid
+    stacks, q_ref = refs[:given], refs[given]
+    w1p, w2p = refs[given + 1 : given + 3]
+    w1s, w2s = refs[given + 3 :]
+    me_dp, me_hid = lax.axis_index("dp"), lax.axis_index("hid")
+    rows = D // dp
+    fold = H // dp
+    each = rows + fold
+    width = (O * EXPERTS) // dp
+    high = H // hid
+    feats = stacks[0].shape[-1]
+    j_step = w1s.shape[2]
+    k_step = w2s.shape[2]
+    for r in range(hid):
+        j = me_hid ^ r
+        for s in range(dp):
+            k = me_dp ^ s
+            near, at = s % inner, s // inner
+            for g in range(3):
+                w1s[j, pl.ds(pl.multiple_of(k * rows, rows), rows), g * feats : (g + 1) * feats] = (
+                    stacks[r][near, at, g * each : g * each + rows, :]
+                )
+            part = jnp.concatenate(
+                [stacks[r][near, at, g * each + rows : (g + 1) * each, :].astype(f32) for g in range(3)],
+                axis=1,
+            )
+            for q in range(high // fold):
+                start = pl.multiple_of(j * high + q * fold, fold)
+                w2s[k, pl.ds(start, fold), :] = part[:, q * width : (q + 1) * width].astype(bf16)
+    span = HALF * EXPERTS
+    for half in range(2):
+        lanes = slice(half * HALF, (half + 1) * HALF)
+        for step, source, out in ((j_step, w1s, w1p), (k_step, w2s, w2p)):
+            value = None
+            for i in range(span // step):
+                p = nn(source[half * (span // step) + i], q_ref[i * step : (i + 1) * step, :])
+                value = p if value is None else value + p
+            for e in range(EXPERTS):
+                out[e, :, lanes] = value[:, e * HALF : (e + 1) * HALF].astype(bf16)
 
 
 def small_plan(hid):
@@ -321,13 +322,16 @@
     return jnp.concatenate([column] * (width // HALF), axis=1) if width > HALF else column
 
 
-def main_kernel(*refs, hid):
+def main_kernel(*refs, dp, hid):
     xts, cots = refs[:hid], refs[hid : 2 * hid]
-    w1p, w1t, w2p, w2t, col_ref, q_ref, q3t_ref, gate_ref = refs[2 * hid : 2 * hid + 8]
-    outs = refs[2 * hid + 8 :]
-    mixed_ref, small_ref, xt, hid_ref, dinner_ref, dpre_ref = outs[:6]
-    dx_outs = outs[6 : 6 + hid]
-    up, upq, mix, work, slope, norm, dout, dx, vec = outs[6 + hid :]
+    w1p, w2p, col_ref, q_ref, q3t_ref, gate_ref = refs[2 * hid : 2 * hid + 6]
+    outs = refs[2 * hid + 6 :]
+    mixed_ref, small_ref, home, away = outs[:4]
+    dx_outs = outs[4 : 4 + hid]
+    xt, hid_ref, dinner_ref, dpre_ref, up, upq, mix, work, slope, norm, dout, dx, vec = outs[
+        4 + hid : 17 + hid
+    ]
+    turned, w1g, w2n, w2g = outs[17 + hid :]
     me = lax.axis_index("hid")
     feats, rows = xts[0].shape
     for m in range(hid):
@@ -353,13 +357,13 @@
             t: chances[t][STREAM_EXPERTS[t].index(e) : STREAM_EXPERTS[t].index(e) + 1]
             for t in streams
         }
-        work[...] = nn(w1t[e], xt[...])
+        work[...] = tn(w1p[e], xt[...])
         for p in parts:
             pre = work[p, :] + wide(col_ref[0, e, p, :], rows)
             phi = 0.5 + 0.5 * lax.erf(pre * 0.7071067811865476)
             hid_ref[e, p, :] = (pre * phi).astype(bf16)
             slope[p, :] = phi + pre * (jnp.exp(-0.5 * pre * pre) * 0.3989422804014327)
-        work[...] = nn(w2t[e], hid_ref[e])
+        work[...] = tn(w2p[e], hid_ref[e])
         total = jnp.zeros((1, rows), f32)
         for p in parts:
             total = total + jnp.sum(work[p, :], axis=0, keepdims=True)
@@ -398,6 +402,7 @@
         work[...] = nn(w2p[e], dinner_ref[e])
         for p in parts:
             dpre_ref[e, p, :] = (work[p, :] * slope[p, :]).astype(bf16)
+        w2n[e] = nt(hid_ref[e], dinner_ref[e]).astype(bf16)
         vec[0, e] = nt(ones, dpre_ref[e])
         vec[1, e] = nt(ones, dout[0])
         vec[2, e] = nt(ones, dout[1])
@@ -437,62 +442,56 @@
             + [jnp.zeros((5, HALF * EXPERTS), f32)],
             axis=0,
         ).astype(bf16)
-        turned = nt(stack, q_ref[...])
+        unturned = nt(stack, q_ref[...])
         for i in range((HALF * EXPERTS) // width):
-            lines.append(turned[0:3, i * width : (i + 1) * width])
+            lines.append(unturned[0:3, i * width : (i + 1) * width])
     spare = small_rows - sum(line.shape[0] for line in lines)
     if spare:
         lines.append(jnp.zeros((spare, width), f32))
     small_ref[...] = jnp.concatenate(lines, axis=0).astype(bf16)
     mixed_ref[...] = tn(mix[...].astype(bf16), q3t_ref[...]).astype(bf16)
-
-
-def grads_kernel(xt, hid_ref, dinner_ref, dpre_ref, q_ref, small_ref, order_ref, *refs, dp, hid):
-    home, away, turned, w1g, w2g = refs
-    me_dp, me_hid = lax.axis_index("dp"), lax.axis_index("hid")
+    me_dp = lax.axis_index("dp")
     span = HALF * EXPERTS
-    rows = D // dp
+    first_rows = D // dp
     fold = H // dp
-    each = rows + fold
-    width = (O * EXPERTS) // dp
+    each = first_rows + fold
+    second_cols = (O * EXPERTS) // dp
     high = H // hid
-    cols = (H * EXPERTS) // hid
     inner = inner_size(dp)
     outer = dp // inner
-    whole = [nt(hid_ref[e], dinner_ref[e]).astype(bf16) for e in range(EXPERTS)]
     for half in range(2):
         part = slice(half * HALF, (half + 1) * HALF)
         block = jnp.concatenate([dpre_ref[e, part, :] for e in range(EXPERTS)], axis=0)
         turned[half * span : (half + 1) * span, :] = nn(q_ref[...], block).astype(bf16)
-        block = jnp.concatenate([w[:, part] for w in whole], axis=1)
+        block = jnp.concatenate([w2n[e, :, part] for e in range(EXPERTS)], axis=1)
         w2g[:, half * span : (half + 1) * span] = nt(block, q_ref[...])
     for m in range(hid):
         out, base = (away if m % 2 else home), (m // 2) * dp * each
-        j = me_hid ^ m
-        left = turned[pl.ds(pl.multiple_of(j * cols, cols), cols), :]
+        j = me ^ m
+        left = turned[pl.ds(pl.multiple_of(j * width, width), width), :]
         w1g[...] = nt(xt[...], left).astype(bf16)
         for near in range(inner):
             for far in range(outer):
                 k = me_dp ^ (far * inner + near)
-                start = pl.multiple_of(k * rows, rows)
+                start = pl.multiple_of(k * first_rows, first_rows)
                 to = base + (near * outer + far) * each
-                out[to : to + rows, :] = w1g[pl.ds(start, rows), :]
+                out[to : to + first_rows, :] = w1g[pl.ds(start, first_rows), :]
         start = pl.multiple_of(j * high, high)
         for k in range(dp):
-            part = w2g[pl.ds(start, high), k * width : (k + 1) * width]
+            part = w2g[pl.ds(start, high), k * second_cols : (k + 1) * second_cols]
             folded = jnp.concatenate(
                 [part[i * fold : (i + 1) * fold, :] for i in range(high // fold)], axis=1
             ).astype(bf16)
             r = me_dp ^ k
-            to = base + ((r % inner) * outer + r // inner) * each + rows
+            to = base + ((r % inner) * outer + r // inner) * each + first_rows
             out[pl.ds(pl.multiple_of(to, fold), fold), :] = folded
     away[(hid // 2) * dp * each :, :] = small_ref[...]
 
 
 def table_kernel(owners_ref, *refs, chunks, dp, hid):
     counts, pieces = refs[:chunks], refs[chunks : chunks + hid]
-    outs = refs[chunks + hid : chunks + hid + dp]
-    back, grads, slots, count_ref = refs[chunks + hid + dp :]
+    outs = refs[chunks + hid + 1 : chunks + hid + 1 + dp]
+    back, grads, slots, count_ref = refs[chunks + hid + 1 + dp :]
     me_dp, me_hid = lax.axis_index("dp"), lax.axis_index("hid")
     rows = pieces[0].shape[1]
     for m in range(hid):
@@ -526,34 +525,44 @@
     return (a.astype(f32) + b.astype(f32)).astype(bf16)
 
 
-def core_merge_kernel(home, come, small, order_ref, *outs, rows):
-    count = len(outs)
-    for i in range(count):
-        outs[i][0:rows, :] = plus(home[i * rows : (i + 1) * rows, :], come[i * rows : (i + 1) * rows, :])
-        outs[i][rows:, :] = plus(small[...], come[count * rows :, :])
-
-
-def chip_merge_kernel(*refs, terms, rows, inner):
-    parts, mixed = refs[:terms], refs[terms]
-    outs, mixed_out = refs[terms + 1 : terms + 1 + inner], refs[terms + 1 + inner]
-    last = total(parts, slice(inner * rows, None)).astype(bf16)
-    for near in range(inner):
-        outs[near][0:rows, :] = total(parts, slice(near * rows, (near + 1) * rows)).astype(bf16)
-        outs[near][rows:, :] = last
-    mixed_out[...] = mixed[...]
-
-
-def near_merge_kernel(*refs, terms, rows, outer):
-    parts, outs = refs[:terms], refs[terms:]
-    last = total(parts, slice(outer * rows, None)).astype(bf16)
+def core_merge_kernel(home, come, small, *outs, rows, inner):
+    last = plus(small[...], come[len(outs) * rows :, :])
+    for i, out in enumerate(outs):
+        part = slice(i * rows, (i + 1) * rows)
+        out[0:rows, :] = plus(home[part, :], come[part, :])
+        if i % inner:
+            out[rows:, :] = last
+
+
+def chip_merge_kernel(*refs, terms):
+    if len(refs) == terms + 3:
+        refs[terms + 2][...] = refs[terms][...]
+        refs[terms + 1][...] = total(refs[:terms]).astype(bf16)
+    else:
+        refs[terms][...] = total(refs[:terms]).astype(bf16)
+
+
+def near_merge_kernel(mine, other, *refs, terms, rows, outer):
+    come, outs = refs[: terms - 1], refs[terms - 1 :]
+    last = total((other, *come), slice(outer * rows, None)).astype(bf16)
     for far in range(outer):
-        outs[far][0:rows, :] = total(parts, slice(far * rows, (far + 1) * rows)).astype(bf16)
+        part = slice(far * rows, (far + 1) * rows)
+        outs[far][0:rows, :] = total((mine, *come), part).astype(bf16)
         outs[far][rows:, :] = last
 
 
 def stack_kernel_ordered(*refs, count, start):
     for r in range(count):
         refs[-1][r] = refs[r][start:, :]
+
+
+def sum_kernel(*refs, terms):
+    refs[-1][...] = total(refs[:terms]).astype(bf16)
+
+
+def join_kernel(*refs, count):
+    for i in range(count):
+        refs[-1][i] = refs[i][...]
 
 
 def mixed_kernel(*refs, hid):
@@ -619,6 +628,14 @@
     new = adam(*[s[...] for s in vector], grad, 0.2)
     for out, value in zip(vector_out, new):
         out[...] = value
+
+
+def finish_kernel(*refs, table_terms, terms, dp, hid):
+    a, b, c = 4 + table_terms, 16 + terms, hid
+    ins, outs = refs[: a + b + c], refs[a + b + c :]
+    mixed_kernel(*ins[a + b :], outs[0], hid=hid)
+    table_adam_kernel(*ins[:a], *outs[1:5], terms=table_terms)
+    weight_adam_kernel(*ins[a : a + b], *outs[5:], terms=terms, dp=dp, hid=hid)
 
 
 def per_device(
@@ -659,11 +676,11 @@
 
     cot_rows = cotangent.shape[1] + 32
     weight_rows = 3 * piece_rows
-    piece, weight_low, *cot_pieces = call(
+    piece, keep, *cot_pieces = call(
         functools.partial(low_kernel, hid=hid),
         [
             shape((slots + weight_rows, feats), bf16),
-            shape((weight_rows, feats), bf16),
+            shape((slots + weight_rows, feats), bf16),
             *[shape((cot_rows, rows), bf16) for m in range(hid)],
         ],
         (table_w, first_w, second_w, vector_w, cotangent.T),
@@ -676,7 +693,7 @@
             pltpu.VMEM(cotangent.shape[::-1], bf16),
             pltpu.SemaphoreType.DMA((5,)),
         ],
-        vmem=8,
+        vmem=62,
     )
     cots = [cot_pieces[0]] + [swap(cot_pieces[m], "hid", m) for m in range(1, hid)]
     nexts = jnp.concatenate([bag_offsets[1:], jnp.full((1,), ids, jnp.int32)])
@@ -703,11 +720,13 @@
             us=5.0,
         )
 
-    far_pieces = [piece] + [None] * (outer - 1)
-    for step in reversed(range(1, outer)):
-        far_pieces[step] = swap(piece, "dp", step * inner)
-    counts = [count_bags(i) for i in range(chunks // 2)]
-    groups = [far_pieces] + [[swap(p, "dp", near) for p in far_pieces] for near in range(1, inner)]
+    far_pieces = {0: piece}
+    step = outer // 2
+    while step:
+        far_pieces.update({f ^ step: swap(p, "dp", step * inner) for f, p in far_pieces.items()})
+        step //= 2
+    far_pieces = [far_pieces[f] for f in range(outer)]
+    groups = [[keep] + far_pieces[1:]] + [[swap(p, "dp", near) for p in far_pieces] for near in range(1, inner)]
 
     def stack(group, *order):
         return call(
@@ -719,38 +738,25 @@
             us=0.7,
         )
 
-    stacks = {(0, 0): stack(groups[0], *counts)}
-    counts += [count_bags(i, stacks[0, 0]) for i in range(chunks // 2, chunks)]
-    for near in range(1, inner):
-        stacks[0, near] = stack(groups[near])
-    for near in range(inner):
-        for m in range(2, hid, 2):
-            stacks[m, near] = swap(stacks[0, near], "hid", m)
-        for m in range(0, hid, 2):
-            stacks[m + 1, near] = swap(stacks[m, near], "hid", 1)
-    pieces = [groups[r % inner][r // inner] for r in range(dp)]
+    stacks = {(0, near): stack(groups[near]) for near in range(inner)}
     span = HALF * EXPERTS
-    w1p, w1t, w2p, w2t, columns, turn, turn3t = call(
-        functools.partial(weights_kernel, dp=dp, hid=hid),
+    columns, turn, turn3t = call(
+        functools.partial(turns_kernel, hid=hid),
         [
-            shape((EXPERTS, D, H), bf16),
-            shape((EXPERTS, H, D), bf16),
-            shape((EXPERTS, H, O), bf16),
-            shape((EXPERTS, O, H), bf16),
             shape((3, EXPERTS, H, HALF), f32),
             shape((span, span), bf16),
             shape((O * STREAMS, O * STREAMS), bf16),
         ],
-        (*[stacks[m, near] for m in range(hid) for near in range(inner)], *cots),
-        scratch=[
-            pltpu.VMEM((hid, D, piece_cols), bf16),
-            pltpu.VMEM((dp, H, (O * EXPERTS) // dp), bf16),
-            pltpu.VMEM((hid, 16, piece_cols), bf16),
-        ],
-        vmem=32,
-        us=8.0,
-    )
-
+        tuple(cots),
+        scratch=[pltpu.VMEM((hid, 16, piece_cols), bf16)],
+        vmem=12,
+        us=2.0,
+    )
+    early = chunks // 2
+    counts = [count_bags(i) for i in range(early)]
+    counts += [count_bags(i, far_pieces[outer // 2], turn3t) for i in range(early, chunks - 1)]
+    counts.append(count_bags(chunks - 1, stacks[0, 0]))
+    pieces = [groups[r % inner][r // inner] for r in range(dp)]
     pooled = call(
         functools.partial(pool_kernel, chunks=chunks, dp=dp, hid=hid),
         [shape((feats, rows), bf16) for m in range(hid)],
@@ -766,23 +772,51 @@
         us=4.0,
     )
     xts = [pooled[0]] + [swap(pooled[m], "hid", m) for m in range(1, hid)]
+    for near in range(inner):
+        for m in range(2, hid, 2):
+            stacks[m, near] = swap(stacks[0, near], "hid", m)
+    joined = {}
+    for m in range(0, hid, 2):
+        joined[m] = call(
+            functools.partial(join_kernel, count=inner),
+            shape((inner, outer, weight_rows, feats), bf16),
+            (*[stacks[m, near] for near in range(inner)], xts[1]),
+            in_specs=[VMEM] * inner + [ANY],
+            vmem=8,
+            us=0.7,
+        )
+        joined[m + 1] = swap(joined[m], "hid", 1)
+    w1p, w2p = call(
+        functools.partial(weights_kernel, dp=dp, hid=hid),
+        [shape((EXPERTS, D, H), bf16), shape((EXPERTS, H, O), bf16)],
+        (*[joined[m] for m in range(hid)], turn),
+        scratch=[
+            pltpu.VMEM((hid, D, piece_cols), bf16),
+            pltpu.VMEM((dp, H, (O * EXPERTS) // dp), bf16),
+        ],
+        vmem=20,
+        us=3.0,
+    )
 
     gates = 16
     gate_pad = jnp.pad(gate_w.T, ((0, gates - gate_w.shape[1]), (0, 0)))
     small_rows = small_plan(hid)[-1]
-    mixed_part, small, xt, hidden, d_inner, d_pre, *d_pieces = call(
-        functools.partial(main_kernel, hid=hid),
+    some = dp * piece_rows
+    mixed_part, small, home, away, *d_pieces = call(
+        functools.partial(main_kernel, dp=dp, hid=hid),
         [
             shape((rows, O * STREAMS), bf16),
             shape((small_rows, piece_cols), bf16),
-            shape((D, rows), bf16),
-            shape((EXPERTS, H, rows), bf16),
-            shape((EXPERTS, O, rows), bf16),
-            shape((EXPERTS, H, rows), bf16),
+            shape((hid // 2 * some, piece_cols), bf16),
+            shape((hid // 2 * some + small_rows, piece_cols), bf16),
             *[shape((feats, rows), bf16) for m in range(hid)],
         ],
-        (*xts, *cots, w1p, w1t, w2p, w2t, columns, turn, turn3t, gate_pad),
+        (*xts, *cots, w1p, w2p, columns, turn, turn3t, gate_pad),
         scratch=[
+            pltpu.VMEM((D, rows), bf16),
+            pltpu.VMEM((EXPERTS, H, rows), bf16),
+            pltpu.VMEM((EXPERTS, O, rows), bf16),
+            pltpu.VMEM((EXPERTS, H, rows), bf16),
             pltpu.VMEM((O * STREAMS, rows), f32),
             pltpu.VMEM((O * STREAMS, rows), bf16),
             pltpu.VMEM((O * STREAMS, rows), f32),
@@ -792,50 +826,45 @@
             pltpu.VMEM((2, H, rows), bf16),
             pltpu.VMEM((D, rows), f32),
             pltpu.VMEM((3, EXPERTS, 8, H), f32),
-        ],
-        vmem=24,
-        us=10.0,
-    )
-    d_pooled = [d_pieces[0]] + [swap(d_pieces[m], "hid", m) for m in range(1, hid)]
-
-    some = dp * piece_rows
-    home, away = call(
-        functools.partial(grads_kernel, dp=dp, hid=hid),
-        [
-            shape((hid // 2 * some, piece_cols), bf16),
-            shape((hid // 2 * some + small_rows, piece_cols), bf16),
-        ],
-        (xt, hidden, d_inner, d_pre, turn, small, d_pooled[1]),
-        in_specs=[VMEM] * 6 + [ANY],
-        scratch=[
             pltpu.VMEM((H * EXPERTS, rows), bf16),
             pltpu.VMEM((D, piece_cols), bf16),
+            pltpu.VMEM((EXPERTS, H, O), bf16),
             pltpu.VMEM((H, O * EXPERTS), f32),
         ],
-        vmem=16,
-        us=3.0,
-    )
-
+        vmem=36,
+        us=10.0,
+    )
+    d_pooled = [d_pieces[0]] + [swap(d_pieces[m], "hid", m) for m in range(1, hid)]
+
+    near_rows = some // inner
     half = call(
-        functools.partial(core_merge_kernel, rows=some),
-        [shape((some + small_rows, piece_cols), bf16)] * (hid // 2),
-        (home, swap(away, "hid", 1), small, d_pooled[hid - 1]),
-        in_specs=[VMEM] * 3 + [ANY],
+        functools.partial(core_merge_kernel, rows=near_rows, inner=inner),
+        [
+            shape((near_rows + small_rows * (near > 0), piece_cols), bf16)
+            for m in range(hid // 2)
+            for near in range(inner)
+        ],
+        (home, swap(away, "hid", 1), small),
         vmem=12,
         us=1.0,
     )
-    *near, mixed_part = call(
-        functools.partial(chip_merge_kernel, terms=hid // 2, rows=some // inner, inner=inner),
-        [shape((some // inner + small_rows, piece_cols), bf16)] * inner
-        + [shape(mixed_part.shape, bf16)],
-        (half[0], *[swap(half[m], "hid", 2 * m) for m in range(1, hid // 2)], mixed_part),
-        vmem=12,
-        us=1.0,
-    )
+    sums = [None] * inner
+    for i in reversed(range(inner)):
+        passing = () if i else (mixed_part,)
+        result = call(
+            functools.partial(chip_merge_kernel, terms=hid // 2),
+            [shape(v.shape, bf16) for v in (half[i], *passing)],
+            (half[i], *[swap(half[m * inner + i], "hid", 2 * m) for m in range(1, hid // 2)])
+            + passing,
+            vmem=12,
+            us=0.7,
+        )
+        sums[i] = result[0]
+    mixed_part = result[1]
     far_parts = call(
         functools.partial(near_merge_kernel, terms=inner, rows=piece_rows, outer=outer),
         [shape((piece_rows + small_rows, piece_cols), bf16)] * outer,
-        (near[0], *[swap(near[m], "dp", m) for m in range(1, inner)]),
+        (sums[0], sums[1], *[swap(sums[i], "dp", i) for i in range(1, inner)]),
         vmem=12,
         us=1.0,
     )
@@ -846,19 +875,11 @@
         mixed_parts[m] = swap(mixed_part, "hid", m)
     for m in range(0, hid, 2):
         mixed_parts[m + 1] = swap(mixed_parts[m], "hid", 1)
-    mixed = call(
-        functools.partial(mixed_kernel, hid=hid),
-        shape((events, O * STREAMS), bf16),
-        tuple(mixed_parts[m] for m in range(hid)),
-        vmem=8,
-        us=2.0,
-    )
-
     d_table = call(
         functools.partial(table_kernel, chunks=chunks, dp=dp, hid=hid),
         [shape((slots, feats), bf16) for r in range(dp)],
-        (block_owners, *counts, *d_pooled),
-        in_specs=[SMEM] + [VMEM] * (chunks + hid),
+        (block_owners, *counts, *d_pooled, half[0]),
+        in_specs=[SMEM] + [VMEM] * (chunks + hid) + [ANY],
         scratch=[
             pltpu.VMEM((feats, events), bf16),
             pltpu.VMEM((vocab, feats), bf16),
@@ -868,49 +889,59 @@
         vmem=20 if vocab <= 4096 else 58,
         us=6.0,
     )
-    table_terms = []
+    order = sums[1]
+    sums = {}
     for far in reversed(range(outer)):
-        value = d_table[far * inner]
-        for m in range(1, inner):
-            value = plus(value, swap(d_table[far * inner + m], "dp", m))
-        table_terms.append(swap(value, "dp", far * inner) if far else value)
-
-    table_new = call(
-        functools.partial(table_adam_kernel, terms=outer),
-        [shape(table_w.shape, f32)] * 4,
-        (table_w, table_m, table_v, table_ema, *table_terms),
-        vmem=8,
-    )
-    weights_new = call(
-        functools.partial(weight_adam_kernel, terms=outer, dp=dp, hid=hid),
-        [shape(first_w.shape, f32)] * 4
-        + [shape(second_w.shape, f32)] * 4
-        + [shape(vector_w.shape, f32)] * 4
-        + [shape((GATES, D), f32)] * 4,
-        (
-            first_w,
-            first_m,
-            first_v,
-            first_ema,
-            second_w,
-            second_m,
-            second_v,
-            second_ema,
-            vector_w,
-            vector_m,
-            vector_v,
-            vector_ema,
-            *[g.T for g in (gate_w, gate_m, gate_v, gate_ema)],
-            *weight_terms,
+        terms = [d_table[far * inner]]
+        terms += [swap(d_table[far * inner + m], "dp", m) for m in range(1, inner)]
+        if far == outer - 1:
+            sums[far] = call(
+                functools.partial(sum_kernel, terms=inner),
+                shape((slots, feats), bf16),
+                (*terms, order),
+                in_specs=[VMEM] * inner + [ANY],
+                vmem=4,
+                us=0.5,
+            )
+        else:
+            sums[far] = functools.reduce(plus, terms)
+    step = 1
+    while step < outer // 2:
+        for far in reversed([f for f in sums if f & step]):
+            sums[far ^ step] = plus(sums[far ^ step], swap(sums.pop(far), "dp", step * inner))
+        step *= 2
+    table_terms = [sums[0], swap(sums[step], "dp", step * inner)]
+
+    states = (
+        table_w,
+        table_m,
+        table_v,
+        table_ema,
+        first_w,
+        first_m,
+        first_v,
+        first_ema,
+        second_w,
+        second_m,
+        second_v,
+        second_ema,
+        vector_w,
+        vector_m,
+        vector_v,
+        vector_ema,
+        *[g.T for g in (gate_w, gate_m, gate_v, gate_ema)],
+    )
+    mixed, *new = call(
+        functools.partial(
+            finish_kernel, table_terms=len(table_terms), terms=outer, dp=dp, hid=hid
         ),
-        vmem=8,
-    )
-    return (
-        mixed,
-        *table_new,
-        *weights_new[0:12],
-        *[g.T for g in weights_new[12:16]],
-    )
+        [shape((events, O * STREAMS), bf16)] + [shape(v.shape, f32) for v in states],
+        (*states[:4], *table_terms, *states[4:], *weight_terms)
+        + tuple(mixed_parts[m] for m in range(hid)),
+        vmem=20,
+        us=3.0,
+    )
+    return (mixed, *new[:16], *[g.T for g in new[16:]])
 
 
 def solution(mesh):

time: 136 us -> 123 us (0.904)
  waiting for transfers between devices: 45.3 us -> 40.5 us
  local copies, waits for them, and re-layouts: 4.61 us -> 0.23 us
  Pallas kernels: 47.6 us -> 45.6 us
  starting transfers between devices: 36.9 us -> 35 us
    ppermute x38 -> x37, waiting for transfers between devices: 45.3 us -> 40.5 us  [swap(): return lax.ppermute(value, axis, [(i, i ^ mask) for i in range(count)])]
    unnamed x56 -> x52, local copies, waits for them, and re-layouts: 4.53 us -> 0.15 us
    ppermute x38 -> x37, starting transfers between devices: 36.9 us -> 35 us  [swap(): return lax.ppermute(value, axis, [(i, i ^ mask) for i in range(count)])]
    pallas_call x18 -> x20, Pallas kernels: 47.6 us -> 45.6 us  [call(): pl.pallas_call(kernel, out_shape=outs, in_specs=in_specs or [VMEM] * len(...]
  transfers between devices with their start and end apart: 38 -> 37, of which waited for: 15 -> 17; matrix products, arithmetic and copies ran while one was open for 0% -> 0% of each run, Pallas kernels for 26% -> 25%
where the time goes in v4:
time: 123 us
  Pallas kernels  45.6 us (37%)
  waiting for transfers between devices  40.5 us (33%)
  starting transfers between devices  35 us (28%)
  between operations  1.42 us (1%)
    pallas_call x20, Pallas kernels, call(): pl.pallas_call(kernel, out_shape=outs, in_specs=in_specs or [VMEM] * len(...  45.6 us
    ppermute x37, waiting for transfers between devices, swap(): return lax.ppermute(value, axis, [(i, i ^ mask) for i in range(count)])  40.5 us
    ppermute x37, starting transfers between devices, swap(): return lax.ppermute(value, axis, [(i, i ^ mask) for i in range(count)])  35 us
  transfers between devices with their start and end apart: 37, of which 17 were waited for; matrix products, arithmetic and copies ran while one was open for 0% of the time, Pallas kernels for 25%

profile of v4, /device:TPU:0, one launch (start us, length us, event | category | flops | bytes accessed | tf_op | source)
XLA Modules:
  0.0 123.0 jit_solution(4453376966589969485)
XLA Ops:
  0.7 2.2 %shard_map.393 = (bf16[1056,128]{1,0:T(8,128)(2,1)}, bf16[1056,128]{1,0:T(8,128)(2,1)}, bf16[224,256]{1,0:T(8,128)(2,1)}, bf16[224,256]{1,0:T(8,128)(2,1)}, bf16...) custom-call(f32[768,128]{1,0:T(8,128)} %refs_0_.1, f32[64,384]{1,0:T(8,128)} %refs_6_.1, f32[64,192]{1,0:T(8,128)} %refs_10_.1, ...), custom_call_target="tpu_custom_call" | custom-call | flops 2000000000 | bytes 6000000 | tf_op jit(solution)/shard_map/pallas_call | solution.py:60
  2.9 3.1 %collective-permute-start.4 = (bf16[1056,128]{1,0:T(8,128)(2,1)}, bf16[1056,128]{1,0:T(8,128)(2,1)S(1)}, u32[]{:S(2)}, u32[]{:S(2)}) collective-permute-start(bf16[1056,128]{1,0:T(8,128)(2,1)} %get-tuple-element.83), channel_id=1, source_target_pairs={{0,8},{4,12},{8,0},{12,4},{16,24},{20,28},{24,16},{28,20},{1,9},{5... | collective-permute-start | bytes 811016 | tf_op jit(solution)/shard_map/ppermute | solution.py:76
  6.0 2.6 %collective-permute-start = (bf16[1056,128]{1,0:T(8,128)(2,1)}, bf16[1056,128]{1,0:T(8,128)(2,1)S(1)}, u32[]{:S(2)}, u32[]{:S(2)}) collective-permute-start(bf16[1056,128]{1,0:T(8,128)(2,1)} %get-tuple-element.83), channel_id=1, source_target_pairs={{0,16},{4,20},{8,24},{12,28},{16,0},{20,4},{24,8},{28,12},{1,17},{... | collective-permute-start | bytes 811016 | tf_op jit(solution)/shard_map/ppermute | solution.py:76
  8.6 1.5 %collective-permute-start.2 = (bf16[224,256]{1,0:T(8,128)(2,1)}, bf16[224,256]{1,0:T(8,128)(2,1)S(1)}, u32[]{:S(2)}, u32[]{:S(2)}) collective-permute-start(bf16[224,256]{1,0:T(8,128)(2,1)} %get-tuple-element.86), channel_id=1, source_target_pairs={{0,2},{1,3},{2,0},{3,1},{4,6},{5,7},{6,4},{7,5},{8,10},{9,11},{10,... | collective-permute-start | bytes 344072 | tf_op jit(solution)/shard_map/ppermute | solution.py:76
  10.1 0.3 collective-permute-start.3
  10.6 4.4 %shard_map.392.refs_1_ = bf16[256,3072]{1,0:T(8,128)(2,1)S(1)} custom-call(s32[1024]{0:T(1024)S(1)} %copy-done.1, s32[32,128]{1,0:T(8,128)S(1)} %bitcast.22, s32[8,128]{1,0:T(8,128)S(1)} %bitcast.15, s32[8,128]{1,0:T(8,128)S(1)} %add_bitcast_fusion.nxt_ref), custom_call_target="tpu_custom_call" | custom-call | flops 5000000000 | bytes 15000000 | tf_op jit(solution)/shard_map/pallas_call | solution.py:60
  15.0 5.1 %shard_map.391.refs_0_ = bf16[256,3072]{1,0:T(8,128)(2,1)S(1)} custom-call(s32[1024]{0:T(1024)S(1)} %copy-done.1, s32[32,128]{1,0:T(8,128)S(1)} %bitcast.23, s32[8,128]{1,0:T(8,128)S(1)} %bitcast.16, s32[8,128]{1,0:T(8,128)S(1)} %add_bitcast_fusion.nxt_ref), custom_call_target="tpu_custom_call" | custom-call | flops 5000000000 | bytes 15000000 | tf_op jit(solution)/shard_map/pallas_call | solution.py:60
  20.1 2.2 %collective-permute-start.6 = (bf16[1056,128]{1,0:T(8,128)(2,1)S(1)}, bf16[1056,128]{1,0:T(8,128)(2,1)S(1)}, u32[]{:S(2)}, u32[]{:S(2)}) collective-permute-start(bf16[1056,128]{1,0:T(8,128)(2,1)S(1)} %copy-done.25), channel_id=1, source_target_pairs={{0,4},{4,0},{8,12},{12,8},{16,20},{20,16},{24,28},{28,24},{1,5},{5... | collective-permute-start | bytes 811016 | tf_op jit(solution)/shard_map/ppermute | solution.py:76
  22.3 2.3 %shard_map.394 = (f32[3,6,256,128]{3,2,1,0:T(8,128)S(1)}, bf16[768,768]{1,0:T(8,128)(2,1)S(1)}, bf16[768,768]{1,0:T(8,128)(2,1)S(1)}) custom-call(bf16[224,256]{1,0:T(8,128)(2,1)S(1)} %copy-done.24, bf16[224,256]{1,0:T(8,128)(2,1)S(1)} %collective-permute-done.1.refs_1_.refs_5_, bf16[224,256]{1,0:T(8,128)(2,1)S(1)} %collective-permute-done.2.refs_2_.refs_6_, ...), custom_call_target="tpu_custom_call" | custom-call | flops 2000000000 | bytes 6000000 | tf_op jit(solution)/shard_map/pallas_call | solution.py:60
  25.1 1.7 %collective-permute-start.7 = (bf16[1056,128]{1,0:T(8,128)(2,1)S(1)}, bf16[1056,128]{1,0:T(8,128)(2,1)S(1)}, u32[]{:S(2)}, u32[]{:S(2)}) collective-permute-start(bf16[1056,128]{1,0:T(8,128)(2,1)S(1)} %collective-permute-done.4.refs_1_.refs_6_), channel_id=1, source_target_pairs={{0,4},{4,0},{8,12},{12,8},{16,20},{20,16},{24,28},{28,24},{1,5},{5... | collective-permute-start | bytes 811016 | tf_op jit(solution)/shard_map/ppermute | solution.py:76
  26.8 5.1 %shard_map.395.refs_2_ = bf16[256,3072]{1,0:T(8,128)(2,1)S(1)} custom-call(s32[1024]{0:T(1024)S(1)} %copy-done.1, s32[32,128]{1,0:T(8,128)S(1)} %bitcast.24, s32[8,128]{1,0:T(8,128)S(1)} %bitcast.17, s32[8,128]{1,0:T(8,128)S(1)} %add_bitcast_fusion.nxt_ref, bf16[1056,128]{1,0:T(8,128)(2,1)S(1)} %collective-permute-done.refs_0_.refs_2_.refs_8_, ...), custom_call_target="tpu_custom_call" | custom-call | flops 5000000000 | bytes 15000000 | tf_op jit(solution)/shard_map/pallas_call | solution.py:60
  31.9 1.3 %collective-permute-done.5.refs_3_.refs_10_ = bf16[1056,128]{1,0:T(8,128)(2,1)S(1)} collective-permute-done((bf16[1056,128]{1,0:T(8,128)(2,1)S(1)}, bf16[1056,128]{1,0:T(8,128)(2,1)S(1)}, u32[]{:S(2)}, u32[]{:S(2)}) %collective-permute-start.5) | collective-permute-done | bytes 270368 | tf_op jit(solution)/shard_map/ppermute | solution.py:76
  33.2 1.6 %collective-permute-start.14 = (bf16[4,288,128]{2,1,0:T(8,128)(2,1)S(1)}, bf16[4,288,128]{2,1,0:T(8,128)(2,1)S(1)}, u32[]{:S(2)}, u32[]{:S(2)}) collective-permute-start(bf16[4,288,128]{2,1,0:T(8,128)(2,1)S(1)} %shard_map.396.refs_0_), channel_id=1, source_target_pairs={{0,2},{1,3},{2,0},{3,1},{4,6},{5,7},{6,4},{7,5},{8,10},{9,11},{10,... | collective-permute-start | bytes 884744 | tf_op jit(solution)/shard_map/ppermute | solution.py:76
  34.8 1.7 %collective-permute-start.9 = (bf16[1056,128]{1,0:T(8,128)(2,1)S(1)}, bf16[1056,128]{1,0:T(8,128)(2,1)S(1)}, u32[]{:S(2)}, u32[]{:S(2)}) collective-permute-start(bf16[1056,128]{1,0:T(8,128)(2,1)S(1)} %collective-permute-done.5.refs_3_.refs_10_), channel_id=1, source_target_pairs={{0,4},{4,0},{8,12},{12,8},{16,20},{20,16},{24,28},{28,24},{1,5},{5... | collective-permute-start | bytes 811016 | tf_op jit(solution)/shard_map/ppermute | solution.py:76
  36.5 5.1 %shard_map.397.refs_3_ = bf16[256,3072]{1,0:T(8,128)(2,1)S(1)} custom-call(s32[1024]{0:T(1024)S(1)} %copy-done.1, s32[32,128]{1,0:T(8,128)S(1)} %bitcast.25, s32[8,128]{1,0:T(8,128)S(1)} %bitcast.18, s32[8,128]{1,0:T(8,128)S(1)} %add_bitcast_fusion.nxt_ref, bf16[4,288,128]{2,1,0:T(8,128)(2,1)S(1)} %shard_map.396.refs_0_), custom_call_target="tpu_custom_call" | custom-call | flops 5000000000 | bytes 15000000 | tf_op jit(solution)/shard_map/pallas_call | solution.py:60
  41.6 5.0 %collective-permute-done.9.refs_11_.refs_3_ = bf16[1056,128]{1,0:T(8,128)(2,1)S(1)} collective-permute-done((bf16[1056,128]{1,0:T(8,128)(2,1)S(1)}, bf16[1056,128]{1,0:T(8,128)(2,1)S(1)}, u32[]{:S(2)}, u32[]{:S(2)}) %collective-permute-start.9) | collective-permute-done | bytes 270368 | tf_op jit(solution)/shard_map/ppermute | solution.py:76
  46.6 1.6 %collective-permute-start.15 = (bf16[4,288,128]{2,1,0:T(8,128)(2,1)S(1)}, bf16[4,288,128]{2,1,0:T(8,128)(2,1)S(1)}, u32[]{:S(2)}, u32[]{:S(2)}) collective-permute-start(bf16[4,288,128]{2,1,0:T(8,128)(2,1)S(1)} %shard_map.399.refs_1_), channel_id=1, source_target_pairs={{0,2},{1,3},{2,0},{3,1},{4,6},{5,7},{6,4},{7,5},{8,10},{9,11},{10,... | collective-permute-start | bytes 884744 | tf_op jit(solution)/shard_map/ppermute | solution.py:76
  48.2 3.3 %shard_map.398 = (bf16[128,256]{1,0:T(8,128)(2,1)S(1)}, bf16[128,256]{1,0:T(8,128)(2,1)S(1)}, bf16[128,256]{1,0:T(8,128)(2,1)S(1)}, bf16[128,256]{1,0:T(8,128)(2,1)S(1)}) custom-call(s32[48]{0:T(128)S(1)} %copy-done.22, bf16[256,3072]{1,0:T(8,128)(2,1)S(1)} %shard_map.391.refs_0_, bf16[256,3072]{1,0:T(8,128)(2,1)S(1)} %shard_map.392.refs_1_, ...), custom_call_target="tpu_custom_call" | custom-call | flops 4000000000 | bytes 12000000 | tf_op jit(solution)/shard_map/pallas_call | solution.py:60
  51.6 1.2 %collective-permute-done.10.refs_2_.refs_1_ = bf16[128,256]{1,0:T(8,128)(2,1)S(1)} collective-permute-done((bf16[128,256]{1,0:T(8,128)(2,1)S(1)}, bf16[128,256]{1,0:T(8,128)(2,1)S(1)}, u32[]{:S(2)}, u32[]{:S(2)}) %collective-permute-start.10) | collective-permute-done | bytes 65568 | tf_op jit(solution)/shard_map/ppermute | solution.py:76
  53.1 2.2 %collective-permute-done.15.refs_1_ = bf16[4,288,128]{2,1,0:T(8,128)(2,1)S(1)} collective-permute-done((bf16[4,288,128]{2,1,0:T(8,128)(2,1)S(1)}, bf16[4,288,128]{2,1,0:T(8,128)(2,1)S(1)}, u32[]{:S(2)}, u32[]{:S(2)}) %collective-permute-start.15) | collective-permute-done | bytes 294944 | tf_op jit(solution)/shard_map/ppermute | solution.py:76
  55.5 1.6 %collective-permute-start.11 = (bf16[128,256]{1,0:T(8,128)(2,1)S(1)}, bf16[128,256]{1,0:T(8,128)(2,1)S(1)}, u32[]{:S(2)}, u32[]{:S(2)}) collective-permute-start(bf16[128,256]{1,0:T(8,128)(2,1)S(1)} %get-tuple-element.92), channel_id=1, source_target_pairs={{0,2},{1,3},{2,0},{3,1},{4,6},{5,7},{6,4},{7,5},{8,10},{9,11},{10,... | collective-permute-start | bytes 196616 | tf_op jit(solution)/shard_map/ppermute | solution.py:76
  57.5 2.9 %shard_map.402 = (bf16[6,512,256]{2,1,0:T(8,128)(2,1)S(1)}, bf16[6,256,256]{2,1,0:T(8,128)(2,1)S(1)}) custom-call(bf16[2,4,288,128]{3,2,1,0:T(8,128)(2,1)S(1)} %shard_map.400.refs_0_, bf16[2,4,288,128]{3,2,1,0:T(8,128)(2,1)S(1)} %collective-permute-done.13.refs_1_, bf16[2,4,288,128]{3,2,1,0:T(8,128)(2,1)S(1)} %shard_map.401.refs_2_, ...), custom_call_target="tpu_custom_call" | custom-call | flops 3000000000 | bytes 9000000 | tf_op jit(solution)/shard_map/pallas_call | solution.py:60
  60.4 0.8 collective-permute-done.12.refs_3_
  61.2 9.7 %shard_map.403 = (bf16[256,768]{1,0:T(8,128)(2,1)S(1)}, bf16[32,384]{1,0:T(8,128)(2,1)S(1)}, bf16[1536,384]{1,0:T(8,128)(2,1)S(1)}, bf16[1568,384]{1,0:T(8,128)(...) custom-call(bf16[128,256]{1,0:T(8,128)(2,1)S(1)} %get-tuple-element., ...), custom_call_target="tpu_custom_call" | custom-call | flops 10000000000 | bytes 30000000 | tf_op jit(solution)/shard_map/pallas_call | solution.py:60
  71.1 0.4 collective-permute-start.17
  71.5 1.4 %collective-permute-start.18 = (bf16[128,256]{1,0:T(8,128)(2,1)S(1)}, bf16[128,256]{1,0:T(8,128)(2,1)S(1)}, u32[]{:S(2)}, u32[]{:S(2)}) collective-permute-start(bf16[128,256]{1,0:T(8,128)(2,1)S(1)} %get-tuple-element.100), channel_id=1, source_target_pairs={{0,2},{1,3},{2,0},{3,1},{4,6},{5,7},{6,4},{7,5},{8,10},{9,11},{10,... | collective-permute-start | bytes 196616 | tf_op jit(solution)/shard_map/ppermute | solution.py:76
  73.0 0.9 collective-permute-done.20.come
  74.2 1.4 %collective-permute-start.29 = (bf16[384,384]{1,0:T(8,128)(2,1)S(1)}, bf16[384,384]{1,0:T(8,128)(2,1)S(1)}, u32[]{:S(2)}, u32[]{:S(2)}) collective-permute-start(bf16[384,384]{1,0:T(8,128)(2,1)S(1)} %get-tuple-element.116), channel_id=1, source_target_pairs={{0,2},{1,3},{2,0},{3,1},{4,6},{5,7},{6,4},{7,5},{8,10},{9,11},{10,... | collective-permute-start | bytes 884744 | tf_op jit(solution)/shard_map/ppermute | solution.py:76
  75.6 0.6 collective-permute-start.26
  76.3 0.8 collective-permute-done.19.refs_7_
  77.1 2.4 %shard_map.405 = (bf16[768,128]{1,0:T(8,128)(2,1)S(1)}, bf16[768,128]{1,0:T(8,128)(2,1)S(1)}, bf16[768,128]{1,0:T(8,128)(2,1)S(1)}, bf16[768,128]{1,0:T(8,128)(2...) custom-call(s32[48]{0:T(128)S(1)} %copy-done.22, ...), custom_call_target="tpu_custom_call" | custom-call | flops 6000000000 | bytes 18000000 | tf_op jit(solution)/shard_map/pallas_call | solution.py:60
  79.5 1.5 %collective-permute-start.25 = (bf16[768,128]{1,0:T(8,128)(2,1)S(1)}, bf16[768,128]{1,0:T(8,128)(2,1)S(1)}, u32[]{:S(2)}, u32[]{:S(2)}) collective-permute-start(bf16[768,128]{1,0:T(8,128)(2,1)S(1)} %get-tuple-element.113), channel_id=1, source_target_pairs={{0,4},{4,0},{8,12},{12,8},{16,20},{20,16},{24,28},{28,24},{1,5},{5... | collective-permute-start | bytes 589832 | tf_op jit(solution)/shard_map/ppermute | solution.py:76
  81.0 0.6 collective-permute-start.22
  81.6 2.6 %collective-permute-done.29.refs_1_ = bf16[384,384]{1,0:T(8,128)(2,1)S(1)} collective-permute-done((bf16[384,384]{1,0:T(8,128)(2,1)S(1)}, bf16[384,384]{1,0:T(8,128)(2,1)S(1)}, u32[]{:S(2)}, u32[]{:S(2)}) %collective-permute-start.29) | collective-permute-done | bytes 294944 | tf_op jit(solution)/shard_map/ppermute | solution.py:76
  84.3 1.3 %collective-permute-start.35 = (bf16[256,768]{1,0:T(8,128)(2,1)S(1)}, bf16[256,768]{1,0:T(8,128)(2,1)S(1)}, u32[]{:S(2)}, u32[]{:S(2)}) collective-permute-start(bf16[256,768]{1,0:T(8,128)(2,1)S(1)} %get-tuple-element.123.refs_26_), channel_id=1, source_target_pairs={{0,2},{1,3},{2,0},{3,1},{4,6},{5,7},{6,4},{7,5},{8,10},{9,11},{10,... | collective-permute-start | bytes 1179656 | tf_op jit(solution)/shard_map/ppermute | solution.py:76
  85.6 1.4 %collective-permute-start.24 = (bf16[768,128]{1,0:T(8,128)(2,1)S(1)}, bf16[768,128]{1,0:T(8,128)(2,1)S(1)}, u32[]{:S(2)}, u32[]{:S(2)}) collective-permute-start(bf16[768,128]{1,0:T(8,128)(2,1)S(1)} %get-tuple-element.111), channel_id=1, source_target_pairs={{0,4},{4,0},{8,12},{12,8},{16,20},{20,16},{24,28},{28,24},{1,5},{5... | collective-permute-start | bytes 589832 | tf_op jit(solution)/shard_map/ppermute | solution.py:76
  87.1 4.0 %collective-permute-done.26.refs_1_ = bf16[416,384]{1,0:T(8,128)(2,1)S(1)} collective-permute-done((bf16[416,384]{1,0:T(8,128)(2,1)S(1)}, bf16[416,384]{1,0:T(8,128)(2,1)S(1)}, u32[]{:S(2)}, u32[]{:S(2)}) %collective-permute-start.26) | collective-permute-done | bytes 319520 | tf_op jit(solution)/shard_map/ppermute | solution.py:76
  91.1 1.5 %collective-permute-start.30 = (bf16[416,384]{1,0:T(8,128)(2,1)S(1)}, bf16[416,384]{1,0:T(8,128)(2,1)S(1)}, u32[]{:S(2)}, u32[]{:S(2)}) collective-permute-start(bf16[416,384]{1,0:T(8,128)(2,1)S(1)} %shard_map.406.refs_2_.other), channel_id=1, source_target_pairs={{0,4},{4,0},{8,12},{12,8},{16,20},{20,16},{24,28},{28,24},{1,5},{5... | collective-permute-start | bytes 958472 | tf_op jit(solution)/shard_map/ppermute | solution.py:76
  92.8 2.8 %collective-permute-done.24 = bf16[768,128]{1,0:T(8,128)(2,1)S(1)} collective-permute-done((bf16[768,128]{1,0:T(8,128)(2,1)S(1)}, bf16[768,128]{1,0:T(8,128)(2,1)S(1)}, u32[]{:S(2)}, u32[]{:S(2)}) %collective-permute-start.24) | collective-permute-done | bytes 196640 | tf_op jit(solution)/shard_map/ppermute | solution.py:76
  95.6 1.4 %collective-permute-start.21 = (bf16[768,128]{1,0:T(8,128)(2,1)S(1)}, bf16[768,128]{1,0:T(8,128)(2,1)S(1)}, u32[]{:S(2)}, u32[]{:S(2)}) collective-permute-start(bf16[768,128]{1,0:T(8,128)(2,1)S(1)} %get-tuple-element.107), channel_id=1, source_target_pairs={{0,4},{4,0},{8,12},{12,8},{16,20},{20,16},{24,28},{28,24},{1,5},{5... | collective-permute-start | bytes 589832 | tf_op jit(solution)/shard_map/ppermute | solution.py:76
  97.0 2.8 %collective-permute-done.27 = bf16[768,128]{1,0:T(8,128)(2,1)S(1)} collective-permute-done((bf16[768,128]{1,0:T(8,128)(2,1)S(1)}, bf16[768,128]{1,0:T(8,128)(2,1)S(1)}, u32[]{:S(2)}, u32[]{:S(2)}) %collective-permute-start.27) | collective-permute-done | bytes 196640 | tf_op jit(solution)/shard_map/ppermute | solution.py:76
  100.2 2.3 %collective-permute-done.30.refs_0_ = bf16[416,384]{1,0:T(8,128)(2,1)S(1)} collective-permute-done((bf16[416,384]{1,0:T(8,128)(2,1)S(1)}, bf16[416,384]{1,0:T(8,128)(2,1)S(1)}, u32[]{:S(2)}, u32[]{:S(2)}) %collective-permute-start.30) | collective-permute-done | bytes 319520 | tf_op jit(solution)/shard_map/ppermute | solution.py:76
  102.8 3.3 %collective-permute-done.21 = bf16[768,128]{1,0:T(8,128)(2,1)S(1)} collective-permute-done((bf16[768,128]{1,0:T(8,128)(2,1)S(1)}, bf16[768,128]{1,0:T(8,128)(2,1)S(1)}, u32[]{:S(2)}, u32[]{:S(2)}) %collective-permute-start.21) | collective-permute-done | bytes 196640 | tf_op jit(solution)/shard_map/ppermute | solution.py:76
  106.1 0.6 collective-permute-done.23
  106.8 3.7 %collective-permute-start.33 = (bf16[128,384]{1,0:T(8,128)(2,1)S(1)}, bf16[128,384]{1,0:T(8,128)(2,1)S(1)}, u32[]{:S(2)}, u32[]{:S(2)}) collective-permute-start(bf16[128,384]{1,0:T(8,128)(2,1)S(1)} %get-tuple-element.122), channel_id=1, source_target_pairs={{0,24},{4,28},{8,16},{12,20},{16,8},{20,12},{24,0},{28,4},{1,25},{... | collective-permute-start | bytes 294920 | tf_op jit(solution)/shard_map/ppermute | solution.py:76
  110.6 7.7 %collective-permute-done.28.refs_5_ = bf16[768,128]{1,0:T(8,128)(2,1)S(1)} collective-permute-done((bf16[768,128]{1,0:T(8,128)(2,1)S(1)}, bf16[768,128]{1,0:T(8,128)(2,1)S(1)}, u32[]{:S(2)}, u32[]{:S(2)}) %collective-permute-start.28) | collective-permute-done | bytes 196640 | tf_op jit(solution)/shard_map/ppermute | solution.py:76
  118.2 2.1 %collective-permute-done.32.refs_24_ = bf16[128,384]{1,0:T(8,128)(2,1)S(1)} collective-permute-done((bf16[128,384]{1,0:T(8,128)(2,1)S(1)}, bf16[128,384]{1,0:T(8,128)(2,1)S(1)}, u32[]{:S(2)}, u32[]{:S(2)}) %collective-permute-start.32) | collective-permute-done | bytes 98336 | tf_op jit(solution)/shard_map/ppermute | solution.py:76
  120.5 2.4 %shard_map.410 = (bf16[1024,768]{1,0:T(8,128)(2,1)}, f32[768,128]{1,0:T(8,128)}, f32[768,128]{1,0:T(8,128)}, f32[768,128]{1,0:T(8,128)}, f32[768,128]{1,0:T(8,12...) custom-call(f32[768,128]{1,0:T(8,128)S(1)} %copy-done.2, ...), custom_call_target="tpu_custom_call" | custom-call | flops 3000000000 | bytes 9000000 | tf_op jit(solution)/shard_map/pallas_call | solution.py:60
  (104 shorter events, 3.1 us)
Async XLA Ops:
  2.9 22.2 %collective-permute-start.4 = (bf16[1056,128]{1,0:T(8,128)(2,1)}, bf16[1056,128]{1,0:T(8,128)(2,1)S(1)}, u32[]{:S(2)}, u32[]{:S(2)}) collective-permute-start(bf16[1056,128]{1,0:T(8,128)(2,1)} %get-tuple-element.83), channel_id=1, source_target_pairs={{0,8},{4,12},{8,0},{12,4},{16,24},{20,28},{24,16},{28,20},{1,9},{5... | collective-permute-start | bytes 811016 | tf_op jit(solution)/shard_map/ppermute | solution.py:76
  6.0 18.7 %collective-permute-start = (bf16[1056,128]{1,0:T(8,128)(2,1)}, bf16[1056,128]{1,0:T(8,128)(2,1)S(1)}, u32[]{:S(2)}, u32[]{:S(2)}) collective-permute-start(bf16[1056,128]{1,0:T(8,128)(2,1)} %get-tuple-element.83), channel_id=1, source_target_pairs={{0,16},{4,20},{8,24},{12,28},{16,0},{20,4},{24,8},{28,12},{1,17},{... | collective-permute-start | bytes 811016 | tf_op jit(solution)/shard_map/ppermute | solution.py:76
  8.6 11.5 %collective-permute-start.1 = (bf16[224,256]{1,0:T(8,128)(2,1)}, bf16[224,256]{1,0:T(8,128)(2,1)S(1)}, u32[]{:S(2)}, u32[]{:S(2)}) collective-permute-start(bf16[224,256]{1,0:T(8,128)(2,1)} %get-tuple-element.85), channel_id=1, source_target_pairs={{0,1},{1,0},{2,3},{3,2},{4,5},{5,4},{6,7},{7,6},{8,9},{9,8},{10,11... | collective-permute-start | bytes 344072 | tf_op jit(solution)/shard_map/ppermute | solution.py:76
  8.6 13.8 %collective-permute-start.2 = (bf16[224,256]{1,0:T(8,128)(2,1)}, bf16[224,256]{1,0:T(8,128)(2,1)S(1)}, u32[]{:S(2)}, u32[]{:S(2)}) collective-permute-start(bf16[224,256]{1,0:T(8,128)(2,1)} %get-tuple-element.86), channel_id=1, source_target_pairs={{0,2},{1,3},{2,0},{3,1},{4,6},{5,7},{6,4},{7,5},{8,10},{9,11},{10,... | collective-permute-start | bytes 344072 | tf_op jit(solution)/shard_map/ppermute | solution.py:76
  10.1 12.3 %collective-permute-start.3 = (bf16[224,256]{1,0:T(8,128)(2,1)}, bf16[224,256]{1,0:T(8,128)(2,1)S(1)}, u32[]{:S(2)}, u32[]{:S(2)}) collective-permute-start(bf16[224,256]{1,0:T(8,128)(2,1)} %get-tuple-element.87), channel_id=1, source_target_pairs={{0,3},{1,2},{2,1},{3,0},{4,7},{5,6},{6,5},{7,4},{8,11},{9,10},{10,... | collective-permute-start | bytes 344072 | tf_op jit(solution)/shard_map/ppermute | solution.py:76
  20.1 21.5 %collective-permute-start.6 = (bf16[1056,128]{1,0:T(8,128)(2,1)S(1)}, bf16[1056,128]{1,0:T(8,128)(2,1)S(1)}, u32[]{:S(2)}, u32[]{:S(2)}) collective-permute-start(bf16[1056,128]{1,0:T(8,128)(2,1)S(1)} %copy-done.25), channel_id=1, source_target_pairs={{0,4},{4,0},{8,12},{12,8},{16,20},{20,16},{24,28},{28,24},{1,5},{5... | collective-permute-start | bytes 811016 | tf_op jit(solution)/shard_map/ppermute | solution.py:76
  24.7 16.9 %collective-permute-start.8 = (bf16[1056,128]{1,0:T(8,128)(2,1)S(1)}, bf16[1056,128]{1,0:T(8,128)(2,1)S(1)}, u32[]{:S(2)}, u32[]{:S(2)}) collective-permute-start(bf16[1056,128]{1,0:T(8,128)(2,1)S(1)} %collective-permute-done.refs_0_.refs_2_.refs_8_), channel_id=1, source_target_pairs={{0,4},{4,0},{8,12},{12,8},{16,20},{20,16},{24,28},{28,24},{1,5},{5... | collective-permute-start | bytes 811016 | tf_op jit(solution)/shard_map/ppermute | solution.py:76
  24.8 8.4 %collective-permute-start.5 = (bf16[1056,128]{1,0:T(8,128)(2,1)S(1)}, bf16[1056,128]{1,0:T(8,128)(2,1)S(1)}, u32[]{:S(2)}, u32[]{:S(2)}) collective-permute-start(bf16[1056,128]{1,0:T(8,128)(2,1)S(1)} %collective-permute-done.refs_0_.refs_2_.refs_8_), channel_id=1, source_target_pairs={{0,8},{4,12},{8,0},{12,4},{16,24},{20,28},{24,16},{28,20},{1,9},{5... | collective-permute-start | bytes 811016 | tf_op jit(solution)/shard_map/ppermute | solution.py:76
  25.1 16.5 %collective-permute-start.7 = (bf16[1056,128]{1,0:T(8,128)(2,1)S(1)}, bf16[1056,128]{1,0:T(8,128)(2,1)S(1)}, u32[]{:S(2)}, u32[]{:S(2)}) collective-permute-start(bf16[1056,128]{1,0:T(8,128)(2,1)S(1)} %collective-permute-done.4.refs_1_.refs_6_), channel_id=1, source_target_pairs={{0,4},{4,0},{8,12},{12,8},{16,20},{20,16},{24,28},{28,24},{1,5},{5... | collective-permute-start | bytes 811016 | tf_op jit(solution)/shard_map/ppermute | solution.py:76
  33.2 19.9 %collective-permute-start.14 = (bf16[4,288,128]{2,1,0:T(8,128)(2,1)S(1)}, bf16[4,288,128]{2,1,0:T(8,128)(2,1)S(1)}, u32[]{:S(2)}, u32[]{:S(2)}) collective-permute-start(bf16[4,288,128]{2,1,0:T(8,128)(2,1)S(1)} %shard_map.396.refs_0_), channel_id=1, source_target_pairs={{0,2},{1,3},{2,0},{3,1},{4,6},{5,7},{6,4},{7,5},{8,10},{9,11},{10,... | collective-permute-start | bytes 884744 | tf_op jit(solution)/shard_map/ppermute | solution.py:76
  34.8 11.8 %collective-permute-start.9 = (bf16[1056,128]{1,0:T(8,128)(2,1)S(1)}, bf16[1056,128]{1,0:T(8,128)(2,1)S(1)}, u32[]{:S(2)}, u32[]{:S(2)}) collective-permute-start(bf16[1056,128]{1,0:T(8,128)(2,1)S(1)} %collective-permute-done.5.refs_3_.refs_10_), channel_id=1, source_target_pairs={{0,4},{4,0},{8,12},{12,8},{16,20},{20,16},{24,28},{28,24},{1,5},{5... | collective-permute-start | bytes 811016 | tf_op jit(solution)/shard_map/ppermute | solution.py:76
  46.6 8.7 %collective-permute-start.15 = (bf16[4,288,128]{2,1,0:T(8,128)(2,1)S(1)}, bf16[4,288,128]{2,1,0:T(8,128)(2,1)S(1)}, u32[]{:S(2)}, u32[]{:S(2)}) collective-permute-start(bf16[4,288,128]{2,1,0:T(8,128)(2,1)S(1)} %shard_map.399.refs_1_), channel_id=1, source_target_pairs={{0,2},{1,3},{2,0},{3,1},{4,6},{5,7},{6,4},{7,5},{8,10},{9,11},{10,... | collective-permute-start | bytes 884744 | tf_op jit(solution)/shard_map/ppermute | solution.py:76
  51.5 1.3 %collective-permute-start.10 = (bf16[128,256]{1,0:T(8,128)(2,1)S(1)}, bf16[128,256]{1,0:T(8,128)(2,1)S(1)}, u32[]{:S(2)}, u32[]{:S(2)}) collective-permute-start(bf16[128,256]{1,0:T(8,128)(2,1)S(1)} %get-tuple-element.91), channel_id=1, source_target_pairs={{0,1},{1,0},{2,3},{3,2},{4,5},{5,4},{6,7},{7,6},{8,9},{9,8},{10,11... | collective-permute-start | bytes 196616 | tf_op jit(solution)/shard_map/ppermute | solution.py:76
  52.9 4.5 %collective-permute-start.13 = (bf16[2,4,288,128]{3,2,1,0:T(8,128)(2,1)S(1)}, bf16[2,4,288,128]{3,2,1,0:T(8,128)(2,1)S(1)}, u32[]{:S(2)}, u32[]{:S(2)}) collective-permute-start(bf16[2,4,288,128]{3,2,1,0:T(8,128)(2,1)S(1)} %shard_map.400.refs_0_), channel_id=1, source_target_pairs={{0,1},{1,0},{2,3},{3,2},{4,5},{5,4},{6,7},{7,6},{8,9},{9,8},{10,11... | collective-permute-start | bytes 1769480 | tf_op jit(solution)/shard_map/ppermute | solution.py:76
  55.4 2.1 %collective-permute-start.16 = (bf16[2,4,288,128]{3,2,1,0:T(8,128)(2,1)S(1)}, bf16[2,4,288,128]{3,2,1,0:T(8,128)(2,1)S(1)}, u32[]{:S(2)}, u32[]{:S(2)}) collective-permute-start(bf16[2,4,288,128]{3,2,1,0:T(8,128)(2,1)S(1)} %shard_map.401.refs_2_), channel_id=1, source_target_pairs={{0,1},{1,0},{2,3},{3,2},{4,5},{5,4},{6,7},{7,6},{8,9},{9,8},{10,11... | collective-permute-start | bytes 1769480 | tf_op jit(solution)/shard_map/ppermute | solution.py:76
  55.5 4.9 %collective-permute-start.11 = (bf16[128,256]{1,0:T(8,128)(2,1)S(1)}, bf16[128,256]{1,0:T(8,128)(2,1)S(1)}, u32[]{:S(2)}, u32[]{:S(2)}) collective-permute-start(bf16[128,256]{1,0:T(8,128)(2,1)S(1)} %get-tuple-element.92), channel_id=1, source_target_pairs={{0,2},{1,3},{2,0},{3,1},{4,6},{5,7},{6,4},{7,5},{8,10},{9,11},{10,... | collective-permute-start | bytes 196616 | tf_op jit(solution)/shard_map/ppermute | solution.py:76
  57.1 4.1 %collective-permute-start.12 = (bf16[128,256]{1,0:T(8,128)(2,1)S(1)}, bf16[128,256]{1,0:T(8,128)(2,1)S(1)}, u32[]{:S(2)}, u32[]{:S(2)}) collective-permute-start(bf16[128,256]{1,0:T(8,128)(2,1)S(1)} %get-tuple-element.93), channel_id=1, source_target_pairs={{0,3},{1,2},{2,1},{3,0},{4,7},{5,6},{6,5},{7,4},{8,11},{9,10},{10,... | collective-permute-start | bytes 196616 | tf_op jit(solution)/shard_map/ppermute | solution.py:76
  70.9 2.9 %collective-permute-start.20 = (bf16[1568,384]{1,0:T(8,128)(2,1)S(1)}, bf16[1568,384]{1,0:T(8,128)(2,1)S(1)}, u32[]{:S(2)}, u32[]{:S(2)}) collective-permute-start(bf16[1568,384]{1,0:T(8,128)(2,1)S(1)} %get-tuple-element.103), channel_id=1, source_target_pairs={{0,1},{1,0},{2,3},{3,2},{4,5},{5,4},{6,7},{7,6},{8,9},{9,8},{10,11... | collective-permute-start | bytes 3612680 | tf_op jit(solution)/shard_map/ppermute | solution.py:76
  71.1 5.1 %collective-permute-start.17 = (bf16[128,256]{1,0:T(8,128)(2,1)S(1)}, bf16[128,256]{1,0:T(8,128)(2,1)S(1)}, u32[]{:S(2)}, u32[]{:S(2)}) collective-permute-start(bf16[128,256]{1,0:T(8,128)(2,1)S(1)} %get-tuple-element.99), channel_id=1, source_target_pairs={{0,1},{1,0},{2,3},{3,2},{4,5},{5,4},{6,7},{7,6},{8,9},{9,8},{10,11... | collective-permute-start | bytes 196616 | tf_op jit(solution)/shard_map/ppermute | solution.py:76
  71.5 4.8 %collective-permute-start.18 = (bf16[128,256]{1,0:T(8,128)(2,1)S(1)}, bf16[128,256]{1,0:T(8,128)(2,1)S(1)}, u32[]{:S(2)}, u32[]{:S(2)}) collective-permute-start(bf16[128,256]{1,0:T(8,128)(2,1)S(1)} %get-tuple-element.100), channel_id=1, source_target_pairs={{0,2},{1,3},{2,0},{3,1},{4,6},{5,7},{6,4},{7,5},{8,10},{9,11},{10,... | collective-permute-start | bytes 196616 | tf_op jit(solution)/shard_map/ppermute | solution.py:76
  72.9 4.2 %collective-permute-start.19 = (bf16[128,256]{1,0:T(8,128)(2,1)S(1)}, bf16[128,256]{1,0:T(8,128)(2,1)S(1)}, u32[]{:S(2)}, u32[]{:S(2)}) collective-permute-start(bf16[128,256]{1,0:T(8,128)(2,1)S(1)} %get-tuple-element.101), channel_id=1, source_target_pairs={{0,3},{1,2},{2,1},{3,0},{4,7},{5,6},{6,5},{7,4},{8,11},{9,10},{10,... | collective-permute-start | bytes 196616 | tf_op jit(solution)/shard_map/ppermute | solution.py:76
  74.2 10.0 %collective-permute-start.29 = (bf16[384,384]{1,0:T(8,128)(2,1)S(1)}, bf16[384,384]{1,0:T(8,128)(2,1)S(1)}, u32[]{:S(2)}, u32[]{:S(2)}) collective-permute-start(bf16[384,384]{1,0:T(8,128)(2,1)S(1)} %get-tuple-element.116), channel_id=1, source_target_pairs={{0,2},{1,3},{2,0},{3,1},{4,6},{5,7},{6,4},{7,5},{8,10},{9,11},{10,... | collective-permute-start | bytes 884744 | tf_op jit(solution)/shard_map/ppermute | solution.py:76
  75.6 15.4 %collective-permute-start.26 = (bf16[416,384]{1,0:T(8,128)(2,1)S(1)}, bf16[416,384]{1,0:T(8,128)(2,1)S(1)}, u32[]{:S(2)}, u32[]{:S(2)}) collective-permute-start(bf16[416,384]{1,0:T(8,128)(2,1)S(1)} %get-tuple-element.115), channel_id=1, source_target_pairs={{0,2},{1,3},{2,0},{3,1},{4,6},{5,7},{6,4},{7,5},{8,10},{9,11},{10,... | collective-permute-start | bytes 958472 | tf_op jit(solution)/shard_map/ppermute | solution.py:76
  79.5 11.6 %collective-permute-start.25 = (bf16[768,128]{1,0:T(8,128)(2,1)S(1)}, bf16[768,128]{1,0:T(8,128)(2,1)S(1)}, u32[]{:S(2)}, u32[]{:S(2)}) collective-permute-start(bf16[768,128]{1,0:T(8,128)(2,1)S(1)} %get-tuple-element.113), channel_id=1, source_target_pairs={{0,4},{4,0},{8,12},{12,8},{16,20},{20,16},{24,28},{28,24},{1,5},{5... | collective-permute-start | bytes 589832 | tf_op jit(solution)/shard_map/ppermute | solution.py:76
  81.0 11.7 %collective-permute-start.22 = (bf16[768,128]{1,0:T(8,128)(2,1)S(1)}, bf16[768,128]{1,0:T(8,128)(2,1)S(1)}, u32[]{:S(2)}, u32[]{:S(2)}) collective-permute-start(bf16[768,128]{1,0:T(8,128)(2,1)S(1)} %get-tuple-element.109), channel_id=1, source_target_pairs={{0,4},{4,0},{8,12},{12,8},{16,20},{20,16},{24,28},{28,24},{1,5},{5... | collective-permute-start | bytes 589832 | tf_op jit(solution)/shard_map/ppermute | solution.py:76
  84.3 15.8 %collective-permute-start.35 = (bf16[256,768]{1,0:T(8,128)(2,1)S(1)}, bf16[256,768]{1,0:T(8,128)(2,1)S(1)}, u32[]{:S(2)}, u32[]{:S(2)}) collective-permute-start(bf16[256,768]{1,0:T(8,128)(2,1)S(1)} %get-tuple-element.123.refs_26_), channel_id=1, source_target_pairs={{0,2},{1,3},{2,0},{3,1},{4,6},{5,7},{6,4},{7,5},{8,10},{9,11},{10,... | collective-permute-start | bytes 1179656 | tf_op jit(solution)/shard_map/ppermute | solution.py:76
  85.6 10.0 %collective-permute-start.24 = (bf16[768,128]{1,0:T(8,128)(2,1)S(1)}, bf16[768,128]{1,0:T(8,128)(2,1)S(1)}, u32[]{:S(2)}, u32[]{:S(2)}) collective-permute-start(bf16[768,128]{1,0:T(8,128)(2,1)S(1)} %get-tuple-element.111), channel_id=1, source_target_pairs={{0,4},{4,0},{8,12},{12,8},{16,20},{20,16},{24,28},{28,24},{1,5},{5... | collective-permute-start | bytes 589832 | tf_op jit(solution)/shard_map/ppermute | solution.py:76
  91.0 15.7 %collective-permute-start.34 = (bf16[256,768]{1,0:T(8,128)(2,1)S(1)}, bf16[256,768]{1,0:T(8,128)(2,1)S(1)}, u32[]{:S(2)}, u32[]{:S(2)}) collective-permute-start(bf16[256,768]{1,0:T(8,128)(2,1)S(1)} %get-tuple-element.123.refs_26_), channel_id=1, source_target_pairs={{0,1},{1,0},{2,3},{3,2},{4,5},{5,4},{6,7},{7,6},{8,9},{9,8},{10,11... | collective-permute-start | bytes 1179656 | tf_op jit(solution)/shard_map/ppermute | solution.py:76
  91.1 11.3 %collective-permute-start.30 = (bf16[416,384]{1,0:T(8,128)(2,1)S(1)}, bf16[416,384]{1,0:T(8,128)(2,1)S(1)}, u32[]{:S(2)}, u32[]{:S(2)}) collective-permute-start(bf16[416,384]{1,0:T(8,128)(2,1)S(1)} %shard_map.406.refs_2_.other), channel_id=1, source_target_pairs={{0,4},{4,0},{8,12},{12,8},{16,20},{20,16},{24,28},{28,24},{1,5},{5... | collective-permute-start | bytes 958472 | tf_op jit(solution)/shard_map/ppermute | solution.py:76
  92.7 7.1 %collective-permute-start.27 = (bf16[768,128]{1,0:T(8,128)(2,1)S(1)}, bf16[768,128]{1,0:T(8,128)(2,1)S(1)}, u32[]{:S(2)}, u32[]{:S(2)}) collective-permute-start(bf16[768,128]{1,0:T(8,128)(2,1)S(1)} %shard_map.407), channel_id=1, source_target_pairs={{0,8},{4,12},{8,0},{12,4},{16,24},{20,28},{24,16},{28,20},{1,9},{5... | collective-permute-start | bytes 589832 | tf_op jit(solution)/shard_map/ppermute | solution.py:76
  95.6 10.4 %collective-permute-start.21 = (bf16[768,128]{1,0:T(8,128)(2,1)S(1)}, bf16[768,128]{1,0:T(8,128)(2,1)S(1)}, u32[]{:S(2)}, u32[]{:S(2)}) collective-permute-start(bf16[768,128]{1,0:T(8,128)(2,1)S(1)} %get-tuple-element.107), channel_id=1, source_target_pairs={{0,4},{4,0},{8,12},{12,8},{16,20},{20,16},{24,28},{28,24},{1,5},{5... | collective-permute-start | bytes 589832 | tf_op jit(solution)/shard_map/ppermute | solution.py:76
  99.8 6.9 %collective-permute-start.23 = (bf16[768,128]{1,0:T(8,128)(2,1)S(1)}, bf16[768,128]{1,0:T(8,128)(2,1)S(1)}, u32[]{:S(2)}, u32[]{:S(2)}) collective-permute-start(bf16[768,128]{1,0:T(8,128)(2,1)S(1)} %add_convert_fusion.3), channel_id=1, source_target_pairs={{0,8},{4,12},{8,0},{12,4},{16,24},{20,28},{24,16},{28,20},{1,9},{5... | collective-permute-start | bytes 589832 | tf_op jit(solution)/shard_map/ppermute | solution.py:76
  100.1 20.3 %collective-permute-start.36 = (bf16[256,768]{1,0:T(8,128)(2,1)S(1)}, bf16[256,768]{1,0:T(8,128)(2,1)S(1)}, u32[]{:S(2)}, u32[]{:S(2)}) collective-permute-start(bf16[256,768]{1,0:T(8,128)(2,1)S(1)} %collective-permute-done.35.refs_28_), channel_id=1, source_target_pairs={{0,1},{1,0},{2,3},{3,2},{4,5},{5,4},{6,7},{7,6},{8,9},{9,8},{10,11... | collective-permute-start | bytes 1179656 | tf_op jit(solution)/shard_map/ppermute | solution.py:76
  102.5 15.7 %collective-permute-start.28 = (bf16[768,128]{1,0:T(8,128)(2,1)S(1)}, bf16[768,128]{1,0:T(8,128)(2,1)S(1)}, u32[]{:S(2)}, u32[]{:S(2)}) collective-permute-start(bf16[768,128]{1,0:T(8,128)(2,1)S(1)} %add_convert_fusion), channel_id=1, source_target_pairs={{0,16},{4,20},{8,24},{12,28},{16,0},{20,4},{24,8},{28,12},{1,17},{... | collective-permute-start | bytes 589832 | tf_op jit(solution)/shard_map/ppermute | solution.py:76
  102.5 17.8 %copy-start.2 = (f32[768,128]{1,0:T(8,128)S(1)}, f32[768,128]{1,0:T(8,128)}, u32[]{:S(2)}) copy-start(f32[768,128]{1,0:T(8,128)} %refs_0_.1) | copy-start | bytes 1179652
  102.5 17.8 %copy-start.3 = (f32[768,128]{1,0:T(8,128)S(1)}, f32[768,128]{1,0:T(8,128)}, u32[]{:S(2)}) copy-start(f32[768,128]{1,0:T(8,128)} %refs_1_.1) | copy-start | bytes 1179652
  102.5 17.9 %copy-start.4 = (f32[768,128]{1,0:T(8,128)S(1)}, f32[768,128]{1,0:T(8,128)}, u32[]{:S(2)}) copy-start(f32[768,128]{1,0:T(8,128)} %refs_2_.1) | copy-start | bytes 1179652
  102.5 17.9 %copy-start.5 = (f32[768,128]{1,0:T(8,128)S(1)}, f32[768,128]{1,0:T(8,128)}, u32[]{:S(2)}) copy-start(f32[768,128]{1,0:T(8,128)} %refs_3_.1) | copy-start | bytes 1179652
  102.5 17.9 %copy-start.6 = (f32[64,384]{1,0:T(8,128)S(1)}, f32[64,384]{1,0:T(8,128)}, u32[]{:S(2)}) copy-start(f32[64,384]{1,0:T(8,128)} %refs_6_.1) | copy-start | bytes 294916
  102.5 17.9 %copy-start.7 = (f32[64,384]{1,0:T(8,128)S(1)}, f32[64,384]{1,0:T(8,128)}, u32[]{:S(2)}) copy-start(f32[64,384]{1,0:T(8,128)} %refs_7_.1) | copy-start | bytes 294916
  102.5 17.9 %copy-start.8 = (f32[64,384]{1,0:T(8,128)S(1)}, f32[64,384]{1,0:T(8,128)}, u32[]{:S(2)}) copy-start(f32[64,384]{1,0:T(8,128)} %refs_8_.1) | copy-start | bytes 294916
  102.6 17.9 %copy-start.9 = (f32[64,384]{1,0:T(8,128)S(1)}, f32[64,384]{1,0:T(8,128)}, u32[]{:S(2)}) copy-start(f32[64,384]{1,0:T(8,128)} %refs_9_.1) | copy-start | bytes 294916
  102.6 17.8 %copy-start.10 = (f32[64,192]{1,0:T(8,128)S(1)}, f32[64,192]{1,0:T(8,128)}, u32[]{:S(2)}) copy-start(f32[64,192]{1,0:T(8,128)} %refs_10_.1) | copy-start | bytes 147460
  102.6 17.8 %copy-start.11 = (f32[64,192]{1,0:T(8,128)S(1)}, f32[64,192]{1,0:T(8,128)}, u32[]{:S(2)}) copy-start(f32[64,192]{1,0:T(8,128)} %refs_11_.1) | copy-start | bytes 147460
  102.6 17.8 %copy-start.12 = (f32[64,192]{1,0:T(8,128)S(1)}, f32[64,192]{1,0:T(8,128)}, u32[]{:S(2)}) copy-start(f32[64,192]{1,0:T(8,128)} %refs_12_.1) | copy-start | bytes 147460
  106.1 12.2 %collective-permute-start.31 = (bf16[128,384]{1,0:T(8,128)(2,1)S(1)}, bf16[128,384]{1,0:T(8,128)(2,1)S(1)}, u32[]{:S(2)}, u32[]{:S(2)}) collective-permute-start(bf16[128,384]{1,0:T(8,128)(2,1)S(1)} %get-tuple-element.120), channel_id=1, source_target_pairs={{0,8},{4,12},{8,0},{12,4},{16,24},{20,28},{24,16},{28,20},{1,9},{5... | collective-permute-start | bytes 294920 | tf_op jit(solution)/shard_map/ppermute | solution.py:76
  106.7 13.6 %collective-permute-start.32 = (bf16[128,384]{1,0:T(8,128)(2,1)S(1)}, bf16[128,384]{1,0:T(8,128)(2,1)S(1)}, u32[]{:S(2)}, u32[]{:S(2)}) collective-permute-start(bf16[128,384]{1,0:T(8,128)(2,1)S(1)} %get-tuple-element.121), channel_id=1, source_target_pairs={{0,16},{4,20},{8,24},{12,28},{16,0},{20,4},{24,8},{28,12},{1,17},{... | collective-permute-start | bytes 294920 | tf_op jit(solution)/shard_map/ppermute | solution.py:76
  106.8 13.6 %collective-permute-start.33 = (bf16[128,384]{1,0:T(8,128)(2,1)S(1)}, bf16[128,384]{1,0:T(8,128)(2,1)S(1)}, u32[]{:S(2)}, u32[]{:S(2)}) collective-permute-start(bf16[128,384]{1,0:T(8,128)(2,1)S(1)} %get-tuple-element.122), channel_id=1, source_target_pairs={{0,24},{4,28},{8,16},{12,20},{16,8},{20,12},{24,0},{28,4},{1,25},{... | collective-permute-start | bytes 294920 | tf_op jit(solution)/shard_map/ppermute | solution.py:76
  (15 other events, 190.4 us)

commit v5 on v4

--- a/solution.py
+++ b/solution.py
@@ -32,6 +32,10 @@
 STREAM_EXPERTS = ((0, 1, 4, 5), (2, 3, 4, 5), (0, 1, 2, 3, 4, 5))
 STREAM_COLS = (0, 4, 8)
 
+COST = {'low': 1.605, 'cut': 0.491, 'turns': 6.876, 'counts': 2.06, 'pool': 4.0, 'stack': 0.045, 'join': 0.7, 'weights': 0.778, 'main': 10.0, 'table': 6.0, 'half': 0.7, 'chip': 0.7, 'near': 1.0, 'sum': 0.5, 'finish': 3.0}
+OPT = {'a': 1, 'b': 0, 'c': 0, 'd': 1, 'e': 0, 'f': 1, 'h': 0, 'i': 0, 'j': 1, 'k': 0, 'm': 3, 'n': 1, 'q': 1, 'g': 2, 'p': 0, 'r': 0}
+RNG = {'a': 4, 'b': 3, 'c': 3, 'd': 2, 'e': 3, 'f': 2, 'h': 2, 'i': 3, 'j': 2, 'k': 2, 'm': 4, 'n': 2, 'q': 2, 'g': 3, 'p': 2, 'r': 2}
+
 VMEM = pl.BlockSpec(memory_space=pltpu.VMEM)
 SMEM = pl.BlockSpec(memory_space=pltpu.SMEM)
 HBM = pl.BlockSpec(memory_space=pltpu.HBM)
@@ -64,6 +68,7 @@
         out_specs=[VMEM] * len(outs),
         scratch_shapes=list(scratch),
         compiler_params=pltpu.CompilerParams(vmem_limit_bytes=vmem * MIB),
+        name=getattr(kernel, "func", kernel).__name__,
         cost_estimate=pl.CostEstimate(
             flops=int(us * 1.0e9), bytes_accessed=int(us * 3.0e6), transcendentals=0
         ),
@@ -80,19 +85,11 @@
     return 1 << ((dp_count.bit_length() - 1) // 2)
 
 
-def low_kernel(table_hbm, first_hbm, second_hbm, vector_hbm, cot_hbm, *refs, hid):
-    piece, keep, cots = refs[0], refs[1], refs[2 : 2 + hid]
-    table, first, second, vector, cot, sems = refs[2 + hid :]
+def low_kernel(table_hbm, first_hbm, second_hbm, piece, keep, table, first, second, sems):
     copies = [
         pltpu.make_async_copy(source, target, sems.at[i])
         for i, (source, target) in enumerate(
-            (
-                (table_hbm, table),
-                (first_hbm, first),
-                (second_hbm, second),
-                (vector_hbm, vector),
-                (cot_hbm, cot),
-            )
+            ((table_hbm, table), (first_hbm, first), (second_hbm, second))
         )
     ]
     for copy in copies:
@@ -115,8 +112,16 @@
         for out in (piece, keep):
             out[start : start + rows, :] = first[:, lanes].astype(bf16)
             out[start + rows : start + each, :] = folded[:, lanes].astype(bf16)
-    copies[3].wait()
-    copies[4].wait()
+
+
+def cut_kernel(vector, cot, ids_ref, order_ref, idb, *cots):
+    id_rows, lanes = ids_ref.shape
+    per = IDS_STEP // lanes
+    idt = ids_ref[...].T
+    for q in range(id_rows):
+        idb[q // per, (q % per) * lanes : (q % per + 1) * lanes, :] = jnp.broadcast_to(
+            idt[:, q : q + 1], (lanes, HALF)
+        ).astype(jnp.int16)
     me = lax.axis_index("hid")
     cols, width = cot.shape[0], cots[0].shape[1]
     rest = vector[...]
@@ -127,24 +132,18 @@
     span = vector.shape[1]
     stack = jnp.concatenate(terms + [jnp.zeros((7, span), f32)], axis=0)
     over = jnp.concatenate([stack[:, width:], jnp.zeros((16, 2 * width - span), f32)], axis=1)
-    for m in range(hid):
+    for m, out in enumerate(cots):
         start = pl.multiple_of((me ^ m) * width, width)
-        cots[m][0:cols, :] = cot[:, pl.ds(start, width)]
-        cots[m][cols : cols + 16, :] = stack[:, 0:width].astype(bf16)
-        cots[m][cols + 16 :, :] = over.astype(bf16)
-
-
-def counts_kernel(offs_ref, ids_ref, off_ref, nxt_ref, *refs, chunk):
-    c_ref, idb, acc = refs[-3:]
-    id_rows, lanes = ids_ref.shape
+        out[0:cols, :] = cot[:, pl.ds(start, width)]
+        out[cols : cols + 16, :] = stack[:, 0:width].astype(bf16)
+        out[cols + 16 :, :] = over.astype(bf16)
+
+
+def counts_kernel(offs_ref, idb, off_ref, nxt_ref, *refs, chunk):
+    c_ref, acc = refs[-2:]
     vocab = c_ref.shape[1]
+    lanes = off_ref.shape[1]
     events = off_ref.shape[0] * lanes
-    per = IDS_STEP // lanes
-    idt = ids_ref[...].T
-    for q in range(id_rows):
-        idb[q // per, (q % per) * lanes : (q % per + 1) * lanes, :] = jnp.broadcast_to(
-            idt[:, q : q + 1], (lanes, HALF)
-        ).astype(jnp.int16)
     offt = off_ref[...].T
     nxtt = nxt_ref[...].T
     cols = EVENTS_STEP // lanes
@@ -158,7 +157,7 @@
     if (chunk + 1) * EVENTS_STEP < events:
         high = offs_ref[(chunk + 1) * EVENTS_STEP]
     else:
-        high = jnp.int32(id_rows * lanes)
+        high = jnp.int32(idb.shape[0] * IDS_STEP)
 
     def body(step, carry):
         place = step * IDS_STEP + lax.broadcasted_iota(jnp.int32, (EVENTS_STEP, IDS_STEP), 1)
@@ -235,7 +234,7 @@
 
 def turns_kernel(*refs, hid):
     cots = refs[:hid]
-    col_ref, q_ref, q3t_ref, vecs = refs[hid:]
+    col_ref, q_ref, q3t_ref, vecs = refs[-4:]
     me_hid = lax.axis_index("hid")
     j_step = vecs.shape[2]
     for r in range(hid):
@@ -279,13 +278,12 @@
         j = me_hid ^ r
         for s in range(dp):
             k = me_dp ^ s
-            near, at = s % inner, s // inner
             for g in range(3):
                 w1s[j, pl.ds(pl.multiple_of(k * rows, rows), rows), g * feats : (g + 1) * feats] = (
-                    stacks[r][near, at, g * each : g * each + rows, :]
+                    stacks[r][s, g * each : g * each + rows, :]
                 )
             part = jnp.concatenate(
-                [stacks[r][near, at, g * each + rows : (g + 1) * each, :].astype(f32) for g in range(3)],
+                [stacks[r][s, g * each + rows : (g + 1) * each, :].astype(f32) for g in range(3)],
                 axis=1,
             )
             for q in range(high // fold):
@@ -525,44 +523,50 @@
     return (a.astype(f32) + b.astype(f32)).astype(bf16)
 
 
-def core_merge_kernel(home, come, small, *outs, rows, inner):
-    last = plus(small[...], come[len(outs) * rows :, :])
-    for i, out in enumerate(outs):
-        part = slice(i * rows, (i + 1) * rows)
-        out[0:rows, :] = plus(home[part, :], come[part, :])
-        if i % inner:
-            out[rows:, :] = last
-
-
-def chip_merge_kernel(*refs, terms):
-    if len(refs) == terms + 3:
-        refs[terms + 2][...] = refs[terms][...]
-        refs[terms + 1][...] = total(refs[:terms]).astype(bf16)
-    else:
-        refs[terms][...] = total(refs[:terms]).astype(bf16)
-
-
-def near_merge_kernel(mine, other, *refs, terms, rows, outer):
-    come, outs = refs[: terms - 1], refs[terms - 1 :]
+def core_merge_kernel(home, come, small, *refs, rows, inner, nears):
+    chips = home.shape[0] // rows // inner
+    outs = refs[-chips * len(nears) :]
+    last = plus(small[...], come[home.shape[0] :, :])
+    for m in range(chips):
+        for i, near in enumerate(nears):
+            out = outs[m * len(nears) + i]
+            part = slice((m * inner + near) * rows, (m * inner + near + 1) * rows)
+            out[0:rows, :] = plus(home[part, :], come[part, :])
+            if near:
+                out[rows:, :] = last
+
+
+def chip_merge_kernel(*refs, terms, passing):
+    outs = refs[-1 - passing :]
+    outs[0][...] = total(refs[:terms]).astype(bf16)
+    if passing:
+        outs[1][...] = refs[terms][...]
+
+
+def near_merge_kernel(mine, other, *refs, terms, rows, outer, passing):
+    come, outs = refs[: terms - 1], refs[terms - 1 + passing :]
     last = total((other, *come), slice(outer * rows, None)).astype(bf16)
     for far in range(outer):
         part = slice(far * rows, (far + 1) * rows)
         outs[far][0:rows, :] = total((mine, *come), part).astype(bf16)
         outs[far][rows:, :] = last
-
-
-def stack_kernel_ordered(*refs, count, start):
-    for r in range(count):
-        refs[-1][r] = refs[r][start:, :]
+    if passing:
+        outs[outer][...] = refs[terms - 1][...]
+
+
+def stack_kernel(*refs, start):
+    for r, ref in enumerate(refs[:-1]):
+        refs[-1][r] = ref[start:, :]
 
 
 def sum_kernel(*refs, terms):
     refs[-1][...] = total(refs[:terms]).astype(bf16)
 
 
-def join_kernel(*refs, count):
-    for i in range(count):
-        refs[-1][i] = refs[i][...]
+def join_kernel(early, late, order_ref, out, *, places):
+    count = early.shape[0]
+    for i, place in enumerate(places):
+        out[place] = early[i] if i < count else late[i - count]
 
 
 def mixed_kernel(*refs, hid):
@@ -676,26 +680,20 @@
 
     cot_rows = cotangent.shape[1] + 32
     weight_rows = 3 * piece_rows
-    piece, keep, *cot_pieces = call(
-        functools.partial(low_kernel, hid=hid),
-        [
-            shape((slots + weight_rows, feats), bf16),
-            shape((slots + weight_rows, feats), bf16),
-            *[shape((cot_rows, rows), bf16) for m in range(hid)],
-        ],
-        (table_w, first_w, second_w, vector_w, cotangent.T),
-        in_specs=[HBM] * 5,
+    piece, keep = call(
+        low_kernel,
+        [shape((slots + weight_rows, feats), bf16)] * 2,
+        (table_w, first_w, second_w),
+        in_specs=[HBM] * 3,
         scratch=[
             pltpu.VMEM(table_w.shape, f32),
             pltpu.VMEM(first_w.shape, f32),
             pltpu.VMEM(second_w.shape, f32),
-            pltpu.VMEM(vector_w.shape, f32),
-            pltpu.VMEM(cotangent.shape[::-1], bf16),
-            pltpu.SemaphoreType.DMA((5,)),
+            pltpu.SemaphoreType.DMA((3,)),
         ],
         vmem=62,
-    )
-    cots = [cot_pieces[0]] + [swap(cot_pieces[m], "hid", m) for m in range(1, hid)]
+        us=COST["low"],
+    )
     nexts = jnp.concatenate([bag_offsets[1:], jnp.full((1,), ids, jnp.int32)])
     lanes = 128
     chunks = events // EVENTS_STEP
@@ -706,18 +704,17 @@
             shape((EVENTS_STEP, vocab), bf16),
             (
                 bag_offsets,
-                embed_ids.reshape(ids // lanes, lanes),
+                id_columns,
                 bag_offsets.reshape(events // lanes, lanes),
                 nexts.reshape(events // lanes, lanes),
                 *order,
             ),
             in_specs=[SMEM, VMEM, VMEM, VMEM] + [ANY] * len(order),
             scratch=[
-                pltpu.VMEM((ids // IDS_STEP, IDS_STEP, HALF), jnp.int16),
                 pltpu.VMEM((EVENTS_STEP, vocab), f32),
             ],
             vmem=12 if vocab <= 4096 else 40,
-            us=5.0,
+            us=COST["counts"],
         )
 
     far_pieces = {0: piece}
@@ -728,34 +725,58 @@
     far_pieces = [far_pieces[f] for f in range(outer)]
     groups = [[keep] + far_pieces[1:]] + [[swap(p, "dp", near) for p in far_pieces] for near in range(1, inner)]
 
-    def stack(group, *order):
+    def stack(group):
         return call(
-            functools.partial(stack_kernel_ordered, count=outer, start=slots),
-            shape((outer, weight_rows, feats), bf16),
-            (*group, *order),
-            in_specs=[VMEM] * outer + [ANY] * len(order),
+            functools.partial(stack_kernel, start=slots),
+            shape((len(group), weight_rows, feats), bf16),
+            tuple(groups[near][far] for far, near in group),
             vmem=8,
-            us=0.7,
+            us=COST["stack"],
         )
 
-    stacks = {(0, near): stack(groups[near]) for near in range(inner)}
+    if OPT["n"]:
+        first = [(far, 0) for far in range(outer)] + [(0, near) for near in range(1, inner)]
+    else:
+        first = [(far, 0) for far in range(outer)]
+    rest = [(far, near) for far in range(outer) for near in range(inner) if (far, near) not in first]
+    stacks = {0: [stack(first), stack(rest)]}
+    id_columns, *cot_pieces = call(
+        cut_kernel,
+        [shape((ids // IDS_STEP, IDS_STEP, HALF), jnp.int16)]
+        + [shape((cot_rows, rows), bf16) for m in range(hid)],
+        (
+            vector_w,
+            cotangent.T,
+            embed_ids.reshape(ids // lanes, lanes),
+            (block_owners, far_pieces[outer // 2], far_pieces[outer - 1])[OPT["b"]],
+        ),
+        in_specs=[VMEM, VMEM, VMEM, ANY],
+        vmem=8,
+        us=COST["cut"],
+    )
+    cots = [cot_pieces[0]] + [swap(cot_pieces[m], "hid", m) for m in range(1, hid)]
     span = HALF * EXPERTS
-    columns, turn, turn3t = call(
-        functools.partial(turns_kernel, hid=hid),
-        [
-            shape((3, EXPERTS, H, HALF), f32),
-            shape((span, span), bf16),
-            shape((O * STREAMS, O * STREAMS), bf16),
-        ],
-        tuple(cots),
-        scratch=[pltpu.VMEM((hid, 16, piece_cols), bf16)],
-        vmem=12,
-        us=2.0,
-    )
+    def make_turns(*order):
+        return call(
+            functools.partial(turns_kernel, hid=hid),
+            [
+                shape((3, EXPERTS, H, HALF), f32),
+                shape((span, span), bf16),
+                shape((O * STREAMS, O * STREAMS), bf16),
+            ],
+            (*cots, *order),
+            in_specs=[VMEM] * hid + [ANY] * len(order),
+            scratch=[pltpu.VMEM((hid, 16, piece_cols), bf16)],
+            vmem=12,
+            us=COST["turns"],
+        )
+
+    if not OPT["r"]:
+        columns, turn, turn3t = make_turns()
     early = chunks // 2
-    counts = [count_bags(i) for i in range(early)]
-    counts += [count_bags(i, far_pieces[outer // 2], turn3t) for i in range(early, chunks - 1)]
-    counts.append(count_bags(chunks - 1, stacks[0, 0]))
+    counts = [count_bags(i, *(((), (groups[1][0],), (far_pieces[1],), (groups[1][0], far_pieces[1]))[OPT["a"]] if i else ())) for i in range(early)]
+    counts += [count_bags(i, *((), (far_pieces[outer // 2],), (far_pieces[outer // 2], far_pieces[1]), (groups[1][1],))[OPT["m"]]) for i in range(early, chunks - 1)]
+    counts.append(count_bags(chunks - 1, *(((stacks[0][0],), ()) if OPT["r"] else ((stacks[0][0], turn3t), (turn3t,)))[OPT["j"]]))
     pieces = [groups[r % inner][r // inner] for r in range(dp)]
     pooled = call(
         functools.partial(pool_kernel, chunks=chunks, dp=dp, hid=hid),
@@ -769,21 +790,23 @@
             pltpu.SMEM((dp,), jnp.int32),
         ],
         vmem=20 if vocab <= 4096 else 58,
-        us=4.0,
-    )
+        us=COST["pool"],
+    )
+    if OPT["r"]:
+        columns, turn, turn3t = make_turns(pooled[0])
     xts = [pooled[0]] + [swap(pooled[m], "hid", m) for m in range(1, hid)]
-    for near in range(inner):
-        for m in range(2, hid, 2):
-            stacks[m, near] = swap(stacks[0, near], "hid", m)
+    for m in range(2, hid, 2):
+        stacks[m] = [swap(part, "hid", m) for part in stacks[0]]
+    places = [far * inner + near for far, near in first + rest]
     joined = {}
     for m in range(0, hid, 2):
         joined[m] = call(
-            functools.partial(join_kernel, count=inner),
-            shape((inner, outer, weight_rows, feats), bf16),
-            (*[stacks[m, near] for near in range(inner)], xts[1]),
-            in_specs=[VMEM] * inner + [ANY],
+            functools.partial(join_kernel, places=places),
+            shape((dp, weight_rows, feats), bf16),
+            (*stacks[m], (pooled[0], xts[1], xts[hid - 1])[OPT["i"]]),
+            in_specs=[VMEM, VMEM, ANY],
             vmem=8,
-            us=0.7,
+            us=COST["join"],
         )
         joined[m + 1] = swap(joined[m], "hid", 1)
     w1p, w2p = call(
@@ -795,7 +818,7 @@
             pltpu.VMEM((dp, H, (O * EXPERTS) // dp), bf16),
         ],
         vmem=20,
-        us=3.0,
+        us=COST["weights"],
     )
 
     gates = 16
@@ -832,42 +855,110 @@
             pltpu.VMEM((H, O * EXPERTS), f32),
         ],
         vmem=36,
-        us=10.0,
+        us=COST["main"],
     )
     d_pooled = [d_pieces[0]] + [swap(d_pieces[m], "hid", m) for m in range(1, hid)]
 
     near_rows = some // inner
-    half = call(
-        functools.partial(core_merge_kernel, rows=near_rows, inner=inner),
-        [
-            shape((near_rows + small_rows * (near > 0), piece_cols), bf16)
-            for m in range(hid // 2)
-            for near in range(inner)
-        ],
-        (home, swap(away, "hid", 1), small),
+    def reduce_table(order):
+        return call(
+            functools.partial(table_kernel, chunks=chunks, dp=dp, hid=hid),
+            [shape((slots, feats), bf16) for r in range(dp)],
+            (block_owners, *counts, *d_pooled, order),
+            in_specs=[SMEM] + [VMEM] * (chunks + hid) + [ANY],
+            scratch=[
+                pltpu.VMEM((feats, events), bf16),
+                pltpu.VMEM((vocab, feats), bf16),
+                pltpu.VMEM((dp, slots, feats), bf16),
+                pltpu.SMEM((dp,), jnp.int32),
+            ],
+            vmem=20 if vocab <= 4096 else 58,
+            us=COST["table"],
+        )
+
+    come = swap(away, "hid", 1)
+
+    def half(nears, *order):
+        return call(
+            functools.partial(core_merge_kernel, rows=near_rows, inner=inner, nears=nears),
+            [
+                shape((near_rows + small_rows * (near > 0), piece_cols), bf16)
+                for m in range(hid // 2)
+                for near in nears
+            ],
+            (home, come, small, *order),
+            in_specs=[VMEM] * 3 + [ANY] * len(order),
+            vmem=12,
+            us=COST["half"],
+        )
+
+    def chip_sum(parts, order, passing):
+        result = call(
+            functools.partial(chip_merge_kernel, terms=hid // 2, passing=len(passing)),
+            [shape(v.shape, bf16) for v in (parts[0], *passing)],
+            (parts[0], *[swap(parts[m], "hid", 2 * m) for m in range(1, hid // 2)])
+            + (*passing, *order),
+            in_specs=[VMEM] * (hid // 2 + len(passing)) + [ANY] * len(order),
+            vmem=12,
+            us=COST["chip"],
+        )
+        return result if passing else result[0]
+
+    order = ((), (d_pooled[1],), (d_pooled[hid - 1],))[OPT["e"]]
+    if OPT["q"]:
+        parts = half(tuple(range(inner)), *order)
+        parts = [parts[i::inner] for i in range(inner)]
+    else:
+        parts = half(tuple(range(1, inner)), *order)
+        parts = [None] + [parts[i :: inner - 1] for i in range(inner - 1)]
+    d_table = reduce_table((block_owners, parts[1][0])[OPT["f"]])
+    sums = {}
+    for far in reversed(range(outer)):
+        terms = [d_table[far * inner]]
+        terms += [swap(d_table[far * inner + m], "dp", m) for m in range(1, inner)]
+        sums[far] = terms
+
+    def add_up(terms, *order):
+        return call(
+            functools.partial(sum_kernel, terms=len(terms)),
+            shape((slots, feats), bf16),
+            (*terms, *order),
+            in_specs=[VMEM] * len(terms) + [ANY] * len(order),
+            vmem=4,
+            us=COST["sum"],
+        )
+
+    last = outer - 1
+    if OPT["c"] == 2:
+        sums[last] = add_up(sums[last])
+    orders = ((), (d_table[0],), (sums[last],))[OPT["c"]]
+    chips = [None] + [chip_sum(parts[i], orders, ()) for i in range(1, inner)]
+    order = ((), (chips[1],))[OPT["k"]]
+    if not OPT["q"]:
+        parts[0], order = half((0,), *order), ()
+    if OPT["g"] == 1:
+        chips[0], mixed_part = chip_sum(parts[0], order, (mixed_part,))
+    else:
+        chips[0] = chip_sum(parts[0], order, ())
+    if OPT["c"] != 2:
+        sums[last] = add_up(sums[last], *((), (chips[1],))[OPT["d"]])
+    later = [far for far in range(1, last) if far % 2] if OPT["p"] and not OPT["h"] else []
+    for far in range(last):
+        if far not in later:
+            sums[far] = functools.reduce(plus, sums[far])
+    passing = (mixed_part,) if OPT["g"] == 0 else ()
+    far_parts = call(
+        functools.partial(
+            near_merge_kernel, terms=inner, rows=piece_rows, outer=outer, passing=len(passing)
+        ),
+        [shape((piece_rows + small_rows, piece_cols), bf16)] * outer
+        + [shape(v.shape, bf16) for v in passing],
+        (chips[0], chips[1], *[swap(chips[i], "dp", i) for i in range(1, inner)], *passing),
         vmem=12,
-        us=1.0,
-    )
-    sums = [None] * inner
-    for i in reversed(range(inner)):
-        passing = () if i else (mixed_part,)
-        result = call(
-            functools.partial(chip_merge_kernel, terms=hid // 2),
-            [shape(v.shape, bf16) for v in (half[i], *passing)],
-            (half[i], *[swap(half[m * inner + i], "hid", 2 * m) for m in range(1, hid // 2)])
-            + passing,
-            vmem=12,
-            us=0.7,
-        )
-        sums[i] = result[0]
-    mixed_part = result[1]
-    far_parts = call(
-        functools.partial(near_merge_kernel, terms=inner, rows=piece_rows, outer=outer),
-        [shape((piece_rows + small_rows, piece_cols), bf16)] * outer,
-        (sums[0], sums[1], *[swap(sums[i], "dp", i) for i in range(1, inner)]),
-        vmem=12,
-        us=1.0,
-    )
+        us=COST["near"],
+    )
+    if passing:
+        mixed_part = far_parts[outer]
     weight_terms = [far_parts[0]] + [swap(far_parts[m], "dp", m * inner) for m in range(1, outer)]
 
     mixed_parts = {0: mixed_part}
@@ -875,42 +966,18 @@
         mixed_parts[m] = swap(mixed_part, "hid", m)
     for m in range(0, hid, 2):
         mixed_parts[m + 1] = swap(mixed_parts[m], "hid", 1)
-    d_table = call(
-        functools.partial(table_kernel, chunks=chunks, dp=dp, hid=hid),
-        [shape((slots, feats), bf16) for r in range(dp)],
-        (block_owners, *counts, *d_pooled, half[0]),
-        in_specs=[SMEM] + [VMEM] * (chunks + hid) + [ANY],
-        scratch=[
-            pltpu.VMEM((feats, events), bf16),
-            pltpu.VMEM((vocab, feats), bf16),
-            pltpu.VMEM((dp, slots, feats), bf16),
-            pltpu.SMEM((dp,), jnp.int32),
-        ],
-        vmem=20 if vocab <= 4096 else 58,
-        us=6.0,
-    )
-    order = sums[1]
-    sums = {}
-    for far in reversed(range(outer)):
-        terms = [d_table[far * inner]]
-        terms += [swap(d_table[far * inner + m], "dp", m) for m in range(1, inner)]
-        if far == outer - 1:
-            sums[far] = call(
-                functools.partial(sum_kernel, terms=inner),
-                shape((slots, feats), bf16),
-                (*terms, order),
-                in_specs=[VMEM] * inner + [ANY],
-                vmem=4,
-                us=0.5,
-            )
-        else:
-            sums[far] = functools.reduce(plus, terms)
-    step = 1
-    while step < outer // 2:
-        for far in reversed([f for f in sums if f & step]):
-            sums[far ^ step] = plus(sums[far ^ step], swap(sums.pop(far), "dp", step * inner))
-        step *= 2
-    table_terms = [sums[0], swap(sums[step], "dp", step * inner)]
+    if OPT["h"]:
+        table_terms = [sums[0]]
+        table_terms += [swap(sums[far], "dp", far * inner) for far in reversed(range(1, outer))]
+    else:
+        step = 1
+        while step < outer // 2:
+            for far in reversed([f for f in sums if f & step]):
+                if far in later and step == 1:
+                    sums[far] = add_up(sums[far], sums[(far ^ step) + 2])
+                sums[far ^ step] = plus(sums[far ^ step], swap(sums.pop(far), "dp", step * inner))
+            step *= 2
+        table_terms = [sums[0], swap(sums[step], "dp", step * inner)]
 
     states = (
         table_w,
@@ -933,13 +1000,17 @@
     )
     mixed, *new = call(
         functools.partial(
-            finish_kernel, table_terms=len(table_terms), terms=outer, dp=dp, hid=hid
+            finish_kernel,
+            table_terms=len(table_terms),
+            terms=len(weight_terms),
+            dp=dp,
+            hid=hid,
         ),
         [shape((events, O * STREAMS), bf16)] + [shape(v.shape, f32) for v in states],
         (*states[:4], *table_terms, *states[4:], *weight_terms)
         + tuple(mixed_parts[m] for m in range(hid)),
         vmem=20,
-        us=3.0,
+        us=COST["finish"],
     )
     return (mixed, *new[:16], *[g.T for g in new[16:]])
 

time: 123 us -> 118 us (0.959)
  waiting for transfers between devices: 40.5 us -> 36.3 us
  Pallas kernels: 45.6 us -> 43.1 us
    ppermute x37, waiting for transfers between devices: 40.5 us -> 36.3 us  [swap(): return lax.ppermute(value, axis, [(i, i ^ mask) for i in range(count)])]
    pallas_call x20 -> x21, Pallas kernels: 45.6 us -> 43.1 us  [call(): pl.pallas_call(kernel, out_shape=outs, in_specs=in_specs or [VMEM] * len(...]
  transfers between devices with their start and end apart: 37 -> 37, of which waited for: 17 -> 18; matrix products, arithmetic and copies ran while one was open for 0% -> 0% of each run, Pallas kernels for 25% -> 25%
where the time goes in v5:
time: 118 us; the launch traced here: 117 us
  Pallas kernels  43.1 us (37%)
  waiting for transfers between devices  36.3 us (31%)
  starting transfers between devices  36 us (31%)
  between operations  1.45 us (1%)
    pallas_call x21, Pallas kernels, call(): pl.pallas_call(kernel, out_shape=outs, in_specs=in_specs or [VMEM] * len(...  43.1 us
    ppermute x37, waiting for transfers between devices, swap(): return lax.ppermute(value, axis, [(i, i ^ mask) for i in range(count)])  36.3 us
    ppermute x37, starting transfers between devices, swap(): return lax.ppermute(value, axis, [(i, i ^ mask) for i in range(count)])  36 us
  transfers between devices with their start and end apart: 37, of which 18 were waited for; matrix products, arithmetic and copies ran while one was open for 0% of the time, Pallas kernels for 25%

profile of v5, /device:TPU:0, one launch (start us, length us, event | category | flops | bytes accessed | tf_op | source)
XLA Modules:
  0.0 117.3 jit_solution(4744392156583067550)
XLA Ops:
  0.7 2.0 %low_kernel.1 = (bf16[1056,128]{1,0:T(8,128)(2,1)}, bf16[1056,128]{1,0:T(8,128)(2,1)}) custom-call(f32[768,128]{1,0:T(8,128)} %refs_0_.1, f32[64,384]{1,0:T(8,128)} %refs_6_.1, f32[64,192]{1,0:T(8,128)} %refs_10_.1), custom_call_target="tpu_custom_call" | custom-call | flops 1604999936 | bytes 4815000 | tf_op jit(solution)/shard_map/low_kernel/pallas_call | solution.py:64
  2.7 4.1 %collective-permute-start.6 = (bf16[1056,128]{1,0:T(8,128)(2,1)}, bf16[1056,128]{1,0:T(8,128)(2,1)S(1)}, u32[]{:S(2)}, u32[]{:S(2)}) collective-permute-start(bf16[1056,128]{1,0:T(8,128)(2,1)} %get-tuple-element.83), channel_id=1, source_target_pairs={{0,16},{4,20},{8,24},{12,28},{16,0},{20,4},{24,8},{28,12},{1,17},{... | collective-permute-start | bytes 811016 | tf_op jit(solution)/shard_map/ppermute | solution.py:81
  6.8 1.6 %collective-permute-start.1 = (bf16[1056,128]{1,0:T(8,128)(2,1)}, bf16[1056,128]{1,0:T(8,128)(2,1)S(1)}, u32[]{:S(2)}, u32[]{:S(2)}) collective-permute-start(bf16[1056,128]{1,0:T(8,128)(2,1)} %get-tuple-element.83), channel_id=1, source_target_pairs={{0,8},{4,12},{8,0},{12,4},{16,24},{20,28},{24,16},{28,20},{1,9},{5... | collective-permute-start | bytes 811016 | tf_op jit(solution)/shard_map/ppermute | solution.py:81
  9.2 1.6 %collective-permute-start.4 = (bf16[224,256]{1,0:T(8,128)(2,1)S(1)}, bf16[224,256]{1,0:T(8,128)(2,1)S(1)}, u32[]{:S(2)}, u32[]{:S(2)}) collective-permute-start(bf16[224,256]{1,0:T(8,128)(2,1)S(1)} %get-tuple-element.86), channel_id=1, source_target_pairs={{0,2},{1,3},{2,0},{3,1},{4,6},{5,7},{6,4},{7,5},{8,10},{9,11},{10,... | collective-permute-start | bytes 344072 | tf_op jit(solution)/shard_map/ppermute | solution.py:81
  11.3 4.3 %counts_kernel.4.refs_0_ = bf16[256,3072]{1,0:T(8,128)(2,1)S(1)} custom-call(s32[1024]{0:T(1024)S(1)} %copy-done.2, s16[16,256,128]{2,1,0:T(8,128)(2,1)S(1)} %get-tuple-element.82.idb, s32[8,128]{1,0:T(8,128)S(1)} %bitcast.15, s32[8,128]{1,0:T(8,128)S(1)} %add_bitcast_fusion.nxt_ref), custom_call_target="tpu_custom_call" | custom-call | flops 2060000000 | bytes 6180000 | tf_op jit(solution)/shard_map/counts_kernel/pallas_call | solution.py:64
  15.6 0.9 collective-permute-start
  16.5 2.9 %collective-permute-done.6.refs_8_.refs_2_ = bf16[1056,128]{1,0:T(8,128)(2,1)S(1)} collective-permute-done((bf16[1056,128]{1,0:T(8,128)(2,1)}, bf16[1056,128]{1,0:T(8,128)(2,1)S(1)}, u32[]{:S(2)}, u32[]{:S(2)}) %collective-permute-start.6) | collective-permute-done | bytes 270368 | tf_op jit(solution)/shard_map/ppermute | solution.py:81
  20.1 2.3 %turns_kernel.1 = (f32[3,6,256,128]{3,2,1,0:T(8,128)S(1)}, bf16[768,768]{1,0:T(8,128)(2,1)S(1)}, bf16[768,768]{1,0:T(8,128)(2,1)S(1)}) custom-call(bf16[224,256]{1,0:T(8,128)(2,1)S(1)} %get-tuple-element.84.refs_0_.refs_4_, bf16[224,256]{1,0:T(8,128)(2,1)S(1)} %collective-permute-done.3.refs_1_.refs_5_, ...), custom_call_target="tpu_custom_call" | custom-call | flops 6876000256 | bytes 20628000 | tf_op jit(solution)/shard_map/turns_kernel/pallas_call | solution.py:64
  22.5 1.6 %collective-permute-start.2 = (bf16[1056,128]{1,0:T(8,128)(2,1)S(1)}, bf16[1056,128]{1,0:T(8,128)(2,1)S(1)}, u32[]{:S(2)}, u32[]{:S(2)}) collective-permute-start(bf16[1056,128]{1,0:T(8,128)(2,1)S(1)} %collective-permute-done.1.refs_6_.refs_1_), channel_id=1, source_target_pairs={{0,4},{4,0},{8,12},{12,8},{16,20},{20,16},{24,28},{28,24},{1,5},{5... | collective-permute-start | bytes 811016 | tf_op jit(solution)/shard_map/ppermute | solution.py:81
  24.0 3.7 %counts_kernel.7.refs_3_ = bf16[256,3072]{1,0:T(8,128)(2,1)S(1)} custom-call(s32[1024]{0:T(1024)S(1)} %copy-done.2, s16[16,256,128]{2,1,0:T(8,128)(2,1)S(1)} %get-tuple-element.82.idb, s32[8,128]{1,0:T(8,128)S(1)} %bitcast.16, s32[8,128]{1,0:T(8,128)S(1)} %add_bitcast_fusion.nxt_ref, bf16[768,768]{1,0:T(8,128)(2,1)S(1)} %get-tuple-element.88.refs_0_.refs_12_), custom_call_target="tpu_custom_call" | custom-call | flops 2060000000 | bytes 6180000 | tf_op jit(solution)/shard_map/counts_kernel/pallas_call | solution.py:64
  27.7 1.3 %collective-permute-start.7 = (bf16[1056,128]{1,0:T(8,128)(2,1)S(1)}, bf16[1056,128]{1,0:T(8,128)(2,1)S(1)}, u32[]{:S(2)}, u32[]{:S(2)}) collective-permute-start(bf16[1056,128]{1,0:T(8,128)(2,1)S(1)} %collective-permute-done.6.refs_8_.refs_2_), channel_id=1, source_target_pairs={{0,4},{4,0},{8,12},{12,8},{16,20},{20,16},{24,28},{28,24},{1,5},{5... | collective-permute-start | bytes 811016 | tf_op jit(solution)/shard_map/ppermute | solution.py:81
  29.0 0.8 collective-permute-start.9
  29.8 3.7 %counts_kernel.5.refs_1_ = bf16[256,3072]{1,0:T(8,128)(2,1)S(1)} custom-call(s32[1024]{0:T(1024)S(1)} %copy-done.2, s16[16,256,128]{2,1,0:T(8,128)(2,1)S(1)} %get-tuple-element.82.idb, s32[8,128]{1,0:T(8,128)S(1)} %bitcast.17, s32[8,128]{1,0:T(8,128)S(1)} %add_bitcast_fusion.nxt_ref, bf16[1056,128]{1,0:T(8,128)(2,1)S(1)} %collective-permute-done.refs_0_.refs_5_.refs_4_), custom_call_target="tpu_custom_call" | custom-call | flops 2060000000 | bytes 6180000 | tf_op jit(solution)/shard_map/counts_kernel/pallas_call | solution.py:64
  33.5 1.6 %collective-permute-start.14 = (bf16[5,288,128]{2,1,0:T(8,128)(2,1)S(1)}, bf16[5,288,128]{2,1,0:T(8,128)(2,1)S(1)}, u32[]{:S(2)}, u32[]{:S(2)}) collective-permute-start(bf16[5,288,128]{2,1,0:T(8,128)(2,1)S(1)} %stack_kernel.2.early), channel_id=1, source_target_pairs={{0,2},{1,3},{2,0},{3,1},{4,6},{5,7},{6,4},{7,5},{8,10},{9,11},{10,... | collective-permute-start | bytes 1105928 | tf_op jit(solution)/shard_map/ppermute | solution.py:81
  35.1 5.0 %counts_kernel.6.refs_2_ = bf16[256,3072]{1,0:T(8,128)(2,1)S(1)} custom-call(s32[1024]{0:T(1024)S(1)} %copy-done.2, s16[16,256,128]{2,1,0:T(8,128)(2,1)S(1)} %get-tuple-element.82.idb, s32[8,128]{1,0:T(8,128)S(1)} %bitcast.18, s32[8,128]{1,0:T(8,128)S(1)} %add_bitcast_fusion.nxt_ref, bf16[1056,128]{1,0:T(8,128)(2,1)S(1)} %collective-permute-done.2.refs_0_.refs_7_), custom_call_target="tpu_custom_call" | custom-call | flops 2060000000 | bytes 6180000 | tf_op jit(solution)/shard_map/counts_kernel/pallas_call | solution.py:64
  40.1 2.1 %collective-permute-done.9.refs_11_.refs_2_ = bf16[1056,128]{1,0:T(8,128)(2,1)S(1)} collective-permute-done((bf16[1056,128]{1,0:T(8,128)(2,1)S(1)}, bf16[1056,128]{1,0:T(8,128)(2,1)S(1)}, u32[]{:S(2)}, u32[]{:S(2)}) %collective-permute-start.9) | collective-permute-done | bytes 270368 | tf_op jit(solution)/shard_map/ppermute | solution.py:81
  42.3 1.6 %collective-permute-start.15 = (bf16[3,288,128]{2,1,0:T(8,128)(2,1)S(1)}, bf16[3,288,128]{2,1,0:T(8,128)(2,1)S(1)}, u32[]{:S(2)}, u32[]{:S(2)}) collective-permute-start(bf16[3,288,128]{2,1,0:T(8,128)(2,1)S(1)} %stack_kernel.3.late), channel_id=1, source_target_pairs={{0,2},{1,3},{2,0},{3,1},{4,6},{5,7},{6,4},{7,5},{8,10},{9,11},{10,... | collective-permute-start | bytes 663560 | tf_op jit(solution)/shard_map/ppermute | solution.py:81
  43.8 3.3 %pool_kernel.1 = (bf16[128,256]{1,0:T(8,128)(2,1)S(1)}, bf16[128,256]{1,0:T(8,128)(2,1)S(1)}, bf16[128,256]{1,0:T(8,128)(2,1)S(1)}, bf16[128,256]{1,0:T(8,128)(2,1)S(1)}) custom-call(s32[48]{0:T(128)S(1)} %copy-done.24, bf16[256,3072]{1,0:T(8,128)(2,1)S(1)} %counts_kernel.4.refs_0_, bf16[256,3072]{1,0:T(8,128)(2,1)S(1)} %counts_kernel.5.refs_1_, ...), custom_call_target="tpu_custom_call" | custom-call | flops 4000000000 | bytes 12000000 | tf_op jit(solution)/shard_map/pool_kernel/pallas_call | solution.py:64
  47.3 1.7 %collective-permute-done.15.late = bf16[3,288,128]{2,1,0:T(8,128)(2,1)S(1)} collective-permute-done((bf16[3,288,128]{2,1,0:T(8,128)(2,1)S(1)}, bf16[3,288,128]{2,1,0:T(8,128)(2,1)S(1)}, u32[]{:S(2)}, u32[]{:S(2)}) %collective-permute-start.15) | collective-permute-done | bytes 221216 | tf_op jit(solution)/shard_map/ppermute | solution.py:81
  49.7 1.5 %collective-permute-start.11 = (bf16[128,256]{1,0:T(8,128)(2,1)S(1)}, bf16[128,256]{1,0:T(8,128)(2,1)S(1)}, u32[]{:S(2)}, u32[]{:S(2)}) collective-permute-start(bf16[128,256]{1,0:T(8,128)(2,1)S(1)} %get-tuple-element.92), channel_id=1, source_target_pairs={{0,2},{1,3},{2,0},{3,1},{4,6},{5,7},{6,4},{7,5},{8,10},{9,11},{10,... | collective-permute-start | bytes 196616 | tf_op jit(solution)/shard_map/ppermute | solution.py:81
  51.2 2.9 %weights_kernel.1 = (bf16[6,512,256]{2,1,0:T(8,128)(2,1)S(1)}, bf16[6,256,256]{2,1,0:T(8,128)(2,1)S(1)}) custom-call(bf16[8,288,128]{2,1,0:T(8,128)(2,1)S(1)} %join_kernel.2.refs_0_, bf16[8,288,128]{2,1,0:T(8,128)(2,1)S(1)} %collective-permute-done.13.refs_1_, bf16[8,288,128]{2,1,0:T(8,128)(2,1)S(1)} %join_kernel.3.refs_2_, ...), custom_call_target="tpu_custom_call" | custom-call | flops 778000000 | bytes 2334000 | tf_op jit(solution)/shard_map/weights_kernel/pallas_call | solution.py:64
  54.2 1.4 %collective-permute-done.12.refs_3_ = bf16[128,256]{1,0:T(8,128)(2,1)S(1)} collective-permute-done((bf16[128,256]{1,0:T(8,128)(2,1)S(1)}, bf16[128,256]{1,0:T(8,128)(2,1)S(1)}, u32[]{:S(2)}, u32[]{:S(2)}) %collective-permute-start.12) | collective-permute-done | bytes 65568 | tf_op jit(solution)/shard_map/ppermute | solution.py:81
  55.6 9.6 %main_kernel.1 = (bf16[256,768]{1,0:T(8,128)(2,1)S(1)}, bf16[32,384]{1,0:T(8,128)(2,1)S(1)}, bf16[1536,384]{1,0:T(8,128)(2,1)S(1)}, bf16[1568,384]{1,0:T(8,128)(...) custom-call(bf16[128,256]{1,0:T(8,128)(2,1)S(1)} %get-tuple-element., ...), custom_call_target="tpu_custom_call" | custom-call | flops 10000000000 | bytes 30000000 | tf_op jit(solution)/shard_map/main_kernel/pallas_call | solution.py:64
  66.5 0.8 collective-permute-start.19
  67.3 0.9 collective-permute-done.20.come
  68.5 0.8 collective-permute-start.26
  69.3 1.4 %collective-permute-done.18.refs_6_ = bf16[128,256]{1,0:T(8,128)(2,1)S(1)} collective-permute-done((bf16[128,256]{1,0:T(8,128)(2,1)S(1)}, bf16[128,256]{1,0:T(8,128)(2,1)S(1)}, u32[]{:S(2)}, u32[]{:S(2)}) %collective-permute-start.18) | collective-permute-done | bytes 65568 | tf_op jit(solution)/shard_map/ppermute | solution.py:81
  70.9 2.4 %table_kernel.1 = (bf16[768,128]{1,0:T(8,128)(2,1)S(1)}, bf16[768,128]{1,0:T(8,128)(2,1)S(1)}, bf16[768,128]{1,0:T(8,128)(2,1)S(1)}, bf16[768,128]{1,0:T(8,128)(...) custom-call(s32[48]{0:T(128)S(1)} %copy-done.24, ...), custom_call_target="tpu_custom_call" | custom-call | flops 6000000000 | bytes 18000000 | tf_op jit(solution)/shard_map/table_kernel/pallas_call | solution.py:64
  73.3 1.3 %collective-permute-start.25 = (bf16[768,128]{1,0:T(8,128)(2,1)S(1)}, bf16[768,128]{1,0:T(8,128)(2,1)S(1)}, u32[]{:S(2)}, u32[]{:S(2)}) collective-permute-start(bf16[768,128]{1,0:T(8,128)(2,1)S(1)} %get-tuple-element.113), channel_id=1, source_target_pairs={{0,4},{4,0},{8,12},{12,8},{16,20},{20,16},{24,28},{28,24},{1,5},{5... | collective-permute-start | bytes 589832 | tf_op jit(solution)/shard_map/ppermute | solution.py:81
  74.5 0.8 collective-permute-start.22
  75.4 1.3 %collective-permute-start.35 = (bf16[256,768]{1,0:T(8,128)(2,1)S(1)}, bf16[256,768]{1,0:T(8,128)(2,1)S(1)}, u32[]{:S(2)}, u32[]{:S(2)}) collective-permute-start(bf16[256,768]{1,0:T(8,128)(2,1)S(1)} %get-tuple-element.121.refs_26_), channel_id=1, source_target_pairs={{0,2},{1,3},{2,0},{3,1},{4,6},{5,7},{6,4},{7,5},{8,10},{9,11},{10,... | collective-permute-start | bytes 1179656 | tf_op jit(solution)/shard_map/ppermute | solution.py:81
  76.7 1.2 %collective-permute-start.24 = (bf16[768,128]{1,0:T(8,128)(2,1)S(1)}, bf16[768,128]{1,0:T(8,128)(2,1)S(1)}, u32[]{:S(2)}, u32[]{:S(2)}) collective-permute-start(bf16[768,128]{1,0:T(8,128)(2,1)S(1)} %get-tuple-element.111), channel_id=1, source_target_pairs={{0,4},{4,0},{8,12},{12,8},{16,20},{20,16},{24,28},{28,24},{1,5},{5... | collective-permute-start | bytes 589832 | tf_op jit(solution)/shard_map/ppermute | solution.py:81
  78.6 0.8 collective-permute-start.29
  79.5 1.5 %collective-permute-done.25.refs_1_ = bf16[768,128]{1,0:T(8,128)(2,1)S(1)} collective-permute-done((bf16[768,128]{1,0:T(8,128)(2,1)S(1)}, bf16[768,128]{1,0:T(8,128)(2,1)S(1)}, u32[]{:S(2)}, u32[]{:S(2)}) %collective-permute-start.25) | collective-permute-done | bytes 196640 | tf_op jit(solution)/shard_map/ppermute | solution.py:81
  81.0 1.2 %collective-permute-start.30 = (bf16[416,384]{1,0:T(8,128)(2,1)S(1)}, bf16[416,384]{1,0:T(8,128)(2,1)S(1)}, u32[]{:S(2)}, u32[]{:S(2)}) collective-permute-start(bf16[416,384]{1,0:T(8,128)(2,1)S(1)} %chip_merge_kernel.2.refs_2_.other), channel_id=1, source_target_pairs={{0,4},{4,0},{8,12},{12,8},{16,20},{20,16},{24,28},{28,24},{1,5},{5... | collective-permute-start | bytes 958472 | tf_op jit(solution)/shard_map/ppermute | solution.py:81
  82.3 3.0 %collective-permute-done.22 = bf16[768,128]{1,0:T(8,128)(2,1)S(1)} collective-permute-done((bf16[768,128]{1,0:T(8,128)(2,1)S(1)}, bf16[768,128]{1,0:T(8,128)(2,1)S(1)}, u32[]{:S(2)}, u32[]{:S(2)}) %collective-permute-start.22) | collective-permute-done | bytes 196640 | tf_op jit(solution)/shard_map/ppermute | solution.py:81
  85.7 1.7 %collective-permute-done.35.refs_28_ = bf16[256,768]{1,0:T(8,128)(2,1)S(1)} collective-permute-done((bf16[256,768]{1,0:T(8,128)(2,1)S(1)}, bf16[256,768]{1,0:T(8,128)(2,1)S(1)}, u32[]{:S(2)}, u32[]{:S(2)}) %collective-permute-start.35) | collective-permute-done | bytes 393248 | tf_op jit(solution)/shard_map/ppermute | solution.py:81
  87.3 5.7 %collective-permute-done.29.refs_1_ = bf16[384,384]{1,0:T(8,128)(2,1)S(1)} collective-permute-done((bf16[384,384]{1,0:T(8,128)(2,1)S(1)}, bf16[384,384]{1,0:T(8,128)(2,1)S(1)}, u32[]{:S(2)}, u32[]{:S(2)}) %collective-permute-start.29) | collective-permute-done | bytes 294944 | tf_op jit(solution)/shard_map/ppermute | solution.py:81
  93.2 1.3 %collective-permute-start.21 = (bf16[768,128]{1,0:T(8,128)(2,1)S(1)}, bf16[768,128]{1,0:T(8,128)(2,1)S(1)}, u32[]{:S(2)}, u32[]{:S(2)}) collective-permute-start(bf16[768,128]{1,0:T(8,128)(2,1)S(1)} %get-tuple-element.107), channel_id=1, source_target_pairs={{0,4},{4,0},{8,12},{12,8},{16,20},{20,16},{24,28},{28,24},{1,5},{5... | collective-permute-start | bytes 589832 | tf_op jit(solution)/shard_map/ppermute | solution.py:81
  94.7 1.3 %collective-permute-done.30.refs_0_ = bf16[416,384]{1,0:T(8,128)(2,1)S(1)} collective-permute-done((bf16[416,384]{1,0:T(8,128)(2,1)S(1)}, bf16[416,384]{1,0:T(8,128)(2,1)S(1)}, u32[]{:S(2)}, u32[]{:S(2)}) %collective-permute-start.30) | collective-permute-done | bytes 319520 | tf_op jit(solution)/shard_map/ppermute | solution.py:81
  96.0 2.7 %collective-permute-start.28 = (bf16[768,128]{1,0:T(8,128)(2,1)S(1)}, bf16[768,128]{1,0:T(8,128)(2,1)S(1)}, u32[]{:S(2)}, u32[]{:S(2)}) collective-permute-start(bf16[768,128]{1,0:T(8,128)(2,1)S(1)} %add_convert_fusion), channel_id=1, source_target_pairs={{0,16},{4,20},{8,24},{12,28},{16,0},{20,4},{24,8},{28,12},{1,17},{... | collective-permute-start | bytes 589832 | tf_op jit(solution)/shard_map/ppermute | solution.py:81
  98.8 1.3 %collective-permute-start.31 = (bf16[128,384]{1,0:T(8,128)(2,1)S(1)}, bf16[128,384]{1,0:T(8,128)(2,1)S(1)}, u32[]{:S(2)}, u32[]{:S(2)}) collective-permute-start(bf16[128,384]{1,0:T(8,128)(2,1)S(1)} %get-tuple-element.118), channel_id=1, source_target_pairs={{0,8},{4,12},{8,0},{12,4},{16,24},{20,28},{24,16},{28,20},{1,9},{5... | collective-permute-start | bytes 294920 | tf_op jit(solution)/shard_map/ppermute | solution.py:81
  100.5 2.7 %collective-permute-start.32 = (bf16[128,384]{1,0:T(8,128)(2,1)S(1)}, bf16[128,384]{1,0:T(8,128)(2,1)S(1)}, u32[]{:S(2)}, u32[]{:S(2)}) collective-permute-start(bf16[128,384]{1,0:T(8,128)(2,1)S(1)} %get-tuple-element.119), channel_id=1, source_target_pairs={{0,16},{4,20},{8,24},{12,28},{16,0},{20,4},{24,8},{28,12},{1,17},{... | collective-permute-start | bytes 294920 | tf_op jit(solution)/shard_map/ppermute | solution.py:81
  103.2 3.7 %collective-permute-done.23 = bf16[768,128]{1,0:T(8,128)(2,1)S(1)} collective-permute-done((bf16[768,128]{1,0:T(8,128)(2,1)S(1)}, bf16[768,128]{1,0:T(8,128)(2,1)S(1)}, u32[]{:S(2)}, u32[]{:S(2)}) %collective-permute-start.23) | collective-permute-done | bytes 196640 | tf_op jit(solution)/shard_map/ppermute | solution.py:81
  107.0 1.9 %collective-permute-done.31.refs_23_ = bf16[128,384]{1,0:T(8,128)(2,1)S(1)} collective-permute-done((bf16[128,384]{1,0:T(8,128)(2,1)S(1)}, bf16[128,384]{1,0:T(8,128)(2,1)S(1)}, u32[]{:S(2)}, u32[]{:S(2)}) %collective-permute-start.31) | collective-permute-done | bytes 98336 | tf_op jit(solution)/shard_map/ppermute | solution.py:81
  108.9 2.2 %collective-permute-done.32.refs_24_ = bf16[128,384]{1,0:T(8,128)(2,1)S(1)} collective-permute-done((bf16[128,384]{1,0:T(8,128)(2,1)S(1)}, bf16[128,384]{1,0:T(8,128)(2,1)S(1)}, u32[]{:S(2)}, u32[]{:S(2)}) %collective-permute-start.32) | collective-permute-done | bytes 98336 | tf_op jit(solution)/shard_map/ppermute | solution.py:81
  111.1 3.5 %collective-permute-done.33.refs_25_ = bf16[128,384]{1,0:T(8,128)(2,1)S(1)} collective-permute-done((bf16[128,384]{1,0:T(8,128)(2,1)S(1)}, bf16[128,384]{1,0:T(8,128)(2,1)S(1)}, u32[]{:S(2)}, u32[]{:S(2)}) %collective-permute-start.33) | collective-permute-done | bytes 98336 | tf_op jit(solution)/shard_map/ppermute | solution.py:81
  114.8 2.3 %finish_kernel.1 = (bf16[1024,768]{1,0:T(8,128)(2,1)}, f32[768,128]{1,0:T(8,128)}, f32[768,128]{1,0:T(8,128)}, f32[768,128]{1,0:T(8,128)}, f32[768,128]{1,0:T(8,...) custom-call(f32[768,128]{1,0:T(8,128)S(1)} %copy-done.4, ...), custom_call_target="tpu_custom_call" | custom-call | flops 3000000000 | bytes 9000000 | tf_op jit(solution)/shard_map/finish_kernel/pallas_call | solution.py:64
  (105 shorter events, 6.7 us)
Async XLA Ops:
  2.7 16.7 %collective-permute-start.6 = (bf16[1056,128]{1,0:T(8,128)(2,1)}, bf16[1056,128]{1,0:T(8,128)(2,1)S(1)}, u32[]{:S(2)}, u32[]{:S(2)}) collective-permute-start(bf16[1056,128]{1,0:T(8,128)(2,1)} %get-tuple-element.83), channel_id=1, source_target_pairs={{0,16},{4,20},{8,24},{12,28},{16,0},{20,4},{24,8},{28,12},{1,17},{... | collective-permute-start | bytes 811016 | tf_op jit(solution)/shard_map/ppermute | solution.py:81
  6.8 15.7 %collective-permute-start.1 = (bf16[1056,128]{1,0:T(8,128)(2,1)}, bf16[1056,128]{1,0:T(8,128)(2,1)S(1)}, u32[]{:S(2)}, u32[]{:S(2)}) collective-permute-start(bf16[1056,128]{1,0:T(8,128)(2,1)} %get-tuple-element.83), channel_id=1, source_target_pairs={{0,8},{4,12},{8,0},{12,4},{16,24},{20,28},{24,16},{28,20},{1,9},{5... | collective-permute-start | bytes 811016 | tf_op jit(solution)/shard_map/ppermute | solution.py:81
  9.2 6.4 %collective-permute-start.3 = (bf16[224,256]{1,0:T(8,128)(2,1)S(1)}, bf16[224,256]{1,0:T(8,128)(2,1)S(1)}, u32[]{:S(2)}, u32[]{:S(2)}) collective-permute-start(bf16[224,256]{1,0:T(8,128)(2,1)S(1)} %get-tuple-element.85), channel_id=1, source_target_pairs={{0,1},{1,0},{2,3},{3,2},{4,5},{5,4},{6,7},{7,6},{8,9},{9,8},{10,11... | collective-permute-start | bytes 344072 | tf_op jit(solution)/shard_map/ppermute | solution.py:81
  9.2 10.9 %collective-permute-start.4 = (bf16[224,256]{1,0:T(8,128)(2,1)S(1)}, bf16[224,256]{1,0:T(8,128)(2,1)S(1)}, u32[]{:S(2)}, u32[]{:S(2)}) collective-permute-start(bf16[224,256]{1,0:T(8,128)(2,1)S(1)} %get-tuple-element.86), channel_id=1, source_target_pairs={{0,2},{1,3},{2,0},{3,1},{4,6},{5,7},{6,4},{7,5},{8,10},{9,11},{10,... | collective-permute-start | bytes 344072 | tf_op jit(solution)/shard_map/ppermute | solution.py:81
  10.8 9.3 %collective-permute-start.5 = (bf16[224,256]{1,0:T(8,128)(2,1)S(1)}, bf16[224,256]{1,0:T(8,128)(2,1)S(1)}, u32[]{:S(2)}, u32[]{:S(2)}) collective-permute-start(bf16[224,256]{1,0:T(8,128)(2,1)S(1)} %get-tuple-element.87), channel_id=1, source_target_pairs={{0,3},{1,2},{2,1},{3,0},{4,7},{5,6},{6,5},{7,4},{8,11},{9,10},{10,... | collective-permute-start | bytes 344072 | tf_op jit(solution)/shard_map/ppermute | solution.py:81
  15.6 14.2 %collective-permute-start = (bf16[1056,128]{1,0:T(8,128)(2,1)S(1)}, bf16[1056,128]{1,0:T(8,128)(2,1)S(1)}, u32[]{:S(2)}, u32[]{:S(2)}) collective-permute-start(bf16[1056,128]{1,0:T(8,128)(2,1)S(1)} %copy-done.25), channel_id=1, source_target_pairs={{0,4},{4,0},{8,12},{12,8},{16,20},{20,16},{24,28},{28,24},{1,5},{5... | collective-permute-start | bytes 811016 | tf_op jit(solution)/shard_map/ppermute | solution.py:81
  19.4 9.6 %collective-permute-start.8 = (bf16[1056,128]{1,0:T(8,128)(2,1)S(1)}, bf16[1056,128]{1,0:T(8,128)(2,1)S(1)}, u32[]{:S(2)}, u32[]{:S(2)}) collective-permute-start(bf16[1056,128]{1,0:T(8,128)(2,1)S(1)} %collective-permute-done.6.refs_8_.refs_2_), channel_id=1, source_target_pairs={{0,8},{4,12},{8,0},{12,4},{16,24},{20,28},{24,16},{28,20},{1,9},{5... | collective-permute-start | bytes 811016 | tf_op jit(solution)/shard_map/ppermute | solution.py:81
  22.5 12.6 %collective-permute-start.2 = (bf16[1056,128]{1,0:T(8,128)(2,1)S(1)}, bf16[1056,128]{1,0:T(8,128)(2,1)S(1)}, u32[]{:S(2)}, u32[]{:S(2)}) collective-permute-start(bf16[1056,128]{1,0:T(8,128)(2,1)S(1)} %collective-permute-done.1.refs_6_.refs_1_), channel_id=1, source_target_pairs={{0,4},{4,0},{8,12},{12,8},{16,20},{20,16},{24,28},{28,24},{1,5},{5... | collective-permute-start | bytes 811016 | tf_op jit(solution)/shard_map/ppermute | solution.py:81
  27.7 12.4 %collective-permute-start.7 = (bf16[1056,128]{1,0:T(8,128)(2,1)S(1)}, bf16[1056,128]{1,0:T(8,128)(2,1)S(1)}, u32[]{:S(2)}, u32[]{:S(2)}) collective-permute-start(bf16[1056,128]{1,0:T(8,128)(2,1)S(1)} %collective-permute-done.6.refs_8_.refs_2_), channel_id=1, source_target_pairs={{0,4},{4,0},{8,12},{12,8},{16,20},{20,16},{24,28},{28,24},{1,5},{5... | collective-permute-start | bytes 811016 | tf_op jit(solution)/shard_map/ppermute | solution.py:81
  29.0 13.3 %collective-permute-start.9 = (bf16[1056,128]{1,0:T(8,128)(2,1)S(1)}, bf16[1056,128]{1,0:T(8,128)(2,1)S(1)}, u32[]{:S(2)}, u32[]{:S(2)}) collective-permute-start(bf16[1056,128]{1,0:T(8,128)(2,1)S(1)} %collective-permute-done.8.refs_10_.refs_3_), channel_id=1, source_target_pairs={{0,4},{4,0},{8,12},{12,8},{16,20},{20,16},{24,28},{28,24},{1,5},{5... | collective-permute-start | bytes 811016 | tf_op jit(solution)/shard_map/ppermute | solution.py:81
  33.5 13.8 %collective-permute-start.14 = (bf16[5,288,128]{2,1,0:T(8,128)(2,1)S(1)}, bf16[5,288,128]{2,1,0:T(8,128)(2,1)S(1)}, u32[]{:S(2)}, u32[]{:S(2)}) collective-permute-start(bf16[5,288,128]{2,1,0:T(8,128)(2,1)S(1)} %stack_kernel.2.early), channel_id=1, source_target_pairs={{0,2},{1,3},{2,0},{3,1},{4,6},{5,7},{6,4},{7,5},{8,10},{9,11},{10,... | collective-permute-start | bytes 1105928 | tf_op jit(solution)/shard_map/ppermute | solution.py:81
  42.3 6.7 %collective-permute-start.15 = (bf16[3,288,128]{2,1,0:T(8,128)(2,1)S(1)}, bf16[3,288,128]{2,1,0:T(8,128)(2,1)S(1)}, u32[]{:S(2)}, u32[]{:S(2)}) collective-permute-start(bf16[3,288,128]{2,1,0:T(8,128)(2,1)S(1)} %stack_kernel.3.late), channel_id=1, source_target_pairs={{0,2},{1,3},{2,0},{3,1},{4,6},{5,7},{6,4},{7,5},{8,10},{9,11},{10,... | collective-permute-start | bytes 663560 | tf_op jit(solution)/shard_map/ppermute | solution.py:81
  47.2 4.0 %collective-permute-start.13 = (bf16[8,288,128]{2,1,0:T(8,128)(2,1)S(1)}, bf16[8,288,128]{2,1,0:T(8,128)(2,1)S(1)}, u32[]{:S(2)}, u32[]{:S(2)}) collective-permute-start(bf16[8,288,128]{2,1,0:T(8,128)(2,1)S(1)} %join_kernel.2.refs_0_), channel_id=1, source_target_pairs={{0,1},{1,0},{2,3},{3,2},{4,5},{5,4},{6,7},{7,6},{8,9},{9,8},{10,11... | collective-permute-start | bytes 1769480 | tf_op jit(solution)/shard_map/ppermute | solution.py:81
  49.0 2.2 %collective-permute-start.16 = (bf16[8,288,128]{2,1,0:T(8,128)(2,1)S(1)}, bf16[8,288,128]{2,1,0:T(8,128)(2,1)S(1)}, u32[]{:S(2)}, u32[]{:S(2)}) collective-permute-start(bf16[8,288,128]{2,1,0:T(8,128)(2,1)S(1)} %join_kernel.3.refs_2_), channel_id=1, source_target_pairs={{0,1},{1,0},{2,3},{3,2},{4,5},{5,4},{6,7},{7,6},{8,9},{9,8},{10,11... | collective-permute-start | bytes 1769480 | tf_op jit(solution)/shard_map/ppermute | solution.py:81
  49.1 5.0 %collective-permute-start.10 = (bf16[128,256]{1,0:T(8,128)(2,1)S(1)}, bf16[128,256]{1,0:T(8,128)(2,1)S(1)}, u32[]{:S(2)}, u32[]{:S(2)}) collective-permute-start(bf16[128,256]{1,0:T(8,128)(2,1)S(1)} %get-tuple-element.91), channel_id=1, source_target_pairs={{0,1},{1,0},{2,3},{3,2},{4,5},{5,4},{6,7},{7,6},{8,9},{9,8},{10,11... | collective-permute-start | bytes 196616 | tf_op jit(solution)/shard_map/ppermute | solution.py:81
  49.7 4.5 %collective-permute-start.11 = (bf16[128,256]{1,0:T(8,128)(2,1)S(1)}, bf16[128,256]{1,0:T(8,128)(2,1)S(1)}, u32[]{:S(2)}, u32[]{:S(2)}) collective-permute-start(bf16[128,256]{1,0:T(8,128)(2,1)S(1)} %get-tuple-element.92), channel_id=1, source_target_pairs={{0,2},{1,3},{2,0},{3,1},{4,6},{5,7},{6,4},{7,5},{8,10},{9,11},{10,... | collective-permute-start | bytes 196616 | tf_op jit(solution)/shard_map/ppermute | solution.py:81
  51.2 4.4 %collective-permute-start.12 = (bf16[128,256]{1,0:T(8,128)(2,1)S(1)}, bf16[128,256]{1,0:T(8,128)(2,1)S(1)}, u32[]{:S(2)}, u32[]{:S(2)}) collective-permute-start(bf16[128,256]{1,0:T(8,128)(2,1)S(1)} %get-tuple-element.93), channel_id=1, source_target_pairs={{0,3},{1,2},{2,1},{3,0},{4,7},{5,6},{6,5},{7,4},{8,11},{9,10},{10,... | collective-permute-start | bytes 196616 | tf_op jit(solution)/shard_map/ppermute | solution.py:81
  65.2 2.9 %collective-permute-start.20 = (bf16[1568,384]{1,0:T(8,128)(2,1)S(1)}, bf16[1568,384]{1,0:T(8,128)(2,1)S(1)}, u32[]{:S(2)}, u32[]{:S(2)}) collective-permute-start(bf16[1568,384]{1,0:T(8,128)(2,1)S(1)} %get-tuple-element.103), channel_id=1, source_target_pairs={{0,1},{1,0},{2,3},{3,2},{4,5},{5,4},{6,7},{7,6},{8,9},{9,8},{10,11... | collective-permute-start | bytes 3612680 | tf_op jit(solution)/shard_map/ppermute | solution.py:81
  65.4 3.9 %collective-permute-start.17 = (bf16[128,256]{1,0:T(8,128)(2,1)S(1)}, bf16[128,256]{1,0:T(8,128)(2,1)S(1)}, u32[]{:S(2)}, u32[]{:S(2)}) collective-permute-start(bf16[128,256]{1,0:T(8,128)(2,1)S(1)} %get-tuple-element.99), channel_id=1, source_target_pairs={{0,1},{1,0},{2,3},{3,2},{4,5},{5,4},{6,7},{7,6},{8,9},{9,8},{10,11... | collective-permute-start | bytes 196616 | tf_op jit(solution)/shard_map/ppermute | solution.py:81
  65.8 4.9 %collective-permute-start.18 = (bf16[128,256]{1,0:T(8,128)(2,1)S(1)}, bf16[128,256]{1,0:T(8,128)(2,1)S(1)}, u32[]{:S(2)}, u32[]{:S(2)}) collective-permute-start(bf16[128,256]{1,0:T(8,128)(2,1)S(1)} %get-tuple-element.100), channel_id=1, source_target_pairs={{0,2},{1,3},{2,0},{3,1},{4,6},{5,7},{6,4},{7,5},{8,10},{9,11},{10,... | collective-permute-start | bytes 196616 | tf_op jit(solution)/shard_map/ppermute | solution.py:81
  66.5 4.4 %collective-permute-start.19 = (bf16[128,256]{1,0:T(8,128)(2,1)S(1)}, bf16[128,256]{1,0:T(8,128)(2,1)S(1)}, u32[]{:S(2)}, u32[]{:S(2)}) collective-permute-start(bf16[128,256]{1,0:T(8,128)(2,1)S(1)} %get-tuple-element.101), channel_id=1, source_target_pairs={{0,3},{1,2},{2,1},{3,0},{4,7},{5,6},{6,5},{7,4},{8,11},{9,10},{10,... | collective-permute-start | bytes 196616 | tf_op jit(solution)/shard_map/ppermute | solution.py:81
  68.5 10.1 %collective-permute-start.26 = (bf16[416,384]{1,0:T(8,128)(2,1)S(1)}, bf16[416,384]{1,0:T(8,128)(2,1)S(1)}, u32[]{:S(2)}, u32[]{:S(2)}) collective-permute-start(bf16[416,384]{1,0:T(8,128)(2,1)S(1)} %get-tuple-element.114), channel_id=1, source_target_pairs={{0,2},{1,3},{2,0},{3,1},{4,6},{5,7},{6,4},{7,5},{8,10},{9,11},{10,... | collective-permute-start | bytes 958472 | tf_op jit(solution)/shard_map/ppermute | solution.py:81
  73.3 7.8 %collective-permute-start.25 = (bf16[768,128]{1,0:T(8,128)(2,1)S(1)}, bf16[768,128]{1,0:T(8,128)(2,1)S(1)}, u32[]{:S(2)}, u32[]{:S(2)}) collective-permute-start(bf16[768,128]{1,0:T(8,128)(2,1)S(1)} %get-tuple-element.113), channel_id=1, source_target_pairs={{0,4},{4,0},{8,12},{12,8},{16,20},{20,16},{24,28},{28,24},{1,5},{5... | collective-permute-start | bytes 589832 | tf_op jit(solution)/shard_map/ppermute | solution.py:81
  74.5 10.7 %collective-permute-start.22 = (bf16[768,128]{1,0:T(8,128)(2,1)S(1)}, bf16[768,128]{1,0:T(8,128)(2,1)S(1)}, u32[]{:S(2)}, u32[]{:S(2)}) collective-permute-start(bf16[768,128]{1,0:T(8,128)(2,1)S(1)} %get-tuple-element.109), channel_id=1, source_target_pairs={{0,4},{4,0},{8,12},{12,8},{16,20},{20,16},{24,28},{28,24},{1,5},{5... | collective-permute-start | bytes 589832 | tf_op jit(solution)/shard_map/ppermute | solution.py:81
  75.4 12.0 %collective-permute-start.35 = (bf16[256,768]{1,0:T(8,128)(2,1)S(1)}, bf16[256,768]{1,0:T(8,128)(2,1)S(1)}, u32[]{:S(2)}, u32[]{:S(2)}) collective-permute-start(bf16[256,768]{1,0:T(8,128)(2,1)S(1)} %get-tuple-element.121.refs_26_), channel_id=1, source_target_pairs={{0,2},{1,3},{2,0},{3,1},{4,6},{5,7},{6,4},{7,5},{8,10},{9,11},{10,... | collective-permute-start | bytes 1179656 | tf_op jit(solution)/shard_map/ppermute | solution.py:81
  76.7 16.5 %collective-permute-start.24 = (bf16[768,128]{1,0:T(8,128)(2,1)S(1)}, bf16[768,128]{1,0:T(8,128)(2,1)S(1)}, u32[]{:S(2)}, u32[]{:S(2)}) collective-permute-start(bf16[768,128]{1,0:T(8,128)(2,1)S(1)} %get-tuple-element.111), channel_id=1, source_target_pairs={{0,4},{4,0},{8,12},{12,8},{16,20},{20,16},{24,28},{28,24},{1,5},{5... | collective-permute-start | bytes 589832 | tf_op jit(solution)/shard_map/ppermute | solution.py:81
  78.6 14.5 %collective-permute-start.29 = (bf16[384,384]{1,0:T(8,128)(2,1)S(1)}, bf16[384,384]{1,0:T(8,128)(2,1)S(1)}, u32[]{:S(2)}, u32[]{:S(2)}) collective-permute-start(bf16[384,384]{1,0:T(8,128)(2,1)S(1)} %get-tuple-element.116), channel_id=1, source_target_pairs={{0,2},{1,3},{2,0},{3,1},{4,6},{5,7},{6,4},{7,5},{8,10},{9,11},{10,... | collective-permute-start | bytes 884744 | tf_op jit(solution)/shard_map/ppermute | solution.py:81
  81.0 15.0 %collective-permute-start.30 = (bf16[416,384]{1,0:T(8,128)(2,1)S(1)}, bf16[416,384]{1,0:T(8,128)(2,1)S(1)}, u32[]{:S(2)}, u32[]{:S(2)}) collective-permute-start(bf16[416,384]{1,0:T(8,128)(2,1)S(1)} %chip_merge_kernel.2.refs_2_.other), channel_id=1, source_target_pairs={{0,4},{4,0},{8,12},{12,8},{16,20},{20,16},{24,28},{28,24},{1,5},{5... | collective-permute-start | bytes 958472 | tf_op jit(solution)/shard_map/ppermute | solution.py:81
  85.2 9.2 %collective-permute-start.27 = (bf16[768,128]{1,0:T(8,128)(2,1)S(1)}, bf16[768,128]{1,0:T(8,128)(2,1)S(1)}, u32[]{:S(2)}, u32[]{:S(2)}) collective-permute-start(bf16[768,128]{1,0:T(8,128)(2,1)S(1)} %sum_kernel.1), channel_id=1, source_target_pairs={{0,8},{4,12},{8,0},{12,4},{16,24},{20,28},{24,16},{28,20},{1,9},{5... | collective-permute-start | bytes 589832 | tf_op jit(solution)/shard_map/ppermute | solution.py:81
  87.3 11.4 %collective-permute-start.34 = (bf16[256,768]{1,0:T(8,128)(2,1)S(1)}, bf16[256,768]{1,0:T(8,128)(2,1)S(1)}, u32[]{:S(2)}, u32[]{:S(2)}) collective-permute-start(bf16[256,768]{1,0:T(8,128)(2,1)S(1)} %get-tuple-element.121.refs_26_), channel_id=1, source_target_pairs={{0,1},{1,0},{2,3},{3,2},{4,5},{5,4},{6,7},{7,6},{8,9},{9,8},{10,11... | collective-permute-start | bytes 1179656 | tf_op jit(solution)/shard_map/ppermute | solution.py:81
  93.1 13.9 %collective-permute-start.36 = (bf16[256,768]{1,0:T(8,128)(2,1)S(1)}, bf16[256,768]{1,0:T(8,128)(2,1)S(1)}, u32[]{:S(2)}, u32[]{:S(2)}) collective-permute-start(bf16[256,768]{1,0:T(8,128)(2,1)S(1)} %collective-permute-done.35.refs_28_), channel_id=1, source_target_pairs={{0,1},{1,0},{2,3},{3,2},{4,5},{5,4},{6,7},{7,6},{8,9},{9,8},{10,11... | collective-permute-start | bytes 1179656 | tf_op jit(solution)/shard_map/ppermute | solution.py:81
  93.2 7.4 %collective-permute-start.21 = (bf16[768,128]{1,0:T(8,128)(2,1)S(1)}, bf16[768,128]{1,0:T(8,128)(2,1)S(1)}, u32[]{:S(2)}, u32[]{:S(2)}) collective-permute-start(bf16[768,128]{1,0:T(8,128)(2,1)S(1)} %get-tuple-element.107), channel_id=1, source_target_pairs={{0,4},{4,0},{8,12},{12,8},{16,20},{20,16},{24,28},{28,24},{1,5},{5... | collective-permute-start | bytes 589832 | tf_op jit(solution)/shard_map/ppermute | solution.py:81
  94.4 12.4 %collective-permute-start.23 = (bf16[768,128]{1,0:T(8,128)(2,1)S(1)}, bf16[768,128]{1,0:T(8,128)(2,1)S(1)}, u32[]{:S(2)}, u32[]{:S(2)}) collective-permute-start(bf16[768,128]{1,0:T(8,128)(2,1)S(1)} %add_convert_fusion.3), channel_id=1, source_target_pairs={{0,8},{4,12},{8,0},{12,4},{16,24},{20,28},{24,16},{28,20},{1,9},{5... | collective-permute-start | bytes 589832 | tf_op jit(solution)/shard_map/ppermute | solution.py:81
  94.5 20.1 %copy-start.4 = (f32[768,128]{1,0:T(8,128)S(1)}, f32[768,128]{1,0:T(8,128)}, u32[]{:S(2)}) copy-start(f32[768,128]{1,0:T(8,128)} %refs_0_.1) | copy-start | bytes 1179652
  94.5 20.1 %copy-start.5 = (f32[768,128]{1,0:T(8,128)S(1)}, f32[768,128]{1,0:T(8,128)}, u32[]{:S(2)}) copy-start(f32[768,128]{1,0:T(8,128)} %refs_1_.1) | copy-start | bytes 1179652
  94.5 20.1 %copy-start.6 = (f32[768,128]{1,0:T(8,128)S(1)}, f32[768,128]{1,0:T(8,128)}, u32[]{:S(2)}) copy-start(f32[768,128]{1,0:T(8,128)} %refs_2_.1) | copy-start | bytes 1179652
  94.6 20.1 %copy-start.7 = (f32[768,128]{1,0:T(8,128)S(1)}, f32[768,128]{1,0:T(8,128)}, u32[]{:S(2)}) copy-start(f32[768,128]{1,0:T(8,128)} %refs_3_.1) | copy-start | bytes 1179652
  94.6 20.1 %copy-start.8 = (f32[64,384]{1,0:T(8,128)S(1)}, f32[64,384]{1,0:T(8,128)}, u32[]{:S(2)}) copy-start(f32[64,384]{1,0:T(8,128)} %refs_6_.1) | copy-start | bytes 294916
  94.6 20.1 %copy-start.9 = (f32[64,384]{1,0:T(8,128)S(1)}, f32[64,384]{1,0:T(8,128)}, u32[]{:S(2)}) copy-start(f32[64,384]{1,0:T(8,128)} %refs_7_.1) | copy-start | bytes 294916
  94.6 20.1 %copy-start.10 = (f32[64,384]{1,0:T(8,128)S(1)}, f32[64,384]{1,0:T(8,128)}, u32[]{:S(2)}) copy-start(f32[64,384]{1,0:T(8,128)} %refs_8_.1) | copy-start | bytes 294916
  94.6 20.1 %copy-start.11 = (f32[64,384]{1,0:T(8,128)S(1)}, f32[64,384]{1,0:T(8,128)}, u32[]{:S(2)}) copy-start(f32[64,384]{1,0:T(8,128)} %refs_9_.1) | copy-start | bytes 294916
  94.6 20.1 %copy-start.12 = (f32[64,192]{1,0:T(8,128)S(1)}, f32[64,192]{1,0:T(8,128)}, u32[]{:S(2)}) copy-start(f32[64,192]{1,0:T(8,128)} %refs_10_.1) | copy-start | bytes 147460
  94.6 20.1 %copy-start.13 = (f32[64,192]{1,0:T(8,128)S(1)}, f32[64,192]{1,0:T(8,128)}, u32[]{:S(2)}) copy-start(f32[64,192]{1,0:T(8,128)} %refs_11_.1) | copy-start | bytes 147460
  94.6 20.1 %copy-start.14 = (f32[64,192]{1,0:T(8,128)S(1)}, f32[64,192]{1,0:T(8,128)}, u32[]{:S(2)}) copy-start(f32[64,192]{1,0:T(8,128)} %refs_12_.1) | copy-start | bytes 147460
  96.0 11.0 %collective-permute-start.28 = (bf16[768,128]{1,0:T(8,128)(2,1)S(1)}, bf16[768,128]{1,0:T(8,128)(2,1)S(1)}, u32[]{:S(2)}, u32[]{:S(2)}) collective-permute-start(bf16[768,128]{1,0:T(8,128)(2,1)S(1)} %add_convert_fusion), channel_id=1, source_target_pairs={{0,16},{4,20},{8,24},{12,28},{16,0},{20,4},{24,8},{28,12},{1,17},{... | collective-permute-start | bytes 589832 | tf_op jit(solution)/shard_map/ppermute | solution.py:81
  98.8 10.1 %collective-permute-start.31 = (bf16[128,384]{1,0:T(8,128)(2,1)S(1)}, bf16[128,384]{1,0:T(8,128)(2,1)S(1)}, u32[]{:S(2)}, u32[]{:S(2)}) collective-permute-start(bf16[128,384]{1,0:T(8,128)(2,1)S(1)} %get-tuple-element.118), channel_id=1, source_target_pairs={{0,8},{4,12},{8,0},{12,4},{16,24},{20,28},{24,16},{28,20},{1,9},{5... | collective-permute-start | bytes 294920 | tf_op jit(solution)/shard_map/ppermute | solution.py:81
  100.5 10.6 %collective-permute-start.32 = (bf16[128,384]{1,0:T(8,128)(2,1)S(1)}, bf16[128,384]{1,0:T(8,128)(2,1)S(1)}, u32[]{:S(2)}, u32[]{:S(2)}) collective-permute-start(bf16[128,384]{1,0:T(8,128)(2,1)S(1)} %get-tuple-element.119), channel_id=1, source_target_pairs={{0,16},{4,20},{8,24},{12,28},{16,0},{20,4},{24,8},{28,12},{1,17},{... | collective-permute-start | bytes 294920 | tf_op jit(solution)/shard_map/ppermute | solution.py:81
  106.9 7.8 %collective-permute-start.33 = (bf16[128,384]{1,0:T(8,128)(2,1)S(1)}, bf16[128,384]{1,0:T(8,128)(2,1)S(1)}, u32[]{:S(2)}, u32[]{:S(2)}) collective-permute-start(bf16[128,384]{1,0:T(8,128)(2,1)S(1)} %get-tuple-element.120), channel_id=1, source_target_pairs={{0,24},{4,28},{8,16},{12,20},{16,8},{20,12},{24,0},{28,4},{1,25},{... | collective-permute-start | bytes 294920 | tf_op jit(solution)/shard_map/ppermute | solution.py:81
  (15 other events, 192.0 us)

commit v6 on v5

--- a/solution.py
+++ b/solution.py
@@ -33,8 +33,8 @@
 STREAM_COLS = (0, 4, 8)
 
 COST = {'low': 1.605, 'cut': 0.491, 'turns': 6.876, 'counts': 2.06, 'pool': 4.0, 'stack': 0.045, 'join': 0.7, 'weights': 0.778, 'main': 10.0, 'table': 6.0, 'half': 0.7, 'chip': 0.7, 'near': 1.0, 'sum': 0.5, 'finish': 3.0}
-OPT = {'a': 1, 'b': 0, 'c': 0, 'd': 1, 'e': 0, 'f': 1, 'h': 0, 'i': 0, 'j': 1, 'k': 0, 'm': 3, 'n': 1, 'q': 1, 'g': 2, 'p': 0, 'r': 0}
-RNG = {'a': 4, 'b': 3, 'c': 3, 'd': 2, 'e': 3, 'f': 2, 'h': 2, 'i': 3, 'j': 2, 'k': 2, 'm': 4, 'n': 2, 'q': 2, 'g': 3, 'p': 2, 'r': 2}
+OPT = {'a': 1, 'b': 0, 'c': 0, 'd': 0, 'e': 0, 'f': 1, 'h': 0, 'i': 0, 'j': 1, 'k': 0, 'm': 3, 'n': 1, 'p': 0, 'r': 0, 's': 1}
+RNG = {'a': 4, 'b': 3, 'c': 3, 'd': 2, 'e': 3, 'f': 2, 'h': 2, 'i': 3, 'j': 2, 'k': 4, 'm': 4, 'n': 2, 'p': 2, 'r': 2, 's': 4}
 
 VMEM = pl.BlockSpec(memory_space=pltpu.VMEM)
 SMEM = pl.BlockSpec(memory_space=pltpu.SMEM)
@@ -536,22 +536,41 @@
                 out[rows:, :] = last
 
 
-def chip_merge_kernel(*refs, terms, passing):
-    outs = refs[-1 - passing :]
-    outs[0][...] = total(refs[:terms]).astype(bf16)
-    if passing:
-        outs[1][...] = refs[terms][...]
-
-
-def near_merge_kernel(mine, other, *refs, terms, rows, outer, passing):
-    come, outs = refs[: terms - 1], refs[terms - 1 + passing :]
+def chip_merge_kernel(*refs, terms):
+    refs[-1][...] = total(refs[:terms]).astype(bf16)
+
+
+def stay_kernel(home, come, mixed, order_ref, *outs, rows, inner):
+    cols = home.shape[1]
+    events = mixed.shape[0]
+    for m, out in enumerate(outs):
+        part = slice(m * inner * rows, (m * inner + 1) * rows)
+        out[0:rows, :] = plus(home[part, :], come[part, :])
+        if m:
+            for i in range(mixed.shape[1] // cols):
+                out[rows + i * events : rows + (i + 1) * events, :] = mixed[:, i * cols : (i + 1) * cols]
+
+
+def stay_merge_kernel(*refs, terms, rows):
+    parts, mixed, sums, pieces = refs[:terms], refs[terms], refs[-2], refs[-1]
+    sums[...] = total(parts, slice(0, rows)).astype(bf16)
+    cols = sums.shape[1]
+    pieces[0] = mixed[...]
+    events = mixed.shape[0]
+    for m in range(1, terms):
+        for i in range(mixed.shape[1] // cols):
+            pieces[m, :, i * cols : (i + 1) * cols] = parts[m][
+                rows + i * events : rows + (i + 1) * events, :
+            ]
+
+
+def near_merge_kernel(mine, other, *refs, terms, rows, outer):
+    come, outs = refs[: terms - 1], refs[terms - 1 :]
     last = total((other, *come), slice(outer * rows, None)).astype(bf16)
     for far in range(outer):
         part = slice(far * rows, (far + 1) * rows)
         outs[far][0:rows, :] = total((mine, *come), part).astype(bf16)
         outs[far][rows:, :] = last
-    if passing:
-        outs[outer][...] = refs[terms - 1][...]
 
 
 def stack_kernel(*refs, start):
@@ -569,12 +588,12 @@
         out[place] = early[i] if i < count else late[i - count]
 
 
-def mixed_kernel(*refs, hid):
-    out = refs[hid]
-    rows = refs[0].shape[0]
+def mixed_kernel(own, other, out, *, hid):
+    rows = own.shape[1]
     me = lax.axis_index("hid")
     for m in range(hid):
-        out[pl.ds(pl.multiple_of((me ^ m) * rows, rows), rows), :] = refs[m][...]
+        start = pl.multiple_of((me ^ m) * rows, rows)
+        out[pl.ds(start, rows), :] = other[m // 2] if m % 2 else own[m // 2]
 
 
 def adam(weight, moment, second, average, grad, rate):
@@ -635,7 +654,7 @@
 
 
 def finish_kernel(*refs, table_terms, terms, dp, hid):
-    a, b, c = 4 + table_terms, 16 + terms, hid
+    a, b, c = 4 + table_terms, 16 + terms, 2
     ins, outs = refs[: a + b + c], refs[a + b + c :]
     mixed_kernel(*ins[a + b :], outs[0], hid=hid)
     table_adam_kernel(*ins[:a], *outs[1:5], terms=table_terms)
@@ -892,25 +911,19 @@
             us=COST["half"],
         )
 
-    def chip_sum(parts, order, passing):
-        result = call(
-            functools.partial(chip_merge_kernel, terms=hid // 2, passing=len(passing)),
-            [shape(v.shape, bf16) for v in (parts[0], *passing)],
-            (parts[0], *[swap(parts[m], "hid", 2 * m) for m in range(1, hid // 2)])
-            + (*passing, *order),
-            in_specs=[VMEM] * (hid // 2 + len(passing)) + [ANY] * len(order),
-            vmem=12,
+    def chip_sum(parts, *order):
+        return call(
+            functools.partial(chip_merge_kernel, terms=hid // 2),
+            shape(parts[0].shape, bf16),
+            (parts[0], *[swap(parts[m], "hid", 2 * m) for m in range(1, hid // 2)], *order),
+            in_specs=[VMEM] * (hid // 2) + [ANY] * len(order),
+            vmem=6,
             us=COST["chip"],
         )
-        return result if passing else result[0]
 
     order = ((), (d_pooled[1],), (d_pooled[hid - 1],))[OPT["e"]]
-    if OPT["q"]:
-        parts = half(tuple(range(inner)), *order)
-        parts = [parts[i::inner] for i in range(inner)]
-    else:
-        parts = half(tuple(range(1, inner)), *order)
-        parts = [None] + [parts[i :: inner - 1] for i in range(inner - 1)]
+    parts = half(tuple(range(1, inner)), *order)
+    parts = [None] + [parts[i :: inner - 1] for i in range(inner - 1)]
     d_table = reduce_table((block_owners, parts[1][0])[OPT["f"]])
     sums = {}
     for far in reversed(range(outer)):
@@ -932,41 +945,28 @@
     if OPT["c"] == 2:
         sums[last] = add_up(sums[last])
     orders = ((), (d_table[0],), (sums[last],))[OPT["c"]]
-    chips = [None] + [chip_sum(parts[i], orders, ()) for i in range(1, inner)]
-    order = ((), (chips[1],))[OPT["k"]]
-    if not OPT["q"]:
-        parts[0], order = half((0,), *order), ()
-    if OPT["g"] == 1:
-        chips[0], mixed_part = chip_sum(parts[0], order, (mixed_part,))
-    else:
-        chips[0] = chip_sum(parts[0], order, ())
+    chips = [None] + [chip_sum(parts[i], *orders) for i in range(1, inner)]
+    blocks = O * STREAMS // piece_cols
+    stay = call(
+        functools.partial(stay_kernel, rows=near_rows, inner=inner),
+        [
+            shape((near_rows + blocks * rows * (m > 0), piece_cols), bf16)
+            for m in range(hid // 2)
+        ],
+        (home, come, mixed_part, (block_owners, chips[1], d_table[0], sums[last] if OPT["c"] == 2 else d_table[1])[OPT["k"]]),
+        in_specs=[VMEM] * 3 + [ANY],
+        vmem=8,
+        us=COST["half"],
+    )
     if OPT["c"] != 2:
         sums[last] = add_up(sums[last], *((), (chips[1],))[OPT["d"]])
     later = [far for far in range(1, last) if far % 2] if OPT["p"] and not OPT["h"] else []
     for far in range(last):
         if far not in later:
             sums[far] = functools.reduce(plus, sums[far])
-    passing = (mixed_part,) if OPT["g"] == 0 else ()
-    far_parts = call(
-        functools.partial(
-            near_merge_kernel, terms=inner, rows=piece_rows, outer=outer, passing=len(passing)
-        ),
-        [shape((piece_rows + small_rows, piece_cols), bf16)] * outer
-        + [shape(v.shape, bf16) for v in passing],
-        (chips[0], chips[1], *[swap(chips[i], "dp", i) for i in range(1, inner)], *passing),
-        vmem=12,
-        us=COST["near"],
-    )
-    if passing:
-        mixed_part = far_parts[outer]
-    weight_terms = [far_parts[0]] + [swap(far_parts[m], "dp", m * inner) for m in range(1, outer)]
-
-    mixed_parts = {0: mixed_part}
-    for m in range(2, hid, 2):
-        mixed_parts[m] = swap(mixed_part, "hid", m)
-    for m in range(0, hid, 2):
-        mixed_parts[m + 1] = swap(mixed_parts[m], "hid", 1)
+    recent = sums[last]
     if OPT["h"]:
+        leaves = sums[1]
         table_terms = [sums[0]]
         table_terms += [swap(sums[far], "dp", far * inner) for far in reversed(range(1, outer))]
     else:
@@ -977,7 +977,29 @@
                     sums[far] = add_up(sums[far], sums[(far ^ step) + 2])
                 sums[far ^ step] = plus(sums[far ^ step], swap(sums.pop(far), "dp", step * inner))
             step *= 2
-        table_terms = [sums[0], swap(sums[step], "dp", step * inner)]
+        leaves = sums[step]
+        table_terms = [sums[0], swap(leaves, "dp", step * inner)]
+    order = (block_owners, leaves, sums[0], recent)[OPT["s"]]
+    chips[0], mixed_own = call(
+        functools.partial(stay_merge_kernel, terms=hid // 2, rows=near_rows),
+        [
+            shape((near_rows, piece_cols), bf16),
+            shape((hid // 2, *mixed_part.shape), bf16),
+        ],
+        (stay[0], *[swap(stay[m], "hid", 2 * m) for m in range(1, hid // 2)], mixed_part, order),
+        in_specs=[VMEM] * (hid // 2 + 1) + [ANY],
+        vmem=8,
+        us=COST["chip"],
+    )
+    mixed_list = [mixed_own, swap(mixed_own, "hid", 1)]
+    far_parts = call(
+        functools.partial(near_merge_kernel, terms=inner, rows=piece_rows, outer=outer),
+        [shape((piece_rows + small_rows, piece_cols), bf16)] * outer,
+        (chips[0], chips[1], *[swap(chips[i], "dp", i) for i in range(1, inner)]),
+        vmem=12,
+        us=COST["near"],
+    )
+    weight_terms = [far_parts[0]] + [swap(far_parts[m], "dp", m * inner) for m in range(1, outer)]
 
     states = (
         table_w,
@@ -1008,7 +1030,7 @@
         ),
         [shape((events, O * STREAMS), bf16)] + [shape(v.shape, f32) for v in states],
         (*states[:4], *table_terms, *states[4:], *weight_terms)
-        + tuple(mixed_parts[m] for m in range(hid)),
+        + tuple(mixed_list),
         vmem=20,
         us=COST["finish"],
     )

time: 118 us -> 117 us (level)
  waiting for transfers between devices: 36.3 us -> 32.6 us
  starting transfers between devices: 36 us -> 39.5 us
    ppermute x37 -> x35, waiting for transfers between devices: 36.3 us -> 32.6 us  [swap(): return lax.ppermute(value, axis, [(i, i ^ mask) for i in range(count)])]
    ppermute x37 -> x35, starting transfers between devices: 36 us -> 39.5 us  [swap(): return lax.ppermute(value, axis, [(i, i ^ mask) for i in range(count)])]
    pallas_call x21 -> x22, Pallas kernels: 43.1 us -> 42.9 us  [call(): pl.pallas_call(kernel, out_shape=outs, in_specs=in_specs or [VMEM] * len(...]
  transfers between devices with their start and end apart: 37 -> 35, of which waited for: 18 -> 13; matrix products, arithmetic and copies ran while one was open for 0% -> 0% of each run, Pallas kernels for 25% -> 25%
where the time goes in v6:
time: 117 us
  Pallas kernels  42.9 us (37%)
  starting transfers between devices  39.5 us (34%)
  waiting for transfers between devices  32.6 us (28%)
  between operations  1.47 us (1%)
    pallas_call x22, Pallas kernels, call(): pl.pallas_call(kernel, out_shape=outs, in_specs=in_specs or [VMEM] * len(...  42.9 us
    ppermute x35, starting transfers between devices, swap(): return lax.ppermute(value, axis, [(i, i ^ mask) for i in range(count)])  39.5 us
    ppermute x35, waiting for transfers between devices, swap(): return lax.ppermute(value, axis, [(i, i ^ mask) for i in range(count)])  32.6 us
  transfers between devices with their start and end apart: 35, of which 13 were waited for; matrix products, arithmetic and copies ran while one was open for 0% of the time, Pallas kernels for 25%

profile of v6, /device:TPU:0, one launch (start us, length us, event | category | flops | bytes accessed | tf_op | source)
XLA Modules:
  0.0 116.9 jit_solution(16471641008463039353)
XLA Ops:
  0.7 2.0 %low_kernel.1 = (bf16[1056,128]{1,0:T(8,128)(2,1)}, bf16[1056,128]{1,0:T(8,128)(2,1)}) custom-call(f32[768,128]{1,0:T(8,128)} %refs_0_.1, f32[64,384]{1,0:T(8,128)} %refs_6_.1, f32[64,192]{1,0:T(8,128)} %refs_10_.1), custom_call_target="tpu_custom_call" | custom-call | flops 1604999936 | bytes 4815000 | tf_op jit(solution)/shard_map/low_kernel/pallas_call | solution.py:64
  2.7 4.1 %collective-permute-start.6 = (bf16[1056,128]{1,0:T(8,128)(2,1)}, bf16[1056,128]{1,0:T(8,128)(2,1)S(1)}, u32[]{:S(2)}, u32[]{:S(2)}) collective-permute-start(bf16[1056,128]{1,0:T(8,128)(2,1)} %get-tuple-element.85), channel_id=1, source_target_pairs={{0,16},{4,20},{8,24},{12,28},{16,0},{20,4},{24,8},{28,12},{1,17},{... | collective-permute-start | bytes 811016 | tf_op jit(solution)/shard_map/ppermute | solution.py:81
  6.8 1.6 %collective-permute-start.1 = (bf16[1056,128]{1,0:T(8,128)(2,1)}, bf16[1056,128]{1,0:T(8,128)(2,1)S(1)}, u32[]{:S(2)}, u32[]{:S(2)}) collective-permute-start(bf16[1056,128]{1,0:T(8,128)(2,1)} %get-tuple-element.85), channel_id=1, source_target_pairs={{0,8},{4,12},{8,0},{12,4},{16,24},{20,28},{24,16},{28,20},{1,9},{5... | collective-permute-start | bytes 811016 | tf_op jit(solution)/shard_map/ppermute | solution.py:81
  8.4 0.8 cut_kernel.1
  9.2 1.6 %collective-permute-start.4 = (bf16[224,256]{1,0:T(8,128)(2,1)S(1)}, bf16[224,256]{1,0:T(8,128)(2,1)S(1)}, u32[]{:S(2)}, u32[]{:S(2)}) collective-permute-start(bf16[224,256]{1,0:T(8,128)(2,1)S(1)} %get-tuple-element.88), channel_id=1, source_target_pairs={{0,2},{1,3},{2,0},{3,1},{4,6},{5,7},{6,4},{7,5},{8,10},{9,11},{10,... | collective-permute-start | bytes 344072 | tf_op jit(solution)/shard_map/ppermute | solution.py:81
  11.3 4.3 %counts_kernel.4.refs_0_ = bf16[256,3072]{1,0:T(8,128)(2,1)S(1)} custom-call(s32[1024]{0:T(1024)S(1)} %copy-done.2, s16[16,256,128]{2,1,0:T(8,128)(2,1)S(1)} %get-tuple-element.84.idb, s32[8,128]{1,0:T(8,128)S(1)} %bitcast.15, s32[8,128]{1,0:T(8,128)S(1)} %add_bitcast_fusion.nxt_ref), custom_call_target="tpu_custom_call" | custom-call | flops 2060000000 | bytes 6180000 | tf_op jit(solution)/shard_map/counts_kernel/pallas_call | solution.py:64
  15.5 1.6 %collective-permute-start = (bf16[1056,128]{1,0:T(8,128)(2,1)S(1)}, bf16[1056,128]{1,0:T(8,128)(2,1)S(1)}, u32[]{:S(2)}, u32[]{:S(2)}) collective-permute-start(bf16[1056,128]{1,0:T(8,128)(2,1)S(1)} %copy-done.25), channel_id=1, source_target_pairs={{0,4},{4,0},{8,12},{12,8},{16,20},{20,16},{24,28},{28,24},{1,5},{5... | collective-permute-start | bytes 811016 | tf_op jit(solution)/shard_map/ppermute | solution.py:81
  17.1 2.3 %collective-permute-done.6.refs_8_.refs_2_ = bf16[1056,128]{1,0:T(8,128)(2,1)S(1)} collective-permute-done((bf16[1056,128]{1,0:T(8,128)(2,1)}, bf16[1056,128]{1,0:T(8,128)(2,1)S(1)}, u32[]{:S(2)}, u32[]{:S(2)}) %collective-permute-start.6) | collective-permute-done | bytes 270368 | tf_op jit(solution)/shard_map/ppermute | solution.py:81
  19.4 0.7 collective-permute-start.8
  20.1 2.3 %turns_kernel.1 = (f32[3,6,256,128]{3,2,1,0:T(8,128)S(1)}, bf16[768,768]{1,0:T(8,128)(2,1)S(1)}, bf16[768,768]{1,0:T(8,128)(2,1)S(1)}) custom-call(bf16[224,256]{1,0:T(8,128)(2,1)S(1)} %get-tuple-element.86.refs_0_.refs_4_, bf16[224,256]{1,0:T(8,128)(2,1)S(1)} %collective-permute-done.3.refs_1_.refs_5_, ...), custom_call_target="tpu_custom_call" | custom-call | flops 6876000256 | bytes 20628000 | tf_op jit(solution)/shard_map/turns_kernel/pallas_call | solution.py:64
  22.5 1.6 %collective-permute-start.2 = (bf16[1056,128]{1,0:T(8,128)(2,1)S(1)}, bf16[1056,128]{1,0:T(8,128)(2,1)S(1)}, u32[]{:S(2)}, u32[]{:S(2)}) collective-permute-start(bf16[1056,128]{1,0:T(8,128)(2,1)S(1)} %collective-permute-done.1.refs_6_.refs_1_), channel_id=1, source_target_pairs={{0,4},{4,0},{8,12},{12,8},{16,20},{20,16},{24,28},{28,24},{1,5},{5... | collective-permute-start | bytes 811016 | tf_op jit(solution)/shard_map/ppermute | solution.py:81
  24.0 4.3 %counts_kernel.7.refs_3_ = bf16[256,3072]{1,0:T(8,128)(2,1)S(1)} custom-call(s32[1024]{0:T(1024)S(1)} %copy-done.2, s16[16,256,128]{2,1,0:T(8,128)(2,1)S(1)} %get-tuple-element.84.idb, s32[8,128]{1,0:T(8,128)S(1)} %bitcast.16, s32[8,128]{1,0:T(8,128)S(1)} %add_bitcast_fusion.nxt_ref, bf16[768,768]{1,0:T(8,128)(2,1)S(1)} %get-tuple-element.90.refs_0_.refs_12_), custom_call_target="tpu_custom_call" | custom-call | flops 2060000000 | bytes 6180000 | tf_op jit(solution)/shard_map/counts_kernel/pallas_call | solution.py:64
  28.4 2.0 %collective-permute-start.9 = (bf16[1056,128]{1,0:T(8,128)(2,1)S(1)}, bf16[1056,128]{1,0:T(8,128)(2,1)S(1)}, u32[]{:S(2)}, u32[]{:S(2)}) collective-permute-start(bf16[1056,128]{1,0:T(8,128)(2,1)S(1)} %collective-permute-done.8.refs_10_.refs_3_), channel_id=1, source_target_pairs={{0,4},{4,0},{8,12},{12,8},{16,20},{20,16},{24,28},{28,24},{1,5},{5... | collective-permute-start | bytes 811016 | tf_op jit(solution)/shard_map/ppermute | solution.py:81
  30.4 3.6 %counts_kernel.5.refs_1_ = bf16[256,3072]{1,0:T(8,128)(2,1)S(1)} custom-call(s32[1024]{0:T(1024)S(1)} %copy-done.2, s16[16,256,128]{2,1,0:T(8,128)(2,1)S(1)} %get-tuple-element.84.idb, s32[8,128]{1,0:T(8,128)S(1)} %bitcast.17, s32[8,128]{1,0:T(8,128)S(1)} %add_bitcast_fusion.nxt_ref, bf16[1056,128]{1,0:T(8,128)(2,1)S(1)} %collective-permute-done.refs_0_.refs_5_.refs_4_), custom_call_target="tpu_custom_call" | custom-call | flops 2060000000 | bytes 6180000 | tf_op jit(solution)/shard_map/counts_kernel/pallas_call | solution.py:64
  34.1 1.6 %collective-permute-start.14 = (bf16[5,288,128]{2,1,0:T(8,128)(2,1)S(1)}, bf16[5,288,128]{2,1,0:T(8,128)(2,1)S(1)}, u32[]{:S(2)}, u32[]{:S(2)}) collective-permute-start(bf16[5,288,128]{2,1,0:T(8,128)(2,1)S(1)} %stack_kernel.2.early), channel_id=1, source_target_pairs={{0,2},{1,3},{2,0},{3,1},{4,6},{5,7},{6,4},{7,5},{8,10},{9,11},{10,... | collective-permute-start | bytes 1105928 | tf_op jit(solution)/shard_map/ppermute | solution.py:81
  35.6 4.3 %counts_kernel.6.refs_2_ = bf16[256,3072]{1,0:T(8,128)(2,1)S(1)} custom-call(s32[1024]{0:T(1024)S(1)} %copy-done.2, s16[16,256,128]{2,1,0:T(8,128)(2,1)S(1)} %get-tuple-element.84.idb, s32[8,128]{1,0:T(8,128)S(1)} %bitcast.18, s32[8,128]{1,0:T(8,128)S(1)} %add_bitcast_fusion.nxt_ref, bf16[1056,128]{1,0:T(8,128)(2,1)S(1)} %collective-permute-done.2.refs_0_.refs_7_), custom_call_target="tpu_custom_call" | custom-call | flops 2060000000 | bytes 6180000 | tf_op jit(solution)/shard_map/counts_kernel/pallas_call | solution.py:64
  39.9 2.3 %collective-permute-done.9.refs_11_.refs_2_ = bf16[1056,128]{1,0:T(8,128)(2,1)S(1)} collective-permute-done((bf16[1056,128]{1,0:T(8,128)(2,1)S(1)}, bf16[1056,128]{1,0:T(8,128)(2,1)S(1)}, u32[]{:S(2)}, u32[]{:S(2)}) %collective-permute-start.9) | collective-permute-done | bytes 270368 | tf_op jit(solution)/shard_map/ppermute | solution.py:81
  42.3 1.6 %collective-permute-start.15 = (bf16[3,288,128]{2,1,0:T(8,128)(2,1)S(1)}, bf16[3,288,128]{2,1,0:T(8,128)(2,1)S(1)}, u32[]{:S(2)}, u32[]{:S(2)}) collective-permute-start(bf16[3,288,128]{2,1,0:T(8,128)(2,1)S(1)} %stack_kernel.3.late), channel_id=1, source_target_pairs={{0,2},{1,3},{2,0},{3,1},{4,6},{5,7},{6,4},{7,5},{8,10},{9,11},{10,... | collective-permute-start | bytes 663560 | tf_op jit(solution)/shard_map/ppermute | solution.py:81
  43.8 3.3 %pool_kernel.1 = (bf16[128,256]{1,0:T(8,128)(2,1)S(1)}, bf16[128,256]{1,0:T(8,128)(2,1)S(1)}, bf16[128,256]{1,0:T(8,128)(2,1)S(1)}, bf16[128,256]{1,0:T(8,128)(2,1)S(1)}) custom-call(s32[48]{0:T(128)S(1)} %copy-done.3, bf16[256,3072]{1,0:T(8,128)(2,1)S(1)} %counts_kernel.4.refs_0_, bf16[256,3072]{1,0:T(8,128)(2,1)S(1)} %counts_kernel.5.refs_1_, ...), custom_call_target="tpu_custom_call" | custom-call | flops 4000000000 | bytes 12000000 | tf_op jit(solution)/shard_map/pool_kernel/pallas_call | solution.py:64
  47.3 1.1 collective-permute-done.15.late
  48.6 0.5 collective-permute-start.10
  49.1 1.5 %collective-permute-start.11 = (bf16[128,256]{1,0:T(8,128)(2,1)S(1)}, bf16[128,256]{1,0:T(8,128)(2,1)S(1)}, u32[]{:S(2)}, u32[]{:S(2)}) collective-permute-start(bf16[128,256]{1,0:T(8,128)(2,1)S(1)} %get-tuple-element.94), channel_id=1, source_target_pairs={{0,2},{1,3},{2,0},{3,1},{4,6},{5,7},{6,4},{7,5},{8,10},{9,11},{10,... | collective-permute-start | bytes 196616 | tf_op jit(solution)/shard_map/ppermute | solution.py:81
  50.7 2.9 %weights_kernel.1 = (bf16[6,512,256]{2,1,0:T(8,128)(2,1)S(1)}, bf16[6,256,256]{2,1,0:T(8,128)(2,1)S(1)}) custom-call(bf16[8,288,128]{2,1,0:T(8,128)(2,1)S(1)} %join_kernel.2.refs_0_, bf16[8,288,128]{2,1,0:T(8,128)(2,1)S(1)} %collective-permute-done.13.refs_1_, bf16[8,288,128]{2,1,0:T(8,128)(2,1)S(1)} %join_kernel.3.refs_2_, ...), custom_call_target="tpu_custom_call" | custom-call | flops 778000000 | bytes 2334000 | tf_op jit(solution)/shard_map/weights_kernel/pallas_call | solution.py:64
  53.6 1.4 %collective-permute-done.12.refs_3_ = bf16[128,256]{1,0:T(8,128)(2,1)S(1)} collective-permute-done((bf16[128,256]{1,0:T(8,128)(2,1)S(1)}, bf16[128,256]{1,0:T(8,128)(2,1)S(1)}, u32[]{:S(2)}, u32[]{:S(2)}) %collective-permute-start.12) | collective-permute-done | bytes 65568 | tf_op jit(solution)/shard_map/ppermute | solution.py:81
  55.0 9.7 %main_kernel.1 = (bf16[256,768]{1,0:T(8,128)(2,1)S(1)}, bf16[32,384]{1,0:T(8,128)(2,1)S(1)}, bf16[1536,384]{1,0:T(8,128)(2,1)S(1)}, bf16[1568,384]{1,0:T(8,128)(...) custom-call(bf16[128,256]{1,0:T(8,128)(2,1)S(1)} %get-tuple-element., ...), custom_call_target="tpu_custom_call" | custom-call | flops 10000000000 | bytes 30000000 | tf_op jit(solution)/shard_map/main_kernel/pallas_call | solution.py:64
  64.8 0.4 collective-permute-start.17
  65.3 0.6 collective-permute-start.18
  65.9 0.8 collective-permute-start.19
  66.7 0.9 collective-permute-done.20.come
  67.8 0.8 collective-permute-start.28
  68.7 1.4 %collective-permute-done.18.refs_6_ = bf16[128,256]{1,0:T(8,128)(2,1)S(1)} collective-permute-done((bf16[128,256]{1,0:T(8,128)(2,1)S(1)}, bf16[128,256]{1,0:T(8,128)(2,1)S(1)}, u32[]{:S(2)}, u32[]{:S(2)}) %collective-permute-start.18) | collective-permute-done | bytes 65568 | tf_op jit(solution)/shard_map/ppermute | solution.py:81
  70.3 2.4 %table_kernel.1 = (bf16[768,128]{1,0:T(8,128)(2,1)S(1)}, bf16[768,128]{1,0:T(8,128)(2,1)S(1)}, bf16[768,128]{1,0:T(8,128)(2,1)S(1)}, bf16[768,128]{1,0:T(8,128)(...) custom-call(s32[48]{0:T(128)S(1)} %copy-done.3, ...), custom_call_target="tpu_custom_call" | custom-call | flops 6000000000 | bytes 18000000 | tf_op jit(solution)/shard_map/table_kernel/pallas_call | solution.py:64
  72.7 1.7 %collective-permute-start.25 = (bf16[768,128]{1,0:T(8,128)(2,1)S(1)}, bf16[768,128]{1,0:T(8,128)(2,1)S(1)}, u32[]{:S(2)}, u32[]{:S(2)}) collective-permute-start(bf16[768,128]{1,0:T(8,128)(2,1)S(1)} %get-tuple-element.115), channel_id=1, source_target_pairs={{0,4},{4,0},{8,12},{12,8},{16,20},{20,16},{24,28},{28,24},{1,5},{5... | collective-permute-start | bytes 589832 | tf_op jit(solution)/shard_map/ppermute | solution.py:81
  74.4 0.4 collective-permute-start.24
  74.8 5.7 %collective-permute-done.25.refs_1_ = bf16[768,128]{1,0:T(8,128)(2,1)S(1)} collective-permute-done((bf16[768,128]{1,0:T(8,128)(2,1)S(1)}, bf16[768,128]{1,0:T(8,128)(2,1)S(1)}, u32[]{:S(2)}, u32[]{:S(2)}) %collective-permute-start.25) | collective-permute-done | bytes 196640 | tf_op jit(solution)/shard_map/ppermute | solution.py:81
  80.8 1.6 %collective-permute-start.22 = (bf16[768,128]{1,0:T(8,128)(2,1)S(1)}, bf16[768,128]{1,0:T(8,128)(2,1)S(1)}, u32[]{:S(2)}, u32[]{:S(2)}) collective-permute-start(bf16[768,128]{1,0:T(8,128)(2,1)S(1)} %get-tuple-element.111), channel_id=1, source_target_pairs={{0,4},{4,0},{8,12},{12,8},{16,20},{20,16},{24,28},{28,24},{1,5},{5... | collective-permute-start | bytes 589832 | tf_op jit(solution)/shard_map/ppermute | solution.py:81
  82.3 1.3 %collective-permute-start.29 = (bf16[416,384]{1,0:T(8,128)(2,1)S(1)}, bf16[416,384]{1,0:T(8,128)(2,1)S(1)}, u32[]{:S(2)}, u32[]{:S(2)}) collective-permute-start(bf16[416,384]{1,0:T(8,128)(2,1)S(1)} %get-tuple-element.120), channel_id=1, source_target_pairs={{0,2},{1,3},{2,0},{3,1},{4,6},{5,7},{6,4},{7,5},{8,10},{9,11},{10,... | collective-permute-start | bytes 958472 | tf_op jit(solution)/shard_map/ppermute | solution.py:81
  83.7 1.1 collective-permute-done.24
  84.8 2.4 %collective-permute-done.26 = bf16[768,128]{1,0:T(8,128)(2,1)S(1)} collective-permute-done((bf16[768,128]{1,0:T(8,128)(2,1)S(1)}, bf16[768,128]{1,0:T(8,128)(2,1)S(1)}, u32[]{:S(2)}, u32[]{:S(2)}) %collective-permute-start.26) | collective-permute-done | bytes 196640 | tf_op jit(solution)/shard_map/ppermute | solution.py:81
  87.4 1.7 %collective-permute-start.21 = (bf16[768,128]{1,0:T(8,128)(2,1)S(1)}, bf16[768,128]{1,0:T(8,128)(2,1)S(1)}, u32[]{:S(2)}, u32[]{:S(2)}) collective-permute-start(bf16[768,128]{1,0:T(8,128)(2,1)S(1)} %get-tuple-element.109), channel_id=1, source_target_pairs={{0,4},{4,0},{8,12},{12,8},{16,20},{20,16},{24,28},{28,24},{1,5},{5... | collective-permute-start | bytes 589832 | tf_op jit(solution)/shard_map/ppermute | solution.py:81
  89.1 3.5 %collective-permute-done.29.refs_1_ = bf16[416,384]{1,0:T(8,128)(2,1)S(1)} collective-permute-done((bf16[416,384]{1,0:T(8,128)(2,1)S(1)}, bf16[416,384]{1,0:T(8,128)(2,1)S(1)}, u32[]{:S(2)}, u32[]{:S(2)}) %collective-permute-start.29) | collective-permute-done | bytes 319520 | tf_op jit(solution)/shard_map/ppermute | solution.py:81
  92.6 1.7 %collective-permute-start.30 = (bf16[416,384]{1,0:T(8,128)(2,1)S(1)}, bf16[416,384]{1,0:T(8,128)(2,1)S(1)}, u32[]{:S(2)}, u32[]{:S(2)}) collective-permute-start(bf16[416,384]{1,0:T(8,128)(2,1)S(1)} %chip_merge_kernel.1.other), channel_id=1, source_target_pairs={{0,4},{4,0},{8,12},{12,8},{16,20},{20,16},{24,28},{28,24},{1,5},{5... | collective-permute-start | bytes 958472 | tf_op jit(solution)/shard_map/ppermute | solution.py:81
  94.4 3.8 %collective-permute-start.27 = (bf16[768,128]{1,0:T(8,128)(2,1)S(1)}, bf16[768,128]{1,0:T(8,128)(2,1)S(1)}, u32[]{:S(2)}, u32[]{:S(2)}) collective-permute-start(bf16[768,128]{1,0:T(8,128)(2,1)S(1)} %add_convert_fusion.refs_3_), channel_id=1, source_target_pairs={{0,16},{4,20},{8,24},{12,28},{16,0},{20,4},{24,8},{28,12},{1,17},{... | collective-permute-start | bytes 589832 | tf_op jit(solution)/shard_map/ppermute | solution.py:81
  98.2 3.5 %collective-permute-done.30.refs_0_ = bf16[416,384]{1,0:T(8,128)(2,1)S(1)} collective-permute-done((bf16[416,384]{1,0:T(8,128)(2,1)S(1)}, bf16[416,384]{1,0:T(8,128)(2,1)S(1)}, u32[]{:S(2)}, u32[]{:S(2)}) %collective-permute-start.30) | collective-permute-done | bytes 319520 | tf_op jit(solution)/shard_map/ppermute | solution.py:81
  102.2 3.8 %collective-permute-start.32 = (bf16[128,384]{1,0:T(8,128)(2,1)S(1)}, bf16[128,384]{1,0:T(8,128)(2,1)S(1)}, u32[]{:S(2)}, u32[]{:S(2)}) collective-permute-start(bf16[128,384]{1,0:T(8,128)(2,1)S(1)} %get-tuple-element.123), channel_id=1, source_target_pairs={{0,16},{4,20},{8,24},{12,28},{16,0},{20,4},{24,8},{28,12},{1,17},{... | collective-permute-start | bytes 294920 | tf_op jit(solution)/shard_map/ppermute | solution.py:81
  106.0 1.4 %collective-permute-start.33 = (bf16[128,384]{1,0:T(8,128)(2,1)S(1)}, bf16[128,384]{1,0:T(8,128)(2,1)S(1)}, u32[]{:S(2)}, u32[]{:S(2)}) collective-permute-start(bf16[128,384]{1,0:T(8,128)(2,1)S(1)} %get-tuple-element.124), channel_id=1, source_target_pairs={{0,24},{4,28},{8,16},{12,20},{16,8},{20,12},{24,0},{28,4},{1,25},{... | collective-permute-start | bytes 294920 | tf_op jit(solution)/shard_map/ppermute | solution.py:81
  107.5 6.8 %collective-permute-done.32.refs_24_ = bf16[128,384]{1,0:T(8,128)(2,1)S(1)} collective-permute-done((bf16[128,384]{1,0:T(8,128)(2,1)S(1)}, bf16[128,384]{1,0:T(8,128)(2,1)S(1)}, u32[]{:S(2)}, u32[]{:S(2)}) %collective-permute-start.32) | collective-permute-done | bytes 98336 | tf_op jit(solution)/shard_map/ppermute | solution.py:81
  114.4 2.3 %finish_kernel.1 = (bf16[1024,768]{1,0:T(8,128)(2,1)}, f32[768,128]{1,0:T(8,128)}, f32[768,128]{1,0:T(8,128)}, f32[768,128]{1,0:T(8,128)}, f32[768,128]{1,0:T(8,...) custom-call(f32[768,128]{1,0:T(8,128)S(1)} %copy-done.5, ...), custom_call_target="tpu_custom_call" | custom-call | flops 3000000000 | bytes 9000000 | tf_op jit(solution)/shard_map/finish_kernel/pallas_call | solution.py:64
  (102 shorter events, 2.7 us)
Async XLA Ops:
  2.7 16.7 %collective-permute-start.6 = (bf16[1056,128]{1,0:T(8,128)(2,1)}, bf16[1056,128]{1,0:T(8,128)(2,1)S(1)}, u32[]{:S(2)}, u32[]{:S(2)}) collective-permute-start(bf16[1056,128]{1,0:T(8,128)(2,1)} %get-tuple-element.85), channel_id=1, source_target_pairs={{0,16},{4,20},{8,24},{12,28},{16,0},{20,4},{24,8},{28,12},{1,17},{... | collective-permute-start | bytes 811016 | tf_op jit(solution)/shard_map/ppermute | solution.py:81
  6.8 15.7 %collective-permute-start.1 = (bf16[1056,128]{1,0:T(8,128)(2,1)}, bf16[1056,128]{1,0:T(8,128)(2,1)S(1)}, u32[]{:S(2)}, u32[]{:S(2)}) collective-permute-start(bf16[1056,128]{1,0:T(8,128)(2,1)} %get-tuple-element.85), channel_id=1, source_target_pairs={{0,8},{4,12},{8,0},{12,4},{16,24},{20,28},{24,16},{28,20},{1,9},{5... | collective-permute-start | bytes 811016 | tf_op jit(solution)/shard_map/ppermute | solution.py:81
  9.2 6.4 %collective-permute-start.3 = (bf16[224,256]{1,0:T(8,128)(2,1)S(1)}, bf16[224,256]{1,0:T(8,128)(2,1)S(1)}, u32[]{:S(2)}, u32[]{:S(2)}) collective-permute-start(bf16[224,256]{1,0:T(8,128)(2,1)S(1)} %get-tuple-element.87), channel_id=1, source_target_pairs={{0,1},{1,0},{2,3},{3,2},{4,5},{5,4},{6,7},{7,6},{8,9},{9,8},{10,11... | collective-permute-start | bytes 344072 | tf_op jit(solution)/shard_map/ppermute | solution.py:81
  9.2 10.9 %collective-permute-start.4 = (bf16[224,256]{1,0:T(8,128)(2,1)S(1)}, bf16[224,256]{1,0:T(8,128)(2,1)S(1)}, u32[]{:S(2)}, u32[]{:S(2)}) collective-permute-start(bf16[224,256]{1,0:T(8,128)(2,1)S(1)} %get-tuple-element.88), channel_id=1, source_target_pairs={{0,2},{1,3},{2,0},{3,1},{4,6},{5,7},{6,4},{7,5},{8,10},{9,11},{10,... | collective-permute-start | bytes 344072 | tf_op jit(solution)/shard_map/ppermute | solution.py:81
  10.8 9.3 %collective-permute-start.5 = (bf16[224,256]{1,0:T(8,128)(2,1)S(1)}, bf16[224,256]{1,0:T(8,128)(2,1)S(1)}, u32[]{:S(2)}, u32[]{:S(2)}) collective-permute-start(bf16[224,256]{1,0:T(8,128)(2,1)S(1)} %get-tuple-element.89), channel_id=1, source_target_pairs={{0,3},{1,2},{2,1},{3,0},{4,7},{5,6},{6,5},{7,4},{8,11},{9,10},{10,... | collective-permute-start | bytes 344072 | tf_op jit(solution)/shard_map/ppermute | solution.py:81
  15.5 14.9 %collective-permute-start = (bf16[1056,128]{1,0:T(8,128)(2,1)S(1)}, bf16[1056,128]{1,0:T(8,128)(2,1)S(1)}, u32[]{:S(2)}, u32[]{:S(2)}) collective-permute-start(bf16[1056,128]{1,0:T(8,128)(2,1)S(1)} %copy-done.25), channel_id=1, source_target_pairs={{0,4},{4,0},{8,12},{12,8},{16,20},{20,16},{24,28},{28,24},{1,5},{5... | collective-permute-start | bytes 811016 | tf_op jit(solution)/shard_map/ppermute | solution.py:81
  19.4 9.0 %collective-permute-start.8 = (bf16[1056,128]{1,0:T(8,128)(2,1)S(1)}, bf16[1056,128]{1,0:T(8,128)(2,1)S(1)}, u32[]{:S(2)}, u32[]{:S(2)}) collective-permute-start(bf16[1056,128]{1,0:T(8,128)(2,1)S(1)} %collective-permute-done.6.refs_8_.refs_2_), channel_id=1, source_target_pairs={{0,8},{4,12},{8,0},{12,4},{16,24},{20,28},{24,16},{28,20},{1,9},{5... | collective-permute-start | bytes 811016 | tf_op jit(solution)/shard_map/ppermute | solution.py:81
  22.5 13.2 %collective-permute-start.2 = (bf16[1056,128]{1,0:T(8,128)(2,1)S(1)}, bf16[1056,128]{1,0:T(8,128)(2,1)S(1)}, u32[]{:S(2)}, u32[]{:S(2)}) collective-permute-start(bf16[1056,128]{1,0:T(8,128)(2,1)S(1)} %collective-permute-done.1.refs_6_.refs_1_), channel_id=1, source_target_pairs={{0,4},{4,0},{8,12},{12,8},{16,20},{20,16},{24,28},{28,24},{1,5},{5... | collective-permute-start | bytes 811016 | tf_op jit(solution)/shard_map/ppermute | solution.py:81
  28.3 11.6 %collective-permute-start.7 = (bf16[1056,128]{1,0:T(8,128)(2,1)S(1)}, bf16[1056,128]{1,0:T(8,128)(2,1)S(1)}, u32[]{:S(2)}, u32[]{:S(2)}) collective-permute-start(bf16[1056,128]{1,0:T(8,128)(2,1)S(1)} %collective-permute-done.6.refs_8_.refs_2_), channel_id=1, source_target_pairs={{0,4},{4,0},{8,12},{12,8},{16,20},{20,16},{24,28},{28,24},{1,5},{5... | collective-permute-start | bytes 811016 | tf_op jit(solution)/shard_map/ppermute | solution.py:81
  28.4 13.9 %collective-permute-start.9 = (bf16[1056,128]{1,0:T(8,128)(2,1)S(1)}, bf16[1056,128]{1,0:T(8,128)(2,1)S(1)}, u32[]{:S(2)}, u32[]{:S(2)}) collective-permute-start(bf16[1056,128]{1,0:T(8,128)(2,1)S(1)} %collective-permute-done.8.refs_10_.refs_3_), channel_id=1, source_target_pairs={{0,4},{4,0},{8,12},{12,8},{16,20},{20,16},{24,28},{28,24},{1,5},{5... | collective-permute-start | bytes 811016 | tf_op jit(solution)/shard_map/ppermute | solution.py:81
  34.1 13.3 %collective-permute-start.14 = (bf16[5,288,128]{2,1,0:T(8,128)(2,1)S(1)}, bf16[5,288,128]{2,1,0:T(8,128)(2,1)S(1)}, u32[]{:S(2)}, u32[]{:S(2)}) collective-permute-start(bf16[5,288,128]{2,1,0:T(8,128)(2,1)S(1)} %stack_kernel.2.early), channel_id=1, source_target_pairs={{0,2},{1,3},{2,0},{3,1},{4,6},{5,7},{6,4},{7,5},{8,10},{9,11},{10,... | collective-permute-start | bytes 1105928 | tf_op jit(solution)/shard_map/ppermute | solution.py:81
  42.3 6.2 %collective-permute-start.15 = (bf16[3,288,128]{2,1,0:T(8,128)(2,1)S(1)}, bf16[3,288,128]{2,1,0:T(8,128)(2,1)S(1)}, u32[]{:S(2)}, u32[]{:S(2)}) collective-permute-start(bf16[3,288,128]{2,1,0:T(8,128)(2,1)S(1)} %stack_kernel.3.late), channel_id=1, source_target_pairs={{0,2},{1,3},{2,0},{3,1},{4,6},{5,7},{6,4},{7,5},{8,10},{9,11},{10,... | collective-permute-start | bytes 663560 | tf_op jit(solution)/shard_map/ppermute | solution.py:81
  47.2 3.4 %collective-permute-start.13 = (bf16[8,288,128]{2,1,0:T(8,128)(2,1)S(1)}, bf16[8,288,128]{2,1,0:T(8,128)(2,1)S(1)}, u32[]{:S(2)}, u32[]{:S(2)}) collective-permute-start(bf16[8,288,128]{2,1,0:T(8,128)(2,1)S(1)} %join_kernel.2.refs_0_), channel_id=1, source_target_pairs={{0,1},{1,0},{2,3},{3,2},{4,5},{5,4},{6,7},{7,6},{8,9},{9,8},{10,11... | collective-permute-start | bytes 1769480 | tf_op jit(solution)/shard_map/ppermute | solution.py:81
  48.5 2.2 %collective-permute-start.16 = (bf16[8,288,128]{2,1,0:T(8,128)(2,1)S(1)}, bf16[8,288,128]{2,1,0:T(8,128)(2,1)S(1)}, u32[]{:S(2)}, u32[]{:S(2)}) collective-permute-start(bf16[8,288,128]{2,1,0:T(8,128)(2,1)S(1)} %join_kernel.3.refs_2_), channel_id=1, source_target_pairs={{0,1},{1,0},{2,3},{3,2},{4,5},{5,4},{6,7},{7,6},{8,9},{9,8},{10,11... | collective-permute-start | bytes 1769480 | tf_op jit(solution)/shard_map/ppermute | solution.py:81
  48.6 5.0 %collective-permute-start.10 = (bf16[128,256]{1,0:T(8,128)(2,1)S(1)}, bf16[128,256]{1,0:T(8,128)(2,1)S(1)}, u32[]{:S(2)}, u32[]{:S(2)}) collective-permute-start(bf16[128,256]{1,0:T(8,128)(2,1)S(1)} %get-tuple-element.93), channel_id=1, source_target_pairs={{0,1},{1,0},{2,3},{3,2},{4,5},{5,4},{6,7},{7,6},{8,9},{9,8},{10,11... | collective-permute-start | bytes 196616 | tf_op jit(solution)/shard_map/ppermute | solution.py:81
  49.1 4.5 %collective-permute-start.11 = (bf16[128,256]{1,0:T(8,128)(2,1)S(1)}, bf16[128,256]{1,0:T(8,128)(2,1)S(1)}, u32[]{:S(2)}, u32[]{:S(2)}) collective-permute-start(bf16[128,256]{1,0:T(8,128)(2,1)S(1)} %get-tuple-element.94), channel_id=1, source_target_pairs={{0,2},{1,3},{2,0},{3,1},{4,6},{5,7},{6,4},{7,5},{8,10},{9,11},{10,... | collective-permute-start | bytes 196616 | tf_op jit(solution)/shard_map/ppermute | solution.py:81
  50.6 4.4 %collective-permute-start.12 = (bf16[128,256]{1,0:T(8,128)(2,1)S(1)}, bf16[128,256]{1,0:T(8,128)(2,1)S(1)}, u32[]{:S(2)}, u32[]{:S(2)}) collective-permute-start(bf16[128,256]{1,0:T(8,128)(2,1)S(1)} %get-tuple-element.95), channel_id=1, source_target_pairs={{0,3},{1,2},{2,1},{3,0},{4,7},{5,6},{6,5},{7,4},{8,11},{9,10},{10,... | collective-permute-start | bytes 196616 | tf_op jit(solution)/shard_map/ppermute | solution.py:81
  64.7 2.9 %collective-permute-start.20 = (bf16[1568,384]{1,0:T(8,128)(2,1)S(1)}, bf16[1568,384]{1,0:T(8,128)(2,1)S(1)}, u32[]{:S(2)}, u32[]{:S(2)}) collective-permute-start(bf16[1568,384]{1,0:T(8,128)(2,1)S(1)} %get-tuple-element.105), channel_id=1, source_target_pairs={{0,1},{1,0},{2,3},{3,2},{4,5},{5,4},{6,7},{7,6},{8,9},{9,8},{10,11... | collective-permute-start | bytes 3612680 | tf_op jit(solution)/shard_map/ppermute | solution.py:81
  64.8 3.9 %collective-permute-start.17 = (bf16[128,256]{1,0:T(8,128)(2,1)S(1)}, bf16[128,256]{1,0:T(8,128)(2,1)S(1)}, u32[]{:S(2)}, u32[]{:S(2)}) collective-permute-start(bf16[128,256]{1,0:T(8,128)(2,1)S(1)} %get-tuple-element.101), channel_id=1, source_target_pairs={{0,1},{1,0},{2,3},{3,2},{4,5},{5,4},{6,7},{7,6},{8,9},{9,8},{10,11... | collective-permute-start | bytes 196616 | tf_op jit(solution)/shard_map/ppermute | solution.py:81
  65.3 4.9 %collective-permute-start.18 = (bf16[128,256]{1,0:T(8,128)(2,1)S(1)}, bf16[128,256]{1,0:T(8,128)(2,1)S(1)}, u32[]{:S(2)}, u32[]{:S(2)}) collective-permute-start(bf16[128,256]{1,0:T(8,128)(2,1)S(1)} %get-tuple-element.102), channel_id=1, source_target_pairs={{0,2},{1,3},{2,0},{3,1},{4,6},{5,7},{6,4},{7,5},{8,10},{9,11},{10,... | collective-permute-start | bytes 196616 | tf_op jit(solution)/shard_map/ppermute | solution.py:81
  65.9 4.4 %collective-permute-start.19 = (bf16[128,256]{1,0:T(8,128)(2,1)S(1)}, bf16[128,256]{1,0:T(8,128)(2,1)S(1)}, u32[]{:S(2)}, u32[]{:S(2)}) collective-permute-start(bf16[128,256]{1,0:T(8,128)(2,1)S(1)} %get-tuple-element.103), channel_id=1, source_target_pairs={{0,3},{1,2},{2,1},{3,0},{4,7},{5,6},{6,5},{7,4},{8,11},{9,10},{10,... | collective-permute-start | bytes 196616 | tf_op jit(solution)/shard_map/ppermute | solution.py:81
  67.8 19.4 %collective-permute-start.28 = (bf16[896,384]{1,0:T(8,128)(2,1)S(1)}, bf16[896,384]{1,0:T(8,128)(2,1)S(1)}, u32[]{:S(2)}, u32[]{:S(2)}) collective-permute-start(bf16[896,384]{1,0:T(8,128)(2,1)S(1)} %get-tuple-element.118), channel_id=1, source_target_pairs={{0,2},{1,3},{2,0},{3,1},{4,6},{5,7},{6,4},{7,5},{8,10},{9,11},{10,... | collective-permute-start | bytes 2064392 | tf_op jit(solution)/shard_map/ppermute | solution.py:81
  72.7 7.8 %collective-permute-start.25 = (bf16[768,128]{1,0:T(8,128)(2,1)S(1)}, bf16[768,128]{1,0:T(8,128)(2,1)S(1)}, u32[]{:S(2)}, u32[]{:S(2)}) collective-permute-start(bf16[768,128]{1,0:T(8,128)(2,1)S(1)} %get-tuple-element.115), channel_id=1, source_target_pairs={{0,4},{4,0},{8,12},{12,8},{16,20},{20,16},{24,28},{28,24},{1,5},{5... | collective-permute-start | bytes 589832 | tf_op jit(solution)/shard_map/ppermute | solution.py:81
  74.4 10.4 %collective-permute-start.24 = (bf16[768,128]{1,0:T(8,128)(2,1)S(1)}, bf16[768,128]{1,0:T(8,128)(2,1)S(1)}, u32[]{:S(2)}, u32[]{:S(2)}) collective-permute-start(bf16[768,128]{1,0:T(8,128)(2,1)S(1)} %get-tuple-element.113), channel_id=1, source_target_pairs={{0,4},{4,0},{8,12},{12,8},{16,20},{20,16},{24,28},{28,24},{1,5},{5... | collective-permute-start | bytes 589832 | tf_op jit(solution)/shard_map/ppermute | solution.py:81
  80.6 6.5 %collective-permute-start.26 = (bf16[768,128]{1,0:T(8,128)(2,1)S(1)}, bf16[768,128]{1,0:T(8,128)(2,1)S(1)}, u32[]{:S(2)}, u32[]{:S(2)}) collective-permute-start(bf16[768,128]{1,0:T(8,128)(2,1)S(1)} %sum_kernel.1), channel_id=1, source_target_pairs={{0,8},{4,12},{8,0},{12,4},{16,24},{20,28},{24,16},{28,20},{1,9},{5... | collective-permute-start | bytes 589832 | tf_op jit(solution)/shard_map/ppermute | solution.py:81
  80.8 13.5 %collective-permute-start.22 = (bf16[768,128]{1,0:T(8,128)(2,1)S(1)}, bf16[768,128]{1,0:T(8,128)(2,1)S(1)}, u32[]{:S(2)}, u32[]{:S(2)}) collective-permute-start(bf16[768,128]{1,0:T(8,128)(2,1)S(1)} %get-tuple-element.111), channel_id=1, source_target_pairs={{0,4},{4,0},{8,12},{12,8},{16,20},{20,16},{24,28},{28,24},{1,5},{5... | collective-permute-start | bytes 589832 | tf_op jit(solution)/shard_map/ppermute | solution.py:81
  82.3 10.2 %collective-permute-start.29 = (bf16[416,384]{1,0:T(8,128)(2,1)S(1)}, bf16[416,384]{1,0:T(8,128)(2,1)S(1)}, u32[]{:S(2)}, u32[]{:S(2)}) collective-permute-start(bf16[416,384]{1,0:T(8,128)(2,1)S(1)} %get-tuple-element.120), channel_id=1, source_target_pairs={{0,2},{1,3},{2,0},{3,1},{4,6},{5,7},{6,4},{7,5},{8,10},{9,11},{10,... | collective-permute-start | bytes 958472 | tf_op jit(solution)/shard_map/ppermute | solution.py:81
  87.3 26.9 %collective-permute-start.34 = (bf16[2,256,768]{2,1,0:T(8,128)(2,1)S(1)}, bf16[2,256,768]{2,1,0:T(8,128)(2,1)S(1)}, u32[]{:S(2)}, u32[]{:S(2)}) collective-permute-start(bf16[2,256,768]{2,1,0:T(8,128)(2,1)S(1)} %get-tuple-element.125.refs_26_), channel_id=1, source_target_pairs={{0,1},{1,0},{2,3},{3,2},{4,5},{5,4},{6,7},{7,6},{8,9},{9,8},{10,11... | collective-permute-start | bytes 2359304 | tf_op jit(solution)/shard_map/ppermute | solution.py:81
  87.4 14.8 %collective-permute-start.21 = (bf16[768,128]{1,0:T(8,128)(2,1)S(1)}, bf16[768,128]{1,0:T(8,128)(2,1)S(1)}, u32[]{:S(2)}, u32[]{:S(2)}) collective-permute-start(bf16[768,128]{1,0:T(8,128)(2,1)S(1)} %get-tuple-element.109), channel_id=1, source_target_pairs={{0,4},{4,0},{8,12},{12,8},{16,20},{20,16},{24,28},{28,24},{1,5},{5... | collective-permute-start | bytes 589832 | tf_op jit(solution)/shard_map/ppermute | solution.py:81
  92.6 9.2 %collective-permute-start.30 = (bf16[416,384]{1,0:T(8,128)(2,1)S(1)}, bf16[416,384]{1,0:T(8,128)(2,1)S(1)}, u32[]{:S(2)}, u32[]{:S(2)}) collective-permute-start(bf16[416,384]{1,0:T(8,128)(2,1)S(1)} %chip_merge_kernel.1.other), channel_id=1, source_target_pairs={{0,4},{4,0},{8,12},{12,8},{16,20},{20,16},{24,28},{28,24},{1,5},{5... | collective-permute-start | bytes 958472 | tf_op jit(solution)/shard_map/ppermute | solution.py:81
  94.3 11.6 %collective-permute-start.23 = (bf16[768,128]{1,0:T(8,128)(2,1)S(1)}, bf16[768,128]{1,0:T(8,128)(2,1)S(1)}, u32[]{:S(2)}, u32[]{:S(2)}) collective-permute-start(bf16[768,128]{1,0:T(8,128)(2,1)S(1)} %add_convert_fusion.3), channel_id=1, source_target_pairs={{0,8},{4,12},{8,0},{12,4},{16,24},{20,28},{24,16},{28,20},{1,9},{5... | collective-permute-start | bytes 589832 | tf_op jit(solution)/shard_map/ppermute | solution.py:81
  94.4 13.1 %collective-permute-start.27 = (bf16[768,128]{1,0:T(8,128)(2,1)S(1)}, bf16[768,128]{1,0:T(8,128)(2,1)S(1)}, u32[]{:S(2)}, u32[]{:S(2)}) collective-permute-start(bf16[768,128]{1,0:T(8,128)(2,1)S(1)} %add_convert_fusion.refs_3_), channel_id=1, source_target_pairs={{0,16},{4,20},{8,24},{12,28},{16,0},{20,4},{24,8},{28,12},{1,17},{... | collective-permute-start | bytes 589832 | tf_op jit(solution)/shard_map/ppermute | solution.py:81
  101.8 12.5 %copy-start.6 = (f32[768,128]{1,0:T(8,128)S(1)}, f32[768,128]{1,0:T(8,128)}, u32[]{:S(2)}) copy-start(f32[768,128]{1,0:T(8,128)} %refs_1_.1) | copy-start | bytes 1179652
  101.8 12.5 %copy-start.7 = (f32[768,128]{1,0:T(8,128)S(1)}, f32[768,128]{1,0:T(8,128)}, u32[]{:S(2)}) copy-start(f32[768,128]{1,0:T(8,128)} %refs_2_.1) | copy-start | bytes 1179652
  101.8 12.5 %copy-start.8 = (f32[768,128]{1,0:T(8,128)S(1)}, f32[768,128]{1,0:T(8,128)}, u32[]{:S(2)}) copy-start(f32[768,128]{1,0:T(8,128)} %refs_3_.1) | copy-start | bytes 1179652
  101.8 12.5 %copy-start.9 = (f32[64,384]{1,0:T(8,128)S(1)}, f32[64,384]{1,0:T(8,128)}, u32[]{:S(2)}) copy-start(f32[64,384]{1,0:T(8,128)} %refs_6_.1) | copy-start | bytes 294916
  101.8 12.5 %copy-start.10 = (f32[64,384]{1,0:T(8,128)S(1)}, f32[64,384]{1,0:T(8,128)}, u32[]{:S(2)}) copy-start(f32[64,384]{1,0:T(8,128)} %refs_7_.1) | copy-start | bytes 294916
  101.8 12.5 %copy-start.11 = (f32[64,384]{1,0:T(8,128)S(1)}, f32[64,384]{1,0:T(8,128)}, u32[]{:S(2)}) copy-start(f32[64,384]{1,0:T(8,128)} %refs_8_.1) | copy-start | bytes 294916
  101.8 12.5 %copy-start.12 = (f32[64,384]{1,0:T(8,128)S(1)}, f32[64,384]{1,0:T(8,128)}, u32[]{:S(2)}) copy-start(f32[64,384]{1,0:T(8,128)} %refs_9_.1) | copy-start | bytes 294916
  101.8 12.5 %copy-start.13 = (f32[64,192]{1,0:T(8,128)S(1)}, f32[64,192]{1,0:T(8,128)}, u32[]{:S(2)}) copy-start(f32[64,192]{1,0:T(8,128)} %refs_10_.1) | copy-start | bytes 147460
  101.8 12.5 %copy-start.14 = (f32[64,192]{1,0:T(8,128)S(1)}, f32[64,192]{1,0:T(8,128)}, u32[]{:S(2)}) copy-start(f32[64,192]{1,0:T(8,128)} %refs_11_.1) | copy-start | bytes 147460
  101.8 12.5 %copy-start.15 = (f32[64,192]{1,0:T(8,128)S(1)}, f32[64,192]{1,0:T(8,128)}, u32[]{:S(2)}) copy-start(f32[64,192]{1,0:T(8,128)} %refs_12_.1) | copy-start | bytes 147460
  101.9 12.5 %copy-start.16 = (f32[64,192]{1,0:T(8,128)S(1)}, f32[64,192]{1,0:T(8,128)}, u32[]{:S(2)}) copy-start(f32[64,192]{1,0:T(8,128)} %refs_13_.1) | copy-start | bytes 147460
  101.9 12.5 %copy-start.17 = (f32[512,14]{0,1:T(8,128)S(1)}, f32[512,14]{0,1:T(8,128)}, u32[]{:S(2)}) copy-start(f32[512,14]{0,1:T(8,128)} %param.45) | copy-start | bytes 86020
  101.9 12.5 %copy-start.18 = (f32[512,14]{0,1:T(8,128)S(1)}, f32[512,14]{0,1:T(8,128)}, u32[]{:S(2)}) copy-start(f32[512,14]{0,1:T(8,128)} %param.46) | copy-start | bytes 86020
  102.0 5.4 %collective-permute-start.31 = (bf16[128,384]{1,0:T(8,128)(2,1)S(1)}, bf16[128,384]{1,0:T(8,128)(2,1)S(1)}, u32[]{:S(2)}, u32[]{:S(2)}) collective-permute-start(bf16[128,384]{1,0:T(8,128)(2,1)S(1)} %get-tuple-element.122), channel_id=1, source_target_pairs={{0,8},{4,12},{8,0},{12,4},{16,24},{20,28},{24,16},{28,20},{1,9},{5... | collective-permute-start | bytes 294920 | tf_op jit(solution)/shard_map/ppermute | solution.py:81
  102.2 12.0 %collective-permute-start.32 = (bf16[128,384]{1,0:T(8,128)(2,1)S(1)}, bf16[128,384]{1,0:T(8,128)(2,1)S(1)}, u32[]{:S(2)}, u32[]{:S(2)}) collective-permute-start(bf16[128,384]{1,0:T(8,128)(2,1)S(1)} %get-tuple-element.123), channel_id=1, source_target_pairs={{0,16},{4,20},{8,24},{12,28},{16,0},{20,4},{24,8},{28,12},{1,17},{... | collective-permute-start | bytes 294920 | tf_op jit(solution)/shard_map/ppermute | solution.py:81
  106.0 8.3 %collective-permute-start.33 = (bf16[128,384]{1,0:T(8,128)(2,1)S(1)}, bf16[128,384]{1,0:T(8,128)(2,1)S(1)}, u32[]{:S(2)}, u32[]{:S(2)}) collective-permute-start(bf16[128,384]{1,0:T(8,128)(2,1)S(1)} %get-tuple-element.124), channel_id=1, source_target_pairs={{0,24},{4,28},{8,16},{12,20},{16,8},{20,12},{24,0},{28,4},{1,25},{... | collective-permute-start | bytes 294920 | tf_op jit(solution)/shard_map/ppermute | solution.py:81
  (13 other events, 113.0 us)
